TPU v7x, 128 devices: a whole 4x4x4 slice. The times are simulated.
128 devices in a mesh: fsdp: 128 (over x, y, z, core).
Axes of the slice: x: 4, y: 4, z: 4, core: 2. Of those that a mesh axis runs over, the one named last changes fastest.
Arguments:
- hidden_in: bfloat16 [16384, 576], P('fsdp'), may hold values from -6 to 6
- segment_ids: int32 [16384], P('fsdp'), may hold values from 0 to 16383, as said below
- weights_flat: bfloat16 [2, 3540096], P(None, 'fsdp'), may hold values from -2 to 2, as said below
- cotangent: bfloat16 [16384, 576], P('fsdp'), may hold values from -6 to 6
Outputs:
- layer_out: bfloat16 [16384, 576], P('fsdp')
- grad_input: float32 [16384, 576], P('fsdp')
- grad_weights: float32 [2, 3540096], P(None, 'fsdp')
Inputs may be any that keep to these rules, and one draw needn't show every extreme that they name: segment_ids[t] is the index of the first token of t's document; ids never fall; every document holds 1 to 1024 tokens and one holds exactly 1024. `weights_flat`: gain entries lie in 0.7 to 1.3.
All inputs are finite; a program needn't handle non-finite values.
Results may differ from a plain program's by a relative error of at most 0.025.
Values may be sent and summed in bfloat16 or wider, within the bound.
No kernel may reach another device: no remote copies, remote signals or barrier semaphores. Data moves between devices by JAX's collectives and lax.ppermute only.
A program may use at most 192 MiB of HBM per device.

v0:
```python
import jax
import jax.numpy as jnp
from jax import lax
from jax.sharding import PartitionSpec as P

D = 576
FF = 1536
QH = 9
KVH = 3
HD = 64
MAXLEN = 1024


epsilon = 1e-05
rope_base = 10000.0


def passed_along(shard, axis, by):
    length = lax.axis_size(axis)
    pairs = [(i, i + by) for i in range(length) if 0 <= i + by < length]
    return lax.ppermute(shard, axis, pairs)


def rotate_half(values):
    half_size = values.shape[-1] // 2
    return jnp.concatenate([-values[..., half_size:], values[..., :half_size]], axis=-1)


def rope_tables(positions, head_size):
    half_size = head_size // 2
    frequency = rope_base ** (-jnp.arange(half_size, dtype=jnp.float32) / half_size)
    angles = positions.astype(jnp.float32)[:, None] * frequency[None, :]
    angles = jnp.concatenate([angles, angles], axis=-1)
    return (jnp.cos(angles), jnp.sin(angles))


def apply_rope(values, cosine, sine):
    return values * cosine[:, None, :] + rotate_half(values) * sine[:, None, :]


def rope_back(values, cosine, sine):
    return values * cosine[:, None, :] - rotate_half(values) * sine[:, None, :]


def unpack(flat):
    qkv_width = (QH + 2 * KVH) * HD
    sizes_list = [D, D * qkv_width, QH * HD * D, D, 2 * D * FF, FF * D]
    shapes_list = [(D,), (D, qkv_width), (QH * HD, D), (D,), (D, 2 * FF), (FF, D)]
    pieces = []
    offset = 0
    for piece_size, piece_shape in zip(sizes_list, shapes_list):
        pieces.append(flat[offset : offset + piece_size].reshape(piece_shape))
        offset = offset + piece_size
    return pieces


def inverse_norm(values):
    return lax.rsqrt(jnp.mean(values * values, axis=-1, keepdims=True) + epsilon)


def norm_back(values, inverse, gain, grad):
    grad_gain = jnp.sum(grad * values * inverse, axis=0)
    weighted = grad * gain.astype(jnp.float32)
    grad_values = inverse * weighted - values * inverse**3 * jnp.mean(
        weighted * values, axis=-1, keepdims=True
    )
    return (grad_gain, grad_values)


def earlier_rows(keys, values, window):
    pieces = []
    for distance in range(window, 0, -1):
        pieces.append(passed_along((keys, values), "fsdp", distance))
    keys_all = jnp.concatenate([piece[0] for piece in pieces] + [keys], axis=0)
    values_all = jnp.concatenate([piece[1] for piece in pieces] + [values], axis=0)
    return (keys_all, values_all)


def return_rows(grad_keys_all, grad_values_all, window, row_count):

    def rows_of(distance):
        begin = (window - distance) * row_count
        return (
            grad_keys_all[begin : begin + row_count],
            grad_values_all[begin : begin + row_count],
        )

    own_keys, own_values = rows_of(0)
    for distance in range(1, window + 1):
        piece = rows_of(distance)
        back = (
            passed_along(piece[0].astype(jnp.bfloat16), "fsdp", -distance).astype(jnp.float32),
            passed_along(piece[1].astype(jnp.bfloat16), "fsdp", -distance).astype(jnp.float32),
        )
        own_keys = own_keys + back[0]
        own_values = own_values + back[1]
    return (own_keys, own_values)


def head_scores(query, keys, allowed):
    scores = jnp.einsum("qgd,td->gqt", query, keys, preferred_element_type=jnp.float32) * HD ** (
        -0.5
    )
    return jnp.where(allowed[None, :, :], scores, -1e30)


def forward_layer(residual, weights, cosine, sine, allowed, window):
    gain_one, w_qkv, w_out, gain_two, w_in, w_down = weights
    row_count = residual.shape[0]
    query_width = QH * HD
    kv_width = KVH * HD
    group = QH // KVH
    inverse_one = inverse_norm(residual)
    normed = (residual * inverse_one * gain_one.astype(jnp.float32)).astype(jnp.bfloat16)
    project = jnp.dot(normed, w_qkv, preferred_element_type=jnp.float32)
    query = apply_rope(project[:, :query_width].reshape(row_count, QH, HD), cosine, sine).astype(
        jnp.bfloat16
    )
    keys = apply_rope(
        project[:, query_width : query_width + kv_width].reshape(row_count, KVH, HD), cosine, sine
    ).astype(jnp.bfloat16)
    values = project[:, query_width + kv_width :].reshape(row_count, KVH, HD).astype(jnp.bfloat16)
    keys_all, values_all = earlier_rows(keys, values, window)
    query_heads = query.reshape(row_count, KVH, group, HD).transpose(1, 0, 2, 3)
    key_heads = keys_all.transpose(1, 0, 2)
    value_heads = values_all.transpose(1, 0, 2)

    def head_forward(pieces):
        head_query, head_keys, head_values = pieces
        scores = head_scores(head_query, head_keys, allowed)
        peak = jnp.max(scores, axis=-1, keepdims=True)
        log_total = peak + jnp.log(jnp.sum(jnp.exp(scores - peak), axis=-1, keepdims=True))
        probs = jnp.exp(scores - log_total).astype(jnp.bfloat16)
        head_mixed = jnp.einsum(
            "gqt,td->qgd", probs, head_values, preferred_element_type=jnp.float32
        )
        return (head_mixed, log_total)

    mixed_heads, log_total = lax.map(head_forward, (query_heads, key_heads, value_heads))
    mixed = mixed_heads.transpose(1, 0, 2, 3).reshape(row_count, query_width).astype(jnp.bfloat16)
    middle = residual + jnp.dot(mixed, w_out, preferred_element_type=jnp.float32)
    inverse_two = inverse_norm(middle)
    normed_two = (middle * inverse_two * gain_two.astype(jnp.float32)).astype(jnp.bfloat16)
    gate_up = jnp.dot(normed_two, w_in, preferred_element_type=jnp.float32)
    gate_part = gate_up[:, :FF]
    up_part = gate_up[:, FF:]
    hidden_units = (gate_part * jax.nn.sigmoid(gate_part) * up_part).astype(jnp.bfloat16)
    result = middle + jnp.dot(hidden_units, w_down, preferred_element_type=jnp.float32)
    saved = (
        residual,
        inverse_one,
        normed,
        query_heads,
        key_heads,
        value_heads,
        log_total,
        mixed,
        middle,
        inverse_two,
        normed_two,
        gate_up,
        hidden_units,
    )
    return (result, saved)


def backward_layer(grad_out, weights, saved, cosine, sine, allowed, window):
    gain_one, w_qkv, w_out, gain_two, w_in, w_down = weights
    (
        residual,
        inverse_one,
        normed,
        query_heads,
        key_heads,
        value_heads,
        log_total,
        mixed,
        middle,
        inverse_two,
        normed_two,
        gate_up,
        hidden_units,
    ) = saved
    row_count = residual.shape[0]
    group = QH // KVH
    grad_branch = grad_out.astype(jnp.bfloat16)
    grad_down = jnp.einsum(
        "rf,rd->fd", hidden_units, grad_branch, preferred_element_type=jnp.float32
    )
    grad_hidden = jnp.einsum("rd,fd->rf", grad_branch, w_down, preferred_element_type=jnp.float32)
    gate_part = gate_up[:, :FF]
    up_part = gate_up[:, FF:]
    sigma = jax.nn.sigmoid(gate_part)
    grad_gate = grad_hidden * up_part * sigma * (1.0 + gate_part * (1.0 - sigma))
    grad_up = grad_hidden * gate_part * sigma
    grad_gate_up = jnp.concatenate([grad_gate, grad_up], axis=-1).astype(jnp.bfloat16)
    grad_in = jnp.einsum("rd,rf->df", normed_two, grad_gate_up, preferred_element_type=jnp.float32)
    grad_normed_two = jnp.einsum(
        "rf,df->rd", grad_gate_up, w_in, preferred_element_type=jnp.float32
    )
    grad_gain_two, grad_middle_part = norm_back(middle, inverse_two, gain_two, grad_normed_two)
    grad_middle = grad_out + grad_middle_part
    grad_attn = grad_middle.astype(jnp.bfloat16)
    grad_out_weight = jnp.einsum("ro,rd->od", mixed, grad_attn, preferred_element_type=jnp.float32)
    grad_mixed = jnp.einsum(
        "rd,od->ro", grad_attn, w_out, preferred_element_type=jnp.float32
    ).astype(jnp.bfloat16)
    grad_heads = grad_mixed.reshape(row_count, KVH, group, HD).transpose(1, 0, 2, 3)
    factor = HD ** (-0.5)

    def head_backward(pieces):
        head_query, head_keys, head_values, head_total, head_grad = pieces
        scores = head_scores(head_query, head_keys, allowed)
        probs = jnp.exp(scores - head_total)
        probs_low = probs.astype(jnp.bfloat16)
        grad_probs = jnp.einsum(
            "qgd,td->gqt", head_grad, head_values, preferred_element_type=jnp.float32
        )
        grad_scores = (
            probs * (grad_probs - jnp.sum(probs * grad_probs, axis=-1, keepdims=True))
        ).astype(jnp.bfloat16)
        grad_query = (
            jnp.einsum("gqt,td->qgd", grad_scores, head_keys, preferred_element_type=jnp.float32)
            * factor
        )
        grad_keys = (
            jnp.einsum("gqt,qgd->td", grad_scores, head_query, preferred_element_type=jnp.float32)
            * factor
        )
        grad_values = jnp.einsum(
            "gqt,qgd->td", probs_low, head_grad, preferred_element_type=jnp.float32
        )
        return (grad_query, grad_keys, grad_values)

    grad_query_heads, grad_key_heads, grad_value_heads = lax.map(
        head_backward, (query_heads, key_heads, value_heads, log_total, grad_heads)
    )
    grad_query = grad_query_heads.transpose(1, 0, 2, 3).reshape(row_count, QH, HD)
    own_keys, own_values = return_rows(
        grad_key_heads.transpose(1, 0, 2), grad_value_heads.transpose(1, 0, 2), window, row_count
    )
    grad_project = jnp.concatenate(
        [
            rope_back(grad_query, cosine, sine).reshape(row_count, QH * HD),
            rope_back(own_keys, cosine, sine).reshape(row_count, KVH * HD),
            own_values.reshape(row_count, KVH * HD),
        ],
        axis=-1,
    ).astype(jnp.bfloat16)
    grad_qkv = jnp.einsum("rd,rc->dc", normed, grad_project, preferred_element_type=jnp.float32)
    grad_normed = jnp.einsum("rc,dc->rd", grad_project, w_qkv, preferred_element_type=jnp.float32)
    grad_gain_one, grad_residual_part = norm_back(residual, inverse_one, gain_one, grad_normed)
    grad_residual = grad_middle + grad_residual_part
    flat_grad = jnp.concatenate(
        [
            grad_gain_one,
            grad_qkv.reshape(-1),
            grad_out_weight.reshape(-1),
            grad_gain_two,
            grad_in.reshape(-1),
            grad_down.reshape(-1),
        ]
    )
    return (grad_residual, flat_grad)


def body(hidden_in, segment_ids, weights_flat, cotangent):
    row_count = hidden_in.shape[0]
    layer_count = weights_flat.shape[0]
    window = (MAXLEN - 1) // row_count + 1
    first_row = lax.axis_index("fsdp") * row_count
    row_order = jnp.arange(row_count, dtype=jnp.int32)
    query_global = first_row + row_order
    positions = query_global - segment_ids
    cosine, sine = rope_tables(positions, HD)
    key_global = (
        first_row - window * row_count + jnp.arange((window + 1) * row_count, dtype=jnp.int32)
    )
    allowed = (key_global[None, :] >= segment_ids[:, None]) & (
        key_global[None, :] <= query_global[:, None]
    )
    residual = hidden_in.astype(jnp.float32)
    saved_layers = []
    held_layers = []
    for layer_index in range(layer_count):
        gathered = lax.all_gather(weights_flat[layer_index], "fsdp", axis=0, tiled=True)
        residual, saved = forward_layer(residual, unpack(gathered), cosine, sine, allowed, window)
        saved_layers.append(saved)
        held_layers.append(gathered)
    layer_out = residual.astype(jnp.bfloat16)
    grad_state = cotangent.astype(jnp.float32)
    flat_grads = [None] * layer_count
    for layer_index in reversed(range(layer_count)):
        gathered = lax.all_gather(weights_flat[layer_index], "fsdp", axis=0, tiled=True)
        grad_state, flat_grad = backward_layer(
            grad_state, unpack(gathered), saved_layers[layer_index], cosine, sine, allowed, window
        )
        flat_grads[layer_index] = flat_grad
    grad_weights = lax.psum_scatter(jnp.stack(flat_grads), "fsdp", scatter_dimension=1, tiled=True)
    return (layer_out, grad_state, grad_weights)


def solution(mesh):
    in_specs = (P("fsdp", None), P("fsdp"), P(None, "fsdp"), P("fsdp", None))
    out_specs = (P("fsdp", None), P("fsdp", None), P(None, "fsdp"))
    return jax.shard_map(body, mesh=mesh, in_specs=in_specs, out_specs=out_specs, check_vma=False)
```

profile of v0, /device:TPU:50, one launch (start us, length us, event | category | flops | bytes accessed | tf_op | source)
XLA Modules:
  0.0 1650.9 jit_solution(3911668081353446242)
XLA Ops:
  8.8 3.4 broadcast.209.clone
  13.8 3.2 broadcast.209.clone.1
  20.9 169.8 %all-reduce.9.cloned.1.call-done = (bf16[3540096]{0:T(1024)(128)(2,1)}, bf16[3540096]{0:T(1024)(128)(2,1)}) async-done(((bf16[3540096]{0:T(1024)(128)(2,1)}, bf16[3540096]{0:T(1024)(128)(2,1)}), (bf16[3540096]{0:T(1024)(128)(2,1)}, bf16[3540096]{0:T(1024)(128)(2,1)})) %all-reduce.9.cloned.1.call-update) | async-done | bytes 14160400
  190.7 67.9 %reshape.431 = bf16[1,3540096]{1,0:T(2,128)(2,1)S(1)} reshape(bf16[3540096]{0:T(1024)(128)(2,1)} %get-tuple-element.399) | data formatting | bytes 14160384
  258.6 23.1 %slice_reduce_fusion.5 = bf16[552960]{0:T(1024)(128)(2,1)S(1)} fusion(bf16[1,3540096]{1,0:T(2,128)(2,1)S(1)} %reshape.431), kind=kLoop, calls=%fused_computation.131 | loop fusion | bytes 2211840 | tf_op jit(solution)/shard_map/slice | solution.py:52
  284.8 3.5 collective-permute-start
  288.3 3.5 collective-permute-start.1
  291.8 4.4 collective-permute-start.2
  298.1 4.8 collective-permute-start.4
  303.0 14.9 slice_reduce_fusion.7
  317.9 71.7 %slice_reduce_fusion.1 = bf16[1769472]{0:T(1024)(128)(2,1)} fusion(bf16[1,3540096]{1,0:T(2,128)(2,1)} %copy-done), kind=kLoop, calls=%fused_computation.124 | loop fusion | bytes 7077888 | tf_op jit(solution)/shard_map/slice | solution.py:52
  389.7 37.0 %slice_reduce_fusion.3 = bf16[884736]{0:T(1024)(128)(2,1)} fusion(bf16[1,3540096]{1,0:T(2,128)(2,1)} %copy-done), kind=kLoop, calls=%fused_computation.126 | loop fusion | bytes 3538944 | tf_op jit(solution)/shard_map/slice | solution.py:52
  426.7 67.9 %reshape.433 = bf16[1,3540096]{1,0:T(2,128)(2,1)S(1)} reshape(bf16[3540096]{0:T(1024)(128)(2,1)} %get-tuple-element.400) | data formatting | bytes 14160384
  494.6 24.2 %slice_reduce_fusion.4 = bf16[552960]{0:T(1024)(128)(2,1)} fusion(bf16[1,3540096]{1,0:T(2,128)(2,1)S(1)} %reshape.433), kind=kLoop, calls=%fused_computation.130 | loop fusion | bytes 2211840 | tf_op jit(solution)/shard_map/slice | solution.py:52
  518.8 14.9 slice_reduce_fusion.6
  533.7 71.7 %slice_reduce_fusion = bf16[1769472]{0:T(1024)(128)(2,1)} fusion(bf16[1,3540096]{1,0:T(2,128)(2,1)} %copy-done.1), kind=kLoop, calls=%fused_computation.123 | loop fusion | bytes 7077888 | tf_op jit(solution)/shard_map/slice | solution.py:52
  605.4 37.1 %slice_reduce_fusion.2 = bf16[884736]{0:T(1024)(128)(2,1)} fusion(bf16[1,3540096]{1,0:T(2,128)(2,1)} %copy-done.1), kind=kLoop, calls=%fused_computation.125 | loop fusion | bytes 3538944 | tf_op jit(solution)/shard_map/slice | solution.py:52
  646.7 5.0 reshape.377
  651.7 4.7 reshape.378
  656.5 3.2 reshape.379
  662.0 6.6 reshape.384
  668.6 4.3 reshape.385
  679.3 3.1 collective-permute-start.7
  683.2 3.7 collective-permute-start.8
  687.7 4.8 collective-permute-start.9
  693.4 4.0 collective-permute-start.10
  704.0 4.6 collective-permute-start.13
  708.6 3.3 collective-permute-start.14
  719.2 13.5 while.56
  744.4 4.3 collective-permute-start.17
  748.6 4.9 collective-permute-start.18
  761.4 3.7 collective-permute-start.22
  771.2 3.3 collective-permute-start.26
  779.6 3.1 collective-permute-start.29
  791.9 13.8 while.57
  815.1 14.9 while.58
  833.2 4.2 collective-permute-start.39
  840.0 7.0 collective-permute-start.37
  847.0 8.1 collective-permute-start.36
  860.0 4.7 collective-permute-start.34
  867.2 4.4 collective-permute-start.32
  871.6 4.0 convolution_bitcast_fusion.8
  878.0 7.5 copy.52
  885.5 3.9 reshape.403
  889.4 3.9 collective-permute-start.47
  895.2 3.1 collective-permute-start.45
  898.3 3.4 collective-permute-start.44
  905.5 4.3 collective-permute-start.42
  935.3 21.6 %while.59 = (s32[]{:T(128)}, f32[3,128,3,64]{1,3,2,0:T(8,128)}, f32[3,1152,64]{1,2,0:T(8,128)}, f32[3,1152,64]{1,2,0:T(8,128)}, bf16[3,1152,64]{1,2,0:T(8,128)(2...) while((s32[]{:T(128)}, f32[3,128,3,64]{1,3,2,0:T(8,128)}, ...), condition=%wide.region_20.21_spmd.clone, body=%wide.region_18.20_spmd.clone.sunk | while | flops 287637120 | bytes 17271488 | solution.py:235
  965.5 4.2 collective-permute-start.52
  972.1 4.6 collective-permute-start.50
  982.5 4.0 convolution_bitcast_fusion.9
  987.3 3.8 reshape.400
  991.1 108.1 %concatenate.101 = f32[3540096]{0:T(1024)} concatenate(f32[576]{0:T(1024)S(1)} %copy-done.100, f32[552960]{0:T(1024)} %reshape.400, f32[331776]{0:T(1024)} %reshape.401, f32[576]{0:T(1024)S(1)} %copy-done.98, f32[1769472]{0:T(1024)} %bitcast.363, f32[884736]{0:T(1024)S(1)} %reshape.403), dimensions={0} | concatenate | bytes 28320768 | tf_op jit(solution)/shard_map/concatenate | solution.py:254
  1099.2 54.2 %stack.10 = f32[1,3540096]{1,0:T(1,128)} reshape(f32[3540096]{0:T(1024)} %concatenate.101) | data formatting | bytes 28320768 | tf_op jit(solution)/shard_map/stack | solution.py:299
  1155.1 7.5 copy.51
  1162.5 3.7 reshape.399
  1174.0 3.8 collective-permute-start.59
  1181.0 3.1 collective-permute-start.57
  1194.2 3.9 reshape.396
  1198.1 108.1 %concatenate.100 = f32[3540096]{0:T(1024)} concatenate(f32[576]{0:T(1024)S(1)} %get-tuple-element.311, f32[552960]{0:T(1024)} %reshape.396, f32[331776]{0:T(1024)} %reshape.397, f32[576]{0:T(1024)S(1)} %copy-done.99, f32[1769472]{0:T(1024)} %bitcast.364, f32[884736]{0:T(1024)S(1)} %reshape.399), dimensions={0} | concatenate | bytes 28320768 | tf_op jit(solution)/shard_map/concatenate | solution.py:254
  1306.2 53.4 %stack.9 = f32[1,3540096]{1,0:T(1,128)S(1)} reshape(f32[3540096]{0:T(1024)} %concatenate.100) | data formatting | bytes 28320768 | tf_op jit(solution)/shard_map/stack | solution.py:299
  1359.6 28.7 %pad_maximum_fusion = f32[2,3540096]{1,0:T(2,128)} fusion(f32[1,3540096]{1,0:T(1,128)} %stack.10, f32[1,3540096]{1,0:T(1,128)S(1)} %stack.9), kind=kLoop, calls=%fused_computation.122 | loop fusion | flops 7080192 | bytes 56641536 | tf_op jit(solution)/shard_map/stack | solution.py:299
  1392.3 249.4 %all-reduce.7.cloned.1.call-done = f32[2,3540096]{1,0:T(2,128)} async-done(((f32[2,3540096]{1,0:T(2,128)}), f32[2,3540096]{1,0:T(2,128)}) %all-reduce.7.cloned.1.call-update) | async-done | bytes 28320784
  (550 shorter events, 245.0 us)
Async XLA Ops:
  7.2 183.6 %all-reduce.9.cloned.1.call-start = ((), (), s32[]{:S(2)}) async-start(), calls=%async_computation.1 | async-start | bytes 28327936
  18.6 1623.0 %all-reduce.7.cloned.1.call-start = ((), (), s32[]{:S(2)}) async-start(), calls=%async_computation | async-start | bytes 56641536
  284.8 388.1 %collective-permute-start = (bf16[128,3,64]{0,2,1:T(8,128)(2,1)}, bf16[128,3,64]{0,2,1:T(8,128)(2,1)}, u32[]{:S(2)}, u32[]{:S(2)}) collective-permute-start(bf16[128,3,64]{0,2,1:T(8,128)(2,1)} %bitcast), channel_id=1, source_target_pairs={{0,8},{1,9},{2,10},{3,11},{4,12},{5,13},{6,14},{7,15},{8,16},{9,17... | collective-permute-start | bytes 147464 | tf_op jit(solution)/shard_map/ppermute | solution.py:21
  288.3 387.3 %collective-permute-start.1 = (bf16[128,3,64]{0,2,1:T(8,128)(2,1)}, bf16[128,3,64]{0,2,1:T(8,128)(2,1)}, u32[]{:S(2)}, u32[]{:S(2)}) collective-permute-start(bf16[128,3,64]{0,2,1:T(8,128)(2,1)} %bitcast), channel_id=1, source_target_pairs={{0,7},{1,8},{2,9},{3,10},{4,11},{5,12},{6,13},{7,14},{8,15},{9,16}... | collective-permute-start | bytes 147464 | tf_op jit(solution)/shard_map/ppermute | solution.py:21
  291.8 387.5 %collective-permute-start.2 = (bf16[128,3,64]{0,2,1:T(8,128)(2,1)}, bf16[128,3,64]{0,2,1:T(8,128)(2,1)}, u32[]{:S(2)}, u32[]{:S(2)}) collective-permute-start(bf16[128,3,64]{0,2,1:T(8,128)(2,1)} %bitcast), channel_id=1, source_target_pairs={{0,6},{1,7},{2,8},{3,9},{4,10},{5,11},{6,12},{7,13},{8,14},{9,15},... | collective-permute-start | bytes 147464 | tf_op jit(solution)/shard_map/ppermute | solution.py:21
  296.2 387.0 %collective-permute-start.3 = (bf16[128,3,64]{0,2,1:T(8,128)(2,1)}, bf16[128,3,64]{0,2,1:T(8,128)(2,1)}, u32[]{:S(2)}, u32[]{:S(2)}) collective-permute-start(bf16[128,3,64]{0,2,1:T(8,128)(2,1)} %bitcast), channel_id=1, source_target_pairs={{0,5},{1,6},{2,7},{3,8},{4,9},{5,10},{6,11},{7,12},{8,13},{9,14},{... | collective-permute-start | bytes 147464 | tf_op jit(solution)/shard_map/ppermute | solution.py:21
  298.1 389.6 %collective-permute-start.4 = (bf16[128,3,64]{0,2,1:T(8,128)(2,1)}, bf16[128,3,64]{0,2,1:T(8,128)(2,1)}, u32[]{:S(2)}, u32[]{:S(2)}) collective-permute-start(bf16[128,3,64]{0,2,1:T(8,128)(2,1)} %bitcast), channel_id=1, source_target_pairs={{0,4},{1,5},{2,6},{3,7},{4,8},{5,9},{6,10},{7,11},{8,12},{9,13},{1... | collective-permute-start | bytes 147464 | tf_op jit(solution)/shard_map/ppermute | solution.py:21
  672.9 20.5 %collective-permute-start.5 = (bf16[128,3,64]{0,2,1:T(8,128)(2,1)}, bf16[128,3,64]{0,2,1:T(8,128)(2,1)S(1)}, u32[]{:S(2)}, u32[]{:S(2)}) collective-permute-start(bf16[128,3,64]{0,2,1:T(8,128)(2,1)} %bitcast), channel_id=1, source_target_pairs={{0,3},{1,4},{2,5},{3,6},{4,7},{5,8},{6,9},{7,10},{8,11},{9,12},{10... | collective-permute-start | bytes 147464 | tf_op jit(solution)/shard_map/ppermute | solution.py:21
  675.6 21.7 %collective-permute-start.6 = (bf16[128,3,64]{0,2,1:T(8,128)(2,1)}, bf16[128,3,64]{0,2,1:T(8,128)(2,1)S(1)}, u32[]{:S(2)}, u32[]{:S(2)}) collective-permute-start(bf16[128,3,64]{0,2,1:T(8,128)(2,1)} %bitcast), channel_id=1, source_target_pairs={{0,2},{1,3},{2,4},{3,5},{4,6},{5,7},{6,8},{7,9},{8,10},{9,11},{10,... | collective-permute-start | bytes 147464 | tf_op jit(solution)/shard_map/ppermute | solution.py:21
  679.3 21.1 %collective-permute-start.7 = (bf16[128,3,64]{0,2,1:T(8,128)(2,1)}, bf16[128,3,64]{0,2,1:T(8,128)(2,1)S(1)}, u32[]{:S(2)}, u32[]{:S(2)}) collective-permute-start(bf16[128,3,64]{0,2,1:T(8,128)(2,1)} %bitcast), channel_id=1, source_target_pairs={{0,1},{1,2},{2,3},{3,4},{4,5},{5,6},{6,7},{7,8},{8,9},{9,10},{10,1... | collective-permute-start | bytes 147464 | tf_op jit(solution)/shard_map/ppermute | solution.py:21
  683.2 20.7 %collective-permute-start.8 = (bf16[128,3,64]{0,2,1:T(8,128)(2,1)}, bf16[128,3,64]{0,2,1:T(8,128)(2,1)S(1)}, u32[]{:S(2)}, u32[]{:S(2)}) collective-permute-start(bf16[128,3,64]{0,2,1:T(8,128)(2,1)} %fusion.151), channel_id=1, source_target_pairs={{0,8},{1,9},{2,10},{3,11},{4,12},{5,13},{6,14},{7,15},{8,16},{9,17... | collective-permute-start | bytes 147464 | tf_op jit(solution)/shard_map/ppermute | solution.py:21
  687.7 20.9 %collective-permute-start.9 = (bf16[128,3,64]{0,2,1:T(8,128)(2,1)}, bf16[128,3,64]{0,2,1:T(8,128)(2,1)S(1)}, u32[]{:S(2)}, u32[]{:S(2)}) collective-permute-start(bf16[128,3,64]{0,2,1:T(8,128)(2,1)} %fusion.151), channel_id=1, source_target_pairs={{0,7},{1,8},{2,9},{3,10},{4,11},{5,12},{6,13},{7,14},{8,15},{9,16}... | collective-permute-start | bytes 147464 | tf_op jit(solution)/shard_map/ppermute | solution.py:21
  693.4 18.6 %collective-permute-start.10 = (bf16[128,3,64]{0,2,1:T(8,128)(2,1)}, bf16[128,3,64]{0,2,1:T(8,128)(2,1)S(1)}, u32[]{:S(2)}, u32[]{:S(2)}) collective-permute-start(bf16[128,3,64]{0,2,1:T(8,128)(2,1)} %fusion.151), channel_id=1, source_target_pairs={{0,6},{1,7},{2,8},{3,9},{4,10},{5,11},{6,12},{7,13},{8,14},{9,15},... | collective-permute-start | bytes 147464 | tf_op jit(solution)/shard_map/ppermute | solution.py:21
  697.4 17.0 %collective-permute-start.11 = (bf16[128,3,64]{0,2,1:T(8,128)(2,1)}, bf16[128,3,64]{0,2,1:T(8,128)(2,1)S(1)}, u32[]{:S(2)}, u32[]{:S(2)}) collective-permute-start(bf16[128,3,64]{0,2,1:T(8,128)(2,1)} %fusion.151), channel_id=1, source_target_pairs={{0,5},{1,6},{2,7},{3,8},{4,9},{5,10},{6,11},{7,12},{8,13},{9,14},{... | collective-permute-start | bytes 147464 | tf_op jit(solution)/shard_map/ppermute | solution.py:21
  700.4 14.0 collective-permute-start.12
  704.0 10.5 collective-permute-start.13
  708.6 6.6 collective-permute-start.14
  712.0 5.6 collective-permute-start.15
  742.1 16.5 %collective-permute-start.16 = (bf16[128,3,64]{0,2,1:T(8,128)(2,1)S(1)}, bf16[128,3,64]{0,2,1:T(8,128)(2,1)S(1)}, u32[]{:S(2)}, u32[]{:S(2)}) collective-permute-start(bf16[128,3,64]{0,2,1:T(8,128)(2,1)S(1)} %bitcast.393), channel_id=1, source_target_pairs={{0,8},{1,9},{2,10},{3,11},{4,12},{5,13},{6,14},{7,15},{8,16},{9,17... | collective-permute-start | bytes 147464 | tf_op jit(solution)/shard_map/ppermute | solution.py:21
  744.4 17.0 %collective-permute-start.17 = (bf16[128,3,64]{0,2,1:T(8,128)(2,1)S(1)}, bf16[128,3,64]{0,2,1:T(8,128)(2,1)S(1)}, u32[]{:S(2)}, u32[]{:S(2)}) collective-permute-start(bf16[128,3,64]{0,2,1:T(8,128)(2,1)S(1)} %bitcast.394), channel_id=1, source_target_pairs={{0,7},{1,8},{2,9},{3,10},{4,11},{5,12},{6,13},{7,14},{8,15},{9,16}... | collective-permute-start | bytes 147464 | tf_op jit(solution)/shard_map/ppermute | solution.py:21
  748.6 16.5 %collective-permute-start.18 = (bf16[128,3,64]{0,2,1:T(8,128)(2,1)S(1)}, bf16[128,3,64]{0,2,1:T(8,128)(2,1)S(1)}, u32[]{:S(2)}, u32[]{:S(2)}) collective-permute-start(bf16[128,3,64]{0,2,1:T(8,128)(2,1)S(1)} %bitcast.395), channel_id=1, source_target_pairs={{0,6},{1,7},{2,8},{3,9},{4,10},{5,11},{6,12},{7,13},{8,14},{9,15},... | collective-permute-start | bytes 147464 | tf_op jit(solution)/shard_map/ppermute | solution.py:21
  753.6 13.7 collective-permute-start.19
  755.5 13.7 collective-permute-start.20
  758.6 12.5 collective-permute-start.21
  761.4 13.0 collective-permute-start.22
  765.2 11.3 collective-permute-start.23
  767.2 12.4 collective-permute-start.24
  769.2 13.6 collective-permute-start.25
  771.2 14.4 collective-permute-start.26
  774.5 13.8 collective-permute-start.27
  776.5 11.8 collective-permute-start.28
  779.6 8.7 collective-permute-start.29
  782.8 6.2 collective-permute-start.30
  785.6 5.4 collective-permute-start.31
  833.2 26.8 %collective-permute-start.39 = (bf16[128,3,64]{0,2,1:T(8,128)(2,1)S(1)}, bf16[128,3,64]{0,2,1:T(8,128)(2,1)S(1)}, u32[]{:S(2)}, u32[]{:S(2)}) collective-permute-start(bf16[128,3,64]{0,2,1:T(8,128)(2,1)S(1)} %get-tuple-element.435), channel_id=1, source_target_pairs={{8,0},{9,1},{10,2},{11,3},{12,4},{13,5},{14,6},{15,7},{16,8},{17,9... | collective-permute-start | bytes 147464 | tf_op jit(solution)/shard_map/ppermute | solution.py:21
  837.5 27.2 %collective-permute-start.38 = (bf16[128,3,64]{0,2,1:T(8,128)(2,1)S(1)}, bf16[128,3,64]{0,2,1:T(8,128)(2,1)S(1)}, u32[]{:S(2)}, u32[]{:S(2)}) collective-permute-start(bf16[128,3,64]{0,2,1:T(8,128)(2,1)S(1)} %get-tuple-element.436), channel_id=1, source_target_pairs={{7,0},{8,1},{9,2},{10,3},{11,4},{12,5},{13,6},{14,7},{15,8},{16,9}... | collective-permute-start | bytes 147464 | tf_op jit(solution)/shard_map/ppermute | solution.py:21
  840.0 27.2 %collective-permute-start.37 = (bf16[128,3,64]{0,2,1:T(8,128)(2,1)S(1)}, bf16[128,3,64]{0,2,1:T(8,128)(2,1)S(1)}, u32[]{:S(2)}, u32[]{:S(2)}) collective-permute-start(bf16[128,3,64]{0,2,1:T(8,128)(2,1)S(1)} %get-tuple-element.437), channel_id=1, source_target_pairs={{6,0},{7,1},{8,2},{9,3},{10,4},{11,5},{12,6},{13,7},{14,8},{15,9},... | collective-permute-start | bytes 147464 | tf_op jit(solution)/shard_map/ppermute | solution.py:21
  847.0 42.4 %collective-permute-start.36 = (bf16[128,3,64]{0,2,1:T(8,128)(2,1)}, bf16[128,3,64]{0,2,1:T(8,128)(2,1)}, u32[]{:S(2)}, u32[]{:S(2)}) collective-permute-start(bf16[128,3,64]{0,2,1:T(8,128)(2,1)} %get-tuple-element.438), channel_id=1, source_target_pairs={{5,0},{6,1},{7,2},{8,3},{9,4},{10,5},{11,6},{12,7},{13,8},{14,9},{... | collective-permute-start | bytes 147464 | tf_op jit(solution)/shard_map/ppermute | solution.py:21
  855.1 38.2 %collective-permute-start.35 = (bf16[128,3,64]{0,2,1:T(8,128)(2,1)}, bf16[128,3,64]{0,2,1:T(8,128)(2,1)}, u32[]{:S(2)}, u32[]{:S(2)}) collective-permute-start(bf16[128,3,64]{0,2,1:T(8,128)(2,1)} %get-tuple-element.439), channel_id=1, source_target_pairs={{4,0},{5,1},{6,2},{7,3},{8,4},{9,5},{10,6},{11,7},{12,8},{13,9},{1... | collective-permute-start | bytes 147464 | tf_op jit(solution)/shard_map/ppermute | solution.py:21
  860.0 35.2 %collective-permute-start.34 = (bf16[128,3,64]{0,2,1:T(8,128)(2,1)}, bf16[128,3,64]{0,2,1:T(8,128)(2,1)}, u32[]{:S(2)}, u32[]{:S(2)}) collective-permute-start(bf16[128,3,64]{0,2,1:T(8,128)(2,1)} %get-tuple-element.440), channel_id=1, source_target_pairs={{3,0},{4,1},{5,2},{6,3},{7,4},{8,5},{9,6},{10,7},{11,8},{12,9},{13... | collective-permute-start | bytes 147464 | tf_op jit(solution)/shard_map/ppermute | solution.py:21
  864.7 33.6 %collective-permute-start.33 = (bf16[128,3,64]{0,2,1:T(8,128)(2,1)}, bf16[128,3,64]{0,2,1:T(8,128)(2,1)}, u32[]{:S(2)}, u32[]{:S(2)}) collective-permute-start(bf16[128,3,64]{0,2,1:T(8,128)(2,1)} %get-tuple-element.441), channel_id=1, source_target_pairs={{2,0},{3,1},{4,2},{5,3},{6,4},{7,5},{8,6},{9,7},{10,8},{11,9},{12,... | collective-permute-start | bytes 147464 | tf_op jit(solution)/shard_map/ppermute | solution.py:21
  867.2 34.6 %collective-permute-start.32 = (bf16[128,3,64]{0,2,1:T(8,128)(2,1)}, bf16[128,3,64]{0,2,1:T(8,128)(2,1)}, u32[]{:S(2)}, u32[]{:S(2)}) collective-permute-start(bf16[128,3,64]{0,2,1:T(8,128)(2,1)} %get-tuple-element.434), channel_id=1, source_target_pairs={{1,0},{2,1},{3,2},{4,3},{5,4},{6,5},{7,6},{8,7},{9,8},{10,9},{11,1... | collective-permute-start | bytes 147464 | tf_op jit(solution)/shard_map/ppermute | solution.py:21
  889.4 16.1 collective-permute-start.47
  893.3 16.6 %collective-permute-start.46 = (bf16[128,3,64]{0,2,1:T(8,128)(2,1)}, bf16[128,3,64]{0,2,1:T(8,128)(2,1)S(1)}, u32[]{:S(2)}, u32[]{:S(2)}) collective-permute-start(bf16[128,3,64]{0,2,1:T(8,128)(2,1)} %get-tuple-element.444), channel_id=1, source_target_pairs={{7,0},{8,1},{9,2},{10,3},{11,4},{12,5},{13,6},{14,7},{15,8},{16,9}... | collective-permute-start | bytes 147464 | tf_op jit(solution)/shard_map/ppermute | solution.py:21
  895.2 16.6 %collective-permute-start.45 = (bf16[128,3,64]{0,2,1:T(8,128)(2,1)}, bf16[128,3,64]{0,2,1:T(8,128)(2,1)S(1)}, u32[]{:S(2)}, u32[]{:S(2)}) collective-permute-start(bf16[128,3,64]{0,2,1:T(8,128)(2,1)} %get-tuple-element.445), channel_id=1, source_target_pairs={{6,0},{7,1},{8,2},{9,3},{10,4},{11,5},{12,6},{13,7},{14,8},{15,9},... | collective-permute-start | bytes 147464 | tf_op jit(solution)/shard_map/ppermute | solution.py:21
  898.3 17.1 %collective-permute-start.44 = (bf16[128,3,64]{0,2,1:T(8,128)(2,1)}, bf16[128,3,64]{0,2,1:T(8,128)(2,1)S(1)}, u32[]{:S(2)}, u32[]{:S(2)}) collective-permute-start(bf16[128,3,64]{0,2,1:T(8,128)(2,1)} %get-tuple-element.446), channel_id=1, source_target_pairs={{5,0},{6,1},{7,2},{8,3},{9,4},{10,5},{11,6},{12,7},{13,8},{14,9},{... | collective-permute-start | bytes 147464 | tf_op jit(solution)/shard_map/ppermute | solution.py:21
  901.8 13.7 collective-permute-start.43
  905.5 9.9 collective-permute-start.42
  909.9 6.2 collective-permute-start.41
  959.8 12.3 collective-permute-start.55
  961.7 15.1 collective-permute-start.54
  963.6 15.7 collective-permute-start.53
  965.5 200.7 %collective-permute-start.52 = (bf16[128,3,64]{0,2,1:T(8,128)(2,1)}, bf16[128,3,64]{0,2,1:T(8,128)(2,1)}, u32[]{:S(2)}, u32[]{:S(2)}) collective-permute-start(bf16[128,3,64]{0,2,1:T(8,128)(2,1)} %get-tuple-element.422), channel_id=1, source_target_pairs={{5,0},{6,1},{7,2},{8,3},{9,4},{10,5},{11,6},{12,7},{13,8},{14,9},{... | collective-permute-start | bytes 147464 | tf_op jit(solution)/shard_map/ppermute | solution.py:21
  969.8 198.4 %collective-permute-start.51 = (bf16[128,3,64]{0,2,1:T(8,128)(2,1)}, bf16[128,3,64]{0,2,1:T(8,128)(2,1)}, u32[]{:S(2)}, u32[]{:S(2)}) collective-permute-start(bf16[128,3,64]{0,2,1:T(8,128)(2,1)} %get-tuple-element.423), channel_id=1, source_target_pairs={{4,0},{5,1},{6,2},{7,3},{8,4},{9,5},{10,6},{11,7},{12,8},{13,9},{1... | collective-permute-start | bytes 147464 | tf_op jit(solution)/shard_map/ppermute | solution.py:21
  972.1 198.0 %collective-permute-start.50 = (bf16[128,3,64]{0,2,1:T(8,128)(2,1)}, bf16[128,3,64]{0,2,1:T(8,128)(2,1)}, u32[]{:S(2)}, u32[]{:S(2)}) collective-permute-start(bf16[128,3,64]{0,2,1:T(8,128)(2,1)} %get-tuple-element.424), channel_id=1, source_target_pairs={{3,0},{4,1},{5,2},{6,3},{7,4},{8,5},{9,6},{10,7},{11,8},{12,9},{13... | collective-permute-start | bytes 147464 | tf_op jit(solution)/shard_map/ppermute | solution.py:21
  976.8 195.3 %collective-permute-start.49 = (bf16[128,3,64]{0,2,1:T(8,128)(2,1)}, bf16[128,3,64]{0,2,1:T(8,128)(2,1)}, u32[]{:S(2)}, u32[]{:S(2)}) collective-permute-start(bf16[128,3,64]{0,2,1:T(8,128)(2,1)} %get-tuple-element.425), channel_id=1, source_target_pairs={{2,0},{3,1},{4,2},{5,3},{6,4},{7,5},{8,6},{9,7},{10,8},{11,9},{12,... | collective-permute-start | bytes 147464 | tf_op jit(solution)/shard_map/ppermute | solution.py:21
  980.0 194.0 %collective-permute-start.48 = (bf16[128,3,64]{0,2,1:T(8,128)(2,1)}, bf16[128,3,64]{0,2,1:T(8,128)(2,1)}, u32[]{:S(2)}, u32[]{:S(2)}) collective-permute-start(bf16[128,3,64]{0,2,1:T(8,128)(2,1)} %get-tuple-element.418), channel_id=1, source_target_pairs={{1,0},{2,1},{3,2},{4,3},{5,4},{6,5},{7,6},{8,7},{9,8},{10,9},{11,1... | collective-permute-start | bytes 147464 | tf_op jit(solution)/shard_map/ppermute | solution.py:21
  1166.2 12.7 collective-permute-start.63
  1168.2 12.8 collective-permute-start.62
  1170.1 14.0 collective-permute-start.61
  1172.1 15.0 collective-permute-start.60
  1174.0 13.0 collective-permute-start.59
  1178.9 8.1 collective-permute-start.58
  1181.0 6.4 collective-permute-start.57
  (119 other events, 2469.9 us)
Sparse Core Ops, SparseCore 0:
  18.7 171.9 all-reduce.8
  1388.4 253.1 all-reduce.6
where the time goes:
time: 1680 us; the launch traced here: 1650 us
  local copies, waits for them, and re-layouts  862 us (51%)
  waiting for transfers between devices  428 us (25%)
  starting transfers between devices  199 us (12%)
  matrix products  89 us (5%)
  other arithmetic  55.5 us (3%)
  between operations  16.9 us (1%)
    unnamed x4, waiting for transfers between devices  419 us
    slice x8, local copies, waits for them, and re-layouts, unpack(): pieces.append(flat[offset:offset + piece_size].reshape(piece_shape))  295 us
    concatenate x2, local copies, waits for them, and re-layouts, backward_layer(): jnp.concatenate([grad_gain_one, grad_qkv.reshape(-1), grad_out_weight.res...  216 us
    ppermute x64, starting transfers between devices, passed_along(): return lax.ppermute(shard, axis, pairs)  199 us
    unnamed x240, local copies, waits for them, and re-layouts  176 us
    another operation x2, local copies, waits for them, and re-layouts, body(): jnp.stack(flat_grads)  108 us
  transfers between devices with their start and end apart: 66, of which 10 were waited for; matrix products, arithmetic and copies ran while one was open for 36% of the time, Pallas kernels for 0%

commit v1 on v0

v1 whole, which is shorter than its diff:
```python
import functools

import jax
import jax.numpy as jnp
from jax import lax
from jax.experimental import pallas as pl
from jax.experimental.pallas import tpu as pltpu
from jax.sharding import PartitionSpec as P

D = 576
FF = 1536
QH = 9
KVH = 3
HD = 64
MAXLEN = 1024
QW = QH * HD
KW = KVH * HD
PW = QW + 2 * KW
GROUP = QH // KVH
DEVICES = 128
ROWS = 128
PARAMS = 3540096
SHARD = PARAMS // DEVICES
CHUNK = 224
FLAT_ROWS = 27904
SAME_CORE = 4
WIN_S = (SAME_CORE + 1) * ROWS
WIN_T = SAME_CORE * ROWS
WIN = WIN_S + WIN_T

bf16 = jnp.bfloat16
f32 = jnp.float32
epsilon = 1e-05
rope_base = 10000.0
FACTOR = HD ** (-0.5)
VMEM_LIMIT = 60 * 1024 * 1024

HALF_GAIN_ONE = 0
HALF_QKV = D // 64
HALF_OUT = HALF_QKV + D * PW // 64
HALF_GAIN_TWO = HALF_OUT + QW * D // 64
HALF_IN = HALF_GAIN_TWO + D // 64
HALF_DOWN = HALF_IN + D * 2 * FF // 64


def mm(a, b):
    return lax.dot_general(a, b, (((1,), (0,)), ((), ())), preferred_element_type=f32)


def mm_t(a, b):
    return lax.dot_general(a, b, (((1,), (1,)), ((), ())), preferred_element_type=f32)


def t_mm(a, b):
    return lax.dot_general(a, b, (((0,), (0,)), ((), ())), preferred_element_type=f32)


def call(kernel, out_shape, args, scratch=(), smem=0, flops=0, nbytes=0):
    in_specs = [
        pl.BlockSpec(memory_space=pltpu.SMEM if at < smem else pltpu.VMEM)
        for at in range(len(args))
    ]
    return pl.pallas_call(
        kernel,
        out_shape=[jax.ShapeDtypeStruct(s, d) for s, d in out_shape],
        in_specs=in_specs,
        out_specs=[pl.BlockSpec(memory_space=pltpu.VMEM) for _ in out_shape],
        scratch_shapes=list(scratch),
        compiler_params=pltpu.CompilerParams(vmem_limit_bytes=VMEM_LIMIT),
        cost_estimate=pl.CostEstimate(flops=flops, bytes_accessed=nbytes, transcendentals=0),
    )(*args)


def low_half(shape):
    return lax.broadcasted_iota(jnp.int32, shape, 1) < 64


def take_rows(flat, start_half, pairs, width_half, store):
    tiles = (width_half + 1) // 2
    if start_half % 2 == 0:
        for t in range(tiles):
            store(t, flat[pl.ds(start_half // 2 + t, pairs, stride=width_half), :])
    else:
        before = None
        for t in range(tiles + 1):
            if t == tiles and width_half % 2 == 1:
                store(t - 1, before)
                break
            now = pltpu.roll(flat[pl.ds(start_half // 2 + t, pairs, stride=width_half), :], 64, 1)
            if before is not None:
                store(t - 1, jnp.where(low_half(now.shape), before, now))
            before = now


def put_rows(flat, start_half, pairs, width_half, load):
    tiles = (width_half + 1) // 2
    if start_half % 2 == 0:
        for t in range(tiles):
            place = pl.ds(start_half // 2 + t, pairs, stride=width_half)
            value = load(t)
            if 2 * t + 1 == width_half:
                value = jnp.where(low_half(value.shape), value, flat[place, :])
            flat[place, :] = value
    else:
        before = None
        for t in range(tiles + 1):
            if t == tiles and width_half % 2 == 1:
                break
            place = pl.ds(start_half // 2 + t, pairs, stride=width_half)
            now = pltpu.roll(load(t), 64, 1) if t < tiles else None
            if before is None:
                value = jnp.where(low_half(now.shape), flat[place, :], now)
            else:
                value = jnp.where(low_half(before.shape), before, now)
            flat[place, :] = value
            before = now


def unpack_kernel(gathered, w_qkv, w_out, w_in, w_down, gains, flat, tile):
    flat[0:8, :] = jnp.zeros((8, 128), f32)
    lane = lax.broadcasted_iota(jnp.int32, (CHUNK, 128), 1)
    first_two = lax.broadcasted_iota(jnp.int32, (8, 128), 0) < 2

    def one_shard(d, carry):
        shift = lax.rem(d * 9, 128)
        base = d * 216 + lax.div(d * 9, 128)
        rows = gathered[pl.ds(pl.multiple_of(d * CHUNK, CHUNK), CHUNK), :].astype(f32)
        turned = pltpu.roll(rows, shift, 1)
        behind = pltpu.roll(turned, 1, 0)
        value = jnp.where(lane >= shift, turned, behind)
        shared = jnp.where(first_two, flat[pl.ds(base, 8), :], 0.0)
        flat[pl.ds(base, 8), :] = shared + value[0:8, :]
        flat[pl.ds(base + 8, CHUNK - 8), :] = value[8:, :]
        return carry

    lax.fori_loop(0, DEVICES, one_shard, 0)

    def matrix(out, start_half, width_half):
        rows, columns = out.shape

        def store(parity, at, value):
            tile[at, pl.ds(parity, rows // 2, stride=2), :] = value

        for parity in range(2):
            take_rows(
                flat, start_half + parity * width_half, rows // 2, width_half,
                functools.partial(store, parity),
            )
        for t in range((width_half + 1) // 2):
            wide = min(128, columns - 128 * t)
            out[:, 128 * t : 128 * t + wide] = tile[t, 0:rows, 0:wide].astype(bf16)

    matrix(w_qkv, HALF_QKV, PW // 64)
    matrix(w_out, HALF_OUT, D // 64)
    matrix(w_down, HALF_DOWN, D // 64)

    def in_tile(c, carry):
        w_in[:, pl.ds(pl.multiple_of(c * 128, 128), 128)] = flat[
            pl.ds(HALF_IN // 2 + c, D, stride=24), :
        ].astype(bf16)
        return carry

    lax.fori_loop(0, 24, in_tile, 0)

    for at, start in ((0, HALF_GAIN_ONE), (1, HALF_GAIN_TWO)):
        first = start // 2
        for t in range(5):
            if start % 2 == 0:
                value = flat[first + t : first + t + 1, :]
            else:
                here = pltpu.roll(flat[first + t : first + t + 1, :], 64, 1)
                after = pltpu.roll(flat[first + t + 1 : first + t + 2, :], 64, 1)
                value = jnp.where(low_half((1, 128)), here, after)
            gains[at : at + 1, 128 * t : 128 * t + 128] = value


def unpack(gathered):
    return call(
        unpack_kernel,
        [((D, PW), bf16), ((QW, D), bf16), ((D, 2 * FF), bf16), ((FF, D), bf16), ((8, 640), f32)],
        [gathered],
        scratch=[pltpu.VMEM((FLAT_ROWS, 128), f32), pltpu.VMEM((8, FF, 128), f32)],
        flops=200_000_000, nbytes=30_000_000,
    )


def turn(value, cosine, sine):
    lane = lax.broadcasted_iota(jnp.int32, (value.shape[0], 128), 1)
    first = lax.rem(lane, 64) < 32
    pieces = []
    for t in range(value.shape[1] // 128):
        part = value[:, 128 * t : 128 * t + 128]
        swapped = jnp.where(first, -pltpu.roll(part, 96, 1), pltpu.roll(part, 32, 1))
        pieces.append(part * cosine + swapped * sine)
    return jnp.concatenate(pieces, axis=1)


def inverse_norm(values):
    return lax.rsqrt(jnp.mean(values * values, axis=-1, keepdims=True) + epsilon)


def heads_zero_kernel(window, cosine, sine, gains, w_qkv, q_out, kv_s, kv_t, normed_out):
    gain = gains[0:1, 0:D]
    for begin, rows in ((0, 384), (384, 384), (768, 384)):
        x = window[begin : begin + rows, :].astype(f32)
        normed = (x * inverse_norm(x) * gain).astype(bf16)
        project = mm(normed, w_qkv[:, 512:PW])
        both = turn(project[:, 0:256], cosine[begin : begin + rows, :], sine[begin : begin + rows, :])
        kv = jnp.concatenate([both[:, 64:256], project[:, 256:448]], axis=1).astype(bf16)
        for r in range(0, rows, 128):
            at = begin + r
            if at < WIN_S:
                kv_s[at : at + 128, :] = kv[r : r + 128, :]
            else:
                kv_t[at - WIN_S : at - WIN_S + 128, :] = kv[r : r + 128, :]
    own = SAME_CORE * ROWS
    x = window[own : own + ROWS, :].astype(f32)
    normed = (x * inverse_norm(x) * gain).astype(bf16)
    normed_out[...] = normed
    project = mm(normed, w_qkv[:, 0:640])
    q_out[...] = turn(project, cosine[own : own + ROWS, :], sine[own : own + ROWS, :])[
        :, 0:QW
    ].astype(bf16)


def heads_kernel(x_in, cosine, sine, gains, w_qkv, q_out, kv_out, normed_out):
    x = x_in[...]
    normed = (x * inverse_norm(x) * gains[0:1, 0:D]).astype(bf16)
    normed_out[...] = normed
    project = mm(normed, w_qkv[...])
    both = turn(project[:, 0:768], cosine[...], sine[...])
    q_out[...] = both[:, 0:QW].astype(bf16)
    kv_out[...] = jnp.concatenate([both[:, QW:768], project[:, 768:PW]], axis=1).astype(bf16)


def allowed_of(segment, key_row, first_row):
    query = first_row + lax.broadcasted_iota(jnp.int32, (ROWS, 1), 0)
    return (key_row >= segment) & (key_row <= query)


def group_rows(value, group):
    return jnp.concatenate(
        [value[:, (GROUP * group + n) * HD : (GROUP * group + n + 1) * HD] for n in range(GROUP)],
        axis=0,
    )


def window_rows(kv_s, kv_t, begin):
    return jnp.concatenate(
        [kv_s[:, begin : begin + HD], kv_t[:, begin : begin + HD]], axis=0
    )


def attend_kernel(
    first, x_in, q_in, kv_s, kv_t, segment, key_row, gains, w_out, w_in, w_down,
    x_out, mixed_out, lse_out, middle_out, normed_out, gate_up_out, hidden_out,
):
    allowed = allowed_of(segment[...], key_row[...], first[0])
    bias = jnp.where(allowed, 0.0, -1e30).astype(f32)
    bias = jnp.concatenate([bias] * GROUP, axis=0)
    q = q_in[...]
    pieces = []
    for group in range(KVH):
        keys = window_rows(kv_s, kv_t, group * HD)
        values = window_rows(kv_s, kv_t, KW + group * HD)
        scores = mm_t(group_rows(q, group), keys) * FACTOR + bias
        peak = jnp.max(scores, axis=-1, keepdims=True)
        powers = jnp.exp(scores - peak)
        total = jnp.sum(powers, axis=-1, keepdims=True)
        lse_out[:, group : group + 1] = peak + jnp.log(total)
        weights = (powers * (1.0 / total)).astype(bf16)
        mixed = mm(weights, values)
        for n in range(GROUP):
            pieces.append(mixed[n * ROWS : (n + 1) * ROWS, :])
    mixed = jnp.concatenate(pieces, axis=1).astype(bf16)
    mixed_out[...] = mixed
    middle = x_in[...].astype(f32) + mm(mixed, w_out[...])
    middle_out[...] = middle
    normed = (middle * inverse_norm(middle) * gains[1:2, 0:D]).astype(bf16)
    normed_out[...] = normed
    gate_up = mm(normed, w_in[...])
    gate_up_out[...] = gate_up
    gate = gate_up[:, 0:FF]
    hidden = (gate * jax.nn.sigmoid(gate) * gate_up[:, FF:]).astype(bf16)
    hidden_out[...] = hidden
    x_out[...] = middle + mm(hidden, w_down[...])


def norm_back(values, inverse, gain, grad):
    weighted = grad * gain
    return inverse * weighted - values * inverse**3 * jnp.mean(
        weighted * values, axis=-1, keepdims=True
    )


def back_kernel(
    first, g_in, q_in, kv_s, kv_t, segment, key_row, cosine, sine, gains, w_out, w_in, w_down,
    lse, middle_in, gate_up,
    branch_out, grad_gu_out, attn_out, middle_grad_out, dq_out, dkv_s, dkv_t, gain_out,
):
    g = g_in[...].astype(f32)
    branch = g.astype(bf16)
    branch_out[...] = branch
    grad_hidden = mm_t(branch, w_down[...])
    gate = gate_up[:, 0:FF]
    up = gate_up[:, FF:]
    sigma = jax.nn.sigmoid(gate)
    grad_gu_out[:, 0:FF] = (
        grad_hidden * up * sigma * (1.0 + gate * (1.0 - sigma))
    ).astype(bf16)
    grad_gu_out[:, FF:] = (grad_hidden * gate * sigma).astype(bf16)
    grad_two = mm_t(grad_gu_out[...], w_in[...])
    middle = middle_in[...]
    inverse = inverse_norm(middle)
    gain_out[...] = jnp.sum(grad_two * middle * inverse, axis=0, keepdims=True)
    grad_middle = g + norm_back(middle, inverse, gains[1:2, 0:D], grad_two)
    middle_grad_out[...] = grad_middle
    attn = grad_middle.astype(bf16)
    attn_out[...] = attn
    grad_mixed = mm_t(attn, w_out[...]).astype(bf16)

    allowed = allowed_of(segment[...], key_row[...], first[0])
    bias = jnp.where(allowed, 0.0, -1e30).astype(f32)
    bias = jnp.concatenate([bias] * GROUP, axis=0)
    q = q_in[...]
    dq, dk, dv = [], [], []
    for group in range(KVH):
        keys = window_rows(kv_s, kv_t, group * HD)
        values = window_rows(kv_s, kv_t, KW + group * HD)
        query = group_rows(q, group)
        grad = group_rows(grad_mixed, group)
        scores = mm_t(query, keys) * FACTOR + bias
        probs = jnp.exp(scores - lse[:, group : group + 1])
        grad_w = mm_t(grad, values)
        delta = jnp.sum(probs * grad_w, axis=-1, keepdims=True)
        grad_scores = (probs * (grad_w - delta)).astype(bf16)
        part = mm(grad_scores, keys) * FACTOR
        for n in range(GROUP):
            dq.append(part[n * ROWS : (n + 1) * ROWS, :])
        dk.append(t_mm(grad_scores, query) * FACTOR)
        dv.append(t_mm(probs.astype(bf16), grad))
    dkv = jnp.concatenate(dk + dv, axis=1)
    dkv_s[...] = dkv[0:WIN_S, :]
    dkv_t[...] = dkv[WIN_S:, :].astype(bf16)
    wide = jnp.concatenate(dq + [jnp.zeros((ROWS, HD), f32)], axis=1)
    dq_out[...] = turn(wide, cosine[...], -sine[...])[:, 0:QW].astype(bf16)


def back_heads_kernel(
    x_in, dq, own, r8, r6, r4, r2, cosine, sine, gains, w_qkv, middle_grad,
    g_out, project_out, gain_out,
):
    total = own[...]
    for piece in (r8, r6, r4, r2):
        total = total + piece[...].astype(f32)
    keys = jnp.concatenate([total[:, 0:KW], jnp.zeros((ROWS, HD), f32)], axis=1)
    keys = turn(keys, cosine[...], -sine[...])[:, 0:KW]
    project = jnp.concatenate(
        [dq[...].astype(f32), keys, total[:, KW:]], axis=1
    ).astype(bf16)
    project_out[...] = project
    grad = mm_t(project, w_qkv[...])
    x = x_in[...].astype(f32)
    inverse = inverse_norm(x)
    gain_out[...] = jnp.sum(grad * x * inverse, axis=0, keepdims=True)
    g_out[...] = middle_grad[...] + norm_back(x, inverse, gains[0:1, 0:D], grad)


def pack_kernel(
    core, normed, project, mixed, attn, normed_two, grad_gu, hidden, branch, gain_one, gain_two,
    keep, send, flat, tile,
):
    for at, start, gain in ((0, HALF_GAIN_ONE, gain_one), (1, HALF_GAIN_TWO, gain_two)):
        row = jnp.concatenate([gain[...], jnp.zeros((1, 64), f32)], axis=1)
        first = start // 2
        before = None
        for t in range(5):
            part = row[:, 128 * t : 128 * t + 128]
            place = slice(first + t, first + t + 1)
            if start % 2 == 0:
                flat[place, :] = part
            else:
                now = pltpu.roll(part, 64, 1)
                if before is None:
                    flat[place, :] = now
                else:
                    flat[place, :] = jnp.where(low_half((1, 128)), before, now)
                before = now

    def matrix(left, right, start_half, width_half):
        rows, columns = left.shape[1], right.shape[1]
        for t in range((width_half + 1) // 2):
            wide = min(128, columns - 128 * t)
            tile[t, 0:rows, 0:wide] = t_mm(left[...], right[:, 128 * t : 128 * t + wide])
        for parity in range(2):
            put_rows(
                flat, start_half + parity * width_half, rows // 2, width_half,
                lambda t, parity=parity: tile[t, pl.ds(parity, rows // 2, stride=2), :],
            )

    matrix(normed, project, HALF_QKV, PW // 64)
    matrix(mixed, attn, HALF_OUT, D // 64)
    matrix(hidden, branch, HALF_DOWN, D // 64)

    def in_tile(c, carry):
        flat[pl.ds(HALF_IN // 2 + c, D, stride=24), :] = t_mm(
            normed_two[...], grad_gu[:, pl.ds(pl.multiple_of(c * 128, 128), 128)]
        )
        return carry

    lax.fori_loop(0, 24, in_tile, 0)

    lane = lax.broadcasted_iota(jnp.int32, (CHUNK, 128), 1)
    for out, flip in ((keep, 0), (send, 1)):
        def one_shard(k, carry):
            d = 2 * k + lax.rem(core[0] + flip, 2)
            shift = lax.rem(d * 9, 128)
            base = d * 216 + lax.div(d * 9, 128)
            turned = pltpu.roll(flat[pl.ds(base, CHUNK), :], lax.rem(128 - shift, 128), 1)
            ahead = pltpu.roll(turned, CHUNK - 1, 0)
            value = jnp.where(lane < 128 - shift, turned, ahead)
            out[pl.ds(pl.multiple_of(k * CHUNK, CHUNK), CHUNK), :] = value.astype(bf16)
            return carry

        lax.fori_loop(0, DEVICES // 2, one_shard, 0)


def hop(value, by):
    pairs = [(i, i + by) for i in range(DEVICES) if 0 <= i + by < DEVICES]
    return lax.ppermute(value, "fsdp", pairs)


def swap(value):
    return lax.ppermute(value, "fsdp", [(i, i ^ 1) for i in range(DEVICES)])


def window_of(value, core):
    blocks = [hop(value, by) for by in (8, 6, 4, 2)] + [value]
    same = jnp.concatenate(blocks, axis=0)
    rows = value.shape[0]
    gift = lax.dynamic_slice_in_dim(same, (1 - core) * rows, SAME_CORE * rows, 0)
    return same, swap(gift)


def give_back(dkv_s, dkv_t, core):
    got = swap(dkv_t).astype(f32)
    blank = jnp.zeros((ROWS, 2 * KW), f32)
    early = jnp.concatenate([got, blank], axis=0)
    late = jnp.concatenate([blank, got], axis=0)
    total = dkv_s + jnp.where(core == 0, late, early)
    pieces = [
        hop(total[at * ROWS : (at + 1) * ROWS].astype(bf16), -by)
        for at, by in enumerate((8, 6, 4, 2))
    ]
    return total[SAME_CORE * ROWS :], pieces


def reduce_packed(keep, send):
    got = swap(send)
    total = (keep.astype(f32) + got.astype(f32)).astype(bf16)
    total = total.reshape(DEVICES // 2, CHUNK, 128)
    groups = [list(range(0, DEVICES, 2)), list(range(1, DEVICES, 2))]
    pieces = lax.all_to_all(
        total, "fsdp", split_axis=0, concat_axis=0, tiled=True, axis_index_groups=groups
    )
    own = jnp.sum(pieces.astype(f32), axis=0)
    return own.reshape(-1)[:SHARD]


def tables(positions):
    half = HD // 2
    frequency = rope_base ** (-jnp.arange(half, dtype=f32) / half)
    angles = positions.astype(f32)[:, None] * frequency[None, :]
    return (
        jnp.concatenate([jnp.cos(angles)] * 4, axis=-1),
        jnp.concatenate([jnp.sin(angles)] * 4, axis=-1),
    )


def body(hidden_in, segment_ids, weights_flat, cotangent):
    device = lax.axis_index("fsdp")
    core = lax.rem(device, 2)
    first_row = device * ROWS
    layers = weights_flat.shape[0]
    gathered = []
    for layer in range(layers):
        padded = jnp.pad(weights_flat[layer], (0, CHUNK * 128 - SHARD))
        gathered.append(lax.all_gather(padded, "fsdp", axis=0, tiled=True))

    x_same, x_sibling = window_of(hidden_in, core)
    window = jnp.concatenate([x_same, x_sibling], axis=0)
    s_same, s_sibling = window_of(segment_ids, core)
    segments = jnp.concatenate([s_same, s_sibling], axis=0)
    order = jnp.arange(ROWS, dtype=jnp.int32)
    same_first = first_row - ROWS * jnp.array([8, 6, 4, 2, 0], jnp.int32)
    sibling_first = first_row - ROWS * jnp.array([7, 5, 3, 1], jnp.int32)
    key_row = jnp.concatenate([same_first, sibling_first])[:, None] + order[None, :]
    key_row = key_row.reshape(-1)
    cosine_all, sine_all = tables(key_row - segments)
    own = SAME_CORE * ROWS
    cosine, sine = cosine_all[own : own + ROWS], sine_all[own : own + ROWS]
    key_row = key_row[None, :]
    segment = segment_ids[:, None]
    first = first_row[None]
    core_in = core[None]

    x = hidden_in
    held = []
    for layer in range(layers):
        w_qkv, w_out, w_in, w_down, gains = unpack(gathered[layer].reshape(DEVICES * CHUNK, 128))
        if layer == 0:
            q, kv_s, kv_t, normed = call(
                heads_zero_kernel,
                [((ROWS, QW), bf16), ((WIN_S, 2 * KW), bf16), ((WIN_T, 2 * KW), bf16),
                 ((ROWS, D), bf16)],
                [window, cosine_all, sine_all, gains, w_qkv],
                flops=800_000_000, nbytes=6_000_000,
            )
        else:
            q, kv, normed = call(
                heads_kernel,
                [((ROWS, QW), bf16), ((ROWS, 2 * KW), bf16), ((ROWS, D), bf16)],
                [x, cosine, sine, gains, w_qkv],
                flops=150_000_000, nbytes=3_000_000,
            )
            kv_s, kv_t = window_of(kv, core)
        x_next, mixed, lse, middle, normed_two, gate_up, hidden = call(
            attend_kernel,
            [((ROWS, D), f32), ((ROWS, QW), bf16), ((GROUP * ROWS, KVH), f32), ((ROWS, D), f32),
             ((ROWS, D), bf16), ((ROWS, 2 * FF), f32), ((ROWS, FF), bf16)],
            [first, x, q, kv_s, kv_t, segment, key_row, gains, w_out, w_in, w_down],
            smem=1, flops=2_000_000_000, nbytes=12_000_000,
        )
        held.append((x, q, kv_s, kv_t, normed, mixed, lse, middle, normed_two, gate_up, hidden,
                     w_qkv, w_out, w_in, w_down, gains))
        x = x_next
    layer_out = x.astype(bf16)

    g = cotangent
    grads = [None] * layers
    for layer in reversed(range(layers)):
        (x, q, kv_s, kv_t, normed, mixed, lse, middle, normed_two, gate_up, hidden,
         w_qkv, w_out, w_in, w_down, gains) = held[layer]
        branch, grad_gu, attn, middle_grad, dq, dkv_s, dkv_t, gain_two = call(
            back_kernel,
            [((ROWS, D), bf16), ((ROWS, 2 * FF), bf16), ((ROWS, D), bf16), ((ROWS, D), f32),
             ((ROWS, QW), bf16), ((WIN_S, 2 * KW), f32), ((WIN_T, 2 * KW), bf16), ((1, D), f32)],
            [first, g, q, kv_s, kv_t, segment, key_row, cosine, sine, gains, w_out, w_in, w_down,
             lse, middle, gate_up],
            smem=1, flops=3_000_000_000, nbytes=15_000_000,
        )
        own_kv, pieces = give_back(dkv_s, dkv_t, core)
        g, project, gain_one = call(
            back_heads_kernel,
            [((ROWS, D), f32), ((ROWS, PW), bf16), ((1, D), f32)],
            [x, dq, own_kv, *pieces, cosine, sine, gains, w_qkv, middle_grad],
            flops=150_000_000, nbytes=3_000_000,
        )
        keep, send = call(
            pack_kernel,
            [((DEVICES // 2 * CHUNK, 128), bf16), ((DEVICES // 2 * CHUNK, 128), bf16)],
            [core_in, normed, project, mixed, attn, normed_two, grad_gu, hidden, branch,
             gain_one, gain_two],
            scratch=[pltpu.VMEM((FLAT_ROWS, 128), f32), pltpu.VMEM((8, FF, 128), f32)],
            smem=1, flops=1_200_000_000, nbytes=30_000_000,
        )
        grads[layer] = reduce_packed(keep, send)
    return (layer_out, g, jnp.stack(grads))


def solution(mesh):
    in_specs = (P("fsdp", None), P("fsdp"), P(None, "fsdp"), P("fsdp", None))
    out_specs = (P("fsdp", None), P("fsdp", None), P(None, "fsdp"))
    return jax.shard_map(body, mesh=mesh, in_specs=in_specs, out_specs=out_specs, check_vma=False)
```

time: 1680 us -> 490 us (0.29); the launches traced: 1650 us -> 482 us
  local copies, waits for them, and re-layouts: 862 us -> 17.2 us
  waiting for transfers between devices: 428 us -> 180 us
  Pallas kernels: 0 us -> 151 us
  starting transfers between devices: 199 us -> 96.6 us
  matrix products: 89 us -> 0 us
  other arithmetic: 55.5 us -> 22.1 us
    unnamed x4 -> x2, waiting for transfers between devices: 419 us -> 0.08 us
    slice x19 -> x7, local copies, waits for them, and re-layouts: 300 us -> 4.39 us  [the longest x1 1.6 us: body(): padded = jnp.pad(weights_flat[layer], (0, CHUNK * 128 - SHARD))]
    concatenate x6, local copies, waits for them, and re-layouts: 218 us -> 3.1 us  [the longest x3 1.62 us: window_of(): same = jnp.concatenate(blocks, axis=0)]
    unnamed x240 -> x53, local copies, waits for them, and re-layouts: 176 us -> 6.5 us
    pallas_call x0 -> x12, Pallas kernels: none -> 151 us  [call(): pl.pallas_call(kernel, out_shape=[jax.ShapeDtypeStruct(s, d) for s, d in...]
    ppermute x64 -> x27, starting transfers between devices: 199 us -> 77.2 us  [the longest x20 75.7 us: hop(): return lax.ppermute(value, 'fsdp', pairs)]
    another operation x10 -> x2, local copies, waits for them, and re-layouts: 113 us -> 0.15 us  [body(): return (layer_out, g, jnp.stack(grads))]
    dot_general x66 -> x0, matrix products: 89 us -> none  [the longest x12 12.8 us: head_scores(): jnp.einsum('qgd,td->gqt', query, keys, preferred_element_type=jnp.float32)]
  transfers between devices with their start and end apart: 66 -> 31, of which waited for: 10 -> 15; matrix products, arithmetic and copies ran while one was open for 36% -> 6% of each run, Pallas kernels for 0% -> 13%
where the time goes in v1:
time: 490 us; the launch traced here: 482 us
  waiting for transfers between devices  180 us (37%)
  Pallas kernels  151 us (31%)
  starting transfers between devices  96.6 us (20%)
  other arithmetic  22.1 us (5%)
  local copies, waits for them, and re-layouts  17.2 us (4%)
  between operations  15.1 us (3%)
    pallas_call x12, Pallas kernels, call(): pl.pallas_call(kernel, out_shape=[jax.ShapeDtypeStruct(s, d) for s, d in...  151 us
    all_to_all x2, waiting for transfers between devices, reduce_packed(): lax.all_to_all(total, 'fsdp', split_axis=0, concat_axis=0, tiled=True, ax...  87 us
    ppermute x20, starting transfers between devices, hop(): return lax.ppermute(value, 'fsdp', pairs)  75.7 us
    all_gather x2, waiting for transfers between devices, body(): gathered.append(lax.all_gather(padded, 'fsdp', axis=0, tiled=True))  69.6 us
    all_to_all x2, starting transfers between devices, reduce_packed(): lax.all_to_all(total, 'fsdp', split_axis=0, concat_axis=0, tiled=True, ax...  19.3 us
    ppermute x20, waiting for transfers between devices, hop(): return lax.ppermute(value, 'fsdp', pairs)  18.7 us
  transfers between devices with their start and end apart: 31, of which 15 were waited for; matrix products, arithmetic and copies ran while one was open for 6% of the time, Pallas kernels for 13%

profile of v1, /device:TPU:50, one launch (start us, length us, event | category | flops | bytes accessed | tf_op | source)
XLA Modules:
  0.0 481.9 jit_solution(12731267532691023758)
XLA Ops:
  7.2 1.6 slice_reduce_fusion
  10.2 1.1 copy.32.x_in
  11.3 3.2 collective-permute-start
  14.5 2.6 collective-permute-start.1
  17.1 5.2 %collective-permute-start.2 = (bf16[128,576]{1,0:T(8,128)(2,1)S(1)}, bf16[128,576]{1,0:T(8,128)(2,1)S(1)}, u32[]{:S(2)}, u32[]{:S(2)}) collective-permute-start(bf16[128,576]{1,0:T(8,128)(2,1)S(1)} %copy.32.x_in), channel_id=1, source_target_pairs={{0,4},{1,5},{2,6},{3,7},{4,8},{5,9},{6,10},{7,11},{8,12},{9,13},{1... | collective-permute-start | bytes 442376 | tf_op jit(solution)/shard_map/ppermute | solution.py:430
  22.3 4.1 collective-permute-start.3
  26.4 3.5 collective-permute-start.5
  32.0 2.7 collective-permute-start.6
  34.7 3.7 collective-permute-done.6
  38.5 3.8 collective-permute-start.7
  42.3 4.2 collective-permute-done.7
  46.4 1.9 collective-permute-start.8
  48.4 3.6 collective-permute-done.8
  52.8 1.4 copy.33.segment
  56.0 2.1 multiply_sine_fusion
  58.1 1.0 pad_maximum_fusion
  60.4 1.4 copy.31
  61.9 20.9 %all-gather.3.cloned.1.call-done = bf16[3670016]{0:T(1024)(128)(2,1)} async-done(((bf16[28672]{0:T(1024)(128)(2,1)}), bf16[3670016]{0:T(1024)(128)(2,1)}) %all-gather.3.cloned.1.call-update) | async-done | bytes 7340048 | tf_op jit(solution)/shard_map/all_gather | solution.py:488
  82.8 21.6 %shard_map.85 = (bf16[576,960]{1,0:T(8,128)(2,1)}, bf16[576,576]{1,0:T(8,128)(2,1)}, bf16[576,3072]{1,0:T(8,128)(2,1)}, bf16[1536,576]{1,0:T(8,128)(2,1)}, f32[8,640]{1,0:T(8,128)}) custom-call(bf16[28672,128]{1,0:T(8,128)(2,1)} %bitcast.23), custom_call_target="tpu_custom_call" | custom-call | flops 200000000 | bytes 30000000 | tf_op jit(solution)/shard_map/pallas_call | solution.py:63
  104.4 48.7 %all-gather.5.cloned.1.call-done = bf16[3670016]{0:T(1024)(128)(2,1)} async-done(((bf16[28672]{0:T(1024)(128)(2,1)}), bf16[3670016]{0:T(1024)(128)(2,1)}) %all-gather.5.cloned.1.call-update) | async-done | bytes 7340048 | tf_op jit(solution)/shard_map/all_gather | solution.py:488
  153.1 21.0 %shard_map.88 = (bf16[576,960]{1,0:T(8,128)(2,1)}, bf16[576,576]{1,0:T(8,128)(2,1)}, bf16[576,3072]{1,0:T(8,128)(2,1)}, bf16[1536,576]{1,0:T(8,128)(2,1)}, f32[8,640]{1,0:T(8,128)}) custom-call(bf16[28672,128]{1,0:T(8,128)(2,1)} %bitcast.24), custom_call_target="tpu_custom_call" | custom-call | flops 200000000 | bytes 30000000 | tf_op jit(solution)/shard_map/pallas_call | solution.py:63
  174.2 4.6 shard_map.86
  178.8 9.2 %shard_map.87 = (f32[128,576]{1,0:T(8,128)}, bf16[128,576]{1,0:T(8,128)(2,1)}, f32[384,3]{1,0:T(8,128)}, f32[128,576]{1,0:T(8,128)}, bf16[128,576]{1,0:T(8,128)(...) custom-call(s32[1]{0:T(128)} %bitcast.first, bf16[128,576]{1,0:T(8,128)(2,1)} %copy-done.3, ...), custom_call_target="tpu_custom_call" | custom-call | flops 2000000000 | bytes 12000000 | tf_op jit(solution)/shard_map/pallas_call | solution.py:63
  188.0 2.8 shard_map.89
  190.8 3.1 collective-permute-start.10
  194.0 5.2 %collective-permute-start.11 = (bf16[128,384]{1,0:T(8,128)(2,1)}, bf16[128,384]{1,0:T(8,128)(2,1)S(1)}, u32[]{:S(2)}, u32[]{:S(2)}) collective-permute-start(bf16[128,384]{1,0:T(8,128)(2,1)} %get-tuple-element.72), channel_id=1, source_target_pairs={{0,6},{1,7},{2,8},{3,9},{4,10},{5,11},{6,12},{7,13},{8,14},{9,15},... | collective-permute-start | bytes 294920 | tf_op jit(solution)/shard_map/ppermute | solution.py:430
  199.1 2.8 collective-permute-start.12
  202.0 4.5 collective-permute-start.13
  206.6 1.7 collective-permute-done.12
  209.0 0.9 constant_dynamic-update-slice_fusion.13.kv_s
  210.3 0.8 copy.35.g_in
  211.1 0.9 collective-permute-done.14.kv_t
  212.8 9.2 %shard_map.90 = (f32[128,576]{1,0:T(8,128)}, bf16[128,576]{1,0:T(8,128)(2,1)}, f32[384,3]{1,0:T(8,128)}, f32[128,576]{1,0:T(8,128)}, bf16[128,576]{1,0:T(8,128)(...) custom-call(s32[1]{0:T(128)} %bitcast.first, f32[128,576]{1,0:T(8,128)} %get-tuple-element.68.x_in, ...), custom_call_target="tpu_custom_call" | custom-call | flops 2000000000 | bytes 12000000 | tf_op jit(solution)/shard_map/pallas_call | solution.py:63
  222.0 12.6 %shard_map.91 = (bf16[128,576]{1,0:T(8,128)(2,1)}, bf16[128,3072]{1,0:T(8,128)(2,1)}, bf16[128,576]{1,0:T(8,128)(2,1)}, f32[128,576]{1,0:T(8,128)}, bf16[128,576...) custom-call(s32[1]{0:T(128)} %bitcast.first, bf16[128,576]{1,0:T(8,128)(2,1)} %copy.35.g_in, ...), custom_call_target="tpu_custom_call" | custom-call | flops 3000000000 | bytes 15000000 | tf_op jit(solution)/shard_map/pallas_call | solution.py:63
  234.7 1.8 collective-permute-done.15
  236.6 1.3 fusion.3
  238.0 1.9 collective-permute-start.16
  239.9 3.8 collective-permute-start.17
  243.7 7.6 %collective-permute-start.18 = (bf16[128,384]{1,0:T(8,128)(2,1)S(1)}, bf16[128,384]{1,0:T(8,128)(2,1)S(1)}, u32[]{:S(2)}, u32[]{:S(2)}) collective-permute-start(bf16[128,384]{1,0:T(8,128)(2,1)S(1)} %get-tuple-element.134), channel_id=1, source_target_pairs={{4,0},{5,1},{6,2},{7,3},{8,4},{9,5},{10,6},{11,7},{12,8},{13,9},{1... | collective-permute-start | bytes 294920 | tf_op jit(solution)/shard_map/ppermute | solution.py:430
  251.3 2.7 collective-permute-start.19
  254.8 3.0 collective-permute-done.19.r2
  258.4 3.2 shard_map.92
  261.6 25.5 %shard_map.96 = (bf16[14336,128]{1,0:T(8,128)(2,1)}, bf16[14336,128]{1,0:T(8,128)(2,1)}) custom-call(s32[1]{0:T(128)} %bitcast.5.core, bf16[128,576]{1,0:T(8,128)(2,1)} %get-tuple-element.105.normed, bf16[128,960]{1,0:T(8,128)(2,1)} %get-tuple-element.106.project, bf16[128,576]{1,0:T(8,128)(2,1)} %get-tuple-element.107.mixed, ...), custom_call_target="tpu_custom_call" | custom-call | flops 1200000000 | bytes 30000000 | tf_op jit(solution)/shard_map/pallas_call | solution.py:63
  287.2 12.6 %shard_map.93 = (bf16[128,576]{1,0:T(8,128)(2,1)}, bf16[128,3072]{1,0:T(8,128)(2,1)}, bf16[128,576]{1,0:T(8,128)(2,1)}, f32[128,576]{1,0:T(8,128)}, bf16[128,576...) custom-call(s32[1]{0:T(128)} %bitcast.first, ...), custom_call_target="tpu_custom_call" | custom-call | flops 3000000000 | bytes 15000000 | tf_op jit(solution)/shard_map/pallas_call | solution.py:63
  300.3 1.6 collective-permute-done.20
  301.9 1.3 fusion.2
  303.3 2.5 collective-permute-start.21
  305.8 2.7 collective-permute-start.22
  308.5 4.6 collective-permute-start.23
  313.1 7.2 %collective-permute-start.24 = (bf16[128,384]{1,0:T(8,128)(2,1)S(1)}, bf16[128,384]{1,0:T(8,128)(2,1)S(1)}, u32[]{:S(2)}, u32[]{:S(2)}) collective-permute-start(bf16[128,384]{1,0:T(8,128)(2,1)S(1)} %get-tuple-element.129), channel_id=1, source_target_pairs={{2,0},{3,1},{4,2},{5,3},{6,4},{7,5},{8,6},{9,7},{10,8},{11,9},{12,... | collective-permute-start | bytes 294920 | tf_op jit(solution)/shard_map/ppermute | solution.py:430
  321.1 1.2 collective-permute-done.24.r2
  322.9 3.2 shard_map.94
  326.1 25.6 %shard_map.95 = (bf16[14336,128]{1,0:T(8,128)(2,1)}, bf16[14336,128]{1,0:T(8,128)(2,1)}) custom-call(s32[1]{0:T(128)} %bitcast.5.core, bf16[128,576]{1,0:T(8,128)(2,1)} %get-tuple-element.93.normed, bf16[128,960]{1,0:T(8,128)(2,1)} %get-tuple-element.94.project, bf16[128,576]{1,0:T(8,128)(2,1)} %get-tuple-element.95.mixed, ...), custom_call_target="tpu_custom_call" | custom-call | flops 1200000000 | bytes 30000000 | tf_op jit(solution)/shard_map/pallas_call | solution.py:63
  351.7 3.8 add_convert_fusion
  355.5 10.1 %all-to-all-start.1 = ((bf16[64,224,128]{2,1,0:T(8,128)(2,1)}), bf16[64,224,128]{2,1,0:T(8,128)(2,1)}, u32[]{:S(2)}, u32[]{:S(2)}) async-start(bf16[64,224,128]{2,1,0:T(8,128)(2,1)} %bitcast.22), calls=%async_computation.1 | async-start | bytes 7340032 | tf_op jit(solution)/shard_map/all_to_all | solution.py:463
  365.7 4.9 %add_convert_fusion.1 = bf16[14336,128]{1,0:T(8,128)(2,1)} fusion(bf16[14336,128]{1,0:T(8,128)(2,1)} %collective-permute-done.25, bf16[14336,128]{1,0:T(8,128)(2,1)} %get-tuple-element.103), kind=kLoop, calls=%fused_computation.3 | loop fusion | flops 7340032 | bytes 11010048 | tf_op jit(solution)/shard_map/convert_element_type | solution.py:460
  370.6 46.3 %all-to-all-done.1 = bf16[64,224,128]{2,1,0:T(8,128)(2,1)} async-done(((bf16[64,224,128]{2,1,0:T(8,128)(2,1)}), bf16[64,224,128]{2,1,0:T(8,128)(2,1)}, u32[]{:S(2)}, u32[]{:S(2)}) %all-to-all-start.1) | async-done | bytes 3670048 | tf_op jit(solution)/shard_map/all_to_all | solution.py:463
  416.9 9.1 %all-to-all-start = ((bf16[64,224,128]{2,1,0:T(8,128)(2,1)}), bf16[64,224,128]{2,1,0:T(8,128)(2,1)}, u32[]{:S(2)}, u32[]{:S(2)}) async-start(bf16[64,224,128]{2,1,0:T(8,128)(2,1)} %bitcast.21), calls=%async_computation | async-start | bytes 7340032 | tf_op jit(solution)/shard_map/all_to_all | solution.py:463
  426.1 0.8 copy.39
  426.8 0.9 copy.40
  427.7 2.6 convert_reduce_fusion
  430.4 40.7 %all-to-all-done = bf16[64,224,128]{2,1,0:T(8,128)(2,1)} async-done(((bf16[64,224,128]{2,1,0:T(8,128)(2,1)}), bf16[64,224,128]{2,1,0:T(8,128)(2,1)}, u32[]{:S(2)}, u32[]{:S(2)}) %all-to-all-start) | async-done | bytes 3670048 | tf_op jit(solution)/shard_map/all_to_all | solution.py:463
  471.1 2.6 convert_reduce_fusion.1
  473.7 0.9 pad_maximum_fusion.2
  (107 shorter events, 13.1 us)
Async XLA Ops:
  7.2 75.6 %all-gather.3.cloned.1.call-start = ((), (), s32[]{:S(2)}) async-start(), calls=%async_computation.2 | async-start | bytes 7397376 | tf_op jit(solution)/shard_map/all_gather | solution.py:488
  9.5 143.7 %all-gather.5.cloned.1.call-start = ((), (), s32[]{:S(2)}) async-start(), calls=%async_computation.3 | async-start | bytes 7397376 | tf_op jit(solution)/shard_map/all_gather | solution.py:488
  11.3 47.8 %copy-start.3 = (bf16[128,576]{1,0:T(8,128)(2,1)}, bf16[128,576]{1,0:T(8,128)(2,1)S(1)}, u32[]{:S(2)}) copy-start(bf16[128,576]{1,0:T(8,128)(2,1)S(1)} %copy.32.x_in) | copy-start | bytes 442372
  11.3 43.5 %collective-permute-start = (bf16[128,576]{1,0:T(8,128)(2,1)S(1)}, bf16[128,576]{1,0:T(8,128)(2,1)S(1)}, u32[]{:S(2)}, u32[]{:S(2)}) collective-permute-start(bf16[128,576]{1,0:T(8,128)(2,1)S(1)} %copy.32.x_in), channel_id=1, source_target_pairs={{0,8},{1,9},{2,10},{3,11},{4,12},{5,13},{6,14},{7,15},{8,16},{9,17... | collective-permute-start | bytes 442376 | tf_op jit(solution)/shard_map/ppermute | solution.py:430
  14.5 40.4 %collective-permute-start.1 = (bf16[128,576]{1,0:T(8,128)(2,1)S(1)}, bf16[128,576]{1,0:T(8,128)(2,1)S(1)}, u32[]{:S(2)}, u32[]{:S(2)}) collective-permute-start(bf16[128,576]{1,0:T(8,128)(2,1)S(1)} %copy.32.x_in), channel_id=1, source_target_pairs={{0,6},{1,7},{2,8},{3,9},{4,10},{5,11},{6,12},{7,13},{8,14},{9,15},... | collective-permute-start | bytes 442376 | tf_op jit(solution)/shard_map/ppermute | solution.py:430
  17.1 37.8 %collective-permute-start.2 = (bf16[128,576]{1,0:T(8,128)(2,1)S(1)}, bf16[128,576]{1,0:T(8,128)(2,1)S(1)}, u32[]{:S(2)}, u32[]{:S(2)}) collective-permute-start(bf16[128,576]{1,0:T(8,128)(2,1)S(1)} %copy.32.x_in), channel_id=1, source_target_pairs={{0,4},{1,5},{2,6},{3,7},{4,8},{5,9},{6,10},{7,11},{8,12},{9,13},{1... | collective-permute-start | bytes 442376 | tf_op jit(solution)/shard_map/ppermute | solution.py:430
  22.3 32.7 %collective-permute-start.3 = (bf16[128,576]{1,0:T(8,128)(2,1)S(1)}, bf16[128,576]{1,0:T(8,128)(2,1)S(1)}, u32[]{:S(2)}, u32[]{:S(2)}) collective-permute-start(bf16[128,576]{1,0:T(8,128)(2,1)S(1)} %copy.32.x_in), channel_id=1, source_target_pairs={{0,2},{1,3},{2,4},{3,5},{4,6},{5,7},{6,8},{7,9},{8,10},{9,11},{10,... | collective-permute-start | bytes 442376 | tf_op jit(solution)/shard_map/ppermute | solution.py:430
  26.4 5.6 %collective-permute-start.5 = (s32[128]{0:T(128)}, s32[128]{0:T(128)S(1)}, u32[]{:S(2)}, u32[]{:S(2)}) collective-permute-start(s32[128]{0:T(128)} %param.7), channel_id=1, source_target_pairs={{0,8},{1,9},{2,10},{3,11},{4,12},{5,13},{6,14},{7,15},{8,16},{9,17... | collective-permute-start | bytes 1544 | tf_op jit(solution)/shard_map/ppermute | solution.py:430
  32.0 6.5 %collective-permute-start.6 = (s32[128]{0:T(128)}, s32[128]{0:T(128)S(1)}, u32[]{:S(2)}, u32[]{:S(2)}) collective-permute-start(s32[128]{0:T(128)} %param.7), channel_id=1, source_target_pairs={{0,6},{1,7},{2,8},{3,9},{4,10},{5,11},{6,12},{7,13},{8,14},{9,15},... | collective-permute-start | bytes 1544 | tf_op jit(solution)/shard_map/ppermute | solution.py:430
  38.5 8.0 %collective-permute-start.7 = (s32[128]{0:T(128)}, s32[128]{0:T(128)S(1)}, u32[]{:S(2)}, u32[]{:S(2)}) collective-permute-start(s32[128]{0:T(128)} %param.7), channel_id=1, source_target_pairs={{0,4},{1,5},{2,6},{3,7},{4,8},{5,9},{6,10},{7,11},{8,12},{9,13},{1... | collective-permute-start | bytes 1544 | tf_op jit(solution)/shard_map/ppermute | solution.py:430
  46.4 5.6 %collective-permute-start.8 = (s32[128]{0:T(128)}, s32[128]{0:T(128)S(1)}, u32[]{:S(2)}, u32[]{:S(2)}) collective-permute-start(s32[128]{0:T(128)} %param.7), channel_id=1, source_target_pairs={{0,2},{1,3},{2,4},{3,5},{4,6},{5,7},{6,8},{7,9},{8,10},{9,11},{10,... | collective-permute-start | bytes 1544 | tf_op jit(solution)/shard_map/ppermute | solution.py:430
  52.7 2.0 collective-permute-start.9
  55.4 5.0 %collective-permute-start.4 = (bf16[512,576]{0,1:T(8,128)(2,1)S(1)}, bf16[512,576]{0,1:T(8,128)(2,1)}, u32[]{:S(2)}, u32[]{:S(2)}) collective-permute-start(bf16[512,576]{0,1:T(8,128)(2,1)S(1)} %copy.29), channel_id=1, source_target_pairs={{0,1},{1,0},{2,3},{3,2},{4,5},{5,4},{6,7},{7,6},{8,9},{9,8},{10,11... | collective-permute-start | bytes 1769480 | tf_op jit(solution)/shard_map/ppermute | solution.py:434
  59.1 45.3 %copy-start.1 = (f32[1152,128]{1,0:T(8,128)}, f32[1152,128]{1,0:T(8,128)S(1)}, u32[]{:S(2)}) copy-start(f32[1152,128]{1,0:T(8,128)S(1)} %get-tuple-element.159.cosine) | copy-start | bytes 1769476
  59.1 45.3 %copy-start.2 = (f32[1152,128]{1,0:T(8,128)}, f32[1152,128]{1,0:T(8,128)S(1)}, u32[]{:S(2)}) copy-start(f32[1152,128]{1,0:T(8,128)S(1)} %get-tuple-element.160.sine) | copy-start | bytes 1769476
  61.9 112.3 %copy-start.5 = (bf16[1152,576]{1,0:T(8,128)(2,1)}, bf16[1152,576]{1,0:T(8,128)(2,1)S(1)}, u32[]{:S(2)}) copy-start(bf16[1152,576]{1,0:T(8,128)(2,1)S(1)} %constant_dynamic-update-slice_fusion.5.window) | copy-start | bytes 3981316
  178.8 31.5 %copy-start.9 = (bf16[128,576]{0,1:T(8,128)(2,1)S(1)}, bf16[128,576]{0,1:T(8,128)(2,1)}, u32[]{:S(2)}) copy-start(bf16[128,576]{0,1:T(8,128)(2,1)} %param.9) | copy-start | bytes 442372
  190.8 15.7 %collective-permute-start.10 = (bf16[128,384]{1,0:T(8,128)(2,1)}, bf16[128,384]{1,0:T(8,128)(2,1)S(1)}, u32[]{:S(2)}, u32[]{:S(2)}) collective-permute-start(bf16[128,384]{1,0:T(8,128)(2,1)} %get-tuple-element.72), channel_id=1, source_target_pairs={{0,8},{1,9},{2,10},{3,11},{4,12},{5,13},{6,14},{7,15},{8,16},{9,17... | collective-permute-start | bytes 294920 | tf_op jit(solution)/shard_map/ppermute | solution.py:430
  194.0 12.6 %collective-permute-start.11 = (bf16[128,384]{1,0:T(8,128)(2,1)}, bf16[128,384]{1,0:T(8,128)(2,1)S(1)}, u32[]{:S(2)}, u32[]{:S(2)}) collective-permute-start(bf16[128,384]{1,0:T(8,128)(2,1)} %get-tuple-element.72), channel_id=1, source_target_pairs={{0,6},{1,7},{2,8},{3,9},{4,10},{5,11},{6,12},{7,13},{8,14},{9,15},... | collective-permute-start | bytes 294920 | tf_op jit(solution)/shard_map/ppermute | solution.py:430
  199.1 9.1 %collective-permute-start.12 = (bf16[128,384]{1,0:T(8,128)(2,1)}, bf16[128,384]{1,0:T(8,128)(2,1)S(1)}, u32[]{:S(2)}, u32[]{:S(2)}) collective-permute-start(bf16[128,384]{1,0:T(8,128)(2,1)} %get-tuple-element.72), channel_id=1, source_target_pairs={{0,4},{1,5},{2,6},{3,7},{4,8},{5,9},{6,10},{7,11},{8,12},{9,13},{1... | collective-permute-start | bytes 294920 | tf_op jit(solution)/shard_map/ppermute | solution.py:430
  202.0 7.0 %collective-permute-start.13 = (bf16[128,384]{1,0:T(8,128)(2,1)}, bf16[128,384]{1,0:T(8,128)(2,1)S(1)}, u32[]{:S(2)}, u32[]{:S(2)}) collective-permute-start(bf16[128,384]{1,0:T(8,128)(2,1)} %get-tuple-element.72), channel_id=1, source_target_pairs={{0,2},{1,3},{2,4},{3,5},{4,6},{5,7},{6,8},{7,9},{8,10},{9,11},{10,... | collective-permute-start | bytes 294920 | tf_op jit(solution)/shard_map/ppermute | solution.py:430
  209.9 2.0 copy-start.4
  210.0 2.0 collective-permute-start.14
  212.0 0.8 copy-start.6
  234.6 1.9 collective-permute-start.15
  238.0 16.8 %collective-permute-start.16 = (bf16[128,384]{1,0:T(8,128)(2,1)S(1)}, bf16[128,384]{1,0:T(8,128)(2,1)S(1)}, u32[]{:S(2)}, u32[]{:S(2)}) collective-permute-start(bf16[128,384]{1,0:T(8,128)(2,1)S(1)} %get-tuple-element.136), channel_id=1, source_target_pairs={{8,0},{9,1},{10,2},{11,3},{12,4},{13,5},{14,6},{15,7},{16,8},{17,9... | collective-permute-start | bytes 294920 | tf_op jit(solution)/shard_map/ppermute | solution.py:430
  239.9 14.9 %collective-permute-start.17 = (bf16[128,384]{1,0:T(8,128)(2,1)S(1)}, bf16[128,384]{1,0:T(8,128)(2,1)S(1)}, u32[]{:S(2)}, u32[]{:S(2)}) collective-permute-start(bf16[128,384]{1,0:T(8,128)(2,1)S(1)} %get-tuple-element.135), channel_id=1, source_target_pairs={{6,0},{7,1},{8,2},{9,3},{10,4},{11,5},{12,6},{13,7},{14,8},{15,9},... | collective-permute-start | bytes 294920 | tf_op jit(solution)/shard_map/ppermute | solution.py:430
  243.7 11.1 %collective-permute-start.18 = (bf16[128,384]{1,0:T(8,128)(2,1)S(1)}, bf16[128,384]{1,0:T(8,128)(2,1)S(1)}, u32[]{:S(2)}, u32[]{:S(2)}) collective-permute-start(bf16[128,384]{1,0:T(8,128)(2,1)S(1)} %get-tuple-element.134), channel_id=1, source_target_pairs={{4,0},{5,1},{6,2},{7,3},{8,4},{9,5},{10,6},{11,7},{12,8},{13,9},{1... | collective-permute-start | bytes 294920 | tf_op jit(solution)/shard_map/ppermute | solution.py:430
  251.3 6.5 %collective-permute-start.19 = (bf16[128,384]{1,0:T(8,128)(2,1)S(1)}, bf16[128,384]{1,0:T(8,128)(2,1)S(1)}, u32[]{:S(2)}, u32[]{:S(2)}) collective-permute-start(bf16[128,384]{1,0:T(8,128)(2,1)S(1)} %get-tuple-element.133), channel_id=1, source_target_pairs={{2,0},{3,1},{4,2},{5,3},{6,4},{7,5},{8,6},{9,7},{10,8},{11,9},{12,... | collective-permute-start | bytes 294920 | tf_op jit(solution)/shard_map/ppermute | solution.py:430
  254.8 3.1 copy-start.14
  254.8 3.0 copy-start.15
  254.8 3.0 copy-start.16
  257.8 0.6 copy-start.17
  287.2 64.6 %collective-permute-start.26 = (bf16[14336,128]{1,0:T(8,128)(2,1)}, bf16[14336,128]{1,0:T(8,128)(2,1)}, u32[]{:S(2)}, u32[]{:S(2)}) collective-permute-start(bf16[14336,128]{1,0:T(8,128)(2,1)} %get-tuple-element.116), channel_id=1, source_target_pairs={{0,1},{1,0},{2,3},{3,2},{4,5},{5,4},{6,7},{7,6},{8,9},{9,8},{10,11... | collective-permute-start | bytes 11010056 | tf_op jit(solution)/shard_map/ppermute | solution.py:434
  299.8 2.1 collective-permute-start.20
  303.3 17.8 %collective-permute-start.21 = (bf16[128,384]{1,0:T(8,128)(2,1)S(1)}, bf16[128,384]{1,0:T(8,128)(2,1)S(1)}, u32[]{:S(2)}, u32[]{:S(2)}) collective-permute-start(bf16[128,384]{1,0:T(8,128)(2,1)S(1)} %get-tuple-element.132), channel_id=1, source_target_pairs={{8,0},{9,1},{10,2},{11,3},{12,4},{13,5},{14,6},{15,7},{16,8},{17,9... | collective-permute-start | bytes 294920 | tf_op jit(solution)/shard_map/ppermute | solution.py:430
  305.8 15.3 %collective-permute-start.22 = (bf16[128,384]{1,0:T(8,128)(2,1)S(1)}, bf16[128,384]{1,0:T(8,128)(2,1)S(1)}, u32[]{:S(2)}, u32[]{:S(2)}) collective-permute-start(bf16[128,384]{1,0:T(8,128)(2,1)S(1)} %get-tuple-element.131), channel_id=1, source_target_pairs={{6,0},{7,1},{8,2},{9,3},{10,4},{11,5},{12,6},{13,7},{14,8},{15,9},... | collective-permute-start | bytes 294920 | tf_op jit(solution)/shard_map/ppermute | solution.py:430
  308.5 12.5 %collective-permute-start.23 = (bf16[128,384]{1,0:T(8,128)(2,1)S(1)}, bf16[128,384]{1,0:T(8,128)(2,1)S(1)}, u32[]{:S(2)}, u32[]{:S(2)}) collective-permute-start(bf16[128,384]{1,0:T(8,128)(2,1)S(1)} %get-tuple-element.130), channel_id=1, source_target_pairs={{4,0},{5,1},{6,2},{7,3},{8,4},{9,5},{10,6},{11,7},{12,8},{13,9},{1... | collective-permute-start | bytes 294920 | tf_op jit(solution)/shard_map/ppermute | solution.py:430
  313.1 9.1 %collective-permute-start.24 = (bf16[128,384]{1,0:T(8,128)(2,1)S(1)}, bf16[128,384]{1,0:T(8,128)(2,1)S(1)}, u32[]{:S(2)}, u32[]{:S(2)}) collective-permute-start(bf16[128,384]{1,0:T(8,128)(2,1)S(1)} %get-tuple-element.129), channel_id=1, source_target_pairs={{2,0},{3,1},{4,2},{5,3},{6,4},{7,5},{8,6},{9,7},{10,8},{11,9},{12,... | collective-permute-start | bytes 294920 | tf_op jit(solution)/shard_map/ppermute | solution.py:430
  320.3 31.4 %copy-start = (bf16[14336,128]{1,0:T(8,128)(2,1)S(1)}, bf16[14336,128]{1,0:T(8,128)(2,1)}, u32[]{:S(2)}) copy-start(bf16[14336,128]{1,0:T(8,128)(2,1)} %get-tuple-element.115) | copy-start | bytes 11010052
  321.0 1.2 copy-start.10
  321.0 1.2 copy-start.11
  321.1 1.2 copy-start.12
  322.3 0.6 copy-start.13
  351.7 14.0 %collective-permute-start.25 = (bf16[14336,128]{1,0:T(8,128)(2,1)}, bf16[14336,128]{1,0:T(8,128)(2,1)}, u32[]{:S(2)}, u32[]{:S(2)}) collective-permute-start(bf16[14336,128]{1,0:T(8,128)(2,1)} %get-tuple-element.104), channel_id=1, source_target_pairs={{0,1},{1,0},{2,3},{3,2},{4,5},{5,4},{6,7},{7,6},{8,9},{9,8},{10,11... | collective-permute-start | bytes 11010056 | tf_op jit(solution)/shard_map/ppermute | solution.py:434
  355.5 61.3 %all-to-all-start.1 = ((bf16[64,224,128]{2,1,0:T(8,128)(2,1)}), bf16[64,224,128]{2,1,0:T(8,128)(2,1)}, u32[]{:S(2)}, u32[]{:S(2)}) async-start(bf16[64,224,128]{2,1,0:T(8,128)(2,1)} %bitcast.22), calls=%async_computation.1 | async-start | bytes 7340032 | tf_op jit(solution)/shard_map/all_to_all | solution.py:463
  416.9 9.1 %copy-start.8 = (f32[128,576]{1,0:T(8,128)S(1)}, f32[128,576]{1,0:T(8,128)}, u32[]{:S(2)}) copy-start(f32[128,576]{1,0:T(8,128)} %get-tuple-element.76) | copy-start | bytes 884740
  416.9 10.0 %copy-start.7 = (f32[128,576]{1,0:T(8,128)S(1)}, f32[128,576]{1,0:T(8,128)}, u32[]{:S(2)}) copy-start(f32[128,576]{1,0:T(8,128)} %get-tuple-element.121) | copy-start | bytes 884740
  416.9 54.2 %all-to-all-start = ((bf16[64,224,128]{2,1,0:T(8,128)(2,1)}), bf16[64,224,128]{2,1,0:T(8,128)(2,1)}, u32[]{:S(2)}, u32[]{:S(2)}) async-start(bf16[64,224,128]{2,1,0:T(8,128)(2,1)} %bitcast.21), calls=%async_computation | async-start | bytes 7340032 | tf_op jit(solution)/shard_map/all_to_all | solution.py:463
Sparse Core Ops, SparseCore 0:
  11.6 71.2 all-gather.2
  86.4 66.7 all-gather.4

commit v2 on v1

--- a/solution.py
+++ b/solution.py
@@ -22,7 +22,10 @@
 PARAMS = 3540096
 SHARD = PARAMS // DEVICES
 CHUNK = 224
-FLAT_ROWS = 27904
+SECTION = 240
+SPLIT = 20
+LOW_PLANES = 11
+EDGE = 456
 SAME_CORE = 4
 WIN_S = (SAME_CORE + 1) * ROWS
 WIN_T = SAME_CORE * ROWS
@@ -116,71 +119,112 @@
             before = now
 
 
-def unpack_kernel(gathered, w_qkv, w_out, w_in, w_down, gains, flat, tile):
-    flat[0:8, :] = jnp.zeros((8, 128), f32)
-    lane = lax.broadcasted_iota(jnp.int32, (CHUNK, 128), 1)
-    first_two = lax.broadcasted_iota(jnp.int32, (8, 128), 0) < 2
-
-    def one_shard(d, carry):
-        shift = lax.rem(d * 9, 128)
-        base = d * 216 + lax.div(d * 9, 128)
-        rows = gathered[pl.ds(pl.multiple_of(d * CHUNK, CHUNK), CHUNK), :].astype(f32)
-        turned = pltpu.roll(rows, shift, 1)
-        behind = pltpu.roll(turned, 1, 0)
-        value = jnp.where(lane >= shift, turned, behind)
-        shared = jnp.where(first_two, flat[pl.ds(base, 8), :], 0.0)
-        flat[pl.ds(base, 8), :] = shared + value[0:8, :]
-        flat[pl.ds(base + 8, CHUNK - 8), :] = value[8:, :]
-        return carry
-
-    lax.fori_loop(0, DEVICES, one_shard, 0)
-
-    def matrix(out, start_half, width_half):
-        rows, columns = out.shape
-
-        def store(parity, at, value):
-            tile[at, pl.ds(parity, rows // 2, stride=2), :] = value
-
-        for parity in range(2):
-            take_rows(
-                flat, start_half + parity * width_half, rows // 2, width_half,
-                functools.partial(store, parity),
+def gather_flat(gathered, layer, first, count, groups, flat, landing, sems):
+    size = count // groups
+    copies = []
+    for n in range(groups):
+        copies.append(
+            pltpu.make_async_copy(
+                gathered.at[pl.ds(first + n * size, size), layer],
+                landing.at[pl.ds(n * size, size)],
+                sems.at[n],
             )
-        for t in range((width_half + 1) // 2):
-            wide = min(128, columns - 128 * t)
-            out[:, 128 * t : 128 * t + wide] = tile[t, 0:rows, 0:wide].astype(bf16)
-
-    matrix(w_qkv, HALF_QKV, PW // 64)
-    matrix(w_out, HALF_OUT, D // 64)
-    matrix(w_down, HALF_DOWN, D // 64)
+        )
+        copies[-1].start()
+    tail = jnp.zeros((SECTION - 216, 128), f32)
+    for n in range(groups):
+        copies[n].wait()
+
+        def one_shard(d, tail):
+            rows = landing[d].astype(f32)
+            base = pl.multiple_of(d * 216, 8)
+            flat[pl.ds(base, 24), :] = tail + rows[0:24, :]
+            flat[pl.ds(base + 24, 192), :] = rows[24:216, :]
+            return rows[216:SECTION, :]
+
+        tail = lax.fori_loop(n * size, (n + 1) * size, one_shard, tail)
+    flat[count * 216 : count * 216 + 24, :] = tail
+
+
+def take_matrix(flat, tile, out, start_half, width_half):
+    rows, columns = out.shape
+
+    def store(parity, at, value):
+        tile[at, pl.ds(parity, rows // 2, stride=2), :] = value
+
+    for parity in range(2):
+        take_rows(
+            flat, start_half + parity * width_half, rows // 2, width_half,
+            functools.partial(store, parity),
+        )
+    for t in range((width_half + 1) // 2):
+        wide = min(128, columns - 128 * t)
+        out[:, 128 * t : 128 * t + wide] = tile[t, 0:rows, 0:wide].astype(bf16)
+
+
+def take_gain(flat, gain, start):
+    first = start // 2
+    for t in range(5):
+        if start % 2 == 0:
+            value = flat[first + t : first + t + 1, :]
+        else:
+            here = pltpu.roll(flat[first + t : first + t + 1, :], 64, 1)
+            after = pltpu.roll(flat[first + t + 1 : first + t + 2, :], 64, 1)
+            value = jnp.where(low_half((1, 128)), here, after)
+        gain[0:1, 128 * t : 128 * t + 128] = value
+
+
+def unpack_first_kernel(layer, gathered, w_qkv, gain, landing, flat, tile, sems):
+    gather_flat(gathered, layer, 0, SPLIT + 1, 3, flat, landing, sems)
+    take_gain(flat, gain, HALF_GAIN_ONE)
+    take_matrix(flat, tile, w_qkv, HALF_QKV, PW // 64)
+
+
+def unpack_rest_kernel(layer, gathered, w_out, w_in, w_down, gain, landing, flat, tile, sems):
+    gather_flat(gathered, layer, SPLIT, DEVICES - SPLIT, 4, flat, landing, sems)
+    skip = 2 * 216 * SPLIT
+    take_matrix(flat, tile, w_out, HALF_OUT - skip, D // 64)
+    take_gain(flat, gain, HALF_GAIN_TWO - skip)
+    take_matrix(flat, tile, w_down, HALF_DOWN - skip, D // 64)
 
     def in_tile(c, carry):
         w_in[:, pl.ds(pl.multiple_of(c * 128, 128), 128)] = flat[
-            pl.ds(HALF_IN // 2 + c, D, stride=24), :
+            pl.ds((HALF_IN - skip) // 2 + c, D, stride=24), :
         ].astype(bf16)
         return carry
 
     lax.fori_loop(0, 24, in_tile, 0)
 
-    for at, start in ((0, HALF_GAIN_ONE), (1, HALF_GAIN_TWO)):
-        first = start // 2
-        for t in range(5):
-            if start % 2 == 0:
-                value = flat[first + t : first + t + 1, :]
-            else:
-                here = pltpu.roll(flat[first + t : first + t + 1, :], 64, 1)
-                after = pltpu.roll(flat[first + t + 1 : first + t + 2, :], 64, 1)
-                value = jnp.where(low_half((1, 128)), here, after)
-            gains[at : at + 1, 128 * t : 128 * t + 128] = value
-
-
-def unpack(gathered):
-    return call(
-        unpack_kernel,
-        [((D, PW), bf16), ((QW, D), bf16), ((D, 2 * FF), bf16), ((FF, D), bf16), ((8, 640), f32)],
-        [gathered],
-        scratch=[pltpu.VMEM((FLAT_ROWS, 128), f32), pltpu.VMEM((8, FF, 128), f32)],
-        flops=200_000_000, nbytes=30_000_000,
+
+def unpack_call(kernel, layer, out_shape, gathered, count, groups, tiles, nbytes):
+    return pl.pallas_call(
+        functools.partial(kernel, layer),
+        out_shape=[jax.ShapeDtypeStruct(s, d) for s, d in out_shape],
+        in_specs=[pl.BlockSpec(memory_space=pl.ANY)],
+        out_specs=[pl.BlockSpec(memory_space=pltpu.VMEM) for _ in out_shape],
+        scratch_shapes=[
+            pltpu.VMEM((count, SECTION, 128), bf16),
+            pltpu.VMEM((count * 216 + 32, 128), f32),
+            pltpu.VMEM(tiles, f32),
+            pltpu.SemaphoreType.DMA((groups,)),
+        ],
+        compiler_params=pltpu.CompilerParams(vmem_limit_bytes=VMEM_LIMIT),
+        cost_estimate=pl.CostEstimate(flops=0, bytes_accessed=nbytes, transcendentals=0),
+    )(gathered)
+
+
+def unpack_first(gathered, layer):
+    return unpack_call(
+        unpack_first_kernel, layer, [((D, PW), bf16), ((1, 640), f32)], gathered,
+        SPLIT + 1, 3, (8, D, 128), 9_000_000,
+    )
+
+
+def unpack_rest(gathered, layer):
+    return unpack_call(
+        unpack_rest_kernel, layer,
+        [((QW, D), bf16), ((D, 2 * FF), bf16), ((FF, D), bf16), ((1, 640), f32)], gathered,
+        DEVICES - SPLIT, 4, (5, FF, 128), 30_000_000,
     )
 
 
@@ -199,8 +243,8 @@
     return lax.rsqrt(jnp.mean(values * values, axis=-1, keepdims=True) + epsilon)
 
 
-def heads_zero_kernel(window, cosine, sine, gains, w_qkv, q_out, kv_s, kv_t, normed_out):
-    gain = gains[0:1, 0:D]
+def heads_zero_kernel(window, cosine, sine, gain_row, w_qkv, q_out, kv_s, kv_t, normed_out):
+    gain = gain_row[:, 0:D]
     for begin, rows in ((0, 384), (384, 384), (768, 384)):
         x = window[begin : begin + rows, :].astype(f32)
         normed = (x * inverse_norm(x) * gain).astype(bf16)
@@ -223,9 +267,9 @@
     ].astype(bf16)
 
 
-def heads_kernel(x_in, cosine, sine, gains, w_qkv, q_out, kv_out, normed_out):
+def heads_kernel(x_in, cosine, sine, gain_row, w_qkv, q_out, kv_out, normed_out):
     x = x_in[...]
-    normed = (x * inverse_norm(x) * gains[0:1, 0:D]).astype(bf16)
+    normed = (x * inverse_norm(x) * gain_row[:, 0:D]).astype(bf16)
     normed_out[...] = normed
     project = mm(normed, w_qkv[...])
     both = turn(project[:, 0:768], cosine[...], sine[...])
@@ -252,7 +296,7 @@
 
 
 def attend_kernel(
-    first, x_in, q_in, kv_s, kv_t, segment, key_row, gains, w_out, w_in, w_down,
+    first, x_in, q_in, kv_s, kv_t, segment, key_row, gain_row, w_out, w_in, w_down,
     x_out, mixed_out, lse_out, middle_out, normed_out, gate_up_out, hidden_out,
 ):
     allowed = allowed_of(segment[...], key_row[...], first[0])
@@ -276,7 +320,7 @@
     mixed_out[...] = mixed
     middle = x_in[...].astype(f32) + mm(mixed, w_out[...])
     middle_out[...] = middle
-    normed = (middle * inverse_norm(middle) * gains[1:2, 0:D]).astype(bf16)
+    normed = (middle * inverse_norm(middle) * gain_row[:, 0:D]).astype(bf16)
     normed_out[...] = normed
     gate_up = mm(normed, w_in[...])
     gate_up_out[...] = gate_up
@@ -294,7 +338,7 @@
 
 
 def back_kernel(
-    first, g_in, q_in, kv_s, kv_t, segment, key_row, cosine, sine, gains, w_out, w_in, w_down,
+    first, g_in, q_in, kv_s, kv_t, segment, key_row, cosine, sine, gain_row, w_out, w_in, w_down,
     lse, middle_in, gate_up,
     branch_out, grad_gu_out, attn_out, middle_grad_out, dq_out, dkv_s, dkv_t, gain_out,
 ):
@@ -313,7 +357,7 @@
     middle = middle_in[...]
     inverse = inverse_norm(middle)
     gain_out[...] = jnp.sum(grad_two * middle * inverse, axis=0, keepdims=True)
-    grad_middle = g + norm_back(middle, inverse, gains[1:2, 0:D], grad_two)
+    grad_middle = g + norm_back(middle, inverse, gain_row[:, 0:D], grad_two)
     middle_grad_out[...] = grad_middle
     attn = grad_middle.astype(bf16)
     attn_out[...] = attn
@@ -347,7 +391,7 @@
 
 
 def back_heads_kernel(
-    x_in, dq, own, r8, r6, r4, r2, cosine, sine, gains, w_qkv, middle_grad,
+    x_in, dq, own, r8, r6, r4, r2, cosine, sine, gain_row, w_qkv, middle_grad,
     g_out, project_out, gain_out,
 ):
     total = own[...]
@@ -363,66 +407,79 @@
     x = x_in[...].astype(f32)
     inverse = inverse_norm(x)
     gain_out[...] = jnp.sum(grad * x * inverse, axis=0, keepdims=True)
-    g_out[...] = middle_grad[...] + norm_back(x, inverse, gains[0:1, 0:D], grad)
-
-
-def pack_kernel(
-    core, normed, project, mixed, attn, normed_two, grad_gu, hidden, branch, gain_one, gain_two,
-    keep, send, flat, tile,
-):
-    for at, start, gain in ((0, HALF_GAIN_ONE, gain_one), (1, HALF_GAIN_TWO, gain_two)):
-        row = jnp.concatenate([gain[...], jnp.zeros((1, 64), f32)], axis=1)
-        first = start // 2
-        before = None
-        for t in range(5):
-            part = row[:, 128 * t : 128 * t + 128]
-            place = slice(first + t, first + t + 1)
-            if start % 2 == 0:
-                flat[place, :] = part
+    g_out[...] = middle_grad[...] + norm_back(x, inverse, gain_row[:, 0:D], grad)
+
+
+def put_gain(flat, gain, start):
+    row = jnp.concatenate([gain[...], jnp.zeros((1, 64), f32)], axis=1)
+    first = start // 2
+    before = None
+    for t in range(5):
+        part = row[:, 128 * t : 128 * t + 128]
+        place = slice(first + t, first + t + 1)
+        if start % 2 == 0:
+            flat[place, :] = part
+        else:
+            now = pltpu.roll(part, 64, 1)
+            if before is None:
+                flat[place, :] = now
             else:
-                now = pltpu.roll(part, 64, 1)
-                if before is None:
-                    flat[place, :] = now
-                else:
-                    flat[place, :] = jnp.where(low_half((1, 128)), before, now)
-                before = now
-
-    def matrix(left, right, start_half, width_half):
-        rows, columns = left.shape[1], right.shape[1]
-        for t in range((width_half + 1) // 2):
-            wide = min(128, columns - 128 * t)
-            tile[t, 0:rows, 0:wide] = t_mm(left[...], right[:, 128 * t : 128 * t + wide])
-        for parity in range(2):
-            put_rows(
-                flat, start_half + parity * width_half, rows // 2, width_half,
-                lambda t, parity=parity: tile[t, pl.ds(parity, rows // 2, stride=2), :],
-            )
-
-    matrix(normed, project, HALF_QKV, PW // 64)
-    matrix(mixed, attn, HALF_OUT, D // 64)
-    matrix(hidden, branch, HALF_DOWN, D // 64)
-
-    def in_tile(c, carry):
-        flat[pl.ds(HALF_IN // 2 + c, D, stride=24), :] = t_mm(
-            normed_two[...], grad_gu[:, pl.ds(pl.multiple_of(c * 128, 128), 128)]
-        )
-        return carry
-
-    lax.fori_loop(0, 24, in_tile, 0)
-
-    lane = lax.broadcasted_iota(jnp.int32, (CHUNK, 128), 1)
+                flat[place, :] = jnp.where(low_half((1, 128)), before, now)
+            before = now
+
+
+def put_matrix(flat, tile, left, right, start_half, width_half):
+    rows, columns = left.shape[1], right.shape[1]
+    for t in range((width_half + 1) // 2):
+        wide = min(128, columns - 128 * t)
+        tile[t, 0:rows, 0:wide] = t_mm(left[...], right[:, 128 * t : 128 * t + wide])
+    for parity in range(2):
+        put_rows(
+            flat, start_half + parity * width_half, rows // 2, width_half,
+            lambda t, parity=parity: tile[t, pl.ds(parity, rows // 2, stride=2), :],
+        )
+
+
+def cut(flat, core, first_plane, planes, skip, keep, send):
+    last = lax.broadcasted_iota(jnp.int32, (CHUNK, 128), 0) == CHUNK - 1
     for out, flip in ((keep, 0), (send, 1)):
-        def one_shard(k, carry):
-            d = 2 * k + lax.rem(core[0] + flip, 2)
-            shift = lax.rem(d * 9, 128)
-            base = d * 216 + lax.div(d * 9, 128)
-            turned = pltpu.roll(flat[pl.ds(base, CHUNK), :], lax.rem(128 - shift, 128), 1)
-            ahead = pltpu.roll(turned, CHUNK - 1, 0)
-            value = jnp.where(lane < 128 - shift, turned, ahead)
+        def one_owner(k, carry, out=out, flip=flip):
+            d = 2 * (first_plane + k) + lax.rem(core[0] + flip, 2)
+            base = pl.multiple_of(d * 216 - skip + 8, 8)
+            odd = jnp.where(d < DEVICES // 2, base - 1, base + CHUNK - 1)
+            value = jnp.where(last, flat[pl.ds(odd, 1), :], flat[pl.ds(base, CHUNK), :])
             out[pl.ds(pl.multiple_of(k * CHUNK, CHUNK), CHUNK), :] = value.astype(bf16)
             return carry
 
-        lax.fori_loop(0, DEVICES // 2, one_shard, 0)
+        lax.fori_loop(0, planes, one_owner, 0)
+
+
+def pack_rest_kernel(
+    core, mixed, attn, normed_two, grad_gu, hidden, branch, gain_two, keep, send, edge, flat, tile
+):
+    skip = 216 * SPLIT
+    half = 2 * (7 - skip)
+    put_gain(flat, gain_two, HALF_GAIN_TWO + half)
+    put_matrix(flat, tile, mixed, attn, HALF_OUT + half, D // 64)
+    put_matrix(flat, tile, hidden, branch, HALF_DOWN + half, D // 64)
+
+    def in_tile(c, carry):
+        flat[pl.ds((HALF_IN + half) // 2 + c, D, stride=24), :] = t_mm(
+            normed_two[...], grad_gu[:, pl.ds(pl.multiple_of(c * 128, 128), 128)]
+        )
+        return carry
+
+    lax.fori_loop(0, 24, in_tile, 0)
+    cut(flat, core, LOW_PLANES, DEVICES // 2 - LOW_PLANES, skip, keep, send)
+    edge[...] = flat[0:EDGE, :]
+
+
+def pack_first_kernel(core, normed, project, gain_one, edge, keep, send, flat, tile):
+    skip = 216 * SPLIT
+    flat[skip : skip + EDGE, :] = edge[...]
+    put_gain(flat, gain_one, HALF_GAIN_ONE + 14)
+    put_matrix(flat, tile, normed, project, HALF_QKV + 14, PW // 64)
+    cut(flat, core, 0, LOW_PLANES, 0, keep, send)
 
 
 def hop(value, by):
@@ -455,16 +512,19 @@
     return total[SAME_CORE * ROWS :], pieces
 
 
-def reduce_packed(keep, send):
-    got = swap(send)
-    total = (keep.astype(f32) + got.astype(f32)).astype(bf16)
-    total = total.reshape(DEVICES // 2, CHUNK, 128)
+def both_cores(keep, send):
+    return (keep.astype(f32) + swap(send).astype(f32)).astype(bf16)
+
+
+def to_owners(first, rest, device):
+    total = jnp.concatenate([first, rest], axis=0).reshape(DEVICES // 2, CHUNK, 128)
     groups = [list(range(0, DEVICES, 2)), list(range(1, DEVICES, 2))]
     pieces = lax.all_to_all(
         total, "fsdp", split_axis=0, concat_axis=0, tiled=True, axis_index_groups=groups
     )
     own = jnp.sum(pieces.astype(f32), axis=0)
-    return own.reshape(-1)[:SHARD]
+    rows = jnp.concatenate([own[CHUNK - 1 :], own], axis=0)
+    return lax.dynamic_slice_in_dim(rows.reshape(-1), 9 * device, SHARD, 0)
 
 
 def tables(positions):
@@ -482,10 +542,12 @@
     core = lax.rem(device, 2)
     first_row = device * ROWS
     layers = weights_flat.shape[0]
-    gathered = []
+    sections = []
     for layer in range(layers):
-        padded = jnp.pad(weights_flat[layer], (0, CHUNK * 128 - SHARD))
-        gathered.append(lax.all_gather(padded, "fsdp", axis=0, tiled=True))
+        blank = jnp.zeros((SECTION * 128,), bf16)
+        sections.append(lax.dynamic_update_slice(blank, weights_flat[layer], (9 * device,)))
+    gathered = lax.all_gather(jnp.concatenate(sections), "fsdp", axis=0, tiled=True)
+    gathered = gathered.reshape(DEVICES, layers, SECTION, 128)
 
     x_same, x_sibling = window_of(hidden_in, core)
     window = jnp.concatenate([x_same, x_sibling], axis=0)
@@ -507,20 +569,21 @@
     x = hidden_in
     held = []
     for layer in range(layers):
-        w_qkv, w_out, w_in, w_down, gains = unpack(gathered[layer].reshape(DEVICES * CHUNK, 128))
+        w_qkv, gain_one = unpack_first(gathered, layer)
+        w_out, w_in, w_down, gain_two = unpack_rest(gathered, layer)
         if layer == 0:
             q, kv_s, kv_t, normed = call(
                 heads_zero_kernel,
                 [((ROWS, QW), bf16), ((WIN_S, 2 * KW), bf16), ((WIN_T, 2 * KW), bf16),
                  ((ROWS, D), bf16)],
-                [window, cosine_all, sine_all, gains, w_qkv],
+                [window, cosine_all, sine_all, gain_one, w_qkv],
                 flops=800_000_000, nbytes=6_000_000,
             )
         else:
             q, kv, normed = call(
                 heads_kernel,
                 [((ROWS, QW), bf16), ((ROWS, 2 * KW), bf16), ((ROWS, D), bf16)],
-                [x, cosine, sine, gains, w_qkv],
+                [x, cosine, sine, gain_one, w_qkv],
                 flops=150_000_000, nbytes=3_000_000,
             )
             kv_s, kv_t = window_of(kv, core)
@@ -528,11 +591,11 @@
             attend_kernel,
             [((ROWS, D), f32), ((ROWS, QW), bf16), ((GROUP * ROWS, KVH), f32), ((ROWS, D), f32),
              ((ROWS, D), bf16), ((ROWS, 2 * FF), f32), ((ROWS, FF), bf16)],
-            [first, x, q, kv_s, kv_t, segment, key_row, gains, w_out, w_in, w_down],
+            [first, x, q, kv_s, kv_t, segment, key_row, gain_two, w_out, w_in, w_down],
             smem=1, flops=2_000_000_000, nbytes=12_000_000,
         )
         held.append((x, q, kv_s, kv_t, normed, mixed, lse, middle, normed_two, gate_up, hidden,
-                     w_qkv, w_out, w_in, w_down, gains))
+                     w_qkv, w_out, w_in, w_down, gain_one, gain_two))
         x = x_next
     layer_out = x.astype(bf16)
 
@@ -540,31 +603,48 @@
     grads = [None] * layers
     for layer in reversed(range(layers)):
         (x, q, kv_s, kv_t, normed, mixed, lse, middle, normed_two, gate_up, hidden,
-         w_qkv, w_out, w_in, w_down, gains) = held[layer]
-        branch, grad_gu, attn, middle_grad, dq, dkv_s, dkv_t, gain_two = call(
+         w_qkv, w_out, w_in, w_down, gain_one, gain_two) = held[layer]
+        branch, grad_gu, attn, middle_grad, dq, dkv_s, dkv_t, grad_two = call(
             back_kernel,
             [((ROWS, D), bf16), ((ROWS, 2 * FF), bf16), ((ROWS, D), bf16), ((ROWS, D), f32),
              ((ROWS, QW), bf16), ((WIN_S, 2 * KW), f32), ((WIN_T, 2 * KW), bf16), ((1, D), f32)],
-            [first, g, q, kv_s, kv_t, segment, key_row, cosine, sine, gains, w_out, w_in, w_down,
+            [first, g, q, kv_s, kv_t, segment, key_row, cosine, sine, gain_two, w_out, w_in, w_down,
              lse, middle, gate_up],
             smem=1, flops=3_000_000_000, nbytes=15_000_000,
         )
+        rest_shape = (((DEVICES // 2 - LOW_PLANES) * CHUNK, 128), bf16)
+        keep, send, edge = call(
+            pack_rest_kernel,
+            [rest_shape, rest_shape, ((EDGE, 128), f32)],
+            [core_in, mixed, attn, normed_two, grad_gu, hidden, branch, grad_two],
+            scratch=[
+                pltpu.VMEM((216 * (DEVICES - SPLIT) + 40, 128), f32), pltpu.VMEM((5, FF, 128), f32)
+            ],
+            smem=1, flops=1_000_000_000, nbytes=25_000_000,
+        )
         own_kv, pieces = give_back(dkv_s, dkv_t, core)
-        g, project, gain_one = call(
+        send, pieces = lax.optimization_barrier((send, pieces))
+        rest_part = both_cores(keep, send)
+        g, project, grad_one = call(
             back_heads_kernel,
             [((ROWS, D), f32), ((ROWS, PW), bf16), ((1, D), f32)],
-            [x, dq, own_kv, *pieces, cosine, sine, gains, w_qkv, middle_grad],
+            [x, dq, own_kv, *pieces, cosine, sine, gain_one, w_qkv, middle_grad],
             flops=150_000_000, nbytes=3_000_000,
         )
+        if layer + 1 < layers:
+            project, grads[layer + 1] = lax.optimization_barrier((project, grads[layer + 1]))
+        low_shape = ((LOW_PLANES * CHUNK, 128), bf16)
         keep, send = call(
-            pack_kernel,
-            [((DEVICES // 2 * CHUNK, 128), bf16), ((DEVICES // 2 * CHUNK, 128), bf16)],
-            [core_in, normed, project, mixed, attn, normed_two, grad_gu, hidden, branch,
-             gain_one, gain_two],
-            scratch=[pltpu.VMEM((FLAT_ROWS, 128), f32), pltpu.VMEM((8, FF, 128), f32)],
-            smem=1, flops=1_200_000_000, nbytes=30_000_000,
-        )
-        grads[layer] = reduce_packed(keep, send)
+            pack_first_kernel,
+            [low_shape, low_shape],
+            [core_in, normed, project, grad_one, edge],
+            scratch=[pltpu.VMEM((216 * SPLIT + 480, 128), f32), pltpu.VMEM((8, D, 128), f32)],
+            smem=1, flops=200_000_000, nbytes=8_000_000,
+        )
+        first_part = both_cores(keep, send)
+        if layer > 0:
+            g, first_part, rest_part = lax.optimization_barrier((g, first_part, rest_part))
+        grads[layer] = to_owners(first_part, rest_part, device)
     return (layer_out, g, jnp.stack(grads))
 
 

time: 490 us -> 390 us (0.80)
  waiting for transfers between devices: 180 us -> 105 us
  Pallas kernels: 151 us -> 117 us
  other arithmetic: 22.1 us -> 31.7 us
    pallas_call x12, Pallas kernels: 151 us -> 92.3 us  [call(): pl.pallas_call(kernel, out_shape=[jax.ShapeDtypeStruct(s, d) for s, d in...]
    all_to_all x2, waiting for transfers between devices: 87 us -> 47.3 us  [to_owners(): lax.all_to_all(total, 'fsdp', split_axis=0, concat_axis=0, tiled=True, ax...]
    all_gather x2 -> x1, waiting for transfers between devices: 69.6 us -> 41.4 us  [body(): lax.all_gather(jnp.concatenate(sections), 'fsdp', axis=0, tiled=True)]
    pallas_call x0 -> x4, Pallas kernels: none -> 24.6 us  [unpack_call(): pl.pallas_call(functools.partial(kernel, layer), out_shape=[jax.ShapeDtyp...]
    concatenate x0 -> x3, other arithmetic: none -> 12 us  [the longest x2 11.4 us: to_owners(): jnp.concatenate([first, rest], axis=0).reshape(DEVICES // 2, CHUNK, 128)]
    ppermute x20, waiting for transfers between devices: 18.7 us -> 10.4 us  [hop(): return lax.ppermute(value, 'fsdp', pairs)]
  transfers between devices with their start and end apart: 31 -> 32, of which waited for: 15 -> 10; matrix products, arithmetic and copies ran while one was open for 6% -> 6% of each run, Pallas kernels for 13% -> 16%
where the time goes in v2:
time: 390 us; the launch traced here: 382 us
  Pallas kernels  117 us (30%)
  waiting for transfers between devices  105 us (27%)
  starting transfers between devices  97.5 us (25%)
  other arithmetic  31.7 us (8%)
  local copies, waits for them, and re-layouts  16.8 us (4%)
  between operations  15 us (4%)
    pallas_call x12, Pallas kernels, call(): pl.pallas_call(kernel, out_shape=[jax.ShapeDtypeStruct(s, d) for s, d in...  92.3 us
    ppermute x20, starting transfers between devices, hop(): return lax.ppermute(value, 'fsdp', pairs)  73.3 us
    all_to_all x2, waiting for transfers between devices, to_owners(): lax.all_to_all(total, 'fsdp', split_axis=0, concat_axis=0, tiled=True, ax...  47.3 us
    all_gather x1, waiting for transfers between devices, body(): lax.all_gather(jnp.concatenate(sections), 'fsdp', axis=0, tiled=True)  41.4 us
    pallas_call x4, Pallas kernels, unpack_call(): pl.pallas_call(functools.partial(kernel, layer), out_shape=[jax.ShapeDtyp...  24.6 us
    all_to_all x2, starting transfers between devices, to_owners(): lax.all_to_all(total, 'fsdp', split_axis=0, concat_axis=0, tiled=True, ax...  22.4 us
    concatenate x2, other arithmetic, to_owners(): jnp.concatenate([first, rest], axis=0).reshape(DEVICES // 2, CHUNK, 128)  11.4 us
    ppermute x20, waiting for transfers between devices, hop(): return lax.ppermute(value, 'fsdp', pairs)  10.4 us
  transfers between devices with their start and end apart: 32, of which 10 were waited for; matrix products, arithmetic and copies ran while one was open for 6% of the time, Pallas kernels for 16%

profile of v2, /device:TPU:50, one launch (start us, length us, event | category | flops | bytes accessed | tf_op | source)
XLA Modules:
  0.0 382.5 jit_solution(4737330768160505662)
XLA Ops:
  7.2 1.6 slice_reduce_fusion.1
  10.8 3.8 %collective-permute-start.8 = (s32[128]{0:T(128)}, s32[128]{0:T(128)S(1)}, u32[]{:S(2)}, u32[]{:S(2)}) collective-permute-start(s32[128]{0:T(128)} %param.7), channel_id=1, source_target_pairs={{0,2},{1,3},{2,4},{3,5},{4,6},{5,7},{6,8},{7,9},{8,10},{9,11},{10,... | collective-permute-start | bytes 1544 | tf_op jit(solution)/shard_map/ppermute | solution.py:487
  14.6 3.0 collective-permute-start.7
  17.6 5.2 %collective-permute-start.6 = (s32[128]{0:T(128)}, s32[128]{0:T(128)S(1)}, u32[]{:S(2)}, u32[]{:S(2)}) collective-permute-start(s32[128]{0:T(128)} %param.7), channel_id=1, source_target_pairs={{0,6},{1,7},{2,8},{3,9},{4,10},{5,11},{6,12},{7,13},{8,14},{9,15},... | collective-permute-start | bytes 1544 | tf_op jit(solution)/shard_map/ppermute | solution.py:487
  22.8 3.1 collective-permute-start.5
  25.9 1.1 copy.32.x_in
  27.0 1.9 collective-permute-start.3
  30.4 6.0 %collective-permute-start.2 = (bf16[128,576]{1,0:T(8,128)(2,1)S(1)}, bf16[128,576]{1,0:T(8,128)(2,1)S(1)}, u32[]{:S(2)}, u32[]{:S(2)}) collective-permute-start(bf16[128,576]{1,0:T(8,128)(2,1)S(1)} %copy.32.x_in), channel_id=1, source_target_pairs={{0,4},{1,5},{2,6},{3,7},{4,8},{5,9},{6,10},{7,11},{8,12},{9,13},{1... | collective-permute-start | bytes 442376 | tf_op jit(solution)/shard_map/ppermute | solution.py:487
  36.4 1.9 collective-permute-start.1
  38.4 3.5 collective-permute-start
  43.3 1.4 copy.33.segment
  46.5 2.1 multiply_sine_fusion
  48.7 1.0 pad_maximum_fusion.2
  51.0 1.4 copy.31
  52.5 41.4 %all-gather.2.cloned.1.call-done = bf16[7864320]{0:T(1024)(128)(2,1)} async-done(((bf16[61440]{0:T(1024)(128)(2,1)}), bf16[7864320]{0:T(1024)(128)(2,1)}) %all-gather.2.cloned.1.call-update) | async-done | bytes 15728656 | tf_op jit(solution)/shard_map/all_gather | solution.py:549
  93.9 3.4 shard_map.89
  97.3 3.0 shard_map.85
  100.3 9.1 %shard_map.87 = (bf16[576,576]{1,0:T(8,128)(2,1)}, bf16[576,3072]{1,0:T(8,128)(2,1)}, bf16[1536,576]{1,0:T(8,128)(2,1)}, f32[1,640]{1,0:T(1,128)}) custom-call(bf16[128,2,240,128]{3,2,1,0:T(8,128)(2,1)} %bitcast.22), custom_call_target="tpu_custom_call" | custom-call | bytes 30000000 | tf_op jit(solution)/shard_map/pallas_call | solution.py:200
  109.4 4.6 %shard_map.86 = (bf16[128,576]{1,0:T(8,128)(2,1)}, bf16[640,384]{1,0:T(8,128)(2,1)}, bf16[512,384]{1,0:T(8,128)(2,1)}, bf16[128,576]{1,0:T(8,128)(2,1)}) custom-call(bf16[1152,576]{1,0:T(8,128)(2,1)} %copy-done.6, f32[1152,128]{1,0:T(8,128)} %copy-done.2, f32[1152,128]{1,0:T(8,128)} %copy-done.3, f32[1,640]{1,0:T(1,128)} %get-tuple-element.83.gain_row, ...), custom_call_target="tpu_custom_call" | custom-call | flops 800000000 | bytes 6000000 | tf_op jit(solution)/shard_map/pallas_call | solution.py:66
  114.0 9.2 %shard_map.88 = (f32[128,576]{1,0:T(8,128)}, bf16[128,576]{1,0:T(8,128)(2,1)}, f32[384,3]{1,0:T(8,128)}, f32[128,576]{1,0:T(8,128)}, bf16[128,576]{1,0:T(8,128)(...) custom-call(s32[1]{0:T(128)} %bitcast.first, bf16[128,576]{1,0:T(8,128)(2,1)} %copy-done.4, ...), custom_call_target="tpu_custom_call" | custom-call | flops 2000000000 | bytes 12000000 | tf_op jit(solution)/shard_map/pallas_call | solution.py:66
  123.3 2.8 shard_map.90
  126.1 3.1 collective-permute-start.10
  129.2 3.1 collective-permute-start.13
  132.4 5.6 %collective-permute-start.12 = (bf16[128,384]{1,0:T(8,128)(2,1)}, bf16[128,384]{1,0:T(8,128)(2,1)S(1)}, u32[]{:S(2)}, u32[]{:S(2)}) collective-permute-start(bf16[128,384]{1,0:T(8,128)(2,1)} %get-tuple-element.96), channel_id=1, source_target_pairs={{0,4},{1,5},{2,6},{3,7},{4,8},{5,9},{6,10},{7,11},{8,12},{9,13},{1... | collective-permute-start | bytes 294920 | tf_op jit(solution)/shard_map/ppermute | solution.py:487
  137.9 3.6 collective-permute-start.11
  141.6 4.0 %collective-permute-done.11 = bf16[128,384]{1,0:T(8,128)(2,1)S(1)} collective-permute-done((bf16[128,384]{1,0:T(8,128)(2,1)}, bf16[128,384]{1,0:T(8,128)(2,1)S(1)}, u32[]{:S(2)}, u32[]{:S(2)}) %collective-permute-start.11) | collective-permute-done | bytes 98336 | tf_op jit(solution)/shard_map/ppermute | solution.py:487
  145.6 0.9 constant_dynamic-update-slice_fusion.13.kv_s
  147.6 9.1 %shard_map.91 = (bf16[576,576]{1,0:T(8,128)(2,1)}, bf16[576,3072]{1,0:T(8,128)(2,1)}, bf16[1536,576]{1,0:T(8,128)(2,1)}, f32[1,640]{1,0:T(1,128)}) custom-call(bf16[128,2,240,128]{3,2,1,0:T(8,128)(2,1)} %bitcast.23), custom_call_target="tpu_custom_call" | custom-call | bytes 30000000 | tf_op jit(solution)/shard_map/pallas_call | solution.py:200
  157.5 9.2 %shard_map.92 = (f32[128,576]{1,0:T(8,128)}, bf16[128,576]{1,0:T(8,128)(2,1)}, f32[384,3]{1,0:T(8,128)}, f32[128,576]{1,0:T(8,128)}, bf16[128,576]{1,0:T(8,128)(...) custom-call(s32[1]{0:T(128)} %bitcast.first, f32[128,576]{1,0:T(8,128)} %get-tuple-element.92.x_in, ...), custom_call_target="tpu_custom_call" | custom-call | flops 2000000000 | bytes 12000000 | tf_op jit(solution)/shard_map/pallas_call | solution.py:66
  166.7 12.6 %shard_map.93 = (bf16[128,576]{1,0:T(8,128)(2,1)}, bf16[128,3072]{1,0:T(8,128)(2,1)}, bf16[128,576]{1,0:T(8,128)(2,1)}, f32[128,576]{1,0:T(8,128)}, bf16[128,576...) custom-call(s32[1]{0:T(128)} %bitcast.first, bf16[128,576]{1,0:T(8,128)(2,1)} %copy.35.g_in, ...), custom_call_target="tpu_custom_call" | custom-call | flops 3000000000 | bytes 15000000 | tf_op jit(solution)/shard_map/pallas_call | solution.py:66
  179.8 1.6 collective-permute-done.15
  181.4 1.3 fusion.3
  183.5 1.9 collective-permute-start.19
  185.4 3.1 collective-permute-start.18
  188.5 4.7 %collective-permute-start.17 = (bf16[128,384]{1,0:T(8,128)(2,1)}, bf16[128,384]{1,0:T(8,128)(2,1)}, u32[]{:S(2)}, u32[]{:S(2)}) collective-permute-start(bf16[128,384]{1,0:T(8,128)(2,1)} %get-tuple-element.181), channel_id=1, source_target_pairs={{6,0},{7,1},{8,2},{9,3},{10,4},{11,5},{12,6},{13,7},{14,8},{15,9},... | collective-permute-start | bytes 294920 | tf_op jit(solution)/shard_map/ppermute | solution.py:487
  193.2 4.8 %collective-permute-start.16 = (bf16[128,384]{1,0:T(8,128)(2,1)}, bf16[128,384]{1,0:T(8,128)(2,1)}, u32[]{:S(2)}, u32[]{:S(2)}) collective-permute-start(bf16[128,384]{1,0:T(8,128)(2,1)} %get-tuple-element.182), channel_id=1, source_target_pairs={{8,0},{9,1},{10,2},{11,3},{12,4},{13,5},{14,6},{15,7},{16,8},{17,9... | collective-permute-start | bytes 294920 | tf_op jit(solution)/shard_map/ppermute | solution.py:487
  198.0 13.9 %shard_map.94 = (bf16[11872,128]{1,0:T(8,128)(2,1)}, bf16[11872,128]{1,0:T(8,128)(2,1)}, f32[456,128]{1,0:T(8,128)}) custom-call(s32[1]{0:T(128)} %bitcast.4.core, bf16[128,576]{1,0:T(8,128)(2,1)} %get-tuple-element.108.mixed, bf16[128,576]{1,0:T(8,128)(2,1)} %get-tuple-element.109.attn, bf16[128,576]{1,0:T(8,128)(2,1)} %get-tuple-element.110.normed_two, ...), custom_call_target="tpu_custom_call" | custom-call | flops 1000000000 | bytes 25000000 | tf_op jit(solution)/shard_map/pallas_call | solution.py:66
  212.8 3.4 shard_map.95
  216.1 3.4 shard_map.96
  219.9 2.0 collective-permute-done.20
  221.8 1.2 add_convert_fusion.3
  223.1 2.3 add_convert_fusion.1
  225.4 5.7 %pad_maximum_fusion = bf16[14336,128]{1,0:T(8,128)(2,1)} fusion(bf16[11872,128]{1,0:T(8,128)(2,1)S(1)} %add_convert_fusion.1, bf16[2464,128]{1,0:T(8,128)(2,1)S(1)} %add_convert_fusion.3), kind=kLoop, calls=%fused_computation.4 | loop fusion | flops 7340032 | bytes 7340032 | tf_op jit(solution)/shard_map/concatenate | solution.py:520
  231.1 11.1 %all-to-all-start = ((bf16[64,224,128]{2,1,0:T(8,128)(2,1)}), bf16[64,224,128]{2,1,0:T(8,128)(2,1)}, u32[]{:S(2)}, u32[]{:S(2)}) async-start(bf16[64,224,128]{2,1,0:T(8,128)(2,1)} %bitcast.24), calls=%async_computation | async-start | bytes 7340032 | tf_op jit(solution)/shard_map/all_to_all | solution.py:522
  242.2 12.6 %shard_map.97 = (bf16[128,576]{1,0:T(8,128)(2,1)}, bf16[128,3072]{1,0:T(8,128)(2,1)}, bf16[128,576]{1,0:T(8,128)(2,1)}, f32[128,576]{1,0:T(8,128)}, bf16[128,576...) custom-call(s32[1]{0:T(128)} %bitcast.first, ...), custom_call_target="tpu_custom_call" | custom-call | flops 3000000000 | bytes 15000000 | tf_op jit(solution)/shard_map/pallas_call | solution.py:66
  254.7 1.9 collective-permute-done.22
  256.7 1.3 fusion.2
  258.1 2.5 collective-permute-start.26
  260.6 4.2 %collective-permute-start.25 = (bf16[128,384]{1,0:T(8,128)(2,1)S(1)}, bf16[128,384]{1,0:T(8,128)(2,1)S(1)}, u32[]{:S(2)}, u32[]{:S(2)}) collective-permute-start(bf16[128,384]{1,0:T(8,128)(2,1)S(1)} %get-tuple-element.176), channel_id=1, source_target_pairs={{4,0},{5,1},{6,2},{7,3},{8,4},{9,5},{10,6},{11,7},{12,8},{13,9},{1... | collective-permute-start | bytes 294920 | tf_op jit(solution)/shard_map/ppermute | solution.py:487
  264.8 3.7 collective-permute-start.24
  268.5 4.6 %collective-permute-start.23 = (bf16[128,384]{1,0:T(8,128)(2,1)S(1)}, bf16[128,384]{1,0:T(8,128)(2,1)S(1)}, u32[]{:S(2)}, u32[]{:S(2)}) collective-permute-start(bf16[128,384]{1,0:T(8,128)(2,1)S(1)} %get-tuple-element.178), channel_id=1, source_target_pairs={{8,0},{9,1},{10,2},{11,3},{12,4},{13,5},{14,6},{15,7},{16,8},{17,9... | collective-permute-start | bytes 294920 | tf_op jit(solution)/shard_map/ppermute | solution.py:487
  273.1 13.9 %shard_map.98 = (bf16[11872,128]{1,0:T(8,128)(2,1)}, bf16[11872,128]{1,0:T(8,128)(2,1)}, f32[456,128]{1,0:T(8,128)}) custom-call(s32[1]{0:T(128)} %bitcast.4.core, bf16[128,576]{1,0:T(8,128)(2,1)} %get-tuple-element.137.mixed, bf16[128,576]{1,0:T(8,128)(2,1)} %get-tuple-element.138.attn, bf16[128,576]{1,0:T(8,128)(2,1)} %get-tuple-element.139.normed_two, ...), custom_call_target="tpu_custom_call" | custom-call | flops 1000000000 | bytes 25000000 | tf_op jit(solution)/shard_map/pallas_call | solution.py:66
  287.0 2.3 collective-permute-done.25.r4
  289.3 2.9 collective-permute-done.24.r6
  293.0 3.2 shard_map.99
  296.2 2.7 convert_reduce_fusion.1
  299.0 3.5 shard_map.100
  303.1 2.3 add_convert_fusion
  305.7 5.7 %pad_maximum_fusion.1 = bf16[14336,128]{1,0:T(8,128)(2,1)} fusion(bf16[11872,128]{1,0:T(8,128)(2,1)S(1)} %add_convert_fusion, bf16[2464,128]{1,0:T(8,128)(2,1)S(1)} %add_convert_fusion.2), kind=kLoop, calls=%fused_computation.5 | loop fusion | flops 7340032 | bytes 7340032 | tf_op jit(solution)/shard_map/concatenate | solution.py:520
  311.3 11.3 %all-to-all-start.1 = ((bf16[64,224,128]{2,1,0:T(8,128)(2,1)}), bf16[64,224,128]{2,1,0:T(8,128)(2,1)}, u32[]{:S(2)}, u32[]{:S(2)}) async-start(bf16[64,224,128]{2,1,0:T(8,128)(2,1)} %bitcast.25), calls=%async_computation.1 | async-start | bytes 7340032 | tf_op jit(solution)/shard_map/all_to_all | solution.py:522
  323.5 0.9 copy.40
  324.4 47.3 %all-to-all-done.1 = bf16[64,224,128]{2,1,0:T(8,128)(2,1)} async-done(((bf16[64,224,128]{2,1,0:T(8,128)(2,1)}), bf16[64,224,128]{2,1,0:T(8,128)(2,1)}, u32[]{:S(2)}, u32[]{:S(2)}) %all-to-all-start.1) | async-done | bytes 3670048 | tf_op jit(solution)/shard_map/all_to_all | solution.py:522
  371.8 2.6 convert_reduce_fusion
  374.5 0.9 pad_maximum_fusion.4
  (123 shorter events, 15.2 us)
Async XLA Ops:
  7.2 86.7 %all-gather.2.cloned.1.call-start = ((), (), s32[]{:S(2)}) async-start(), calls=%async_computation.2 | async-start | bytes 15851520 | tf_op jit(solution)/shard_map/all_gather | solution.py:549
  10.8 31.1 %collective-permute-start.8 = (s32[128]{0:T(128)}, s32[128]{0:T(128)S(1)}, u32[]{:S(2)}, u32[]{:S(2)}) collective-permute-start(s32[128]{0:T(128)} %param.7), channel_id=1, source_target_pairs={{0,2},{1,3},{2,4},{3,5},{4,6},{5,7},{6,8},{7,9},{8,10},{9,11},{10,... | collective-permute-start | bytes 1544 | tf_op jit(solution)/shard_map/ppermute | solution.py:487
  14.6 23.8 %collective-permute-start.7 = (s32[128]{0:T(128)}, s32[128]{0:T(128)S(1)}, u32[]{:S(2)}, u32[]{:S(2)}) collective-permute-start(s32[128]{0:T(128)} %param.7), channel_id=1, source_target_pairs={{0,4},{1,5},{2,6},{3,7},{4,8},{5,9},{6,10},{7,11},{8,12},{9,13},{1... | collective-permute-start | bytes 1544 | tf_op jit(solution)/shard_map/ppermute | solution.py:487
  17.6 18.8 %collective-permute-start.6 = (s32[128]{0:T(128)}, s32[128]{0:T(128)S(1)}, u32[]{:S(2)}, u32[]{:S(2)}) collective-permute-start(s32[128]{0:T(128)} %param.7), channel_id=1, source_target_pairs={{0,6},{1,7},{2,8},{3,9},{4,10},{5,11},{6,12},{7,13},{8,14},{9,15},... | collective-permute-start | bytes 1544 | tf_op jit(solution)/shard_map/ppermute | solution.py:487
  22.8 7.6 %collective-permute-start.5 = (s32[128]{0:T(128)}, s32[128]{0:T(128)S(1)}, u32[]{:S(2)}, u32[]{:S(2)}) collective-permute-start(s32[128]{0:T(128)} %param.7), channel_id=1, source_target_pairs={{0,8},{1,9},{2,10},{3,11},{4,12},{5,13},{6,14},{7,15},{8,16},{9,17... | collective-permute-start | bytes 1544 | tf_op jit(solution)/shard_map/ppermute | solution.py:487
  27.0 21.7 %copy-start.4 = (bf16[128,576]{1,0:T(8,128)(2,1)}, bf16[128,576]{1,0:T(8,128)(2,1)S(1)}, u32[]{:S(2)}) copy-start(bf16[128,576]{1,0:T(8,128)(2,1)S(1)} %copy.32.x_in) | copy-start | bytes 442372
  27.0 19.1 %collective-permute-start.3 = (bf16[128,576]{1,0:T(8,128)(2,1)S(1)}, bf16[128,576]{1,0:T(8,128)(2,1)S(1)}, u32[]{:S(2)}, u32[]{:S(2)}) collective-permute-start(bf16[128,576]{1,0:T(8,128)(2,1)S(1)} %copy.32.x_in), channel_id=1, source_target_pairs={{0,2},{1,3},{2,4},{3,5},{4,6},{5,7},{6,8},{7,9},{8,10},{9,11},{10,... | collective-permute-start | bytes 442376 | tf_op jit(solution)/shard_map/ppermute | solution.py:487
  30.4 15.6 %collective-permute-start.2 = (bf16[128,576]{1,0:T(8,128)(2,1)S(1)}, bf16[128,576]{1,0:T(8,128)(2,1)S(1)}, u32[]{:S(2)}, u32[]{:S(2)}) collective-permute-start(bf16[128,576]{1,0:T(8,128)(2,1)S(1)} %copy.32.x_in), channel_id=1, source_target_pairs={{0,4},{1,5},{2,6},{3,7},{4,8},{5,9},{6,10},{7,11},{8,12},{9,13},{1... | collective-permute-start | bytes 442376 | tf_op jit(solution)/shard_map/ppermute | solution.py:487
  36.4 9.5 %collective-permute-start.1 = (bf16[128,576]{1,0:T(8,128)(2,1)S(1)}, bf16[128,576]{1,0:T(8,128)(2,1)S(1)}, u32[]{:S(2)}, u32[]{:S(2)}) collective-permute-start(bf16[128,576]{1,0:T(8,128)(2,1)S(1)} %copy.32.x_in), channel_id=1, source_target_pairs={{0,6},{1,7},{2,8},{3,9},{4,10},{5,11},{6,12},{7,13},{8,14},{9,15},... | collective-permute-start | bytes 442376 | tf_op jit(solution)/shard_map/ppermute | solution.py:487
  38.4 7.2 %collective-permute-start = (bf16[128,576]{1,0:T(8,128)(2,1)S(1)}, bf16[128,576]{1,0:T(8,128)(2,1)S(1)}, u32[]{:S(2)}, u32[]{:S(2)}) collective-permute-start(bf16[128,576]{1,0:T(8,128)(2,1)S(1)} %copy.32.x_in), channel_id=1, source_target_pairs={{0,8},{1,9},{2,10},{3,11},{4,12},{5,13},{6,14},{7,15},{8,16},{9,17... | collective-permute-start | bytes 442376 | tf_op jit(solution)/shard_map/ppermute | solution.py:487
  42.6 2.0 collective-permute-start.9
  46.5 4.5 %collective-permute-start.4 = (bf16[512,576]{0,1:T(8,128)(2,1)S(1)}, bf16[512,576]{0,1:T(8,128)(2,1)}, u32[]{:S(2)}, u32[]{:S(2)}) collective-permute-start(bf16[512,576]{0,1:T(8,128)(2,1)S(1)} %copy.29), channel_id=1, source_target_pairs={{0,1},{1,0},{2,3},{3,2},{4,5},{5,4},{6,7},{7,6},{8,9},{9,8},{10,11... | collective-permute-start | bytes 1769480 | tf_op jit(solution)/shard_map/ppermute | solution.py:491
  49.7 47.6 %copy-start.2 = (f32[1152,128]{1,0:T(8,128)}, f32[1152,128]{1,0:T(8,128)S(1)}, u32[]{:S(2)}) copy-start(f32[1152,128]{1,0:T(8,128)S(1)} %get-tuple-element.205.cosine) | copy-start | bytes 1769476
  49.7 47.6 %copy-start.3 = (f32[1152,128]{1,0:T(8,128)}, f32[1152,128]{1,0:T(8,128)S(1)}, u32[]{:S(2)}) copy-start(f32[1152,128]{1,0:T(8,128)S(1)} %get-tuple-element.206.sine) | copy-start | bytes 1769476
  52.5 47.8 %copy-start.6 = (bf16[1152,576]{1,0:T(8,128)(2,1)}, bf16[1152,576]{1,0:T(8,128)(2,1)S(1)}, u32[]{:S(2)}) copy-start(bf16[1152,576]{1,0:T(8,128)(2,1)S(1)} %constant_dynamic-update-slice_fusion.5.window) | copy-start | bytes 3981316
  123.3 23.5 %copy-start.11 = (bf16[128,576]{0,1:T(8,128)(2,1)S(1)}, bf16[128,576]{0,1:T(8,128)(2,1)}, u32[]{:S(2)}) copy-start(bf16[128,576]{0,1:T(8,128)(2,1)} %param.9) | copy-start | bytes 442372
  126.1 15.4 %collective-permute-start.10 = (bf16[128,384]{1,0:T(8,128)(2,1)}, bf16[128,384]{1,0:T(8,128)(2,1)S(1)}, u32[]{:S(2)}, u32[]{:S(2)}) collective-permute-start(bf16[128,384]{1,0:T(8,128)(2,1)} %get-tuple-element.96), channel_id=1, source_target_pairs={{0,8},{1,9},{2,10},{3,11},{4,12},{5,13},{6,14},{7,15},{8,16},{9,17... | collective-permute-start | bytes 294920 | tf_op jit(solution)/shard_map/ppermute | solution.py:487
  129.2 16.4 %collective-permute-start.13 = (bf16[128,384]{1,0:T(8,128)(2,1)}, bf16[128,384]{1,0:T(8,128)(2,1)S(1)}, u32[]{:S(2)}, u32[]{:S(2)}) collective-permute-start(bf16[128,384]{1,0:T(8,128)(2,1)} %get-tuple-element.96), channel_id=1, source_target_pairs={{0,2},{1,3},{2,4},{3,5},{4,6},{5,7},{6,8},{7,9},{8,10},{9,11},{10,... | collective-permute-start | bytes 294920 | tf_op jit(solution)/shard_map/ppermute | solution.py:487
  132.4 13.2 %collective-permute-start.12 = (bf16[128,384]{1,0:T(8,128)(2,1)}, bf16[128,384]{1,0:T(8,128)(2,1)S(1)}, u32[]{:S(2)}, u32[]{:S(2)}) collective-permute-start(bf16[128,384]{1,0:T(8,128)(2,1)} %get-tuple-element.96), channel_id=1, source_target_pairs={{0,4},{1,5},{2,6},{3,7},{4,8},{5,9},{6,10},{7,11},{8,12},{9,13},{1... | collective-permute-start | bytes 294920 | tf_op jit(solution)/shard_map/ppermute | solution.py:487
  137.9 7.6 %collective-permute-start.11 = (bf16[128,384]{1,0:T(8,128)(2,1)}, bf16[128,384]{1,0:T(8,128)(2,1)S(1)}, u32[]{:S(2)}, u32[]{:S(2)}) collective-permute-start(bf16[128,384]{1,0:T(8,128)(2,1)} %get-tuple-element.96), channel_id=1, source_target_pairs={{0,6},{1,7},{2,8},{3,9},{4,10},{5,11},{6,12},{7,13},{8,14},{9,15},... | collective-permute-start | bytes 294920 | tf_op jit(solution)/shard_map/ppermute | solution.py:487
  146.6 10.1 %copy-start.5 = (bf16[640,384]{1,0:T(8,128)(2,1)}, bf16[640,384]{1,0:T(8,128)(2,1)S(1)}, u32[]{:S(2)}) copy-start(bf16[640,384]{1,0:T(8,128)(2,1)S(1)} %constant_dynamic-update-slice_fusion.13.kv_s) | copy-start | bytes 1474564
  146.6 10.1 %collective-permute-start.14 = (bf16[512,384]{1,0:T(8,128)(2,1)S(1)}, bf16[512,384]{1,0:T(8,128)(2,1)S(1)}, u32[]{:S(2)}, u32[]{:S(2)}) collective-permute-start(bf16[512,384]{1,0:T(8,128)(2,1)S(1)} %constant_dynamic-slice_fusion), channel_id=1, source_target_pairs={{0,1},{1,0},{2,3},{3,2},{4,5},{5,4},{6,7},{7,6},{8,9},{9,8},{10,11... | collective-permute-start | bytes 1179656 | tf_op jit(solution)/shard_map/ppermute | solution.py:491
  156.7 0.8 copy-start.8
  179.3 2.0 collective-permute-start.15
  183.5 28.5 %collective-permute-start.19 = (bf16[128,384]{1,0:T(8,128)(2,1)}, bf16[128,384]{1,0:T(8,128)(2,1)S(1)}, u32[]{:S(2)}, u32[]{:S(2)}) collective-permute-start(bf16[128,384]{1,0:T(8,128)(2,1)} %get-tuple-element.179), channel_id=1, source_target_pairs={{2,0},{3,1},{4,2},{5,3},{6,4},{7,5},{8,6},{9,7},{10,8},{11,9},{12,... | collective-permute-start | bytes 294920 | tf_op jit(solution)/shard_map/ppermute | solution.py:487
  185.4 26.6 %collective-permute-start.18 = (bf16[128,384]{1,0:T(8,128)(2,1)}, bf16[128,384]{1,0:T(8,128)(2,1)}, u32[]{:S(2)}, u32[]{:S(2)}) collective-permute-start(bf16[128,384]{1,0:T(8,128)(2,1)} %get-tuple-element.180), channel_id=1, source_target_pairs={{4,0},{5,1},{6,2},{7,3},{8,4},{9,5},{10,6},{11,7},{12,8},{13,9},{1... | collective-permute-start | bytes 294920 | tf_op jit(solution)/shard_map/ppermute | solution.py:487
  188.5 23.4 %collective-permute-start.17 = (bf16[128,384]{1,0:T(8,128)(2,1)}, bf16[128,384]{1,0:T(8,128)(2,1)}, u32[]{:S(2)}, u32[]{:S(2)}) collective-permute-start(bf16[128,384]{1,0:T(8,128)(2,1)} %get-tuple-element.181), channel_id=1, source_target_pairs={{6,0},{7,1},{8,2},{9,3},{10,4},{11,5},{12,6},{13,7},{14,8},{15,9},... | collective-permute-start | bytes 294920 | tf_op jit(solution)/shard_map/ppermute | solution.py:487
  193.2 18.7 %collective-permute-start.16 = (bf16[128,384]{1,0:T(8,128)(2,1)}, bf16[128,384]{1,0:T(8,128)(2,1)}, u32[]{:S(2)}, u32[]{:S(2)}) collective-permute-start(bf16[128,384]{1,0:T(8,128)(2,1)} %get-tuple-element.182), channel_id=1, source_target_pairs={{8,0},{9,1},{10,2},{11,3},{12,4},{13,5},{14,6},{15,7},{16,8},{17,9... | collective-permute-start | bytes 294920 | tf_op jit(solution)/shard_map/ppermute | solution.py:487
  211.9 11.2 %copy-start.1 = (bf16[11872,128]{1,0:T(8,128)(2,1)S(1)}, bf16[11872,128]{1,0:T(8,128)(2,1)}, u32[]{:S(2)}) copy-start(bf16[11872,128]{1,0:T(8,128)(2,1)} %get-tuple-element.128) | copy-start | bytes 9117700
  211.9 0.8 copy-start.15
  212.0 11.1 %collective-permute-start.21 = (bf16[11872,128]{1,0:T(8,128)(2,1)}, bf16[11872,128]{1,0:T(8,128)(2,1)}, u32[]{:S(2)}, u32[]{:S(2)}) collective-permute-start(bf16[11872,128]{1,0:T(8,128)(2,1)} %get-tuple-element.129), channel_id=1, source_target_pairs={{0,1},{1,0},{2,3},{3,2},{4,5},{5,4},{6,7},{7,6},{8,9},{9,8},{10,11... | collective-permute-start | bytes 9117704 | tf_op jit(solution)/shard_map/ppermute | solution.py:491
  219.6 2.3 collective-permute-start.20
  231.1 65.1 %all-to-all-start = ((bf16[64,224,128]{2,1,0:T(8,128)(2,1)}), bf16[64,224,128]{2,1,0:T(8,128)(2,1)}, u32[]{:S(2)}, u32[]{:S(2)}) async-start(bf16[64,224,128]{2,1,0:T(8,128)(2,1)} %bitcast.24), calls=%async_computation | async-start | bytes 7340032 | tf_op jit(solution)/shard_map/all_to_all | solution.py:522
  254.7 1.9 collective-permute-start.22
  258.1 28.9 %collective-permute-start.26 = (bf16[128,384]{1,0:T(8,128)(2,1)S(1)}, bf16[128,384]{1,0:T(8,128)(2,1)S(1)}, u32[]{:S(2)}, u32[]{:S(2)}) collective-permute-start(bf16[128,384]{1,0:T(8,128)(2,1)S(1)} %get-tuple-element.175), channel_id=1, source_target_pairs={{2,0},{3,1},{4,2},{5,3},{6,4},{7,5},{8,6},{9,7},{10,8},{11,9},{12,... | collective-permute-start | bytes 294920 | tf_op jit(solution)/shard_map/ppermute | solution.py:487
  260.6 28.7 %collective-permute-start.25 = (bf16[128,384]{1,0:T(8,128)(2,1)S(1)}, bf16[128,384]{1,0:T(8,128)(2,1)S(1)}, u32[]{:S(2)}, u32[]{:S(2)}) collective-permute-start(bf16[128,384]{1,0:T(8,128)(2,1)S(1)} %get-tuple-element.176), channel_id=1, source_target_pairs={{4,0},{5,1},{6,2},{7,3},{8,4},{9,5},{10,6},{11,7},{12,8},{13,9},{1... | collective-permute-start | bytes 294920 | tf_op jit(solution)/shard_map/ppermute | solution.py:487
  264.8 27.4 %collective-permute-start.24 = (bf16[128,384]{1,0:T(8,128)(2,1)S(1)}, bf16[128,384]{1,0:T(8,128)(2,1)S(1)}, u32[]{:S(2)}, u32[]{:S(2)}) collective-permute-start(bf16[128,384]{1,0:T(8,128)(2,1)S(1)} %get-tuple-element.177), channel_id=1, source_target_pairs={{6,0},{7,1},{8,2},{9,3},{10,4},{11,5},{12,6},{13,7},{14,8},{15,9},... | collective-permute-start | bytes 294920 | tf_op jit(solution)/shard_map/ppermute | solution.py:487
  268.5 23.7 %collective-permute-start.23 = (bf16[128,384]{1,0:T(8,128)(2,1)S(1)}, bf16[128,384]{1,0:T(8,128)(2,1)S(1)}, u32[]{:S(2)}, u32[]{:S(2)}) collective-permute-start(bf16[128,384]{1,0:T(8,128)(2,1)S(1)} %get-tuple-element.178), channel_id=1, source_target_pairs={{8,0},{9,1},{10,2},{11,3},{12,4},{13,5},{14,6},{15,7},{16,8},{17,9... | collective-permute-start | bytes 294920 | tf_op jit(solution)/shard_map/ppermute | solution.py:487
  287.0 6.0 %copy-start.12 = (bf16[128,384]{1,0:T(8,128)(2,1)}, bf16[128,384]{1,0:T(8,128)(2,1)S(1)}, u32[]{:S(2)}) copy-start(bf16[128,384]{1,0:T(8,128)(2,1)S(1)} %collective-permute-done.26.r2) | copy-start | bytes 294916
  289.3 3.7 copy-start.13
  292.2 0.8 copy-start.14
  292.2 0.8 copy-start.16
  292.2 10.9 %collective-permute-start.28 = (bf16[11872,128]{1,0:T(8,128)(2,1)}, bf16[11872,128]{1,0:T(8,128)(2,1)}, u32[]{:S(2)}, u32[]{:S(2)}) collective-permute-start(bf16[11872,128]{1,0:T(8,128)(2,1)} %get-tuple-element.161), channel_id=1, source_target_pairs={{0,1},{1,0},{2,3},{3,2},{4,5},{5,4},{6,7},{7,6},{8,9},{9,8},{10,11... | collective-permute-start | bytes 9117704 | tf_op jit(solution)/shard_map/ppermute | solution.py:491
  296.2 7.0 %copy-start = (bf16[11872,128]{1,0:T(8,128)(2,1)S(1)}, bf16[11872,128]{1,0:T(8,128)(2,1)}, u32[]{:S(2)}) copy-start(bf16[11872,128]{1,0:T(8,128)(2,1)} %get-tuple-element.160) | copy-start | bytes 9117700
  302.5 3.0 collective-permute-start.27
  303.1 2.3 copy-start.7
  311.3 11.3 %copy-start.10 = (f32[128,576]{1,0:T(8,128)S(1)}, f32[128,576]{1,0:T(8,128)}, u32[]{:S(2)}) copy-start(f32[128,576]{1,0:T(8,128)} %get-tuple-element.101) | copy-start | bytes 884740
  311.3 12.1 %copy-start.9 = (f32[128,576]{1,0:T(8,128)S(1)}, f32[128,576]{1,0:T(8,128)}, u32[]{:S(2)}) copy-start(f32[128,576]{1,0:T(8,128)} %get-tuple-element.167) | copy-start | bytes 884740
  311.3 60.4 %all-to-all-start.1 = ((bf16[64,224,128]{2,1,0:T(8,128)(2,1)}), bf16[64,224,128]{2,1,0:T(8,128)(2,1)}, u32[]{:S(2)}, u32[]{:S(2)}) async-start(bf16[64,224,128]{2,1,0:T(8,128)(2,1)} %bitcast.25), calls=%async_computation.1 | async-start | bytes 7340032 | tf_op jit(solution)/shard_map/all_to_all | solution.py:522
Sparse Core Ops, SparseCore 0:
  11.6 82.2 all-gather.1

commit v3 on v2

--- a/solution.py
+++ b/solution.py
@@ -24,8 +24,9 @@
 CHUNK = 224
 SECTION = 240
 SPLIT = 20
-LOW_PLANES = 11
-EDGE = 456
+LOW_PLANES = 16
+JOIN = 8
+EDGE = 2616
 SAME_CORE = 4
 WIN_S = (SAME_CORE + 1) * ROWS
 WIN_T = SAME_CORE * ROWS
@@ -58,9 +59,12 @@
     return lax.dot_general(a, b, (((0,), (0,)), ((), ())), preferred_element_type=f32)
 
 
-def call(kernel, out_shape, args, scratch=(), smem=0, flops=0, nbytes=0):
+def call(kernel, out_shape, args, scratch=(), smem=0, apart=0, flops=0, nbytes=0):
     in_specs = [
-        pl.BlockSpec(memory_space=pltpu.SMEM if at < smem else pltpu.VMEM)
+        pl.BlockSpec(
+            memory_space=pltpu.SMEM if at < smem
+            else pl.ANY if at >= len(args) - apart else pltpu.VMEM
+        )
         for at in range(len(args))
     ]
     return pl.pallas_call(
@@ -119,6 +123,22 @@
             before = now
 
 
+WEIGHT_SCRATCH = (
+    pltpu.VMEM((QW, D), bf16),
+    pltpu.VMEM((D, 2 * FF), bf16),
+    pltpu.VMEM((FF, D), bf16),
+    pltpu.SemaphoreType.DMA((3,)),
+)
+
+
+def fetch(sources, places, sems):
+    copies = [
+        pltpu.make_async_copy(source, place, sems.at[n])
+        for n, (source, place) in enumerate(zip(sources, places))
+    ]
+    return copies
+
+
 def gather_flat(gathered, layer, first, count, groups, flat, landing, sems):
     size = count // groups
     copies = []
@@ -180,12 +200,12 @@
     take_matrix(flat, tile, w_qkv, HALF_QKV, PW // 64)
 
 
-def unpack_rest_kernel(layer, gathered, w_out, w_in, w_down, gain, landing, flat, tile, sems):
+def unpack_rest_kernel(
+    layer, gathered, w_out_at, w_in_at, w_down_at, gain, landing, flat, tile, sems,
+    w_out, w_in, w_down, out_sems,
+):
     gather_flat(gathered, layer, SPLIT, DEVICES - SPLIT, 4, flat, landing, sems)
     skip = 2 * 216 * SPLIT
-    take_matrix(flat, tile, w_out, HALF_OUT - skip, D // 64)
-    take_gain(flat, gain, HALF_GAIN_TWO - skip)
-    take_matrix(flat, tile, w_down, HALF_DOWN - skip, D // 64)
 
     def in_tile(c, carry):
         w_in[:, pl.ds(pl.multiple_of(c * 128, 128), 128)] = flat[
@@ -194,22 +214,37 @@
         return carry
 
     lax.fori_loop(0, 24, in_tile, 0)
-
-
-def unpack_call(kernel, layer, out_shape, gathered, count, groups, tiles, nbytes):
+    copies = fetch((w_out, w_in, w_down), (w_out_at, w_in_at, w_down_at), out_sems)
+    copies[1].start()
+    take_matrix(flat, tile, w_down, HALF_DOWN - skip, D // 64)
+    copies[2].start()
+    take_matrix(flat, tile, w_out, HALF_OUT - skip, D // 64)
+    copies[0].start()
+    take_gain(flat, gain, HALF_GAIN_TWO - skip)
+    for copy in copies:
+        copy.wait()
+
+
+def unpack_call(
+    kernel, layer, out_shape, gathered, count, groups, tiles, nbytes, apart=0, scratch=()
+):
     return pl.pallas_call(
         functools.partial(kernel, layer),
         out_shape=[jax.ShapeDtypeStruct(s, d) for s, d in out_shape],
         in_specs=[pl.BlockSpec(memory_space=pl.ANY)],
-        out_specs=[pl.BlockSpec(memory_space=pltpu.VMEM) for _ in out_shape],
+        out_specs=[
+            pl.BlockSpec(memory_space=pl.ANY if at < apart else pltpu.VMEM)
+            for at in range(len(out_shape))
+        ],
         scratch_shapes=[
             pltpu.VMEM((count, SECTION, 128), bf16),
             pltpu.VMEM((count * 216 + 32, 128), f32),
             pltpu.VMEM(tiles, f32),
             pltpu.SemaphoreType.DMA((groups,)),
+            *scratch,
         ],
         compiler_params=pltpu.CompilerParams(vmem_limit_bytes=VMEM_LIMIT),
-        cost_estimate=pl.CostEstimate(flops=0, bytes_accessed=nbytes, transcendentals=0),
+        cost_estimate=pl.CostEstimate(flops=2_000_000_000, bytes_accessed=nbytes, transcendentals=0),
     )(gathered)
 
 
@@ -224,7 +259,7 @@
     return unpack_call(
         unpack_rest_kernel, layer,
         [((QW, D), bf16), ((D, 2 * FF), bf16), ((FF, D), bf16), ((1, 640), f32)], gathered,
-        DEVICES - SPLIT, 4, (5, FF, 128), 30_000_000,
+        DEVICES - SPLIT, 4, (5, FF, 128), 30_000_000, apart=3, scratch=WEIGHT_SCRATCH,
     )
 
 
@@ -296,9 +331,13 @@
 
 
 def attend_kernel(
-    first, x_in, q_in, kv_s, kv_t, segment, key_row, gain_row, w_out, w_in, w_down,
+    first, x_in, q_in, kv_s, kv_t, segment, key_row, gain_row, w_out_at, w_in_at, w_down_at,
     x_out, mixed_out, lse_out, middle_out, normed_out, gate_up_out, hidden_out,
+    w_out, w_in, w_down, sems,
 ):
+    copies = fetch((w_out_at, w_in_at, w_down_at), (w_out, w_in, w_down), sems)
+    for copy in copies:
+        copy.start()
     allowed = allowed_of(segment[...], key_row[...], first[0])
     bias = jnp.where(allowed, 0.0, -1e30).astype(f32)
     bias = jnp.concatenate([bias] * GROUP, axis=0)
@@ -318,15 +357,18 @@
             pieces.append(mixed[n * ROWS : (n + 1) * ROWS, :])
     mixed = jnp.concatenate(pieces, axis=1).astype(bf16)
     mixed_out[...] = mixed
+    copies[0].wait()
     middle = x_in[...].astype(f32) + mm(mixed, w_out[...])
     middle_out[...] = middle
     normed = (middle * inverse_norm(middle) * gain_row[:, 0:D]).astype(bf16)
     normed_out[...] = normed
+    copies[1].wait()
     gate_up = mm(normed, w_in[...])
     gate_up_out[...] = gate_up
     gate = gate_up[:, 0:FF]
     hidden = (gate * jax.nn.sigmoid(gate) * gate_up[:, FF:]).astype(bf16)
     hidden_out[...] = hidden
+    copies[2].wait()
     x_out[...] = middle + mm(hidden, w_down[...])
 
 
@@ -338,14 +380,32 @@
 
 
 def back_kernel(
-    first, g_in, q_in, kv_s, kv_t, segment, key_row, cosine, sine, gain_row, w_out, w_in, w_down,
-    lse, middle_in, gate_up,
+    first, g_in, q_in, kv_s, kv_t, segment, key_row, cosine, sine, gain_row, lse, middle_in,
+    gate_up_at, w_out_at, w_in_at, w_down_at,
     branch_out, grad_gu_out, attn_out, middle_grad_out, dq_out, dkv_s, dkv_t, gain_out,
+    w_out, w_in, w_down, sems, gate_up, gate_sem,
 ):
+    copies = fetch((w_out_at, w_in_at, w_down_at), (w_out, w_in, w_down), sems)
+    gate_copy = pltpu.make_async_copy(gate_up_at, gate_up, gate_sem)
+    copies[2].start()
+    gate_copy.start()
+    copies[1].start()
+    copies[0].start()
+    allowed = allowed_of(segment[...], key_row[...], first[0])
+    bias = jnp.where(allowed, 0.0, -1e30).astype(f32)
+    bias = jnp.concatenate([bias] * GROUP, axis=0)
+    q = q_in[...]
+    held = []
+    for group in range(KVH):
+        keys = window_rows(kv_s, kv_t, group * HD)
+        scores = mm_t(group_rows(q, group), keys) * FACTOR + bias
+        held.append(jnp.exp(scores - lse[:, group : group + 1]))
     g = g_in[...].astype(f32)
     branch = g.astype(bf16)
     branch_out[...] = branch
+    copies[2].wait()
     grad_hidden = mm_t(branch, w_down[...])
+    gate_copy.wait()
     gate = gate_up[:, 0:FF]
     up = gate_up[:, FF:]
     sigma = jax.nn.sigmoid(gate)
@@ -353,6 +413,7 @@
         grad_hidden * up * sigma * (1.0 + gate * (1.0 - sigma))
     ).astype(bf16)
     grad_gu_out[:, FF:] = (grad_hidden * gate * sigma).astype(bf16)
+    copies[1].wait()
     grad_two = mm_t(grad_gu_out[...], w_in[...])
     middle = middle_in[...]
     inverse = inverse_norm(middle)
@@ -361,29 +422,25 @@
     middle_grad_out[...] = grad_middle
     attn = grad_middle.astype(bf16)
     attn_out[...] = attn
+    copies[0].wait()
     grad_mixed = mm_t(attn, w_out[...]).astype(bf16)
 
-    allowed = allowed_of(segment[...], key_row[...], first[0])
-    bias = jnp.where(allowed, 0.0, -1e30).astype(f32)
-    bias = jnp.concatenate([bias] * GROUP, axis=0)
-    q = q_in[...]
     dq, dk, dv = [], [], []
     for group in range(KVH):
         keys = window_rows(kv_s, kv_t, group * HD)
         values = window_rows(kv_s, kv_t, KW + group * HD)
         query = group_rows(q, group)
         grad = group_rows(grad_mixed, group)
-        scores = mm_t(query, keys) * FACTOR + bias
-        probs = jnp.exp(scores - lse[:, group : group + 1])
+        probs = held[group]
         grad_w = mm_t(grad, values)
         delta = jnp.sum(probs * grad_w, axis=-1, keepdims=True)
         grad_scores = (probs * (grad_w - delta)).astype(bf16)
         part = mm(grad_scores, keys) * FACTOR
         for n in range(GROUP):
             dq.append(part[n * ROWS : (n + 1) * ROWS, :])
-        dk.append(t_mm(grad_scores, query) * FACTOR)
-        dv.append(t_mm(probs.astype(bf16), grad))
-    dkv = jnp.concatenate(dk + dv, axis=1)
+        dk.append(mm(query.T, grad_scores) * FACTOR)
+        dv.append(mm(grad.T, probs.astype(bf16)))
+    dkv = jnp.concatenate(dk + dv, axis=0).T
     dkv_s[...] = dkv[0:WIN_S, :]
     dkv_t[...] = dkv[WIN_S:, :].astype(bf16)
     wide = jnp.concatenate(dq + [jnp.zeros((ROWS, HD), f32)], axis=1)
@@ -430,9 +487,10 @@
 
 def put_matrix(flat, tile, left, right, start_half, width_half):
     rows, columns = left.shape[1], right.shape[1]
+    turned = left[...].T
     for t in range((width_half + 1) // 2):
         wide = min(128, columns - 128 * t)
-        tile[t, 0:rows, 0:wide] = t_mm(left[...], right[:, 128 * t : 128 * t + wide])
+        tile[t, 0:rows, 0:wide] = mm(turned, right[:, 128 * t : 128 * t + wide])
     for parity in range(2):
         put_rows(
             flat, start_half + parity * width_half, rows // 2, width_half,
@@ -463,9 +521,11 @@
     put_matrix(flat, tile, mixed, attn, HALF_OUT + half, D // 64)
     put_matrix(flat, tile, hidden, branch, HALF_DOWN + half, D // 64)
 
+    turned = normed_two[...].T
+
     def in_tile(c, carry):
-        flat[pl.ds((HALF_IN + half) // 2 + c, D, stride=24), :] = t_mm(
-            normed_two[...], grad_gu[:, pl.ds(pl.multiple_of(c * 128, 128), 128)]
+        flat[pl.ds((HALF_IN + half) // 2 + c, D, stride=24), :] = mm(
+            turned, grad_gu[:, pl.ds(pl.multiple_of(c * 128, 128), 128)]
         )
         return carry
 
@@ -491,11 +551,13 @@
     return lax.ppermute(value, "fsdp", [(i, i ^ 1) for i in range(DEVICES)])
 
 
-def window_of(value, core):
+def window_of(value, core, beside=()):
     blocks = [hop(value, by) for by in (8, 6, 4, 2)] + [value]
     same = jnp.concatenate(blocks, axis=0)
     rows = value.shape[0]
     gift = lax.dynamic_slice_in_dim(same, (1 - core) * rows, SAME_CORE * rows, 0)
+    if beside:
+        gift, _ = lax.optimization_barrier((gift, beside))
     return same, swap(gift)
 
 
@@ -512,12 +574,36 @@
     return total[SAME_CORE * ROWS :], pieces
 
 
-def both_cores(keep, send):
-    return (keep.astype(f32) + swap(send).astype(f32)).astype(bf16)
-
-
-def to_owners(first, rest, device):
-    total = jnp.concatenate([first, rest], axis=0).reshape(DEVICES // 2, CHUNK, 128)
+def join_kernel(keep_first, got_first, keep_rest, got_rest, out):
+    low = LOW_PLANES // JOIN
+
+    @pl.when(pl.program_id(0) < low)
+    def _():
+        out[...] = (keep_first[...].astype(f32) + got_first[...].astype(f32)).astype(bf16)
+
+    @pl.when(pl.program_id(0) >= low)
+    def _():
+        out[...] = (keep_rest[...].astype(f32) + got_rest[...].astype(f32)).astype(bf16)
+
+
+def join(keep_first, got_first, keep_rest, got_rest):
+    low = LOW_PLANES // JOIN
+    block = (JOIN * CHUNK, 128)
+    first = pl.BlockSpec(block, lambda i: (jnp.minimum(i, low - 1), 0))
+    rest = pl.BlockSpec(block, lambda i: (jnp.maximum(i - low, 0), 0))
+    return pl.pallas_call(
+        join_kernel,
+        grid=(DEVICES // 2 // JOIN,),
+        out_shape=jax.ShapeDtypeStruct((DEVICES // 2 * CHUNK, 128), bf16),
+        in_specs=[first, first, rest, rest],
+        out_specs=pl.BlockSpec(block, lambda i: (i, 0)),
+        compiler_params=pltpu.CompilerParams(vmem_limit_bytes=16 * 1024 * 1024),
+        cost_estimate=pl.CostEstimate(flops=0, bytes_accessed=11_000_000, transcendentals=0),
+    )(keep_first, got_first, keep_rest, got_rest)
+
+
+def to_owners(total, device):
+    total = total.reshape(DEVICES // 2, CHUNK, 128)
     groups = [list(range(0, DEVICES, 2)), list(range(1, DEVICES, 2))]
     pieces = lax.all_to_all(
         total, "fsdp", split_axis=0, concat_axis=0, tiled=True, axis_index_groups=groups
@@ -586,13 +672,13 @@
                 [x, cosine, sine, gain_one, w_qkv],
                 flops=150_000_000, nbytes=3_000_000,
             )
-            kv_s, kv_t = window_of(kv, core)
+            kv_s, kv_t = window_of(kv, core, (w_out,))
         x_next, mixed, lse, middle, normed_two, gate_up, hidden = call(
             attend_kernel,
             [((ROWS, D), f32), ((ROWS, QW), bf16), ((GROUP * ROWS, KVH), f32), ((ROWS, D), f32),
              ((ROWS, D), bf16), ((ROWS, 2 * FF), f32), ((ROWS, FF), bf16)],
             [first, x, q, kv_s, kv_t, segment, key_row, gain_two, w_out, w_in, w_down],
-            smem=1, flops=2_000_000_000, nbytes=12_000_000,
+            scratch=WEIGHT_SCRATCH, smem=1, apart=3, flops=2_000_000_000, nbytes=12_000_000,
         )
         held.append((x, q, kv_s, kv_t, normed, mixed, lse, middle, normed_two, gate_up, hidden,
                      w_qkv, w_out, w_in, w_down, gain_one, gain_two))
@@ -608,9 +694,11 @@
             back_kernel,
             [((ROWS, D), bf16), ((ROWS, 2 * FF), bf16), ((ROWS, D), bf16), ((ROWS, D), f32),
              ((ROWS, QW), bf16), ((WIN_S, 2 * KW), f32), ((WIN_T, 2 * KW), bf16), ((1, D), f32)],
-            [first, g, q, kv_s, kv_t, segment, key_row, cosine, sine, gain_two, w_out, w_in, w_down,
-             lse, middle, gate_up],
-            smem=1, flops=3_000_000_000, nbytes=15_000_000,
+            [first, g, q, kv_s, kv_t, segment, key_row, cosine, sine, gain_two, lse, middle,
+             gate_up, w_out, w_in, w_down],
+            scratch=WEIGHT_SCRATCH
+            + (pltpu.VMEM((ROWS, 2 * FF), f32), pltpu.SemaphoreType.DMA),
+            smem=1, apart=4, flops=3_000_000_000, nbytes=15_000_000,
         )
         rest_shape = (((DEVICES // 2 - LOW_PLANES) * CHUNK, 128), bf16)
         keep, send, edge = call(
@@ -624,7 +712,7 @@
         )
         own_kv, pieces = give_back(dkv_s, dkv_t, core)
         send, pieces = lax.optimization_barrier((send, pieces))
-        rest_part = both_cores(keep, send)
+        keep_rest, got_rest = keep, swap(send)
         g, project, grad_one = call(
             back_heads_kernel,
             [((ROWS, D), f32), ((ROWS, PW), bf16), ((1, D), f32)],
@@ -638,13 +726,15 @@
             pack_first_kernel,
             [low_shape, low_shape],
             [core_in, normed, project, grad_one, edge],
-            scratch=[pltpu.VMEM((216 * SPLIT + 480, 128), f32), pltpu.VMEM((8, D, 128), f32)],
+            scratch=[
+                pltpu.VMEM((216 * SPLIT + EDGE + 8, 128), f32), pltpu.VMEM((8, D, 128), f32)
+            ],
             smem=1, flops=200_000_000, nbytes=8_000_000,
         )
-        first_part = both_cores(keep, send)
+        total = join(keep, swap(send), keep_rest, got_rest)
         if layer > 0:
-            g, first_part, rest_part = lax.optimization_barrier((g, first_part, rest_part))
-        grads[layer] = to_owners(first_part, rest_part, device)
+            g, total = lax.optimization_barrier((g, total))
+        grads[layer] = to_owners(total, device)
     return (layer_out, g, jnp.stack(grads))
 
 

time: 390 us -> 377 us (0.967)
  other arithmetic: 31.7 us -> 11.9 us
  local copies, waits for them, and re-layouts: 16.8 us -> 21.8 us
  waiting for transfers between devices: 105 us -> 109 us
    concatenate x2 -> x0, other arithmetic: 11.4 us -> none  [to_owners(): jnp.concatenate([first, rest], axis=0).reshape(DEVICES // 2, CHUNK, 128)]
    pallas_call x0 -> x2, Pallas kernels: none -> 9.42 us  [join(): pl.pallas_call(join_kernel, grid=(DEVICES // 2 // JOIN,), out_shape=jax.S...]
    unnamed x51 -> x71, local copies, waits for them, and re-layouts: 5.22 us -> 12.7 us
    pallas_call x12, Pallas kernels: 92.3 us -> 85 us  [call(): pl.pallas_call(kernel, out_shape=[jax.ShapeDtypeStruct(s, d) for s, d in...]
    convert_element_type x4 -> x0, other arithmetic: 6 us -> none  [both_cores(): return (keep.astype(f32) + swap(send).astype(f32)).astype(bf16)]
  transfers between devices with their start and end apart: 32 -> 32, of which waited for: 10 -> 12; matrix products, arithmetic and copies ran while one was open for 6% -> 5% of each run, Pallas kernels for 16% -> 16%
where the time goes in v3:
time: 377 us; the launch traced here: 371 us
  Pallas kernels  118 us (31%)
  waiting for transfers between devices  109 us (29%)
  starting transfers between devices  95.3 us (25%)
  local copies, waits for them, and re-layouts  21.8 us (6%)
  between operations  15.3 us (4%)
  other arithmetic  11.9 us (3%)
    pallas_call x12, Pallas kernels, call(): pl.pallas_call(kernel, out_shape=[jax.ShapeDtypeStruct(s, d) for s, d in...  85 us
    ppermute x20, starting transfers between devices, hop(): return lax.ppermute(value, 'fsdp', pairs)  72.7 us
    all_to_all x2, waiting for transfers between devices, to_owners(): lax.all_to_all(total, 'fsdp', split_axis=0, concat_axis=0, tiled=True, ax...  48.2 us
    all_gather x1, waiting for transfers between devices, body(): lax.all_gather(jnp.concatenate(sections), 'fsdp', axis=0, tiled=True)  40.6 us
    pallas_call x4, Pallas kernels, unpack_call(): pl.pallas_call(functools.partial(kernel, layer), out_shape=[jax.ShapeDtyp...  23.4 us
    all_to_all x2, starting transfers between devices, to_owners(): lax.all_to_all(total, 'fsdp', split_axis=0, concat_axis=0, tiled=True, ax...  20.7 us
    unnamed x71, local copies, waits for them, and re-layouts  12.7 us
    ppermute x20, waiting for transfers between devices, hop(): return lax.ppermute(value, 'fsdp', pairs)  10.9 us
  transfers between devices with their start and end apart: 32, of which 12 were waited for; matrix products, arithmetic and copies ran while one was open for 5% of the time, Pallas kernels for 16%

profile of v3, /device:TPU:50, one launch (start us, length us, event | category | flops | bytes accessed | tf_op | source)
XLA Modules:
  0.0 370.7 jit_solution(767553747113681316)
XLA Ops:
  7.2 1.6 slice_reduce_fusion.1
  10.8 3.8 %collective-permute-start.8 = (s32[128]{0:T(128)}, s32[128]{0:T(128)S(1)}, u32[]{:S(2)}, u32[]{:S(2)}) collective-permute-start(s32[128]{0:T(128)} %param.7), channel_id=1, source_target_pairs={{0,2},{1,3},{2,4},{3,5},{4,6},{5,7},{6,8},{7,9},{8,10},{9,11},{10,... | collective-permute-start | bytes 1544 | tf_op jit(solution)/shard_map/ppermute | solution.py:547
  14.6 3.0 collective-permute-start.7
  17.6 5.2 %collective-permute-start.6 = (s32[128]{0:T(128)}, s32[128]{0:T(128)S(1)}, u32[]{:S(2)}, u32[]{:S(2)}) collective-permute-start(s32[128]{0:T(128)} %param.7), channel_id=1, source_target_pairs={{0,6},{1,7},{2,8},{3,9},{4,10},{5,11},{6,12},{7,13},{8,14},{9,15},... | collective-permute-start | bytes 1544 | tf_op jit(solution)/shard_map/ppermute | solution.py:547
  22.8 3.1 collective-permute-start.5
  25.9 1.1 copy.32.x_in
  27.0 1.9 collective-permute-start.3
  30.4 6.0 %collective-permute-start.2 = (bf16[128,576]{1,0:T(8,128)(2,1)S(1)}, bf16[128,576]{1,0:T(8,128)(2,1)S(1)}, u32[]{:S(2)}, u32[]{:S(2)}) collective-permute-start(bf16[128,576]{1,0:T(8,128)(2,1)S(1)} %copy.32.x_in), channel_id=1, source_target_pairs={{0,4},{1,5},{2,6},{3,7},{4,8},{5,9},{6,10},{7,11},{8,12},{9,13},{1... | collective-permute-start | bytes 442376 | tf_op jit(solution)/shard_map/ppermute | solution.py:547
  36.4 1.9 collective-permute-start.1
  38.4 3.5 collective-permute-start
  44.1 1.5 collective-permute-done
  46.2 1.1 copy-done.10
  47.7 2.1 multiply_sine_fusion
  49.8 1.0 pad_maximum_fusion
  52.4 0.9 constant_dynamic-update-slice_fusion.5.window
  53.3 40.6 %all-gather.2.cloned.1.call-done = bf16[7864320]{0:T(1024)(128)(2,1)} async-done(((bf16[61440]{0:T(1024)(128)(2,1)}), bf16[7864320]{0:T(1024)(128)(2,1)}) %all-gather.2.cloned.1.call-update) | async-done | bytes 15728656 | tf_op jit(solution)/shard_map/all_gather | solution.py:635
  93.9 3.3 shard_map.89
  97.2 3.0 shard_map.85
  100.3 8.6 %shard_map.87 = (bf16[576,576]{1,0:T(8,128)(2,1)}, bf16[576,3072]{1,0:T(8,128)(2,1)}, bf16[1536,576]{1,0:T(8,128)(2,1)}, f32[1,640]{1,0:T(1,128)}) custom-call(bf16[128,2,240,128]{3,2,1,0:T(8,128)(2,1)} %bitcast.24), custom_call_target="tpu_custom_call" | custom-call | flops 2000000000 | bytes 30000000 | tf_op jit(solution)/shard_map/pallas_call | solution.py:231
  108.8 4.6 %shard_map.86 = (bf16[128,576]{1,0:T(8,128)(2,1)}, bf16[640,384]{1,0:T(8,128)(2,1)}, bf16[512,384]{1,0:T(8,128)(2,1)}, bf16[128,576]{1,0:T(8,128)(2,1)}) custom-call(bf16[1152,576]{1,0:T(8,128)(2,1)} %constant_dynamic-update-slice_fusion.5.window, f32[1152,128]{1,0:T(8,128)} %copy-done.6, f32[1152,128]{1,0:T(8,128)} %copy-done.7, ...), custom_call_target="tpu_custom_call" | custom-call | flops 800000000 | bytes 6000000 | tf_op jit(solution)/shard_map/pallas_call | solution.py:70
  113.4 7.6 %shard_map.88 = (f32[128,576]{1,0:T(8,128)}, bf16[128,576]{1,0:T(8,128)(2,1)}, f32[384,3]{1,0:T(8,128)}, f32[128,576]{1,0:T(8,128)}, bf16[128,576]{1,0:T(8,128)(...) custom-call(s32[1]{0:T(128)} %bitcast.first, bf16[128,576]{1,0:T(8,128)(2,1)} %copy-done.8, ...), custom_call_target="tpu_custom_call" | custom-call | flops 2000000000 | bytes 12000000 | tf_op jit(solution)/shard_map/pallas_call | solution.py:70
  121.1 2.8 shard_map.90
  123.9 3.3 collective-permute-start.13
  127.2 5.3 %collective-permute-start.12 = (bf16[128,384]{1,0:T(8,128)(2,1)}, bf16[128,384]{1,0:T(8,128)(2,1)S(1)}, u32[]{:S(2)}, u32[]{:S(2)}) collective-permute-start(bf16[128,384]{1,0:T(8,128)(2,1)} %get-tuple-element.96), channel_id=1, source_target_pairs={{0,4},{1,5},{2,6},{3,7},{4,8},{5,9},{6,10},{7,11},{8,12},{9,13},{1... | collective-permute-start | bytes 294920 | tf_op jit(solution)/shard_map/ppermute | solution.py:547
  132.5 2.4 collective-permute-start.11
  134.9 4.5 %collective-permute-start.10 = (bf16[128,384]{1,0:T(8,128)(2,1)}, bf16[128,384]{1,0:T(8,128)(2,1)S(1)}, u32[]{:S(2)}, u32[]{:S(2)}) collective-permute-start(bf16[128,384]{1,0:T(8,128)(2,1)} %get-tuple-element.96), channel_id=1, source_target_pairs={{0,8},{1,9},{2,10},{3,11},{4,12},{5,13},{6,14},{7,15},{8,16},{9,17... | collective-permute-start | bytes 294920 | tf_op jit(solution)/shard_map/ppermute | solution.py:547
  139.5 8.5 %shard_map.91 = (bf16[576,576]{1,0:T(8,128)(2,1)}, bf16[576,3072]{1,0:T(8,128)(2,1)}, bf16[1536,576]{1,0:T(8,128)(2,1)}, f32[1,640]{1,0:T(1,128)}) custom-call(bf16[128,2,240,128]{3,2,1,0:T(8,128)(2,1)} %bitcast.25), custom_call_target="tpu_custom_call" | custom-call | flops 2000000000 | bytes 30000000 | tf_op jit(solution)/shard_map/pallas_call | solution.py:231
  148.9 0.8 copy.35.g_in
  151.0 7.7 %shard_map.92 = (f32[128,576]{1,0:T(8,128)}, bf16[128,576]{1,0:T(8,128)(2,1)}, f32[384,3]{1,0:T(8,128)}, f32[128,576]{1,0:T(8,128)}, bf16[128,576]{1,0:T(8,128)(...) custom-call(s32[1]{0:T(128)} %bitcast.first, f32[128,576]{1,0:T(8,128)} %get-tuple-element.92.x_in, ...), custom_call_target="tpu_custom_call" | custom-call | flops 2000000000 | bytes 12000000 | tf_op jit(solution)/shard_map/pallas_call | solution.py:70
  158.7 11.5 %shard_map.93 = (bf16[128,576]{1,0:T(8,128)(2,1)}, bf16[128,3072]{1,0:T(8,128)(2,1)}, bf16[128,576]{1,0:T(8,128)(2,1)}, f32[128,576]{1,0:T(8,128)}, bf16[128,576...) custom-call(s32[1]{0:T(128)} %bitcast.first, bf16[128,576]{1,0:T(8,128)(2,1)} %copy.35.g_in, ...), custom_call_target="tpu_custom_call" | custom-call | flops 3000000000 | bytes 15000000 | tf_op jit(solution)/shard_map/pallas_call | solution.py:70
  170.4 1.8 collective-permute-done.15
  172.4 3.3 collective-permute-start.19
  175.7 3.2 collective-permute-start.18
  178.9 2.0 collective-permute-start.17
  180.9 5.1 %collective-permute-start.16 = (bf16[128,384]{1,0:T(8,128)(2,1)S(1)}, bf16[128,384]{1,0:T(8,128)(2,1)S(1)}, u32[]{:S(2)}, u32[]{:S(2)}) collective-permute-start(bf16[128,384]{1,0:T(8,128)(2,1)S(1)} %get-tuple-element.182), channel_id=1, source_target_pairs={{8,0},{9,1},{10,2},{11,3},{12,4},{13,5},{14,6},{15,7},{16,8},{17,9... | collective-permute-start | bytes 294920 | tf_op jit(solution)/shard_map/ppermute | solution.py:547
  186.0 12.3 %shard_map.94 = (bf16[10752,128]{1,0:T(8,128)(2,1)}, bf16[10752,128]{1,0:T(8,128)(2,1)}, f32[2616,128]{1,0:T(8,128)}) custom-call(s32[1]{0:T(128)} %bitcast.4.core, bf16[128,576]{1,0:T(8,128)(2,1)} %get-tuple-element.109.mixed, bf16[128,576]{1,0:T(8,128)(2,1)} %get-tuple-element.110.attn, bf16[128,576]{1,0:T(8,128)(2,1)} %get-tuple-element.111.normed_two, ...), custom_call_target="tpu_custom_call" | custom-call | flops 1000000000 | bytes 25000000 | tf_op jit(solution)/shard_map/pallas_call | solution.py:70
  199.2 3.3 shard_map.95
  202.5 4.1 %shard_map.96 = (bf16[3584,128]{1,0:T(8,128)(2,1)}, bf16[3584,128]{1,0:T(8,128)(2,1)}) custom-call(s32[1]{0:T(128)} %bitcast.4.core, bf16[128,576]{1,0:T(8,128)(2,1)} %get-tuple-element.123.normed, bf16[128,960]{1,0:T(8,128)(2,1)} %get-tuple-element.124.project, f32[1,576]{1,0:T(1,128)} %get-tuple-element.125.gain_one, f32[2616,128]{1,0:T(8,128)} %get-tuple-element.126.edge), custom_call_target="tpu_custom_call" | custom-call | flops 200000000 | bytes 8000000 | tf_op jit(solution)/shard_map/pallas_call | solution.py:70
  207.1 2.3 collective-permute-done.20.got_first
  209.4 1.2 copy-done.5
  210.6 4.7 %shard_map.97 = bf16[14336,128]{1,0:T(8,128)(2,1)S(1)} custom-call(bf16[3584,128]{1,0:T(8,128)(2,1)S(1)} %copy-done.5, bf16[3584,128]{1,0:T(8,128)(2,1)S(1)} %collective-permute-done.20.got_first, bf16[10752,128]{1,0:T(8,128)(2,1)S(1)} %copy-done.3, bf16[10752,128]{1,0:T(8,128)(2,1)} %collective-permute-done.21.got_rest), custom_call_target="tpu_custom_call" | custom-call | bytes 11000000 | tf_op jit(solution)/shard_map/pallas_call | solution.py:594
  215.3 1.8 copy-done
  217.1 9.4 %all-to-all-start = ((bf16[64,224,128]{2,1,0:T(8,128)(2,1)}), bf16[64,224,128]{2,1,0:T(8,128)(2,1)}, u32[]{:S(2)}, u32[]{:S(2)}) async-start(bf16[64,224,128]{2,1,0:T(8,128)(2,1)} %bitcast.20), calls=%async_computation | async-start | bytes 7340032 | tf_op jit(solution)/shard_map/all_to_all | solution.py:608
  226.5 11.5 %shard_map.98 = (bf16[128,576]{1,0:T(8,128)(2,1)}, bf16[128,3072]{1,0:T(8,128)(2,1)}, bf16[128,576]{1,0:T(8,128)(2,1)}, f32[128,576]{1,0:T(8,128)}, bf16[128,576...) custom-call(s32[1]{0:T(128)} %bitcast.first, ...), custom_call_target="tpu_custom_call" | custom-call | flops 3000000000 | bytes 15000000 | tf_op jit(solution)/shard_map/pallas_call | solution.py:70
  238.1 1.9 collective-permute-done.22
  240.3 2.5 collective-permute-start.26
  242.8 4.3 %collective-permute-start.25 = (bf16[128,384]{1,0:T(8,128)(2,1)S(1)}, bf16[128,384]{1,0:T(8,128)(2,1)S(1)}, u32[]{:S(2)}, u32[]{:S(2)}) collective-permute-start(bf16[128,384]{1,0:T(8,128)(2,1)S(1)} %get-tuple-element.176), channel_id=1, source_target_pairs={{4,0},{5,1},{6,2},{7,3},{8,4},{9,5},{10,6},{11,7},{12,8},{13,9},{1... | collective-permute-start | bytes 294920 | tf_op jit(solution)/shard_map/ppermute | solution.py:547
  247.0 3.7 collective-permute-start.24
  250.7 4.8 %collective-permute-start.23 = (bf16[128,384]{1,0:T(8,128)(2,1)S(1)}, bf16[128,384]{1,0:T(8,128)(2,1)S(1)}, u32[]{:S(2)}, u32[]{:S(2)}) collective-permute-start(bf16[128,384]{1,0:T(8,128)(2,1)S(1)} %get-tuple-element.178), channel_id=1, source_target_pairs={{8,0},{9,1},{10,2},{11,3},{12,4},{13,5},{14,6},{15,7},{16,8},{17,9... | collective-permute-start | bytes 294920 | tf_op jit(solution)/shard_map/ppermute | solution.py:547
  255.5 12.4 %shard_map.99 = (bf16[10752,128]{1,0:T(8,128)(2,1)}, bf16[10752,128]{1,0:T(8,128)(2,1)}, f32[2616,128]{1,0:T(8,128)}) custom-call(s32[1]{0:T(128)} %bitcast.4.core, bf16[128,576]{1,0:T(8,128)(2,1)} %get-tuple-element.138.mixed, bf16[128,576]{1,0:T(8,128)(2,1)} %get-tuple-element.139.attn, bf16[128,576]{1,0:T(8,128)(2,1)} %get-tuple-element.140.normed_two, ...), custom_call_target="tpu_custom_call" | custom-call | flops 1000000000 | bytes 25000000 | tf_op jit(solution)/shard_map/pallas_call | solution.py:70
  268.2 6.0 %collective-permute-done.25.r4 = bf16[128,384]{1,0:T(8,128)(2,1)S(1)} collective-permute-done((bf16[128,384]{1,0:T(8,128)(2,1)S(1)}, bf16[128,384]{1,0:T(8,128)(2,1)S(1)}, u32[]{:S(2)}, u32[]{:S(2)}) %collective-permute-start.25) | collective-permute-done | bytes 98336 | tf_op jit(solution)/shard_map/ppermute | solution.py:547
  274.2 2.8 collective-permute-done.24.r6
  277.8 3.2 shard_map.100
  281.0 2.7 convert_reduce_fusion.1
  283.9 4.1 %shard_map.101 = (bf16[3584,128]{1,0:T(8,128)(2,1)}, bf16[3584,128]{1,0:T(8,128)(2,1)}) custom-call(s32[1]{0:T(128)} %bitcast.4.core, bf16[128,576]{1,0:T(8,128)(2,1)} %get-tuple-element.152.normed, bf16[128,960]{1,0:T(8,128)(2,1)} %get-tuple-element.155.project, f32[1,576]{1,0:T(1,128)} %get-tuple-element.156.gain_one, f32[2616,128]{1,0:T(8,128)} %get-tuple-element.157.edge), custom_call_target="tpu_custom_call" | custom-call | flops 200000000 | bytes 8000000 | tf_op jit(solution)/shard_map/pallas_call | solution.py:70
  288.4 2.3 collective-permute-done.27.got_first
  290.7 1.2 copy-done.4
  291.9 4.7 %shard_map.102 = bf16[14336,128]{1,0:T(8,128)(2,1)S(1)} custom-call(bf16[3584,128]{1,0:T(8,128)(2,1)S(1)} %copy-done.4, bf16[3584,128]{1,0:T(8,128)(2,1)S(1)} %collective-permute-done.27.got_first, bf16[10752,128]{1,0:T(8,128)(2,1)S(1)} %copy-done.2, bf16[10752,128]{1,0:T(8,128)(2,1)} %collective-permute-done.28.got_rest), custom_call_target="tpu_custom_call" | custom-call | bytes 11000000 | tf_op jit(solution)/shard_map/pallas_call | solution.py:594
  296.6 1.8 copy-done.1
  298.5 11.3 %all-to-all-start.1 = ((bf16[64,224,128]{2,1,0:T(8,128)(2,1)}), bf16[64,224,128]{2,1,0:T(8,128)(2,1)}, u32[]{:S(2)}, u32[]{:S(2)}) async-start(bf16[64,224,128]{2,1,0:T(8,128)(2,1)} %bitcast.21), calls=%async_computation.1 | async-start | bytes 7340032 | tf_op jit(solution)/shard_map/all_to_all | solution.py:608
  310.6 0.9 copy.40
  311.5 48.2 %all-to-all-done.1 = bf16[64,224,128]{2,1,0:T(8,128)(2,1)} async-done(((bf16[64,224,128]{2,1,0:T(8,128)(2,1)}), bf16[64,224,128]{2,1,0:T(8,128)(2,1)}, u32[]{:S(2)}, u32[]{:S(2)}) %all-to-all-start.1) | async-done | bytes 3670048 | tf_op jit(solution)/shard_map/all_to_all | solution.py:608
  359.8 2.6 convert_reduce_fusion
  362.6 0.9 pad_maximum_fusion.2
  (139 shorter events, 15.1 us)
Async XLA Ops:
  7.2 36.1 %copy-start.26 = (s32[128]{0:T(128)S(1)}, s32[128]{0:T(128)}, u32[]{:S(2)}) copy-start(s32[128]{0:T(128)} %param.7) | copy-start | bytes 1540
  7.2 86.7 %all-gather.2.cloned.1.call-start = ((), (), s32[]{:S(2)}) async-start(), calls=%async_computation.2 | async-start | bytes 15851520 | tf_op jit(solution)/shard_map/all_gather | solution.py:635
  10.8 31.1 %collective-permute-start.8 = (s32[128]{0:T(128)}, s32[128]{0:T(128)S(1)}, u32[]{:S(2)}, u32[]{:S(2)}) collective-permute-start(s32[128]{0:T(128)} %param.7), channel_id=1, source_target_pairs={{0,2},{1,3},{2,4},{3,5},{4,6},{5,7},{6,8},{7,9},{8,10},{9,11},{10,... | collective-permute-start | bytes 1544 | tf_op jit(solution)/shard_map/ppermute | solution.py:547
  14.6 23.8 %collective-permute-start.7 = (s32[128]{0:T(128)}, s32[128]{0:T(128)S(1)}, u32[]{:S(2)}, u32[]{:S(2)}) collective-permute-start(s32[128]{0:T(128)} %param.7), channel_id=1, source_target_pairs={{0,4},{1,5},{2,6},{3,7},{4,8},{5,9},{6,10},{7,11},{8,12},{9,13},{1... | collective-permute-start | bytes 1544 | tf_op jit(solution)/shard_map/ppermute | solution.py:547
  17.6 18.8 %collective-permute-start.6 = (s32[128]{0:T(128)}, s32[128]{0:T(128)S(1)}, u32[]{:S(2)}, u32[]{:S(2)}) collective-permute-start(s32[128]{0:T(128)} %param.7), channel_id=1, source_target_pairs={{0,6},{1,7},{2,8},{3,9},{4,10},{5,11},{6,12},{7,13},{8,14},{9,15},... | collective-permute-start | bytes 1544 | tf_op jit(solution)/shard_map/ppermute | solution.py:547
  22.8 7.6 %collective-permute-start.5 = (s32[128]{0:T(128)}, s32[128]{0:T(128)S(1)}, u32[]{:S(2)}, u32[]{:S(2)}) collective-permute-start(s32[128]{0:T(128)} %param.7), channel_id=1, source_target_pairs={{0,8},{1,9},{2,10},{3,11},{4,12},{5,13},{6,14},{7,15},{8,16},{9,17... | collective-permute-start | bytes 1544 | tf_op jit(solution)/shard_map/ppermute | solution.py:547
  27.0 20.3 %copy-start.8 = (bf16[128,576]{1,0:T(8,128)(2,1)}, bf16[128,576]{1,0:T(8,128)(2,1)S(1)}, u32[]{:S(2)}) copy-start(bf16[128,576]{1,0:T(8,128)(2,1)S(1)} %copy.32.x_in) | copy-start | bytes 442372
  27.0 19.1 %collective-permute-start.3 = (bf16[128,576]{1,0:T(8,128)(2,1)S(1)}, bf16[128,576]{1,0:T(8,128)(2,1)S(1)}, u32[]{:S(2)}, u32[]{:S(2)}) collective-permute-start(bf16[128,576]{1,0:T(8,128)(2,1)S(1)} %copy.32.x_in), channel_id=1, source_target_pairs={{0,2},{1,3},{2,4},{3,5},{4,6},{5,7},{6,8},{7,9},{8,10},{9,11},{10,... | collective-permute-start | bytes 442376 | tf_op jit(solution)/shard_map/ppermute | solution.py:547
  30.4 15.6 %collective-permute-start.2 = (bf16[128,576]{1,0:T(8,128)(2,1)S(1)}, bf16[128,576]{1,0:T(8,128)(2,1)S(1)}, u32[]{:S(2)}, u32[]{:S(2)}) collective-permute-start(bf16[128,576]{1,0:T(8,128)(2,1)S(1)} %copy.32.x_in), channel_id=1, source_target_pairs={{0,4},{1,5},{2,6},{3,7},{4,8},{5,9},{6,10},{7,11},{8,12},{9,13},{1... | collective-permute-start | bytes 442376 | tf_op jit(solution)/shard_map/ppermute | solution.py:547
  36.4 9.5 %collective-permute-start.1 = (bf16[128,576]{1,0:T(8,128)(2,1)S(1)}, bf16[128,576]{1,0:T(8,128)(2,1)S(1)}, u32[]{:S(2)}, u32[]{:S(2)}) collective-permute-start(bf16[128,576]{1,0:T(8,128)(2,1)S(1)} %copy.32.x_in), channel_id=1, source_target_pairs={{0,6},{1,7},{2,8},{3,9},{4,10},{5,11},{6,12},{7,13},{8,14},{9,15},... | collective-permute-start | bytes 442376 | tf_op jit(solution)/shard_map/ppermute | solution.py:547
  38.4 7.2 %collective-permute-start = (bf16[128,576]{1,0:T(8,128)(2,1)S(1)}, bf16[128,576]{1,0:T(8,128)(2,1)S(1)}, u32[]{:S(2)}, u32[]{:S(2)}) collective-permute-start(bf16[128,576]{1,0:T(8,128)(2,1)S(1)} %copy.32.x_in), channel_id=1, source_target_pairs={{0,8},{1,9},{2,10},{3,11},{4,12},{5,13},{6,14},{7,15},{8,16},{9,17... | collective-permute-start | bytes 442376 | tf_op jit(solution)/shard_map/ppermute | solution.py:547
  42.7 1.4 collective-permute-start.9
  46.1 1.1 copy-start.10
  47.6 4.5 %collective-permute-start.4 = (bf16[512,576]{0,1:T(8,128)(2,1)S(1)}, bf16[512,576]{0,1:T(8,128)(2,1)S(1)}, u32[]{:S(2)}, u32[]{:S(2)}) collective-permute-start(bf16[512,576]{0,1:T(8,128)(2,1)S(1)} %copy.29), channel_id=1, source_target_pairs={{0,1},{1,0},{2,3},{3,2},{4,5},{5,4},{6,7},{7,6},{8,9},{9,8},{10,11... | collective-permute-start | bytes 1769480 | tf_op jit(solution)/shard_map/ppermute | solution.py:551
  50.8 46.4 %copy-start.6 = (f32[1152,128]{1,0:T(8,128)}, f32[1152,128]{1,0:T(8,128)S(1)}, u32[]{:S(2)}) copy-start(f32[1152,128]{1,0:T(8,128)S(1)} %get-tuple-element.205.cosine) | copy-start | bytes 1769476
  50.8 46.4 %copy-start.7 = (f32[1152,128]{1,0:T(8,128)}, f32[1152,128]{1,0:T(8,128)S(1)}, u32[]{:S(2)}) copy-start(f32[1152,128]{1,0:T(8,128)S(1)} %get-tuple-element.206.sine) | copy-start | bytes 1769476
  123.9 24.3 %copy-start.25 = (bf16[128,384]{1,0:T(8,128)(2,1)S(1)}, bf16[128,384]{1,0:T(8,128)(2,1)}, u32[]{:S(2)}) copy-start(bf16[128,384]{1,0:T(8,128)(2,1)} %get-tuple-element.96) | copy-start | bytes 294916
  123.9 24.2 %collective-permute-start.13 = (bf16[128,384]{1,0:T(8,128)(2,1)}, bf16[128,384]{1,0:T(8,128)(2,1)S(1)}, u32[]{:S(2)}, u32[]{:S(2)}) collective-permute-start(bf16[128,384]{1,0:T(8,128)(2,1)} %get-tuple-element.96), channel_id=1, source_target_pairs={{0,2},{1,3},{2,4},{3,5},{4,6},{5,7},{6,8},{7,9},{8,10},{9,11},{10,... | collective-permute-start | bytes 294920 | tf_op jit(solution)/shard_map/ppermute | solution.py:547
  127.2 20.9 %collective-permute-start.12 = (bf16[128,384]{1,0:T(8,128)(2,1)}, bf16[128,384]{1,0:T(8,128)(2,1)S(1)}, u32[]{:S(2)}, u32[]{:S(2)}) collective-permute-start(bf16[128,384]{1,0:T(8,128)(2,1)} %get-tuple-element.96), channel_id=1, source_target_pairs={{0,4},{1,5},{2,6},{3,7},{4,8},{5,9},{6,10},{7,11},{8,12},{9,13},{1... | collective-permute-start | bytes 294920 | tf_op jit(solution)/shard_map/ppermute | solution.py:547
  132.5 15.5 %collective-permute-start.11 = (bf16[128,384]{1,0:T(8,128)(2,1)}, bf16[128,384]{1,0:T(8,128)(2,1)S(1)}, u32[]{:S(2)}, u32[]{:S(2)}) collective-permute-start(bf16[128,384]{1,0:T(8,128)(2,1)} %get-tuple-element.96), channel_id=1, source_target_pairs={{0,6},{1,7},{2,8},{3,9},{4,10},{5,11},{6,12},{7,13},{8,14},{9,15},... | collective-permute-start | bytes 294920 | tf_op jit(solution)/shard_map/ppermute | solution.py:547
  134.9 13.1 %collective-permute-start.10 = (bf16[128,384]{1,0:T(8,128)(2,1)}, bf16[128,384]{1,0:T(8,128)(2,1)S(1)}, u32[]{:S(2)}, u32[]{:S(2)}) collective-permute-start(bf16[128,384]{1,0:T(8,128)(2,1)} %get-tuple-element.96), channel_id=1, source_target_pairs={{0,8},{1,9},{2,10},{3,11},{4,12},{5,13},{6,14},{7,15},{8,16},{9,17... | collective-permute-start | bytes 294920 | tf_op jit(solution)/shard_map/ppermute | solution.py:547
  148.0 0.9 copy-start.16
  148.2 2.0 copy-start.9
  148.2 2.0 collective-permute-start.14
  150.2 0.8 copy-start.13
  170.1 2.1 copy-start.12
  170.2 2.0 collective-permute-start.15
  172.4 25.9 %collective-permute-start.19 = (bf16[128,384]{1,0:T(8,128)(2,1)S(1)}, bf16[128,384]{1,0:T(8,128)(2,1)S(1)}, u32[]{:S(2)}, u32[]{:S(2)}) collective-permute-start(bf16[128,384]{1,0:T(8,128)(2,1)S(1)} %get-tuple-element.179), channel_id=1, source_target_pairs={{2,0},{3,1},{4,2},{5,3},{6,4},{7,5},{8,6},{9,7},{10,8},{11,9},{12,... | collective-permute-start | bytes 294920 | tf_op jit(solution)/shard_map/ppermute | solution.py:547
  175.7 22.6 %collective-permute-start.18 = (bf16[128,384]{1,0:T(8,128)(2,1)S(1)}, bf16[128,384]{1,0:T(8,128)(2,1)S(1)}, u32[]{:S(2)}, u32[]{:S(2)}) collective-permute-start(bf16[128,384]{1,0:T(8,128)(2,1)S(1)} %get-tuple-element.180), channel_id=1, source_target_pairs={{4,0},{5,1},{6,2},{7,3},{8,4},{9,5},{10,6},{11,7},{12,8},{13,9},{1... | collective-permute-start | bytes 294920 | tf_op jit(solution)/shard_map/ppermute | solution.py:547
  178.9 19.4 %collective-permute-start.17 = (bf16[128,384]{1,0:T(8,128)(2,1)S(1)}, bf16[128,384]{1,0:T(8,128)(2,1)S(1)}, u32[]{:S(2)}, u32[]{:S(2)}) collective-permute-start(bf16[128,384]{1,0:T(8,128)(2,1)S(1)} %get-tuple-element.181), channel_id=1, source_target_pairs={{6,0},{7,1},{8,2},{9,3},{10,4},{11,5},{12,6},{13,7},{14,8},{15,9},... | collective-permute-start | bytes 294920 | tf_op jit(solution)/shard_map/ppermute | solution.py:547
  180.9 17.4 %collective-permute-start.16 = (bf16[128,384]{1,0:T(8,128)(2,1)S(1)}, bf16[128,384]{1,0:T(8,128)(2,1)S(1)}, u32[]{:S(2)}, u32[]{:S(2)}) collective-permute-start(bf16[128,384]{1,0:T(8,128)(2,1)S(1)} %get-tuple-element.182), channel_id=1, source_target_pairs={{8,0},{9,1},{10,2},{11,3},{12,4},{13,5},{14,6},{15,7},{16,8},{17,9... | collective-permute-start | bytes 294920 | tf_op jit(solution)/shard_map/ppermute | solution.py:547
  198.3 0.9 copy-start.20
  198.3 0.8 copy-start.22
  198.3 0.8 copy-start.23
  198.4 0.8 copy-start.24
  198.4 11.0 %collective-permute-start.21 = (bf16[10752,128]{1,0:T(8,128)(2,1)}, bf16[10752,128]{1,0:T(8,128)(2,1)}, u32[]{:S(2)}, u32[]{:S(2)}) collective-permute-start(bf16[10752,128]{1,0:T(8,128)(2,1)} %get-tuple-element.130), channel_id=1, source_target_pairs={{0,1},{1,0},{2,3},{3,2},{4,5},{5,4},{6,7},{7,6},{8,9},{9,8},{10,11... | collective-permute-start | bytes 8257544 | tf_op jit(solution)/shard_map/ppermute | solution.py:551
  199.2 10.2 %copy-start.3 = (bf16[10752,128]{1,0:T(8,128)(2,1)S(1)}, bf16[10752,128]{1,0:T(8,128)(2,1)}, u32[]{:S(2)}) copy-start(bf16[10752,128]{1,0:T(8,128)(2,1)} %get-tuple-element.129.keep_rest) | copy-start | bytes 8257540
  206.6 2.8 collective-permute-start.20
  209.4 1.2 copy-start.5
  215.3 1.8 copy-start
  217.1 63.9 %all-to-all-start = ((bf16[64,224,128]{2,1,0:T(8,128)(2,1)}), bf16[64,224,128]{2,1,0:T(8,128)(2,1)}, u32[]{:S(2)}, u32[]{:S(2)}) async-start(bf16[64,224,128]{2,1,0:T(8,128)(2,1)} %bitcast.20), calls=%async_computation | async-start | bytes 7340032 | tf_op jit(solution)/shard_map/all_to_all | solution.py:608
  238.0 2.1 copy-start.11
  238.0 2.0 collective-permute-start.22
  240.3 27.9 %collective-permute-start.26 = (bf16[128,384]{1,0:T(8,128)(2,1)S(1)}, bf16[128,384]{1,0:T(8,128)(2,1)S(1)}, u32[]{:S(2)}, u32[]{:S(2)}) collective-permute-start(bf16[128,384]{1,0:T(8,128)(2,1)S(1)} %get-tuple-element.175), channel_id=1, source_target_pairs={{2,0},{3,1},{4,2},{5,3},{6,4},{7,5},{8,6},{9,7},{10,8},{11,9},{12,... | collective-permute-start | bytes 294920 | tf_op jit(solution)/shard_map/ppermute | solution.py:547
  242.8 31.5 %collective-permute-start.25 = (bf16[128,384]{1,0:T(8,128)(2,1)S(1)}, bf16[128,384]{1,0:T(8,128)(2,1)S(1)}, u32[]{:S(2)}, u32[]{:S(2)}) collective-permute-start(bf16[128,384]{1,0:T(8,128)(2,1)S(1)} %get-tuple-element.176), channel_id=1, source_target_pairs={{4,0},{5,1},{6,2},{7,3},{8,4},{9,5},{10,6},{11,7},{12,8},{13,9},{1... | collective-permute-start | bytes 294920 | tf_op jit(solution)/shard_map/ppermute | solution.py:547
  247.0 30.0 %collective-permute-start.24 = (bf16[128,384]{1,0:T(8,128)(2,1)S(1)}, bf16[128,384]{1,0:T(8,128)(2,1)S(1)}, u32[]{:S(2)}, u32[]{:S(2)}) collective-permute-start(bf16[128,384]{1,0:T(8,128)(2,1)S(1)} %get-tuple-element.177), channel_id=1, source_target_pairs={{6,0},{7,1},{8,2},{9,3},{10,4},{11,5},{12,6},{13,7},{14,8},{15,9},... | collective-permute-start | bytes 294920 | tf_op jit(solution)/shard_map/ppermute | solution.py:547
  250.7 26.3 %collective-permute-start.23 = (bf16[128,384]{1,0:T(8,128)(2,1)S(1)}, bf16[128,384]{1,0:T(8,128)(2,1)S(1)}, u32[]{:S(2)}, u32[]{:S(2)}) collective-permute-start(bf16[128,384]{1,0:T(8,128)(2,1)S(1)} %get-tuple-element.178), channel_id=1, source_target_pairs={{8,0},{9,1},{10,2},{11,3},{12,4},{13,5},{14,6},{15,7},{16,8},{17,9... | collective-permute-start | bytes 294920 | tf_op jit(solution)/shard_map/ppermute | solution.py:547
  268.2 9.6 %copy-start.17 = (bf16[128,384]{1,0:T(8,128)(2,1)}, bf16[128,384]{1,0:T(8,128)(2,1)S(1)}, u32[]{:S(2)}) copy-start(bf16[128,384]{1,0:T(8,128)(2,1)S(1)} %collective-permute-done.26.r2) | copy-start | bytes 294916
  274.2 3.6 copy-start.18
  277.0 0.8 copy-start.19
  277.0 0.8 copy-start.21
  277.0 11.4 %collective-permute-start.28 = (bf16[10752,128]{1,0:T(8,128)(2,1)}, bf16[10752,128]{1,0:T(8,128)(2,1)}, u32[]{:S(2)}, u32[]{:S(2)}) collective-permute-start(bf16[10752,128]{1,0:T(8,128)(2,1)} %get-tuple-element.161), channel_id=1, source_target_pairs={{0,1},{1,0},{2,3},{3,2},{4,5},{5,4},{6,7},{7,6},{8,9},{9,8},{10,11... | collective-permute-start | bytes 8257544 | tf_op jit(solution)/shard_map/ppermute | solution.py:551
  281.0 9.7 %copy-start.2 = (bf16[10752,128]{1,0:T(8,128)(2,1)S(1)}, bf16[10752,128]{1,0:T(8,128)(2,1)}, u32[]{:S(2)}) copy-start(bf16[10752,128]{1,0:T(8,128)(2,1)} %get-tuple-element.160.keep_rest) | copy-start | bytes 8257540
  287.9 2.8 collective-permute-start.27
  290.7 1.2 copy-start.4
  296.6 1.8 copy-start.1
  298.4 11.3 %copy-start.15 = (f32[128,576]{1,0:T(8,128)S(1)}, f32[128,576]{1,0:T(8,128)}, u32[]{:S(2)}) copy-start(f32[128,576]{1,0:T(8,128)} %get-tuple-element.102) | copy-start | bytes 884740
  298.4 12.1 %copy-start.14 = (f32[128,576]{1,0:T(8,128)S(1)}, f32[128,576]{1,0:T(8,128)}, u32[]{:S(2)}) copy-start(f32[128,576]{1,0:T(8,128)} %get-tuple-element.167) | copy-start | bytes 884740
  298.5 61.3 %all-to-all-start.1 = ((bf16[64,224,128]{2,1,0:T(8,128)(2,1)}), bf16[64,224,128]{2,1,0:T(8,128)(2,1)}, u32[]{:S(2)}, u32[]{:S(2)}) async-start(bf16[64,224,128]{2,1,0:T(8,128)(2,1)} %bitcast.21), calls=%async_computation.1 | async-start | bytes 7340032 | tf_op jit(solution)/shard_map/all_to_all | solution.py:608
Sparse Core Ops, SparseCore 0:
  11.6 82.2 all-gather.1

commit v4 on v3

--- a/solution.py
+++ b/solution.py
@@ -448,8 +448,8 @@
 
 
 def back_heads_kernel(
-    x_in, dq, own, r8, r6, r4, r2, cosine, sine, gain_row, w_qkv, middle_grad,
-    g_out, project_out, gain_out,
+    core, x_in, dq, own, r8, r6, r4, r2, cosine, sine, gain_row, w_qkv, middle_grad, normed, edge,
+    g_out, keep, send, flat, tile, project_out, gain_out,
 ):
     total = own[...]
     for piece in (r8, r6, r4, r2):
@@ -465,6 +465,7 @@
     inverse = inverse_norm(x)
     gain_out[...] = jnp.sum(grad * x * inverse, axis=0, keepdims=True)
     g_out[...] = middle_grad[...] + norm_back(x, inverse, gain_row[:, 0:D], grad)
+    pack_first(core, normed, project_out, gain_out, edge, keep, send, flat, tile)
 
 
 def put_gain(flat, gain, start):
@@ -534,7 +535,7 @@
     edge[...] = flat[0:EDGE, :]
 
 
-def pack_first_kernel(core, normed, project, gain_one, edge, keep, send, flat, tile):
+def pack_first(core, normed, project, gain_one, edge, keep, send, flat, tile):
     skip = 216 * SPLIT
     flat[skip : skip + EDGE, :] = edge[...]
     put_gain(flat, gain_one, HALF_GAIN_ONE + 14)
@@ -594,7 +595,7 @@
     return pl.pallas_call(
         join_kernel,
         grid=(DEVICES // 2 // JOIN,),
-        out_shape=jax.ShapeDtypeStruct((DEVICES // 2 * CHUNK, 128), bf16),
+        out_shape=pltpu.HBM((DEVICES // 2 * CHUNK, 128), bf16),
         in_specs=[first, first, rest, rest],
         out_specs=pl.BlockSpec(block, lambda i: (i, 0)),
         compiler_params=pltpu.CompilerParams(vmem_limit_bytes=16 * 1024 * 1024),
@@ -602,12 +603,15 @@
     )(keep_first, got_first, keep_rest, got_rest)
 
 
-def to_owners(total, device):
-    total = total.reshape(DEVICES // 2, CHUNK, 128)
+def to_owners(total):
     groups = [list(range(0, DEVICES, 2)), list(range(1, DEVICES, 2))]
-    pieces = lax.all_to_all(
-        total, "fsdp", split_axis=0, concat_axis=0, tiled=True, axis_index_groups=groups
+    return lax.all_to_all(
+        total.reshape(DEVICES // 2, CHUNK, 128),
+        "fsdp", split_axis=0, concat_axis=0, tiled=True, axis_index_groups=groups,
     )
+
+
+def own_part(pieces, device):
     own = jnp.sum(pieces.astype(f32), axis=0)
     rows = jnp.concatenate([own[CHUNK - 1 :], own], axis=0)
     return lax.dynamic_slice_in_dim(rows.reshape(-1), 9 * device, SHARD, 0)
@@ -713,29 +717,25 @@
         own_kv, pieces = give_back(dkv_s, dkv_t, core)
         send, pieces = lax.optimization_barrier((send, pieces))
         keep_rest, got_rest = keep, swap(send)
-        g, project, grad_one = call(
+        if layer + 1 < layers:
+            own_kv, grads[layer + 1] = lax.optimization_barrier((own_kv, grads[layer + 1]))
+        low_shape = ((LOW_PLANES * CHUNK, 128), bf16)
+        g, keep, send = call(
             back_heads_kernel,
-            [((ROWS, D), f32), ((ROWS, PW), bf16), ((1, D), f32)],
-            [x, dq, own_kv, *pieces, cosine, sine, gain_one, w_qkv, middle_grad],
-            flops=150_000_000, nbytes=3_000_000,
-        )
-        if layer + 1 < layers:
-            project, grads[layer + 1] = lax.optimization_barrier((project, grads[layer + 1]))
-        low_shape = ((LOW_PLANES * CHUNK, 128), bf16)
-        keep, send = call(
-            pack_first_kernel,
-            [low_shape, low_shape],
-            [core_in, normed, project, grad_one, edge],
+            [((ROWS, D), f32), low_shape, low_shape],
+            [core_in, x, dq, own_kv, *pieces, cosine, sine, gain_one, w_qkv, middle_grad, normed,
+             edge],
             scratch=[
-                pltpu.VMEM((216 * SPLIT + EDGE + 8, 128), f32), pltpu.VMEM((8, D, 128), f32)
+                pltpu.VMEM((216 * SPLIT + EDGE + 8, 128), f32), pltpu.VMEM((8, D, 128), f32),
+                pltpu.VMEM((ROWS, PW), bf16), pltpu.VMEM((1, D), f32),
             ],
-            smem=1, flops=200_000_000, nbytes=8_000_000,
+            smem=1, flops=350_000_000, nbytes=10_000_000,
         )
         total = join(keep, swap(send), keep_rest, got_rest)
         if layer > 0:
             g, total = lax.optimization_barrier((g, total))
-        grads[layer] = to_owners(total, device)
-    return (layer_out, g, jnp.stack(grads))
+        grads[layer] = to_owners(total)
+    return (layer_out, g, jnp.stack([own_part(pieces, device) for pieces in grads]))
 
 
 def solution(mesh):

time: 377 us -> 371 us (0.984)
    unnamed x71 -> x67, local copies, waits for them, and re-layouts: 12.7 us -> 9.07 us
    pallas_call x12 -> x10, Pallas kernels: 85 us -> 81.5 us  [call(): pl.pallas_call(kernel, out_shape=[jax.ShapeDtypeStruct(s, d) for s, d in...]
  transfers between devices with their start and end apart: 32 -> 32, of which waited for: 12 -> 12; matrix products, arithmetic and copies ran while one was open for 5% -> 5% of each run, Pallas kernels for 16% -> 15%
where the time goes in v4:
time: 371 us; the launch traced here: 365 us
  Pallas kernels  118 us (32%)
  waiting for transfers between devices  106 us (29%)
  starting transfers between devices  95.4 us (26%)
  local copies, waits for them, and re-layouts  18.1 us (5%)
  between operations  15.3 us (4%)
  other arithmetic  11.8 us (3%)
    pallas_call x10, Pallas kernels, call(): pl.pallas_call(kernel, out_shape=[jax.ShapeDtypeStruct(s, d) for s, d in...  81.5 us
    ppermute x20, starting transfers between devices, hop(): return lax.ppermute(value, 'fsdp', pairs)  72.7 us
    all_to_all x2, waiting for transfers between devices, to_owners(): lax.all_to_all(total.reshape(DEVICES // 2, CHUNK, 128), 'fsdp', split_axi...  45.5 us
    all_gather x1, waiting for transfers between devices, body(): lax.all_gather(jnp.concatenate(sections), 'fsdp', axis=0, tiled=True)  40.6 us
    pallas_call x4, Pallas kernels, unpack_call(): pl.pallas_call(functools.partial(kernel, layer), out_shape=[jax.ShapeDtyp...  23.5 us
    all_to_all x2, starting transfers between devices, to_owners(): lax.all_to_all(total.reshape(DEVICES // 2, CHUNK, 128), 'fsdp', split_axi...  20.8 us
    pallas_call x2, Pallas kernels, join(): pl.pallas_call(join_kernel, grid=(DEVICES // 2 // JOIN,), out_shape=pltpu...  13.1 us
    ppermute x20, waiting for transfers between devices, hop(): return lax.ppermute(value, 'fsdp', pairs)  10.9 us
  transfers between devices with their start and end apart: 32, of which 12 were waited for; matrix products, arithmetic and copies ran while one was open for 5% of the time, Pallas kernels for 15%

profile of v4, /device:TPU:50, one launch (start us, length us, event | category | flops | bytes accessed | tf_op | source)
XLA Modules:
  0.0 364.6 jit_solution(6073717265387977483)
XLA Ops:
  7.2 1.6 slice_reduce_fusion.1
  10.8 3.8 %collective-permute-start.8 = (s32[128]{0:T(128)}, s32[128]{0:T(128)S(1)}, u32[]{:S(2)}, u32[]{:S(2)}) collective-permute-start(s32[128]{0:T(128)} %param.7), channel_id=1, source_target_pairs={{0,2},{1,3},{2,4},{3,5},{4,6},{5,7},{6,8},{7,9},{8,10},{9,11},{10,... | collective-permute-start | bytes 1544 | tf_op jit(solution)/shard_map/ppermute | solution.py:548
  14.6 3.0 collective-permute-start.7
  17.6 5.2 %collective-permute-start.6 = (s32[128]{0:T(128)}, s32[128]{0:T(128)S(1)}, u32[]{:S(2)}, u32[]{:S(2)}) collective-permute-start(s32[128]{0:T(128)} %param.7), channel_id=1, source_target_pairs={{0,6},{1,7},{2,8},{3,9},{4,10},{5,11},{6,12},{7,13},{8,14},{9,15},... | collective-permute-start | bytes 1544 | tf_op jit(solution)/shard_map/ppermute | solution.py:548
  22.8 3.1 collective-permute-start.5
  25.9 1.1 copy.32.x_in
  27.0 1.9 collective-permute-start.3
  30.4 6.0 %collective-permute-start.2 = (bf16[128,576]{1,0:T(8,128)(2,1)S(1)}, bf16[128,576]{1,0:T(8,128)(2,1)S(1)}, u32[]{:S(2)}, u32[]{:S(2)}) collective-permute-start(bf16[128,576]{1,0:T(8,128)(2,1)S(1)} %copy.32.x_in), channel_id=1, source_target_pairs={{0,4},{1,5},{2,6},{3,7},{4,8},{5,9},{6,10},{7,11},{8,12},{9,13},{1... | collective-permute-start | bytes 442376 | tf_op jit(solution)/shard_map/ppermute | solution.py:548
  36.4 1.9 collective-permute-start.1
  38.4 3.5 collective-permute-start
  43.3 0.7 copy.33.segment
  44.1 1.5 collective-permute-done
  46.2 1.1 copy-done.8
  47.7 2.1 multiply_sine_fusion
  49.8 1.0 pad_maximum_fusion
  52.4 0.9 constant_dynamic-update-slice_fusion.5.window
  53.3 40.6 %all-gather.2.cloned.1.call-done = bf16[7864320]{0:T(1024)(128)(2,1)} async-done(((bf16[61440]{0:T(1024)(128)(2,1)}), bf16[7864320]{0:T(1024)(128)(2,1)}) %all-gather.2.cloned.1.call-update) | async-done | bytes 15728656 | tf_op jit(solution)/shard_map/all_gather | solution.py:639
  93.9 3.3 shard_map.89
  97.2 3.0 shard_map.85
  100.3 8.6 %shard_map.87 = (bf16[576,576]{1,0:T(8,128)(2,1)}, bf16[576,3072]{1,0:T(8,128)(2,1)}, bf16[1536,576]{1,0:T(8,128)(2,1)}, f32[1,640]{1,0:T(1,128)}) custom-call(bf16[128,2,240,128]{3,2,1,0:T(8,128)(2,1)} %bitcast.22), custom_call_target="tpu_custom_call" | custom-call | flops 2000000000 | bytes 30000000 | tf_op jit(solution)/shard_map/pallas_call | solution.py:231
  108.9 4.6 %shard_map.86 = (bf16[128,576]{1,0:T(8,128)(2,1)}, bf16[640,384]{1,0:T(8,128)(2,1)}, bf16[512,384]{1,0:T(8,128)(2,1)}, bf16[128,576]{1,0:T(8,128)(2,1)}) custom-call(bf16[1152,576]{1,0:T(8,128)(2,1)} %constant_dynamic-update-slice_fusion.5.window, f32[1152,128]{1,0:T(8,128)} %copy-done.4, f32[1152,128]{1,0:T(8,128)} %copy-done.5, ...), custom_call_target="tpu_custom_call" | custom-call | flops 800000000 | bytes 6000000 | tf_op jit(solution)/shard_map/pallas_call | solution.py:70
  113.5 7.6 %shard_map.88 = (f32[128,576]{1,0:T(8,128)}, bf16[128,576]{1,0:T(8,128)(2,1)}, f32[384,3]{1,0:T(8,128)}, f32[128,576]{1,0:T(8,128)}, bf16[128,576]{1,0:T(8,128)(...) custom-call(s32[1]{0:T(128)} %bitcast.first, bf16[128,576]{1,0:T(8,128)(2,1)} %copy-done.6, ...), custom_call_target="tpu_custom_call" | custom-call | flops 2000000000 | bytes 12000000 | tf_op jit(solution)/shard_map/pallas_call | solution.py:70
  121.1 2.8 shard_map.90
  123.9 3.3 collective-permute-start.13
  127.2 5.3 %collective-permute-start.12 = (bf16[128,384]{1,0:T(8,128)(2,1)}, bf16[128,384]{1,0:T(8,128)(2,1)S(1)}, u32[]{:S(2)}, u32[]{:S(2)}) collective-permute-start(bf16[128,384]{1,0:T(8,128)(2,1)} %get-tuple-element.92), channel_id=1, source_target_pairs={{0,4},{1,5},{2,6},{3,7},{4,8},{5,9},{6,10},{7,11},{8,12},{9,13},{1... | collective-permute-start | bytes 294920 | tf_op jit(solution)/shard_map/ppermute | solution.py:548
  132.5 2.4 collective-permute-start.11
  135.0 4.5 %collective-permute-start.10 = (bf16[128,384]{1,0:T(8,128)(2,1)}, bf16[128,384]{1,0:T(8,128)(2,1)S(1)}, u32[]{:S(2)}, u32[]{:S(2)}) collective-permute-start(bf16[128,384]{1,0:T(8,128)(2,1)} %get-tuple-element.92), channel_id=1, source_target_pairs={{0,8},{1,9},{2,10},{3,11},{4,12},{5,13},{6,14},{7,15},{8,16},{9,17... | collective-permute-start | bytes 294920 | tf_op jit(solution)/shard_map/ppermute | solution.py:548
  139.5 8.6 %shard_map.91 = (bf16[576,576]{1,0:T(8,128)(2,1)}, bf16[576,3072]{1,0:T(8,128)(2,1)}, bf16[1536,576]{1,0:T(8,128)(2,1)}, f32[1,640]{1,0:T(1,128)}) custom-call(bf16[128,2,240,128]{3,2,1,0:T(8,128)(2,1)} %bitcast.23), custom_call_target="tpu_custom_call" | custom-call | flops 2000000000 | bytes 30000000 | tf_op jit(solution)/shard_map/pallas_call | solution.py:231
  148.9 0.8 copy.35.g_in
  150.3 0.7 copy-done.11
  151.0 7.7 %shard_map.92 = (f32[128,576]{1,0:T(8,128)}, bf16[128,576]{1,0:T(8,128)(2,1)}, f32[384,3]{1,0:T(8,128)}, f32[128,576]{1,0:T(8,128)}, bf16[128,576]{1,0:T(8,128)(...) custom-call(s32[1]{0:T(128)} %bitcast.first, f32[128,576]{1,0:T(8,128)} %get-tuple-element.88.x_in, ...), custom_call_target="tpu_custom_call" | custom-call | flops 2000000000 | bytes 12000000 | tf_op jit(solution)/shard_map/pallas_call | solution.py:70
  158.7 11.4 %shard_map.93 = (bf16[128,576]{1,0:T(8,128)(2,1)}, bf16[128,3072]{1,0:T(8,128)(2,1)}, bf16[128,576]{1,0:T(8,128)(2,1)}, f32[128,576]{1,0:T(8,128)}, bf16[128,576...) custom-call(s32[1]{0:T(128)} %bitcast.first, bf16[128,576]{1,0:T(8,128)(2,1)} %copy.35.g_in, ...), custom_call_target="tpu_custom_call" | custom-call | flops 3000000000 | bytes 15000000 | tf_op jit(solution)/shard_map/pallas_call | solution.py:70
  170.4 1.8 collective-permute-done.15
  172.4 3.3 collective-permute-start.19
  175.7 3.2 collective-permute-start.18
  178.9 2.0 collective-permute-start.17
  181.0 5.0 %collective-permute-start.16 = (bf16[128,384]{1,0:T(8,128)(2,1)S(1)}, bf16[128,384]{1,0:T(8,128)(2,1)S(1)}, u32[]{:S(2)}, u32[]{:S(2)}) collective-permute-start(bf16[128,384]{1,0:T(8,128)(2,1)S(1)} %get-tuple-element.174), channel_id=1, source_target_pairs={{8,0},{9,1},{10,2},{11,3},{12,4},{13,5},{14,6},{15,7},{16,8},{17,9... | collective-permute-start | bytes 294920 | tf_op jit(solution)/shard_map/ppermute | solution.py:548
  186.0 12.2 %shard_map.94 = (bf16[10752,128]{1,0:T(8,128)(2,1)}, bf16[10752,128]{1,0:T(8,128)(2,1)}, f32[2616,128]{1,0:T(8,128)}) custom-call(s32[1]{0:T(128)} %bitcast.4.core, bf16[128,576]{1,0:T(8,128)(2,1)} %get-tuple-element.105.mixed, bf16[128,576]{1,0:T(8,128)(2,1)} %get-tuple-element.106.attn, bf16[128,576]{1,0:T(8,128)(2,1)} %get-tuple-element.107.normed_two, ...), custom_call_target="tpu_custom_call" | custom-call | flops 1000000000 | bytes 25000000 | tf_op jit(solution)/shard_map/pallas_call | solution.py:70
  198.4 0.7 slice.74.own
  199.1 5.7 %shard_map.95 = (f32[128,576]{1,0:T(8,128)}, bf16[3584,128]{1,0:T(8,128)(2,1)}, bf16[3584,128]{1,0:T(8,128)(2,1)}) custom-call(s32[1]{0:T(128)} %bitcast.4.core, f32[128,576]{1,0:T(8,128)} %get-tuple-element.88.x_in, bf16[128,576]{1,0:T(8,128)(2,1)} %get-tuple-element.102.dq, f32[128,384]{1,0:T(8,128)} %slice.74.own, bf16[128,384]{1,0:T(8,128)(2,1)} %copy-done.23, ...), custom_call_target="tpu_custom_call" | custom-call | flops 350000000 | bytes 10000000 | tf_op jit(solution)/shard_map/pallas_call | solution.py:70
  205.3 2.3 collective-permute-done.20.got_first
  207.6 1.2 copy-done.3
  208.7 6.5 %shard_map.96 = bf16[14336,128]{1,0:T(8,128)(2,1)} custom-call(bf16[3584,128]{1,0:T(8,128)(2,1)S(1)} %copy-done.3, bf16[3584,128]{1,0:T(8,128)(2,1)S(1)} %collective-permute-done.20.got_first, bf16[10752,128]{1,0:T(8,128)(2,1)S(1)} %copy-done.1, bf16[10752,128]{1,0:T(8,128)(2,1)} %collective-permute-done.21.got_rest), custom_call_target="tpu_custom_call" | custom-call | bytes 11000000 | tf_op jit(solution)/shard_map/pallas_call | solution.py:595
  215.3 9.4 %all-to-all-start = ((bf16[64,224,128]{2,1,0:T(8,128)(2,1)}), bf16[64,224,128]{2,1,0:T(8,128)(2,1)}, u32[]{:S(2)}, u32[]{:S(2)}) async-start(bf16[64,224,128]{2,1,0:T(8,128)(2,1)} %bitcast.24), calls=%async_computation | async-start | bytes 7340032 | tf_op jit(solution)/shard_map/all_to_all | solution.py:608
  224.7 11.5 %shard_map.97 = (bf16[128,576]{1,0:T(8,128)(2,1)}, bf16[128,3072]{1,0:T(8,128)(2,1)}, bf16[128,576]{1,0:T(8,128)(2,1)}, f32[128,576]{1,0:T(8,128)}, bf16[128,576...) custom-call(s32[1]{0:T(128)} %bitcast.first, ...), custom_call_target="tpu_custom_call" | custom-call | flops 3000000000 | bytes 15000000 | tf_op jit(solution)/shard_map/pallas_call | solution.py:70
  236.3 1.9 collective-permute-done.22
  238.5 2.5 collective-permute-start.26
  241.0 4.3 %collective-permute-start.25 = (bf16[128,384]{1,0:T(8,128)(2,1)S(1)}, bf16[128,384]{1,0:T(8,128)(2,1)S(1)}, u32[]{:S(2)}, u32[]{:S(2)}) collective-permute-start(bf16[128,384]{1,0:T(8,128)(2,1)S(1)} %get-tuple-element.168), channel_id=1, source_target_pairs={{4,0},{5,1},{6,2},{7,3},{8,4},{9,5},{10,6},{11,7},{12,8},{13,9},{1... | collective-permute-start | bytes 294920 | tf_op jit(solution)/shard_map/ppermute | solution.py:548
  245.2 3.7 %collective-permute-start.24 = (bf16[128,384]{1,0:T(8,128)(2,1)S(1)}, bf16[128,384]{1,0:T(8,128)(2,1)S(1)}, u32[]{:S(2)}, u32[]{:S(2)}) collective-permute-start(bf16[128,384]{1,0:T(8,128)(2,1)S(1)} %get-tuple-element.169), channel_id=1, source_target_pairs={{6,0},{7,1},{8,2},{9,3},{10,4},{11,5},{12,6},{13,7},{14,8},{15,9},... | collective-permute-start | bytes 294920 | tf_op jit(solution)/shard_map/ppermute | solution.py:548
  248.9 4.8 %collective-permute-start.23 = (bf16[128,384]{1,0:T(8,128)(2,1)S(1)}, bf16[128,384]{1,0:T(8,128)(2,1)S(1)}, u32[]{:S(2)}, u32[]{:S(2)}) collective-permute-start(bf16[128,384]{1,0:T(8,128)(2,1)S(1)} %get-tuple-element.170), channel_id=1, source_target_pairs={{8,0},{9,1},{10,2},{11,3},{12,4},{13,5},{14,6},{15,7},{16,8},{17,9... | collective-permute-start | bytes 294920 | tf_op jit(solution)/shard_map/ppermute | solution.py:548
  253.7 12.4 %shard_map.98 = (bf16[10752,128]{1,0:T(8,128)(2,1)}, bf16[10752,128]{1,0:T(8,128)(2,1)}, f32[2616,128]{1,0:T(8,128)}) custom-call(s32[1]{0:T(128)} %bitcast.4.core, bf16[128,576]{1,0:T(8,128)(2,1)} %get-tuple-element.134.mixed, bf16[128,576]{1,0:T(8,128)(2,1)} %get-tuple-element.135.attn, bf16[128,576]{1,0:T(8,128)(2,1)} %get-tuple-element.136.normed_two, ...), custom_call_target="tpu_custom_call" | custom-call | flops 1000000000 | bytes 25000000 | tf_op jit(solution)/shard_map/pallas_call | solution.py:70
  266.5 6.0 %collective-permute-done.25.r4 = bf16[128,384]{1,0:T(8,128)(2,1)S(1)} collective-permute-done((bf16[128,384]{1,0:T(8,128)(2,1)S(1)}, bf16[128,384]{1,0:T(8,128)(2,1)S(1)}, u32[]{:S(2)}, u32[]{:S(2)}) %collective-permute-start.25) | collective-permute-done | bytes 98336 | tf_op jit(solution)/shard_map/ppermute | solution.py:548
  272.5 2.8 collective-permute-done.24.r6
  276.1 5.6 %shard_map.99 = (f32[128,576]{1,0:T(8,128)}, bf16[3584,128]{1,0:T(8,128)(2,1)}, bf16[3584,128]{1,0:T(8,128)(2,1)}) custom-call(s32[1]{0:T(128)} %bitcast.4.core, bf16[128,576]{1,0:T(8,128)(2,1)} %copy-done.6, bf16[128,576]{1,0:T(8,128)(2,1)} %get-tuple-element.129.dq, f32[128,384]{1,0:T(8,128)} %slice.79.own, bf16[128,384]{1,0:T(8,128)(2,1)} %copy-done.20, ...), custom_call_target="tpu_custom_call" | custom-call | flops 350000000 | bytes 10000000 | tf_op jit(solution)/shard_map/pallas_call | solution.py:70
  282.2 2.3 collective-permute-done.27.got_first
  284.5 1.2 copy-done.2
  285.7 6.5 %shard_map.100 = bf16[14336,128]{1,0:T(8,128)(2,1)} custom-call(bf16[3584,128]{1,0:T(8,128)(2,1)S(1)} %copy-done.2, bf16[3584,128]{1,0:T(8,128)(2,1)S(1)} %collective-permute-done.27.got_first, bf16[10752,128]{1,0:T(8,128)(2,1)S(1)} %copy-done, bf16[10752,128]{1,0:T(8,128)(2,1)} %collective-permute-done.28.got_rest), custom_call_target="tpu_custom_call" | custom-call | bytes 11000000 | tf_op jit(solution)/shard_map/pallas_call | solution.py:595
  292.3 11.3 %all-to-all-start.1 = ((bf16[64,224,128]{2,1,0:T(8,128)(2,1)}), bf16[64,224,128]{2,1,0:T(8,128)(2,1)}, u32[]{:S(2)}, u32[]{:S(2)}) async-start(bf16[64,224,128]{2,1,0:T(8,128)(2,1)} %bitcast.25), calls=%async_computation.1 | async-start | bytes 7340032 | tf_op jit(solution)/shard_map/all_to_all | solution.py:608
  303.6 0.8 copy.39
  304.4 2.6 convert_reduce_fusion
  307.2 0.9 copy.40
  308.1 45.5 %all-to-all-done.1 = bf16[64,224,128]{2,1,0:T(8,128)(2,1)} async-done(((bf16[64,224,128]{2,1,0:T(8,128)(2,1)}), bf16[64,224,128]{2,1,0:T(8,128)(2,1)}, u32[]{:S(2)}, u32[]{:S(2)}) %all-to-all-start.1) | async-done | bytes 3670048 | tf_op jit(solution)/shard_map/all_to_all | solution.py:608
  353.6 2.6 convert_reduce_fusion.1
  356.4 0.9 pad_maximum_fusion.2
  (133 shorter events, 12.1 us)
Async XLA Ops:
  7.2 36.1 %copy-start.24 = (s32[128]{0:T(128)S(1)}, s32[128]{0:T(128)}, u32[]{:S(2)}) copy-start(s32[128]{0:T(128)} %param.7) | copy-start | bytes 1540
  7.2 86.7 %all-gather.2.cloned.1.call-start = ((), (), s32[]{:S(2)}) async-start(), calls=%async_computation.2 | async-start | bytes 15851520 | tf_op jit(solution)/shard_map/all_gather | solution.py:639
  10.8 31.1 %collective-permute-start.8 = (s32[128]{0:T(128)}, s32[128]{0:T(128)S(1)}, u32[]{:S(2)}, u32[]{:S(2)}) collective-permute-start(s32[128]{0:T(128)} %param.7), channel_id=1, source_target_pairs={{0,2},{1,3},{2,4},{3,5},{4,6},{5,7},{6,8},{7,9},{8,10},{9,11},{10,... | collective-permute-start | bytes 1544 | tf_op jit(solution)/shard_map/ppermute | solution.py:548
  14.6 23.8 %collective-permute-start.7 = (s32[128]{0:T(128)}, s32[128]{0:T(128)S(1)}, u32[]{:S(2)}, u32[]{:S(2)}) collective-permute-start(s32[128]{0:T(128)} %param.7), channel_id=1, source_target_pairs={{0,4},{1,5},{2,6},{3,7},{4,8},{5,9},{6,10},{7,11},{8,12},{9,13},{1... | collective-permute-start | bytes 1544 | tf_op jit(solution)/shard_map/ppermute | solution.py:548
  17.6 18.8 %collective-permute-start.6 = (s32[128]{0:T(128)}, s32[128]{0:T(128)S(1)}, u32[]{:S(2)}, u32[]{:S(2)}) collective-permute-start(s32[128]{0:T(128)} %param.7), channel_id=1, source_target_pairs={{0,6},{1,7},{2,8},{3,9},{4,10},{5,11},{6,12},{7,13},{8,14},{9,15},... | collective-permute-start | bytes 1544 | tf_op jit(solution)/shard_map/ppermute | solution.py:548
  22.8 7.6 %collective-permute-start.5 = (s32[128]{0:T(128)}, s32[128]{0:T(128)S(1)}, u32[]{:S(2)}, u32[]{:S(2)}) collective-permute-start(s32[128]{0:T(128)} %param.7), channel_id=1, source_target_pairs={{0,8},{1,9},{2,10},{3,11},{4,12},{5,13},{6,14},{7,15},{8,16},{9,17... | collective-permute-start | bytes 1544 | tf_op jit(solution)/shard_map/ppermute | solution.py:548
  27.0 20.4 %copy-start.6 = (bf16[128,576]{1,0:T(8,128)(2,1)}, bf16[128,576]{1,0:T(8,128)(2,1)S(1)}, u32[]{:S(2)}) copy-start(bf16[128,576]{1,0:T(8,128)(2,1)S(1)} %copy.32.x_in) | copy-start | bytes 442372
  27.0 19.1 %collective-permute-start.3 = (bf16[128,576]{1,0:T(8,128)(2,1)S(1)}, bf16[128,576]{1,0:T(8,128)(2,1)S(1)}, u32[]{:S(2)}, u32[]{:S(2)}) collective-permute-start(bf16[128,576]{1,0:T(8,128)(2,1)S(1)} %copy.32.x_in), channel_id=1, source_target_pairs={{0,2},{1,3},{2,4},{3,5},{4,6},{5,7},{6,8},{7,9},{8,10},{9,11},{10,... | collective-permute-start | bytes 442376 | tf_op jit(solution)/shard_map/ppermute | solution.py:548
  30.4 15.6 %collective-permute-start.2 = (bf16[128,576]{1,0:T(8,128)(2,1)S(1)}, bf16[128,576]{1,0:T(8,128)(2,1)S(1)}, u32[]{:S(2)}, u32[]{:S(2)}) collective-permute-start(bf16[128,576]{1,0:T(8,128)(2,1)S(1)} %copy.32.x_in), channel_id=1, source_target_pairs={{0,4},{1,5},{2,6},{3,7},{4,8},{5,9},{6,10},{7,11},{8,12},{9,13},{1... | collective-permute-start | bytes 442376 | tf_op jit(solution)/shard_map/ppermute | solution.py:548
  36.4 9.5 %collective-permute-start.1 = (bf16[128,576]{1,0:T(8,128)(2,1)S(1)}, bf16[128,576]{1,0:T(8,128)(2,1)S(1)}, u32[]{:S(2)}, u32[]{:S(2)}) collective-permute-start(bf16[128,576]{1,0:T(8,128)(2,1)S(1)} %copy.32.x_in), channel_id=1, source_target_pairs={{0,6},{1,7},{2,8},{3,9},{4,10},{5,11},{6,12},{7,13},{8,14},{9,15},... | collective-permute-start | bytes 442376 | tf_op jit(solution)/shard_map/ppermute | solution.py:548
  38.4 7.2 %collective-permute-start = (bf16[128,576]{1,0:T(8,128)(2,1)S(1)}, bf16[128,576]{1,0:T(8,128)(2,1)S(1)}, u32[]{:S(2)}, u32[]{:S(2)}) collective-permute-start(bf16[128,576]{1,0:T(8,128)(2,1)S(1)} %copy.32.x_in), channel_id=1, source_target_pairs={{0,8},{1,9},{2,10},{3,11},{4,12},{5,13},{6,14},{7,15},{8,16},{9,17... | collective-permute-start | bytes 442376 | tf_op jit(solution)/shard_map/ppermute | solution.py:548
  42.7 1.4 collective-permute-start.9
  46.1 1.1 copy-start.8
  47.6 4.5 %collective-permute-start.4 = (bf16[512,576]{0,1:T(8,128)(2,1)S(1)}, bf16[512,576]{0,1:T(8,128)(2,1)S(1)}, u32[]{:S(2)}, u32[]{:S(2)}) collective-permute-start(bf16[512,576]{0,1:T(8,128)(2,1)S(1)} %copy.29), channel_id=1, source_target_pairs={{0,1},{1,0},{2,3},{3,2},{4,5},{5,4},{6,7},{7,6},{8,9},{9,8},{10,11... | collective-permute-start | bytes 1769480 | tf_op jit(solution)/shard_map/ppermute | solution.py:552
  50.8 46.4 %copy-start.4 = (f32[1152,128]{1,0:T(8,128)}, f32[1152,128]{1,0:T(8,128)S(1)}, u32[]{:S(2)}) copy-start(f32[1152,128]{1,0:T(8,128)S(1)} %get-tuple-element.197.cosine) | copy-start | bytes 1769476
  50.8 46.4 %copy-start.5 = (f32[1152,128]{1,0:T(8,128)}, f32[1152,128]{1,0:T(8,128)S(1)}, u32[]{:S(2)}) copy-start(f32[1152,128]{1,0:T(8,128)S(1)} %get-tuple-element.198.sine) | copy-start | bytes 1769476
  123.9 24.3 %copy-start.15 = (bf16[128,384]{1,0:T(8,128)(2,1)S(1)}, bf16[128,384]{1,0:T(8,128)(2,1)}, u32[]{:S(2)}) copy-start(bf16[128,384]{1,0:T(8,128)(2,1)} %get-tuple-element.92) | copy-start | bytes 294916
  123.9 24.2 %collective-permute-start.13 = (bf16[128,384]{1,0:T(8,128)(2,1)}, bf16[128,384]{1,0:T(8,128)(2,1)S(1)}, u32[]{:S(2)}, u32[]{:S(2)}) collective-permute-start(bf16[128,384]{1,0:T(8,128)(2,1)} %get-tuple-element.92), channel_id=1, source_target_pairs={{0,2},{1,3},{2,4},{3,5},{4,6},{5,7},{6,8},{7,9},{8,10},{9,11},{10,... | collective-permute-start | bytes 294920 | tf_op jit(solution)/shard_map/ppermute | solution.py:548
  127.2 20.9 %collective-permute-start.12 = (bf16[128,384]{1,0:T(8,128)(2,1)}, bf16[128,384]{1,0:T(8,128)(2,1)S(1)}, u32[]{:S(2)}, u32[]{:S(2)}) collective-permute-start(bf16[128,384]{1,0:T(8,128)(2,1)} %get-tuple-element.92), channel_id=1, source_target_pairs={{0,4},{1,5},{2,6},{3,7},{4,8},{5,9},{6,10},{7,11},{8,12},{9,13},{1... | collective-permute-start | bytes 294920 | tf_op jit(solution)/shard_map/ppermute | solution.py:548
  132.5 15.5 %collective-permute-start.11 = (bf16[128,384]{1,0:T(8,128)(2,1)}, bf16[128,384]{1,0:T(8,128)(2,1)S(1)}, u32[]{:S(2)}, u32[]{:S(2)}) collective-permute-start(bf16[128,384]{1,0:T(8,128)(2,1)} %get-tuple-element.92), channel_id=1, source_target_pairs={{0,6},{1,7},{2,8},{3,9},{4,10},{5,11},{6,12},{7,13},{8,14},{9,15},... | collective-permute-start | bytes 294920 | tf_op jit(solution)/shard_map/ppermute | solution.py:548
  135.0 13.1 %collective-permute-start.10 = (bf16[128,384]{1,0:T(8,128)(2,1)}, bf16[128,384]{1,0:T(8,128)(2,1)S(1)}, u32[]{:S(2)}, u32[]{:S(2)}) collective-permute-start(bf16[128,384]{1,0:T(8,128)(2,1)} %get-tuple-element.92), channel_id=1, source_target_pairs={{0,8},{1,9},{2,10},{3,11},{4,12},{5,13},{6,14},{7,15},{8,16},{9,17... | collective-permute-start | bytes 294920 | tf_op jit(solution)/shard_map/ppermute | solution.py:548
  148.0 0.9 copy-start.14
  148.2 2.0 copy-start.7
  148.3 2.0 collective-permute-start.14
  150.3 0.7 copy-start.11
  170.1 2.1 copy-start.10
  170.2 2.0 collective-permute-start.15
  172.4 25.8 %collective-permute-start.19 = (bf16[128,384]{1,0:T(8,128)(2,1)S(1)}, bf16[128,384]{1,0:T(8,128)(2,1)S(1)}, u32[]{:S(2)}, u32[]{:S(2)}) collective-permute-start(bf16[128,384]{1,0:T(8,128)(2,1)S(1)} %get-tuple-element.171), channel_id=1, source_target_pairs={{2,0},{3,1},{4,2},{5,3},{6,4},{7,5},{8,6},{9,7},{10,8},{11,9},{12,... | collective-permute-start | bytes 294920 | tf_op jit(solution)/shard_map/ppermute | solution.py:548
  175.7 22.5 %collective-permute-start.18 = (bf16[128,384]{1,0:T(8,128)(2,1)S(1)}, bf16[128,384]{1,0:T(8,128)(2,1)S(1)}, u32[]{:S(2)}, u32[]{:S(2)}) collective-permute-start(bf16[128,384]{1,0:T(8,128)(2,1)S(1)} %get-tuple-element.172), channel_id=1, source_target_pairs={{4,0},{5,1},{6,2},{7,3},{8,4},{9,5},{10,6},{11,7},{12,8},{13,9},{1... | collective-permute-start | bytes 294920 | tf_op jit(solution)/shard_map/ppermute | solution.py:548
  178.9 19.3 %collective-permute-start.17 = (bf16[128,384]{1,0:T(8,128)(2,1)S(1)}, bf16[128,384]{1,0:T(8,128)(2,1)S(1)}, u32[]{:S(2)}, u32[]{:S(2)}) collective-permute-start(bf16[128,384]{1,0:T(8,128)(2,1)S(1)} %get-tuple-element.173), channel_id=1, source_target_pairs={{6,0},{7,1},{8,2},{9,3},{10,4},{11,5},{12,6},{13,7},{14,8},{15,9},... | collective-permute-start | bytes 294920 | tf_op jit(solution)/shard_map/ppermute | solution.py:548
  181.0 17.3 %collective-permute-start.16 = (bf16[128,384]{1,0:T(8,128)(2,1)S(1)}, bf16[128,384]{1,0:T(8,128)(2,1)S(1)}, u32[]{:S(2)}, u32[]{:S(2)}) collective-permute-start(bf16[128,384]{1,0:T(8,128)(2,1)S(1)} %get-tuple-element.174), channel_id=1, source_target_pairs={{8,0},{9,1},{10,2},{11,3},{12,4},{13,5},{14,6},{15,7},{16,8},{17,9... | collective-permute-start | bytes 294920 | tf_op jit(solution)/shard_map/ppermute | solution.py:548
  198.2 0.8 copy-start.19
  198.2 0.8 copy-start.21
  198.2 0.8 copy-start.22
  198.3 0.8 copy-start.23
  198.3 9.3 %collective-permute-start.21 = (bf16[10752,128]{1,0:T(8,128)(2,1)}, bf16[10752,128]{1,0:T(8,128)(2,1)}, u32[]{:S(2)}, u32[]{:S(2)}) collective-permute-start(bf16[10752,128]{1,0:T(8,128)(2,1)} %get-tuple-element.124), channel_id=1, source_target_pairs={{0,1},{1,0},{2,3},{3,2},{4,5},{5,4},{6,7},{7,6},{8,9},{9,8},{10,11... | collective-permute-start | bytes 8257544 | tf_op jit(solution)/shard_map/ppermute | solution.py:552
  199.1 8.5 %copy-start.1 = (bf16[10752,128]{1,0:T(8,128)(2,1)S(1)}, bf16[10752,128]{1,0:T(8,128)(2,1)}, u32[]{:S(2)}) copy-start(bf16[10752,128]{1,0:T(8,128)(2,1)} %get-tuple-element.123.keep_rest) | copy-start | bytes 8257540
  204.8 2.8 collective-permute-start.20
  207.6 1.2 copy-start.3
  215.3 60.7 %all-to-all-start = ((bf16[64,224,128]{2,1,0:T(8,128)(2,1)}), bf16[64,224,128]{2,1,0:T(8,128)(2,1)}, u32[]{:S(2)}, u32[]{:S(2)}) async-start(bf16[64,224,128]{2,1,0:T(8,128)(2,1)} %bitcast.24), calls=%async_computation | async-start | bytes 7340032 | tf_op jit(solution)/shard_map/all_to_all | solution.py:608
  236.2 2.1 copy-start.9
  236.2 2.0 collective-permute-start.22
  238.5 28.0 %collective-permute-start.26 = (bf16[128,384]{1,0:T(8,128)(2,1)S(1)}, bf16[128,384]{1,0:T(8,128)(2,1)S(1)}, u32[]{:S(2)}, u32[]{:S(2)}) collective-permute-start(bf16[128,384]{1,0:T(8,128)(2,1)S(1)} %get-tuple-element.167), channel_id=1, source_target_pairs={{2,0},{3,1},{4,2},{5,3},{6,4},{7,5},{8,6},{9,7},{10,8},{11,9},{12,... | collective-permute-start | bytes 294920 | tf_op jit(solution)/shard_map/ppermute | solution.py:548
  241.0 31.5 %collective-permute-start.25 = (bf16[128,384]{1,0:T(8,128)(2,1)S(1)}, bf16[128,384]{1,0:T(8,128)(2,1)S(1)}, u32[]{:S(2)}, u32[]{:S(2)}) collective-permute-start(bf16[128,384]{1,0:T(8,128)(2,1)S(1)} %get-tuple-element.168), channel_id=1, source_target_pairs={{4,0},{5,1},{6,2},{7,3},{8,4},{9,5},{10,6},{11,7},{12,8},{13,9},{1... | collective-permute-start | bytes 294920 | tf_op jit(solution)/shard_map/ppermute | solution.py:548
  245.2 30.0 %collective-permute-start.24 = (bf16[128,384]{1,0:T(8,128)(2,1)S(1)}, bf16[128,384]{1,0:T(8,128)(2,1)S(1)}, u32[]{:S(2)}, u32[]{:S(2)}) collective-permute-start(bf16[128,384]{1,0:T(8,128)(2,1)S(1)} %get-tuple-element.169), channel_id=1, source_target_pairs={{6,0},{7,1},{8,2},{9,3},{10,4},{11,5},{12,6},{13,7},{14,8},{15,9},... | collective-permute-start | bytes 294920 | tf_op jit(solution)/shard_map/ppermute | solution.py:548
  248.9 26.3 %collective-permute-start.23 = (bf16[128,384]{1,0:T(8,128)(2,1)S(1)}, bf16[128,384]{1,0:T(8,128)(2,1)S(1)}, u32[]{:S(2)}, u32[]{:S(2)}) collective-permute-start(bf16[128,384]{1,0:T(8,128)(2,1)S(1)} %get-tuple-element.170), channel_id=1, source_target_pairs={{8,0},{9,1},{10,2},{11,3},{12,4},{13,5},{14,6},{15,7},{16,8},{17,9... | collective-permute-start | bytes 294920 | tf_op jit(solution)/shard_map/ppermute | solution.py:548
  266.5 9.6 %copy-start.16 = (bf16[128,384]{1,0:T(8,128)(2,1)}, bf16[128,384]{1,0:T(8,128)(2,1)S(1)}, u32[]{:S(2)}) copy-start(bf16[128,384]{1,0:T(8,128)(2,1)S(1)} %collective-permute-done.26.r2) | copy-start | bytes 294916
  272.5 3.6 copy-start.17
  275.2 0.8 copy-start.18
  275.2 0.8 copy-start.20
  275.2 7.0 %collective-permute-start.28 = (bf16[10752,128]{1,0:T(8,128)(2,1)}, bf16[10752,128]{1,0:T(8,128)(2,1)}, u32[]{:S(2)}, u32[]{:S(2)}) collective-permute-start(bf16[10752,128]{1,0:T(8,128)(2,1)} %get-tuple-element.153), channel_id=1, source_target_pairs={{0,1},{1,0},{2,3},{3,2},{4,5},{5,4},{6,7},{7,6},{8,9},{9,8},{10,11... | collective-permute-start | bytes 8257544 | tf_op jit(solution)/shard_map/ppermute | solution.py:552
  276.1 8.5 %copy-start = (bf16[10752,128]{1,0:T(8,128)(2,1)S(1)}, bf16[10752,128]{1,0:T(8,128)(2,1)}, u32[]{:S(2)}) copy-start(bf16[10752,128]{1,0:T(8,128)(2,1)} %get-tuple-element.152.keep_rest) | copy-start | bytes 8257540
  281.7 2.8 collective-permute-start.27
  284.5 1.2 copy-start.2
  292.3 11.3 %copy-start.13 = (f32[128,576]{1,0:T(8,128)S(1)}, f32[128,576]{1,0:T(8,128)}, u32[]{:S(2)}) copy-start(f32[128,576]{1,0:T(8,128)} %get-tuple-element.98) | copy-start | bytes 884740
  292.3 61.3 %all-to-all-start.1 = ((bf16[64,224,128]{2,1,0:T(8,128)(2,1)}), bf16[64,224,128]{2,1,0:T(8,128)(2,1)}, u32[]{:S(2)}, u32[]{:S(2)}) async-start(bf16[64,224,128]{2,1,0:T(8,128)(2,1)} %bitcast.25), calls=%async_computation.1 | async-start | bytes 7340032 | tf_op jit(solution)/shard_map/all_to_all | solution.py:608
  304.4 2.8 copy-start.12
Sparse Core Ops, SparseCore 0:
  11.6 82.2 all-gather.1

commit v5 on v4

--- a/solution.py
+++ b/solution.py
@@ -330,35 +330,34 @@
     )
 
 
-def attend_kernel(
-    first, x_in, q_in, kv_s, kv_t, segment, key_row, gain_row, w_out_at, w_in_at, w_down_at,
-    x_out, mixed_out, lse_out, middle_out, normed_out, gate_up_out, hidden_out,
-    w_out, w_in, w_down, sems,
-):
-    copies = fetch((w_out_at, w_in_at, w_down_at), (w_out, w_in, w_down), sems)
-    for copy in copies:
-        copy.start()
-    allowed = allowed_of(segment[...], key_row[...], first[0])
-    bias = jnp.where(allowed, 0.0, -1e30).astype(f32)
-    bias = jnp.concatenate([bias] * GROUP, axis=0)
-    q = q_in[...]
-    pieces = []
+def bias_of(first, segment, key_row):
+    bias = jnp.where(allowed_of(segment[...], key_row[...], first[0]), 0.0, -1e30).astype(f32)
+    return jnp.concatenate([bias] * GROUP, axis=0)
+
+
+def attend(q, kv_s, kv_t, bias, lse_out=None):
+    pieces, held = [], []
     for group in range(KVH):
         keys = window_rows(kv_s, kv_t, group * HD)
         values = window_rows(kv_s, kv_t, KW + group * HD)
-        scores = mm_t(group_rows(q, group), keys) * FACTOR + bias
+        scores = mm_t(group_rows(q, group), keys) + bias
         peak = jnp.max(scores, axis=-1, keepdims=True)
         powers = jnp.exp(scores - peak)
         total = jnp.sum(powers, axis=-1, keepdims=True)
-        lse_out[:, group : group + 1] = peak + jnp.log(total)
-        weights = (powers * (1.0 / total)).astype(bf16)
-        mixed = mm(weights, values)
+        if lse_out is not None:
+            lse_out[:, group : group + 1] = peak + jnp.log(total)
+        held.append(powers * (1.0 / total))
+        mixed = mm(held[-1].astype(bf16), values)
         for n in range(GROUP):
             pieces.append(mixed[n * ROWS : (n + 1) * ROWS, :])
-    mixed = jnp.concatenate(pieces, axis=1).astype(bf16)
-    mixed_out[...] = mixed
+    return jnp.concatenate(pieces, axis=1).astype(bf16), held
+
+
+def feed_forward(
+    x, mixed, gain_row, w_out, w_in, w_down, copies, middle_out, normed_out, gate_up_out, hidden_out
+):
     copies[0].wait()
-    middle = x_in[...].astype(f32) + mm(mixed, w_out[...])
+    middle = x + mm(mixed, w_out[...])
     middle_out[...] = middle
     normed = (middle * inverse_norm(middle) * gain_row[:, 0:D]).astype(bf16)
     normed_out[...] = normed
@@ -369,7 +368,24 @@
     hidden = (gate * jax.nn.sigmoid(gate) * gate_up[:, FF:]).astype(bf16)
     hidden_out[...] = hidden
     copies[2].wait()
-    x_out[...] = middle + mm(hidden, w_down[...])
+    return middle + mm(hidden, w_down[...])
+
+
+def attend_kernel(
+    first, x_in, q_in, kv_s, kv_t, segment, key_row, gain_row, w_out_at, w_in_at, w_down_at,
+    x_out, mixed_out, lse_out, middle_out, normed_out, gate_up_out, hidden_out,
+    w_out, w_in, w_down, sems,
+):
+    copies = fetch((w_out_at, w_in_at, w_down_at), (w_out, w_in, w_down), sems)
+    for copy in copies:
+        copy.start()
+    q = q_in[...] * FACTOR
+    mixed, _ = attend(q, kv_s, kv_t, bias_of(first, segment, key_row), lse_out)
+    mixed_out[...] = mixed
+    x_out[...] = feed_forward(
+        x_in[...].astype(f32), mixed, gain_row, w_out, w_in, w_down, copies,
+        middle_out, normed_out, gate_up_out, hidden_out,
+    )
 
 
 def norm_back(values, inverse, gain, grad):
@@ -379,33 +395,15 @@
     )
 
 
-def back_kernel(
-    first, g_in, q_in, kv_s, kv_t, segment, key_row, cosine, sine, gain_row, lse, middle_in,
-    gate_up_at, w_out_at, w_in_at, w_down_at,
-    branch_out, grad_gu_out, attn_out, middle_grad_out, dq_out, dkv_s, dkv_t, gain_out,
-    w_out, w_in, w_down, sems, gate_up, gate_sem,
+def feed_back(
+    g, middle_in, gate_up, gain_row, w_out, w_in, w_down, waits,
+    branch_out, grad_gu_out, attn_out, middle_grad_out, gain_out,
 ):
-    copies = fetch((w_out_at, w_in_at, w_down_at), (w_out, w_in, w_down), sems)
-    gate_copy = pltpu.make_async_copy(gate_up_at, gate_up, gate_sem)
-    copies[2].start()
-    gate_copy.start()
-    copies[1].start()
-    copies[0].start()
-    allowed = allowed_of(segment[...], key_row[...], first[0])
-    bias = jnp.where(allowed, 0.0, -1e30).astype(f32)
-    bias = jnp.concatenate([bias] * GROUP, axis=0)
-    q = q_in[...]
-    held = []
-    for group in range(KVH):
-        keys = window_rows(kv_s, kv_t, group * HD)
-        scores = mm_t(group_rows(q, group), keys) * FACTOR + bias
-        held.append(jnp.exp(scores - lse[:, group : group + 1]))
-    g = g_in[...].astype(f32)
     branch = g.astype(bf16)
     branch_out[...] = branch
-    copies[2].wait()
+    for wait in waits[0]:
+        wait.wait()
     grad_hidden = mm_t(branch, w_down[...])
-    gate_copy.wait()
     gate = gate_up[:, 0:FF]
     up = gate_up[:, FF:]
     sigma = jax.nn.sigmoid(gate)
@@ -413,7 +411,8 @@
         grad_hidden * up * sigma * (1.0 + gate * (1.0 - sigma))
     ).astype(bf16)
     grad_gu_out[:, FF:] = (grad_hidden * gate * sigma).astype(bf16)
-    copies[1].wait()
+    for wait in waits[1]:
+        wait.wait()
     grad_two = mm_t(grad_gu_out[...], w_in[...])
     middle = middle_in[...]
     inverse = inverse_norm(middle)
@@ -422,9 +421,12 @@
     middle_grad_out[...] = grad_middle
     attn = grad_middle.astype(bf16)
     attn_out[...] = attn
-    copies[0].wait()
-    grad_mixed = mm_t(attn, w_out[...]).astype(bf16)
-
+    for wait in waits[2]:
+        wait.wait()
+    return mm_t(attn, w_out[...]).astype(bf16)
+
+
+def attend_back(q, kv_s, kv_t, held, grad_mixed, cosine, sine, dq_out, dkv_s, dkv_t):
     dq, dk, dv = [], [], []
     for group in range(KVH):
         keys = window_rows(kv_s, kv_t, group * HD)
@@ -438,13 +440,64 @@
         part = mm(grad_scores, keys) * FACTOR
         for n in range(GROUP):
             dq.append(part[n * ROWS : (n + 1) * ROWS, :])
-        dk.append(mm(query.T, grad_scores) * FACTOR)
+        dk.append(mm(query.T, grad_scores))
         dv.append(mm(grad.T, probs.astype(bf16)))
     dkv = jnp.concatenate(dk + dv, axis=0).T
     dkv_s[...] = dkv[0:WIN_S, :]
     dkv_t[...] = dkv[WIN_S:, :].astype(bf16)
     wide = jnp.concatenate(dq + [jnp.zeros((ROWS, HD), f32)], axis=1)
     dq_out[...] = turn(wide, cosine[...], -sine[...])[:, 0:QW].astype(bf16)
+
+
+def back_kernel(
+    first, g_in, q_in, kv_s, kv_t, segment, key_row, cosine, sine, gain_row, lse, middle_in,
+    gate_up_at, w_out_at, w_in_at, w_down_at,
+    branch_out, grad_gu_out, attn_out, middle_grad_out, dq_out, dkv_s, dkv_t, gain_out,
+    w_out, w_in, w_down, sems, gate_up, gate_sem,
+):
+    copies = fetch((w_out_at, w_in_at, w_down_at), (w_out, w_in, w_down), sems)
+    gate_copy = pltpu.make_async_copy(gate_up_at, gate_up, gate_sem)
+    copies[2].start()
+    gate_copy.start()
+    copies[1].start()
+    copies[0].start()
+    bias = bias_of(first, segment, key_row)
+    q = q_in[...] * FACTOR
+    held = []
+    for group in range(KVH):
+        keys = window_rows(kv_s, kv_t, group * HD)
+        scores = mm_t(group_rows(q, group), keys) + bias
+        held.append(jnp.exp(scores - lse[:, group : group + 1]))
+    grad_mixed = feed_back(
+        g_in[...].astype(f32), middle_in, gate_up, gain_row, w_out, w_in, w_down,
+        ((copies[2], gate_copy), (copies[1],), (copies[0],)),
+        branch_out, grad_gu_out, attn_out, middle_grad_out, gain_out,
+    )
+    attend_back(q, kv_s, kv_t, held, grad_mixed, cosine, sine, dq_out, dkv_s, dkv_t)
+
+
+def last_kernel(
+    first, x_in, g_in, q_in, kv_s, kv_t, segment, key_row, cosine, sine, gain_row,
+    w_out_at, w_in_at, w_down_at,
+    x_out, mixed_out, normed_out, hidden_out,
+    branch_out, grad_gu_out, attn_out, middle_grad_out, dq_out, dkv_s, dkv_t, gain_out,
+    w_out, w_in, w_down, sems, gate_up, middle,
+):
+    copies = fetch((w_out_at, w_in_at, w_down_at), (w_out, w_in, w_down), sems)
+    for copy in copies:
+        copy.start()
+    q = q_in[...] * FACTOR
+    mixed, held = attend(q, kv_s, kv_t, bias_of(first, segment, key_row))
+    mixed_out[...] = mixed
+    x_out[...] = feed_forward(
+        x_in[...].astype(f32), mixed, gain_row, w_out, w_in, w_down, copies,
+        middle, normed_out, gate_up, hidden_out,
+    ).astype(bf16)
+    grad_mixed = feed_back(
+        g_in[...].astype(f32), middle, gate_up, gain_row, w_out, w_in, w_down, ((), (), ()),
+        branch_out, grad_gu_out, attn_out, middle_grad_out, gain_out,
+    )
+    attend_back(q, kv_s, kv_t, held, grad_mixed, cosine, sine, dq_out, dkv_s, dkv_t)
 
 
 def back_heads_kernel(
@@ -580,11 +633,11 @@
 
     @pl.when(pl.program_id(0) < low)
     def _():
-        out[...] = (keep_first[...].astype(f32) + got_first[...].astype(f32)).astype(bf16)
+        out[...] = keep_first[...] + got_first[...]
 
     @pl.when(pl.program_id(0) >= low)
     def _():
-        out[...] = (keep_rest[...].astype(f32) + got_rest[...].astype(f32)).astype(bf16)
+        out[...] = keep_rest[...] + got_rest[...]
 
 
 def join(keep_first, got_first, keep_rest, got_rest):
@@ -677,6 +730,21 @@
                 flops=150_000_000, nbytes=3_000_000,
             )
             kv_s, kv_t = window_of(kv, core, (w_out,))
+        if layer == layers - 1:
+            (layer_out, mixed, normed_two, hidden, *last_back) = call(
+                last_kernel,
+                [((ROWS, D), bf16), ((ROWS, QW), bf16), ((ROWS, D), bf16), ((ROWS, FF), bf16)]
+                + [((ROWS, D), bf16), ((ROWS, 2 * FF), bf16), ((ROWS, D), bf16), ((ROWS, D), f32),
+                 ((ROWS, QW), bf16), ((WIN_S, 2 * KW), f32), ((WIN_T, 2 * KW), bf16), ((1, D), f32)],
+                [first, x, cotangent, q, kv_s, kv_t, segment, key_row, cosine, sine, gain_two,
+                 w_out, w_in, w_down],
+                scratch=WEIGHT_SCRATCH
+                + (pltpu.VMEM((ROWS, 2 * FF), f32), pltpu.VMEM((ROWS, D), f32)),
+                smem=1, apart=3, flops=5_000_000_000, nbytes=20_000_000,
+            )
+            held.append((x, q, kv_s, kv_t, normed, mixed, None, None, normed_two, None, hidden,
+                         w_qkv, w_out, w_in, w_down, gain_one, gain_two))
+            break
         x_next, mixed, lse, middle, normed_two, gate_up, hidden = call(
             attend_kernel,
             [((ROWS, D), f32), ((ROWS, QW), bf16), ((GROUP * ROWS, KVH), f32), ((ROWS, D), f32),
@@ -687,23 +755,25 @@
         held.append((x, q, kv_s, kv_t, normed, mixed, lse, middle, normed_two, gate_up, hidden,
                      w_qkv, w_out, w_in, w_down, gain_one, gain_two))
         x = x_next
-    layer_out = x.astype(bf16)
 
     g = cotangent
     grads = [None] * layers
     for layer in reversed(range(layers)):
         (x, q, kv_s, kv_t, normed, mixed, lse, middle, normed_two, gate_up, hidden,
          w_qkv, w_out, w_in, w_down, gain_one, gain_two) = held[layer]
-        branch, grad_gu, attn, middle_grad, dq, dkv_s, dkv_t, grad_two = call(
-            back_kernel,
-            [((ROWS, D), bf16), ((ROWS, 2 * FF), bf16), ((ROWS, D), bf16), ((ROWS, D), f32),
-             ((ROWS, QW), bf16), ((WIN_S, 2 * KW), f32), ((WIN_T, 2 * KW), bf16), ((1, D), f32)],
-            [first, g, q, kv_s, kv_t, segment, key_row, cosine, sine, gain_two, lse, middle,
-             gate_up, w_out, w_in, w_down],
-            scratch=WEIGHT_SCRATCH
-            + (pltpu.VMEM((ROWS, 2 * FF), f32), pltpu.SemaphoreType.DMA),
-            smem=1, apart=4, flops=3_000_000_000, nbytes=15_000_000,
-        )
+        if layer == layers - 1:
+            branch, grad_gu, attn, middle_grad, dq, dkv_s, dkv_t, grad_two = last_back
+        else:
+            branch, grad_gu, attn, middle_grad, dq, dkv_s, dkv_t, grad_two = call(
+                back_kernel,
+                [((ROWS, D), bf16), ((ROWS, 2 * FF), bf16), ((ROWS, D), bf16), ((ROWS, D), f32),
+                 ((ROWS, QW), bf16), ((WIN_S, 2 * KW), f32), ((WIN_T, 2 * KW), bf16), ((1, D), f32)],
+                [first, g, q, kv_s, kv_t, segment, key_row, cosine, sine, gain_two, lse, middle,
+                 gate_up, w_out, w_in, w_down],
+                scratch=WEIGHT_SCRATCH
+                + (pltpu.VMEM((ROWS, 2 * FF), f32), pltpu.SemaphoreType.DMA),
+                smem=1, apart=4, flops=3_000_000_000, nbytes=15_000_000,
+            )
         rest_shape = (((DEVICES // 2 - LOW_PLANES) * CHUNK, 128), bf16)
         keep, send, edge = call(
             pack_rest_kernel,

time: 371 us -> 366 us (0.987)
  Pallas kernels: 118 us -> 113 us
    pallas_call x10 -> x9, Pallas kernels: 81.5 us -> 76.7 us  [call(): pl.pallas_call(kernel, out_shape=[jax.ShapeDtypeStruct(s, d) for s, d in...]
  transfers between devices with their start and end apart: 32 -> 32, of which waited for: 12 -> 11; matrix products, arithmetic and copies ran while one was open for 5% -> 5% of each run, Pallas kernels for 15% -> 16%
where the time goes in v5:
time: 366 us; the launch traced here: 359 us
  Pallas kernels  113 us (31%)
  waiting for transfers between devices  106 us (29%)
  starting transfers between devices  95.4 us (26%)
  local copies, waits for them, and re-layouts  18.1 us (5%)
  between operations  15.1 us (4%)
  other arithmetic  11.8 us (3%)
    pallas_call x9, Pallas kernels, call(): pl.pallas_call(kernel, out_shape=[jax.ShapeDtypeStruct(s, d) for s, d in...  76.7 us
    ppermute x20, starting transfers between devices, hop(): return lax.ppermute(value, 'fsdp', pairs)  72.3 us
    all_to_all x2, waiting for transfers between devices, to_owners(): lax.all_to_all(total.reshape(DEVICES // 2, CHUNK, 128), 'fsdp', split_axi...  45.5 us
    all_gather x1, waiting for transfers between devices, body(): lax.all_gather(jnp.concatenate(sections), 'fsdp', axis=0, tiled=True)  40.6 us
    pallas_call x4, Pallas kernels, unpack_call(): pl.pallas_call(functools.partial(kernel, layer), out_shape=[jax.ShapeDtyp...  23.2 us
    all_to_all x2, starting transfers between devices, to_owners(): lax.all_to_all(total.reshape(DEVICES // 2, CHUNK, 128), 'fsdp', split_axi...  20.7 us
    pallas_call x2, Pallas kernels, join(): pl.pallas_call(join_kernel, grid=(DEVICES // 2 // JOIN,), out_shape=pltpu...  13.2 us
    ppermute x20, waiting for transfers between devices, hop(): return lax.ppermute(value, 'fsdp', pairs)  10.7 us
  transfers between devices with their start and end apart: 32, of which 11 were waited for; matrix products, arithmetic and copies ran while one was open for 5% of the time, Pallas kernels for 16%

profile of v5, /device:TPU:50, one launch (start us, length us, event | category | flops | bytes accessed | tf_op | source)
XLA Modules:
  0.0 359.1 jit_solution(3994290882919289815)
XLA Ops:
  7.2 1.6 slice_reduce_fusion.1
  10.8 3.8 %collective-permute-start.8 = (s32[128]{0:T(128)}, s32[128]{0:T(128)S(1)}, u32[]{:S(2)}, u32[]{:S(2)}) collective-permute-start(s32[128]{0:T(128)} %param.7), channel_id=1, source_target_pairs={{0,2},{1,3},{2,4},{3,5},{4,6},{5,7},{6,8},{7,9},{8,10},{9,11},{10,... | collective-permute-start | bytes 1544 | tf_op jit(solution)/shard_map/ppermute | solution.py:601
  14.6 3.0 collective-permute-start.7
  17.6 5.2 %collective-permute-start.6 = (s32[128]{0:T(128)}, s32[128]{0:T(128)S(1)}, u32[]{:S(2)}, u32[]{:S(2)}) collective-permute-start(s32[128]{0:T(128)} %param.7), channel_id=1, source_target_pairs={{0,6},{1,7},{2,8},{3,9},{4,10},{5,11},{6,12},{7,13},{8,14},{9,15},... | collective-permute-start | bytes 1544 | tf_op jit(solution)/shard_map/ppermute | solution.py:601
  22.8 3.1 collective-permute-start.5
  25.9 1.1 copy.31.x_in
  27.0 1.9 collective-permute-start.3
  30.4 6.0 %collective-permute-start.2 = (bf16[128,576]{1,0:T(8,128)(2,1)S(1)}, bf16[128,576]{1,0:T(8,128)(2,1)S(1)}, u32[]{:S(2)}, u32[]{:S(2)}) collective-permute-start(bf16[128,576]{1,0:T(8,128)(2,1)S(1)} %copy.31.x_in), channel_id=1, source_target_pairs={{0,4},{1,5},{2,6},{3,7},{4,8},{5,9},{6,10},{7,11},{8,12},{9,13},{1... | collective-permute-start | bytes 442376 | tf_op jit(solution)/shard_map/ppermute | solution.py:601
  36.4 1.9 collective-permute-start.1
  38.4 3.5 collective-permute-start
  43.3 0.7 copy.32.segment
  44.1 1.5 collective-permute-done
  46.2 1.1 copy-done.7
  47.7 2.1 multiply_sine_fusion
  49.8 1.0 pad_maximum_fusion
  50.8 0.7 slice.72.cosine
  52.4 0.9 constant_dynamic-update-slice_fusion.5.window
  53.3 40.6 %all-gather.2.cloned.1.call-done = bf16[7864320]{0:T(1024)(128)(2,1)} async-done(((bf16[61440]{0:T(1024)(128)(2,1)}), bf16[7864320]{0:T(1024)(128)(2,1)}) %all-gather.2.cloned.1.call-update) | async-done | bytes 15728656 | tf_op jit(solution)/shard_map/all_gather | solution.py:692
  93.9 3.0 shard_map.89
  96.9 3.0 shard_map.85
  100.0 8.6 %shard_map.87 = (bf16[576,576]{1,0:T(8,128)(2,1)}, bf16[576,3072]{1,0:T(8,128)(2,1)}, bf16[1536,576]{1,0:T(8,128)(2,1)}, f32[1,640]{1,0:T(1,128)}) custom-call(bf16[128,2,240,128]{3,2,1,0:T(8,128)(2,1)} %bitcast.22), custom_call_target="tpu_custom_call" | custom-call | flops 2000000000 | bytes 30000000 | tf_op jit(solution)/shard_map/pallas_call | solution.py:231
  108.6 4.6 %shard_map.86 = (bf16[128,576]{1,0:T(8,128)(2,1)}, bf16[640,384]{1,0:T(8,128)(2,1)}, bf16[512,384]{1,0:T(8,128)(2,1)}, bf16[128,576]{1,0:T(8,128)(2,1)}) custom-call(bf16[1152,576]{1,0:T(8,128)(2,1)} %constant_dynamic-update-slice_fusion.5.window, f32[1152,128]{1,0:T(8,128)} %copy-done.4, f32[1152,128]{1,0:T(8,128)} %copy-done.5, ...), custom_call_target="tpu_custom_call" | custom-call | flops 800000000 | bytes 6000000 | tf_op jit(solution)/shard_map/pallas_call | solution.py:70
  113.2 7.7 %shard_map.88 = (f32[128,576]{1,0:T(8,128)}, bf16[128,576]{1,0:T(8,128)(2,1)}, f32[384,3]{1,0:T(8,128)}, f32[128,576]{1,0:T(8,128)}, bf16[128,576]{1,0:T(8,128)(...) custom-call(s32[1]{0:T(128)} %bitcast.first, bf16[128,576]{1,0:T(8,128)(2,1)} %copy-done.6, ...), custom_call_target="tpu_custom_call" | custom-call | flops 2000000000 | bytes 12000000 | tf_op jit(solution)/shard_map/pallas_call | solution.py:70
  120.9 2.8 shard_map.90
  123.7 3.3 collective-permute-start.13
  127.0 5.3 %collective-permute-start.12 = (bf16[128,384]{1,0:T(8,128)(2,1)}, bf16[128,384]{1,0:T(8,128)(2,1)S(1)}, u32[]{:S(2)}, u32[]{:S(2)}) collective-permute-start(bf16[128,384]{1,0:T(8,128)(2,1)} %get-tuple-element.89), channel_id=1, source_target_pairs={{0,4},{1,5},{2,6},{3,7},{4,8},{5,9},{6,10},{7,11},{8,12},{9,13},{1... | collective-permute-start | bytes 294920 | tf_op jit(solution)/shard_map/ppermute | solution.py:601
  132.3 2.5 collective-permute-start.11
  134.8 4.5 %collective-permute-start.10 = (bf16[128,384]{1,0:T(8,128)(2,1)}, bf16[128,384]{1,0:T(8,128)(2,1)S(1)}, u32[]{:S(2)}, u32[]{:S(2)}) collective-permute-start(bf16[128,384]{1,0:T(8,128)(2,1)} %get-tuple-element.89), channel_id=1, source_target_pairs={{0,8},{1,9},{2,10},{3,11},{4,12},{5,13},{6,14},{7,15},{8,16},{9,17... | collective-permute-start | bytes 294920 | tf_op jit(solution)/shard_map/ppermute | solution.py:601
  139.3 8.5 %shard_map.91 = (bf16[576,576]{1,0:T(8,128)(2,1)}, bf16[576,3072]{1,0:T(8,128)(2,1)}, bf16[1536,576]{1,0:T(8,128)(2,1)}, f32[1,640]{1,0:T(1,128)}) custom-call(bf16[128,2,240,128]{3,2,1,0:T(8,128)(2,1)} %bitcast.23), custom_call_target="tpu_custom_call" | custom-call | flops 2000000000 | bytes 30000000 | tf_op jit(solution)/shard_map/pallas_call | solution.py:231
  148.7 0.8 copy.33.g_in
  150.1 0.8 copy-done.24
  150.9 13.7 %shard_map.92 = (bf16[128,576]{1,0:T(8,128)(2,1)}, bf16[128,576]{1,0:T(8,128)(2,1)}, bf16[128,576]{1,0:T(8,128)(2,1)}, bf16[128,1536]{1,0:T(8,128)(2,1)}, bf16[1...) custom-call(s32[1]{0:T(128)} %bitcast.first, ...), custom_call_target="tpu_custom_call" | custom-call | flops 5000000000 | bytes 20000000 | tf_op jit(solution)/shard_map/pallas_call | solution.py:70
  164.8 1.8 collective-permute-done.15
  166.8 3.2 collective-permute-start.19
  170.1 3.2 collective-permute-start.18
  173.3 2.0 collective-permute-start.17
  175.4 4.8 %collective-permute-start.16 = (bf16[128,384]{1,0:T(8,128)(2,1)S(1)}, bf16[128,384]{1,0:T(8,128)(2,1)S(1)}, u32[]{:S(2)}, u32[]{:S(2)}) collective-permute-start(bf16[128,384]{1,0:T(8,128)(2,1)S(1)} %get-tuple-element.168), channel_id=1, source_target_pairs={{8,0},{9,1},{10,2},{11,3},{12,4},{13,5},{14,6},{15,7},{16,8},{17,9... | collective-permute-start | bytes 294920 | tf_op jit(solution)/shard_map/ppermute | solution.py:601
  180.2 12.2 %shard_map.93 = (bf16[10752,128]{1,0:T(8,128)(2,1)}, bf16[10752,128]{1,0:T(8,128)(2,1)}, f32[2616,128]{1,0:T(8,128)}) custom-call(s32[1]{0:T(128)} %bitcast.4.core, bf16[128,576]{1,0:T(8,128)(2,1)} %get-tuple-element.99.mixed, bf16[128,576]{1,0:T(8,128)(2,1)} %get-tuple-element.100.attn, bf16[128,576]{1,0:T(8,128)(2,1)} %get-tuple-element.101.normed_two, ...), custom_call_target="tpu_custom_call" | custom-call | flops 1000000000 | bytes 25000000 | tf_op jit(solution)/shard_map/pallas_call | solution.py:70
  193.0 0.7 slice.74.own
  193.7 5.7 %shard_map.94 = (f32[128,576]{1,0:T(8,128)}, bf16[3584,128]{1,0:T(8,128)(2,1)}, bf16[3584,128]{1,0:T(8,128)(2,1)}) custom-call(s32[1]{0:T(128)} %bitcast.4.core, f32[128,576]{1,0:T(8,128)} %get-tuple-element.85.x_in, bf16[128,576]{1,0:T(8,128)(2,1)} %get-tuple-element.96.dq, f32[128,384]{1,0:T(8,128)} %slice.74.own, bf16[128,384]{1,0:T(8,128)(2,1)} %copy-done.22, ...), custom_call_target="tpu_custom_call" | custom-call | flops 350000000 | bytes 10000000 | tf_op jit(solution)/shard_map/pallas_call | solution.py:70
  199.9 2.3 collective-permute-done.20.got_first
  202.2 1.2 copy-done.3
  203.4 6.6 %shard_map.95 = bf16[14336,128]{1,0:T(8,128)(2,1)} custom-call(bf16[3584,128]{1,0:T(8,128)(2,1)S(1)} %copy-done.3, bf16[3584,128]{1,0:T(8,128)(2,1)S(1)} %collective-permute-done.20.got_first, bf16[10752,128]{1,0:T(8,128)(2,1)S(1)} %copy-done.1, bf16[10752,128]{1,0:T(8,128)(2,1)} %collective-permute-done.21.got_rest), custom_call_target="tpu_custom_call" | custom-call | bytes 11000000 | tf_op jit(solution)/shard_map/pallas_call | solution.py:648
  209.9 9.4 %all-to-all-start = ((bf16[64,224,128]{2,1,0:T(8,128)(2,1)}), bf16[64,224,128]{2,1,0:T(8,128)(2,1)}, u32[]{:S(2)}, u32[]{:S(2)}) async-start(bf16[64,224,128]{2,1,0:T(8,128)(2,1)} %bitcast.24), calls=%async_computation | async-start | bytes 7340032 | tf_op jit(solution)/shard_map/all_to_all | solution.py:661
  219.4 12.0 %shard_map.96 = (bf16[128,576]{1,0:T(8,128)(2,1)}, bf16[128,3072]{1,0:T(8,128)(2,1)}, bf16[128,576]{1,0:T(8,128)(2,1)}, f32[128,576]{1,0:T(8,128)}, bf16[128,576...) custom-call(s32[1]{0:T(128)} %bitcast.first, ...), custom_call_target="tpu_custom_call" | custom-call | flops 3000000000 | bytes 15000000 | tf_op jit(solution)/shard_map/pallas_call | solution.py:70
  231.4 1.9 collective-permute-done.22
  233.6 2.5 collective-permute-start.26
  236.1 4.3 %collective-permute-start.25 = (bf16[128,384]{1,0:T(8,128)(2,1)S(1)}, bf16[128,384]{1,0:T(8,128)(2,1)S(1)}, u32[]{:S(2)}, u32[]{:S(2)}) collective-permute-start(bf16[128,384]{1,0:T(8,128)(2,1)S(1)} %get-tuple-element.162), channel_id=1, source_target_pairs={{4,0},{5,1},{6,2},{7,3},{8,4},{9,5},{10,6},{11,7},{12,8},{13,9},{1... | collective-permute-start | bytes 294920 | tf_op jit(solution)/shard_map/ppermute | solution.py:601
  240.4 3.7 %collective-permute-start.24 = (bf16[128,384]{1,0:T(8,128)(2,1)S(1)}, bf16[128,384]{1,0:T(8,128)(2,1)S(1)}, u32[]{:S(2)}, u32[]{:S(2)}) collective-permute-start(bf16[128,384]{1,0:T(8,128)(2,1)S(1)} %get-tuple-element.163), channel_id=1, source_target_pairs={{6,0},{7,1},{8,2},{9,3},{10,4},{11,5},{12,6},{13,7},{14,8},{15,9},... | collective-permute-start | bytes 294920 | tf_op jit(solution)/shard_map/ppermute | solution.py:601
  244.0 4.6 %collective-permute-start.23 = (bf16[128,384]{1,0:T(8,128)(2,1)S(1)}, bf16[128,384]{1,0:T(8,128)(2,1)S(1)}, u32[]{:S(2)}, u32[]{:S(2)}) collective-permute-start(bf16[128,384]{1,0:T(8,128)(2,1)S(1)} %get-tuple-element.164), channel_id=1, source_target_pairs={{8,0},{9,1},{10,2},{11,3},{12,4},{13,5},{14,6},{15,7},{16,8},{17,9... | collective-permute-start | bytes 294920 | tf_op jit(solution)/shard_map/ppermute | solution.py:601
  248.6 12.4 %shard_map.97 = (bf16[10752,128]{1,0:T(8,128)(2,1)}, bf16[10752,128]{1,0:T(8,128)(2,1)}, f32[2616,128]{1,0:T(8,128)}) custom-call(s32[1]{0:T(128)} %bitcast.4.core, bf16[128,576]{1,0:T(8,128)(2,1)} %get-tuple-element.128.mixed, bf16[128,576]{1,0:T(8,128)(2,1)} %get-tuple-element.129.attn, bf16[128,576]{1,0:T(8,128)(2,1)} %get-tuple-element.130.normed_two, ...), custom_call_target="tpu_custom_call" | custom-call | flops 1000000000 | bytes 25000000 | tf_op jit(solution)/shard_map/pallas_call | solution.py:70
  261.1 5.8 %collective-permute-done.25.r4 = bf16[128,384]{1,0:T(8,128)(2,1)S(1)} collective-permute-done((bf16[128,384]{1,0:T(8,128)(2,1)S(1)}, bf16[128,384]{1,0:T(8,128)(2,1)S(1)}, u32[]{:S(2)}, u32[]{:S(2)}) %collective-permute-start.25) | collective-permute-done | bytes 98336 | tf_op jit(solution)/shard_map/ppermute | solution.py:601
  266.9 3.0 collective-permute-done.24.r6
  270.9 5.6 %shard_map.98 = (f32[128,576]{1,0:T(8,128)}, bf16[3584,128]{1,0:T(8,128)(2,1)}, bf16[3584,128]{1,0:T(8,128)(2,1)}) custom-call(s32[1]{0:T(128)} %bitcast.4.core, bf16[128,576]{1,0:T(8,128)(2,1)} %copy-done.6, bf16[128,576]{1,0:T(8,128)(2,1)} %get-tuple-element.123.dq, f32[128,384]{1,0:T(8,128)} %slice.79.own, bf16[128,384]{1,0:T(8,128)(2,1)} %copy-done.19, ...), custom_call_target="tpu_custom_call" | custom-call | flops 350000000 | bytes 10000000 | tf_op jit(solution)/shard_map/pallas_call | solution.py:70
  277.0 2.3 collective-permute-done.27.got_first
  279.3 1.2 copy-done.2
  280.5 6.6 %shard_map.99 = bf16[14336,128]{1,0:T(8,128)(2,1)} custom-call(bf16[3584,128]{1,0:T(8,128)(2,1)S(1)} %copy-done.2, bf16[3584,128]{1,0:T(8,128)(2,1)S(1)} %collective-permute-done.27.got_first, bf16[10752,128]{1,0:T(8,128)(2,1)S(1)} %copy-done, bf16[10752,128]{1,0:T(8,128)(2,1)} %collective-permute-done.28.got_rest), custom_call_target="tpu_custom_call" | custom-call | bytes 11000000 | tf_op jit(solution)/shard_map/pallas_call | solution.py:648
  287.1 11.3 %all-to-all-start.1 = ((bf16[64,224,128]{2,1,0:T(8,128)(2,1)}), bf16[64,224,128]{2,1,0:T(8,128)(2,1)}, u32[]{:S(2)}, u32[]{:S(2)}) async-start(bf16[64,224,128]{2,1,0:T(8,128)(2,1)} %bitcast.25), calls=%async_computation.1 | async-start | bytes 7340032 | tf_op jit(solution)/shard_map/all_to_all | solution.py:661
  298.4 0.8 copy.37
  299.2 2.6 convert_reduce_fusion
  302.0 0.9 copy.38
  302.9 45.5 %all-to-all-done.1 = bf16[64,224,128]{2,1,0:T(8,128)(2,1)} async-done(((bf16[64,224,128]{2,1,0:T(8,128)(2,1)}), bf16[64,224,128]{2,1,0:T(8,128)(2,1)}, u32[]{:S(2)}, u32[]{:S(2)}) %all-to-all-start.1) | async-done | bytes 3670048 | tf_op jit(solution)/shard_map/all_to_all | solution.py:661
  348.4 2.6 convert_reduce_fusion.1
  351.2 0.9 pad_maximum_fusion.2
  (131 shorter events, 11.8 us)
Async XLA Ops:
  7.2 36.1 %copy-start.23 = (s32[128]{0:T(128)S(1)}, s32[128]{0:T(128)}, u32[]{:S(2)}) copy-start(s32[128]{0:T(128)} %param.7) | copy-start | bytes 1540
  7.2 86.7 %all-gather.2.cloned.1.call-start = ((), (), s32[]{:S(2)}) async-start(), calls=%async_computation.2 | async-start | bytes 15851520 | tf_op jit(solution)/shard_map/all_gather | solution.py:692
  10.8 31.1 %collective-permute-start.8 = (s32[128]{0:T(128)}, s32[128]{0:T(128)S(1)}, u32[]{:S(2)}, u32[]{:S(2)}) collective-permute-start(s32[128]{0:T(128)} %param.7), channel_id=1, source_target_pairs={{0,2},{1,3},{2,4},{3,5},{4,6},{5,7},{6,8},{7,9},{8,10},{9,11},{10,... | collective-permute-start | bytes 1544 | tf_op jit(solution)/shard_map/ppermute | solution.py:601
  14.6 23.8 %collective-permute-start.7 = (s32[128]{0:T(128)}, s32[128]{0:T(128)S(1)}, u32[]{:S(2)}, u32[]{:S(2)}) collective-permute-start(s32[128]{0:T(128)} %param.7), channel_id=1, source_target_pairs={{0,4},{1,5},{2,6},{3,7},{4,8},{5,9},{6,10},{7,11},{8,12},{9,13},{1... | collective-permute-start | bytes 1544 | tf_op jit(solution)/shard_map/ppermute | solution.py:601
  17.6 18.8 %collective-permute-start.6 = (s32[128]{0:T(128)}, s32[128]{0:T(128)S(1)}, u32[]{:S(2)}, u32[]{:S(2)}) collective-permute-start(s32[128]{0:T(128)} %param.7), channel_id=1, source_target_pairs={{0,6},{1,7},{2,8},{3,9},{4,10},{5,11},{6,12},{7,13},{8,14},{9,15},... | collective-permute-start | bytes 1544 | tf_op jit(solution)/shard_map/ppermute | solution.py:601
  22.8 7.6 %collective-permute-start.5 = (s32[128]{0:T(128)}, s32[128]{0:T(128)S(1)}, u32[]{:S(2)}, u32[]{:S(2)}) collective-permute-start(s32[128]{0:T(128)} %param.7), channel_id=1, source_target_pairs={{0,8},{1,9},{2,10},{3,11},{4,12},{5,13},{6,14},{7,15},{8,16},{9,17... | collective-permute-start | bytes 1544 | tf_op jit(solution)/shard_map/ppermute | solution.py:601
  27.0 20.4 %copy-start.6 = (bf16[128,576]{1,0:T(8,128)(2,1)}, bf16[128,576]{1,0:T(8,128)(2,1)S(1)}, u32[]{:S(2)}) copy-start(bf16[128,576]{1,0:T(8,128)(2,1)S(1)} %copy.31.x_in) | copy-start | bytes 442372
  27.0 19.1 %collective-permute-start.3 = (bf16[128,576]{1,0:T(8,128)(2,1)S(1)}, bf16[128,576]{1,0:T(8,128)(2,1)S(1)}, u32[]{:S(2)}, u32[]{:S(2)}) collective-permute-start(bf16[128,576]{1,0:T(8,128)(2,1)S(1)} %copy.31.x_in), channel_id=1, source_target_pairs={{0,2},{1,3},{2,4},{3,5},{4,6},{5,7},{6,8},{7,9},{8,10},{9,11},{10,... | collective-permute-start | bytes 442376 | tf_op jit(solution)/shard_map/ppermute | solution.py:601
  30.4 15.6 %collective-permute-start.2 = (bf16[128,576]{1,0:T(8,128)(2,1)S(1)}, bf16[128,576]{1,0:T(8,128)(2,1)S(1)}, u32[]{:S(2)}, u32[]{:S(2)}) collective-permute-start(bf16[128,576]{1,0:T(8,128)(2,1)S(1)} %copy.31.x_in), channel_id=1, source_target_pairs={{0,4},{1,5},{2,6},{3,7},{4,8},{5,9},{6,10},{7,11},{8,12},{9,13},{1... | collective-permute-start | bytes 442376 | tf_op jit(solution)/shard_map/ppermute | solution.py:601
  36.4 9.5 %collective-permute-start.1 = (bf16[128,576]{1,0:T(8,128)(2,1)S(1)}, bf16[128,576]{1,0:T(8,128)(2,1)S(1)}, u32[]{:S(2)}, u32[]{:S(2)}) collective-permute-start(bf16[128,576]{1,0:T(8,128)(2,1)S(1)} %copy.31.x_in), channel_id=1, source_target_pairs={{0,6},{1,7},{2,8},{3,9},{4,10},{5,11},{6,12},{7,13},{8,14},{9,15},... | collective-permute-start | bytes 442376 | tf_op jit(solution)/shard_map/ppermute | solution.py:601
  38.4 7.2 %collective-permute-start = (bf16[128,576]{1,0:T(8,128)(2,1)S(1)}, bf16[128,576]{1,0:T(8,128)(2,1)S(1)}, u32[]{:S(2)}, u32[]{:S(2)}) collective-permute-start(bf16[128,576]{1,0:T(8,128)(2,1)S(1)} %copy.31.x_in), channel_id=1, source_target_pairs={{0,8},{1,9},{2,10},{3,11},{4,12},{5,13},{6,14},{7,15},{8,16},{9,17... | collective-permute-start | bytes 442376 | tf_op jit(solution)/shard_map/ppermute | solution.py:601
  42.7 1.4 collective-permute-start.9
  46.1 1.1 copy-start.7
  47.6 4.5 %collective-permute-start.4 = (bf16[512,576]{0,1:T(8,128)(2,1)S(1)}, bf16[512,576]{0,1:T(8,128)(2,1)S(1)}, u32[]{:S(2)}, u32[]{:S(2)}) collective-permute-start(bf16[512,576]{0,1:T(8,128)(2,1)S(1)} %copy.28), channel_id=1, source_target_pairs={{0,1},{1,0},{2,3},{3,2},{4,5},{5,4},{6,7},{7,6},{8,9},{9,8},{10,11... | collective-permute-start | bytes 1769480 | tf_op jit(solution)/shard_map/ppermute | solution.py:605
  50.8 46.1 %copy-start.4 = (f32[1152,128]{1,0:T(8,128)}, f32[1152,128]{1,0:T(8,128)S(1)}, u32[]{:S(2)}) copy-start(f32[1152,128]{1,0:T(8,128)S(1)} %get-tuple-element.191.cosine) | copy-start | bytes 1769476
  50.8 46.1 %copy-start.5 = (f32[1152,128]{1,0:T(8,128)}, f32[1152,128]{1,0:T(8,128)S(1)}, u32[]{:S(2)}) copy-start(f32[1152,128]{1,0:T(8,128)S(1)} %get-tuple-element.192.sine) | copy-start | bytes 1769476
  123.7 24.3 %copy-start.14 = (bf16[128,384]{1,0:T(8,128)(2,1)S(1)}, bf16[128,384]{1,0:T(8,128)(2,1)}, u32[]{:S(2)}) copy-start(bf16[128,384]{1,0:T(8,128)(2,1)} %get-tuple-element.89) | copy-start | bytes 294916
  123.7 24.3 %collective-permute-start.13 = (bf16[128,384]{1,0:T(8,128)(2,1)}, bf16[128,384]{1,0:T(8,128)(2,1)S(1)}, u32[]{:S(2)}, u32[]{:S(2)}) collective-permute-start(bf16[128,384]{1,0:T(8,128)(2,1)} %get-tuple-element.89), channel_id=1, source_target_pairs={{0,2},{1,3},{2,4},{3,5},{4,6},{5,7},{6,8},{7,9},{8,10},{9,11},{10,... | collective-permute-start | bytes 294920 | tf_op jit(solution)/shard_map/ppermute | solution.py:601
  127.0 20.9 %collective-permute-start.12 = (bf16[128,384]{1,0:T(8,128)(2,1)}, bf16[128,384]{1,0:T(8,128)(2,1)S(1)}, u32[]{:S(2)}, u32[]{:S(2)}) collective-permute-start(bf16[128,384]{1,0:T(8,128)(2,1)} %get-tuple-element.89), channel_id=1, source_target_pairs={{0,4},{1,5},{2,6},{3,7},{4,8},{5,9},{6,10},{7,11},{8,12},{9,13},{1... | collective-permute-start | bytes 294920 | tf_op jit(solution)/shard_map/ppermute | solution.py:601
  132.3 15.6 %collective-permute-start.11 = (bf16[128,384]{1,0:T(8,128)(2,1)}, bf16[128,384]{1,0:T(8,128)(2,1)S(1)}, u32[]{:S(2)}, u32[]{:S(2)}) collective-permute-start(bf16[128,384]{1,0:T(8,128)(2,1)} %get-tuple-element.89), channel_id=1, source_target_pairs={{0,6},{1,7},{2,8},{3,9},{4,10},{5,11},{6,12},{7,13},{8,14},{9,15},... | collective-permute-start | bytes 294920 | tf_op jit(solution)/shard_map/ppermute | solution.py:601
  134.8 13.1 %collective-permute-start.10 = (bf16[128,384]{1,0:T(8,128)(2,1)}, bf16[128,384]{1,0:T(8,128)(2,1)S(1)}, u32[]{:S(2)}, u32[]{:S(2)}) collective-permute-start(bf16[128,384]{1,0:T(8,128)(2,1)} %get-tuple-element.89), channel_id=1, source_target_pairs={{0,8},{1,9},{2,10},{3,11},{4,12},{5,13},{6,14},{7,15},{8,16},{9,17... | collective-permute-start | bytes 294920 | tf_op jit(solution)/shard_map/ppermute | solution.py:601
  147.8 0.9 copy-start.13
  148.0 2.1 copy-start.10
  148.1 2.0 collective-permute-start.14
  150.1 0.8 copy-start.24
  164.6 2.1 copy-start.9
  164.6 2.0 collective-permute-start.15
  166.8 25.5 %collective-permute-start.19 = (bf16[128,384]{1,0:T(8,128)(2,1)S(1)}, bf16[128,384]{1,0:T(8,128)(2,1)S(1)}, u32[]{:S(2)}, u32[]{:S(2)}) collective-permute-start(bf16[128,384]{1,0:T(8,128)(2,1)S(1)} %get-tuple-element.165), channel_id=1, source_target_pairs={{2,0},{3,1},{4,2},{5,3},{6,4},{7,5},{8,6},{9,7},{10,8},{11,9},{12,... | collective-permute-start | bytes 294920 | tf_op jit(solution)/shard_map/ppermute | solution.py:601
  170.1 22.3 %collective-permute-start.18 = (bf16[128,384]{1,0:T(8,128)(2,1)S(1)}, bf16[128,384]{1,0:T(8,128)(2,1)S(1)}, u32[]{:S(2)}, u32[]{:S(2)}) collective-permute-start(bf16[128,384]{1,0:T(8,128)(2,1)S(1)} %get-tuple-element.166), channel_id=1, source_target_pairs={{4,0},{5,1},{6,2},{7,3},{8,4},{9,5},{10,6},{11,7},{12,8},{13,9},{1... | collective-permute-start | bytes 294920 | tf_op jit(solution)/shard_map/ppermute | solution.py:601
  173.3 19.1 %collective-permute-start.17 = (bf16[128,384]{1,0:T(8,128)(2,1)S(1)}, bf16[128,384]{1,0:T(8,128)(2,1)S(1)}, u32[]{:S(2)}, u32[]{:S(2)}) collective-permute-start(bf16[128,384]{1,0:T(8,128)(2,1)S(1)} %get-tuple-element.167), channel_id=1, source_target_pairs={{6,0},{7,1},{8,2},{9,3},{10,4},{11,5},{12,6},{13,7},{14,8},{15,9},... | collective-permute-start | bytes 294920 | tf_op jit(solution)/shard_map/ppermute | solution.py:601
  175.4 17.1 %collective-permute-start.16 = (bf16[128,384]{1,0:T(8,128)(2,1)S(1)}, bf16[128,384]{1,0:T(8,128)(2,1)S(1)}, u32[]{:S(2)}, u32[]{:S(2)}) collective-permute-start(bf16[128,384]{1,0:T(8,128)(2,1)S(1)} %get-tuple-element.168), channel_id=1, source_target_pairs={{8,0},{9,1},{10,2},{11,3},{12,4},{13,5},{14,6},{15,7},{16,8},{17,9... | collective-permute-start | bytes 294920 | tf_op jit(solution)/shard_map/ppermute | solution.py:601
  192.4 1.3 copy-start.18
  192.4 1.2 copy-start.20
  192.4 1.2 copy-start.21
  192.4 1.2 copy-start.22
  192.5 9.7 %collective-permute-start.21 = (bf16[10752,128]{1,0:T(8,128)(2,1)}, bf16[10752,128]{1,0:T(8,128)(2,1)}, u32[]{:S(2)}, u32[]{:S(2)}) collective-permute-start(bf16[10752,128]{1,0:T(8,128)(2,1)} %get-tuple-element.118), channel_id=1, source_target_pairs={{0,1},{1,0},{2,3},{3,2},{4,5},{5,4},{6,7},{7,6},{8,9},{9,8},{10,11... | collective-permute-start | bytes 8257544 | tf_op jit(solution)/shard_map/ppermute | solution.py:605
  193.7 8.5 %copy-start.1 = (bf16[10752,128]{1,0:T(8,128)(2,1)S(1)}, bf16[10752,128]{1,0:T(8,128)(2,1)}, u32[]{:S(2)}) copy-start(bf16[10752,128]{1,0:T(8,128)(2,1)} %get-tuple-element.117.keep_rest) | copy-start | bytes 8257540
  199.4 2.8 collective-permute-start.20
  202.2 1.2 copy-start.3
  209.9 60.9 %all-to-all-start = ((bf16[64,224,128]{2,1,0:T(8,128)(2,1)}), bf16[64,224,128]{2,1,0:T(8,128)(2,1)}, u32[]{:S(2)}, u32[]{:S(2)}) async-start(bf16[64,224,128]{2,1,0:T(8,128)(2,1)} %bitcast.24), calls=%async_computation | async-start | bytes 7340032 | tf_op jit(solution)/shard_map/all_to_all | solution.py:661
  231.3 2.1 copy-start.8
  231.4 2.0 collective-permute-start.22
  233.6 27.4 %collective-permute-start.26 = (bf16[128,384]{1,0:T(8,128)(2,1)S(1)}, bf16[128,384]{1,0:T(8,128)(2,1)S(1)}, u32[]{:S(2)}, u32[]{:S(2)}) collective-permute-start(bf16[128,384]{1,0:T(8,128)(2,1)S(1)} %get-tuple-element.161), channel_id=1, source_target_pairs={{2,0},{3,1},{4,2},{5,3},{6,4},{7,5},{8,6},{9,7},{10,8},{11,9},{12,... | collective-permute-start | bytes 294920 | tf_op jit(solution)/shard_map/ppermute | solution.py:601
  236.1 30.8 %collective-permute-start.25 = (bf16[128,384]{1,0:T(8,128)(2,1)S(1)}, bf16[128,384]{1,0:T(8,128)(2,1)S(1)}, u32[]{:S(2)}, u32[]{:S(2)}) collective-permute-start(bf16[128,384]{1,0:T(8,128)(2,1)S(1)} %get-tuple-element.162), channel_id=1, source_target_pairs={{4,0},{5,1},{6,2},{7,3},{8,4},{9,5},{10,6},{11,7},{12,8},{13,9},{1... | collective-permute-start | bytes 294920 | tf_op jit(solution)/shard_map/ppermute | solution.py:601
  240.4 29.5 %collective-permute-start.24 = (bf16[128,384]{1,0:T(8,128)(2,1)S(1)}, bf16[128,384]{1,0:T(8,128)(2,1)S(1)}, u32[]{:S(2)}, u32[]{:S(2)}) collective-permute-start(bf16[128,384]{1,0:T(8,128)(2,1)S(1)} %get-tuple-element.163), channel_id=1, source_target_pairs={{6,0},{7,1},{8,2},{9,3},{10,4},{11,5},{12,6},{13,7},{14,8},{15,9},... | collective-permute-start | bytes 294920 | tf_op jit(solution)/shard_map/ppermute | solution.py:601
  244.0 25.8 %collective-permute-start.23 = (bf16[128,384]{1,0:T(8,128)(2,1)S(1)}, bf16[128,384]{1,0:T(8,128)(2,1)S(1)}, u32[]{:S(2)}, u32[]{:S(2)}) collective-permute-start(bf16[128,384]{1,0:T(8,128)(2,1)S(1)} %get-tuple-element.164), channel_id=1, source_target_pairs={{8,0},{9,1},{10,2},{11,3},{12,4},{13,5},{14,6},{15,7},{16,8},{17,9... | collective-permute-start | bytes 294920 | tf_op jit(solution)/shard_map/ppermute | solution.py:601
  261.1 9.8 %copy-start.15 = (bf16[128,384]{1,0:T(8,128)(2,1)}, bf16[128,384]{1,0:T(8,128)(2,1)S(1)}, u32[]{:S(2)}) copy-start(bf16[128,384]{1,0:T(8,128)(2,1)S(1)} %collective-permute-done.26.r2) | copy-start | bytes 294916
  266.9 3.9 %copy-start.16 = (bf16[128,384]{1,0:T(8,128)(2,1)}, bf16[128,384]{1,0:T(8,128)(2,1)S(1)}, u32[]{:S(2)}) copy-start(bf16[128,384]{1,0:T(8,128)(2,1)S(1)} %collective-permute-done.25.r4) | copy-start | bytes 294916
  269.9 1.0 copy-start.17
  269.9 1.0 copy-start.19
  269.9 7.1 %collective-permute-start.28 = (bf16[10752,128]{1,0:T(8,128)(2,1)}, bf16[10752,128]{1,0:T(8,128)(2,1)}, u32[]{:S(2)}, u32[]{:S(2)}) collective-permute-start(bf16[10752,128]{1,0:T(8,128)(2,1)} %get-tuple-element.147), channel_id=1, source_target_pairs={{0,1},{1,0},{2,3},{3,2},{4,5},{5,4},{6,7},{7,6},{8,9},{9,8},{10,11... | collective-permute-start | bytes 8257544 | tf_op jit(solution)/shard_map/ppermute | solution.py:605
  270.8 8.5 %copy-start = (bf16[10752,128]{1,0:T(8,128)(2,1)S(1)}, bf16[10752,128]{1,0:T(8,128)(2,1)}, u32[]{:S(2)}) copy-start(bf16[10752,128]{1,0:T(8,128)(2,1)} %get-tuple-element.146.keep_rest) | copy-start | bytes 8257540
  276.5 2.8 collective-permute-start.27
  279.3 1.2 copy-start.2
  287.1 11.3 %copy-start.12 = (bf16[128,576]{1,0:T(8,128)(2,1)S(1)}, bf16[128,576]{1,0:T(8,128)(2,1)}, u32[]{:S(2)}) copy-start(bf16[128,576]{1,0:T(8,128)(2,1)} %get-tuple-element.152) | copy-start | bytes 442372
  287.1 61.3 %all-to-all-start.1 = ((bf16[64,224,128]{2,1,0:T(8,128)(2,1)}), bf16[64,224,128]{2,1,0:T(8,128)(2,1)}, u32[]{:S(2)}, u32[]{:S(2)}) async-start(bf16[64,224,128]{2,1,0:T(8,128)(2,1)} %bitcast.25), calls=%async_computation.1 | async-start | bytes 7340032 | tf_op jit(solution)/shard_map/all_to_all | solution.py:661
  299.2 2.8 copy-start.11
Sparse Core Ops, SparseCore 0:
  11.6 82.2 all-gather.1

commit v6 on v5

--- a/solution.py
+++ b/solution.py
@@ -194,7 +194,7 @@
         gain[0:1, 128 * t : 128 * t + 128] = value
 
 
-def unpack_first_kernel(layer, gathered, w_qkv, gain, landing, flat, tile, sems):
+def unpack_first(layer, gathered, w_qkv, gain, landing, flat, tile, sems):
     gather_flat(gathered, layer, 0, SPLIT + 1, 3, flat, landing, sems)
     take_gain(flat, gain, HALF_GAIN_ONE)
     take_matrix(flat, tile, w_qkv, HALF_QKV, PW // 64)
@@ -248,11 +248,12 @@
     )(gathered)
 
 
-def unpack_first(gathered, layer):
-    return unpack_call(
-        unpack_first_kernel, layer, [((D, PW), bf16), ((1, 640), f32)], gathered,
-        SPLIT + 1, 3, (8, D, 128), 9_000_000,
-    )
+FIRST_SCRATCH = (
+    pltpu.VMEM((SPLIT + 1, SECTION, 128), bf16),
+    pltpu.VMEM(((SPLIT + 1) * 216 + 32, 128), f32),
+    pltpu.VMEM((8, D, 128), f32),
+    pltpu.SemaphoreType.DMA((3,)),
+)
 
 
 def unpack_rest(gathered, layer):
@@ -278,7 +279,10 @@
     return lax.rsqrt(jnp.mean(values * values, axis=-1, keepdims=True) + epsilon)
 
 
-def heads_zero_kernel(window, cosine, sine, gain_row, w_qkv, q_out, kv_s, kv_t, normed_out):
+def heads_zero_kernel(
+    window, cosine, sine, gathered, w_qkv, gain_row, q_out, kv_s, kv_t, normed_out, *scratch
+):
+    unpack_first(0, gathered, w_qkv, gain_row, *scratch)
     gain = gain_row[:, 0:D]
     for begin, rows in ((0, 384), (384, 384), (768, 384)):
         x = window[begin : begin + rows, :].astype(f32)
@@ -302,7 +306,10 @@
     ].astype(bf16)
 
 
-def heads_kernel(x_in, cosine, sine, gain_row, w_qkv, q_out, kv_out, normed_out):
+def heads_kernel(
+    layer, x_in, cosine, sine, gathered, w_qkv, gain_row, q_out, kv_out, normed_out, *scratch
+):
+    unpack_first(layer, gathered, w_qkv, gain_row, *scratch)
     x = x_in[...]
     normed = (x * inverse_norm(x) * gain_row[:, 0:D]).astype(bf16)
     normed_out[...] = normed
@@ -628,32 +635,26 @@
     return total[SAME_CORE * ROWS :], pieces
 
 
-def join_kernel(keep_first, got_first, keep_rest, got_rest, out):
-    low = LOW_PLANES // JOIN
-
-    @pl.when(pl.program_id(0) < low)
-    def _():
-        out[...] = keep_first[...] + got_first[...]
-
-    @pl.when(pl.program_id(0) >= low)
-    def _():
-        out[...] = keep_rest[...] + got_rest[...]
-
-
-def join(keep_first, got_first, keep_rest, got_rest):
-    low = LOW_PLANES // JOIN
+def add_kernel(keep, got, *refs):
+    refs[-1][...] = keep[...] + got[...]
+
+
+def join(keep, got, first_plane, total=None):
     block = (JOIN * CHUNK, 128)
-    first = pl.BlockSpec(block, lambda i: (jnp.minimum(i, low - 1), 0))
-    rest = pl.BlockSpec(block, lambda i: (jnp.maximum(i - low, 0), 0))
+    part = pl.BlockSpec(block, lambda i: (i, 0))
+    given = () if total is None else (total,)
     return pl.pallas_call(
-        join_kernel,
-        grid=(DEVICES // 2 // JOIN,),
+        add_kernel,
+        grid=(keep.shape[0] // block[0],),
         out_shape=pltpu.HBM((DEVICES // 2 * CHUNK, 128), bf16),
-        in_specs=[first, first, rest, rest],
-        out_specs=pl.BlockSpec(block, lambda i: (i, 0)),
+        in_specs=[part, part] + [pl.BlockSpec(memory_space=pl.ANY) for _ in given],
+        out_specs=pl.BlockSpec(block, lambda i: (i + first_plane // JOIN, 0)),
+        input_output_aliases={2: 0} if given else {},
         compiler_params=pltpu.CompilerParams(vmem_limit_bytes=16 * 1024 * 1024),
-        cost_estimate=pl.CostEstimate(flops=0, bytes_accessed=11_000_000, transcendentals=0),
-    )(keep_first, got_first, keep_rest, got_rest)
+        cost_estimate=pl.CostEstimate(
+            flops=0, bytes_accessed=6 * keep.size, transcendentals=0
+        ),
+    )(keep, got, *given)
 
 
 def to_owners(total):
@@ -712,22 +713,21 @@
     x = hidden_in
     held = []
     for layer in range(layers):
-        w_qkv, gain_one = unpack_first(gathered, layer)
         w_out, w_in, w_down, gain_two = unpack_rest(gathered, layer)
         if layer == 0:
-            q, kv_s, kv_t, normed = call(
+            w_qkv, gain_one, q, kv_s, kv_t, normed = call(
                 heads_zero_kernel,
-                [((ROWS, QW), bf16), ((WIN_S, 2 * KW), bf16), ((WIN_T, 2 * KW), bf16),
+                [((D, PW), bf16), ((1, 640), f32), ((ROWS, QW), bf16), ((WIN_S, 2 * KW), bf16), ((WIN_T, 2 * KW), bf16),
                  ((ROWS, D), bf16)],
-                [window, cosine_all, sine_all, gain_one, w_qkv],
-                flops=800_000_000, nbytes=6_000_000,
+                [window, cosine_all, sine_all, gathered],
+                scratch=FIRST_SCRATCH, apart=1, flops=800_000_000, nbytes=6_000_000,
             )
         else:
-            q, kv, normed = call(
-                heads_kernel,
-                [((ROWS, QW), bf16), ((ROWS, 2 * KW), bf16), ((ROWS, D), bf16)],
-                [x, cosine, sine, gain_one, w_qkv],
-                flops=150_000_000, nbytes=3_000_000,
+            w_qkv, gain_one, q, kv, normed = call(
+                functools.partial(heads_kernel, layer),
+                [((D, PW), bf16), ((1, 640), f32), ((ROWS, QW), bf16), ((ROWS, 2 * KW), bf16), ((ROWS, D), bf16)],
+                [x, cosine, sine, gathered],
+                scratch=FIRST_SCRATCH, apart=1, flops=150_000_000, nbytes=3_000_000,
             )
             kv_s, kv_t = window_of(kv, core, (w_out,))
         if layer == layers - 1:
@@ -801,7 +801,7 @@
             ],
             smem=1, flops=350_000_000, nbytes=10_000_000,
         )
-        total = join(keep, swap(send), keep_rest, got_rest)
+        total = join(keep, swap(send), 0, join(keep_rest, got_rest, LOW_PLANES))
         if layer > 0:
             g, total = lax.optimization_barrier((g, total))
         grads[layer] = to_owners(total)

time: 366 us -> 355 us (0.970)
  waiting for transfers between devices: 106 us -> 99.1 us
    pallas_call x4 -> x2, Pallas kernels: 23.2 us -> 17.2 us  [unpack_call(): pl.pallas_call(functools.partial(kernel, layer), out_shape=[jax.ShapeDtyp...]
    ppermute x9, waiting for transfers between devices: 8.88 us -> 4.28 us  [swap(): return lax.ppermute(value, 'fsdp', [(i, i ^ 1) for i in range(DEVICES)])]
    pallas_call x9, Pallas kernels: 76.7 us -> 80.9 us  [call(): pl.pallas_call(kernel, out_shape=[jax.ShapeDtypeStruct(s, d) for s, d in...]
    unnamed x67 -> x65, local copies, waits for them, and re-layouts: 9.06 us -> 6.71 us
    pallas_call x2 -> x4, Pallas kernels: 13.2 us -> 13 us  [join(): pl.pallas_call(add_kernel, grid=(keep.shape[0] // block[0],), out_shape=p...]
  transfers between devices with their start and end apart: 32 -> 32, of which waited for: 11 -> 10; matrix products, arithmetic and copies ran while one was open for 5% -> 5% of each run, Pallas kernels for 16% -> 19%
where the time goes in v6:
time: 355 us; the launch traced here: 349 us
  Pallas kernels  111 us (31%)
  waiting for transfers between devices  99.1 us (28%)
  starting transfers between devices  95.2 us (27%)
  local copies, waits for them, and re-layouts  16.4 us (5%)
  between operations  15.1 us (4%)
  other arithmetic  11.8 us (3%)
    pallas_call x9, Pallas kernels, call(): pl.pallas_call(kernel, out_shape=[jax.ShapeDtypeStruct(s, d) for s, d in...  80.9 us
    ppermute x20, starting transfers between devices, hop(): return lax.ppermute(value, 'fsdp', pairs)  72.3 us
    all_to_all x2, waiting for transfers between devices, to_owners(): lax.all_to_all(total.reshape(DEVICES // 2, CHUNK, 128), 'fsdp', split_axi...  44.3 us
    all_gather x1, waiting for transfers between devices, body(): lax.all_gather(jnp.concatenate(sections), 'fsdp', axis=0, tiled=True)  40.5 us
    all_to_all x2, starting transfers between devices, to_owners(): lax.all_to_all(total.reshape(DEVICES // 2, CHUNK, 128), 'fsdp', split_axi...  20.4 us
    pallas_call x2, Pallas kernels, unpack_call(): pl.pallas_call(functools.partial(kernel, layer), out_shape=[jax.ShapeDtyp...  17.2 us
    pallas_call x4, Pallas kernels, join(): pl.pallas_call(add_kernel, grid=(keep.shape[0] // block[0],), out_shape=p...  13 us
    ppermute x20, waiting for transfers between devices, hop(): return lax.ppermute(value, 'fsdp', pairs)  9.94 us
  transfers between devices with their start and end apart: 32, of which 10 were waited for; matrix products, arithmetic and copies ran while one was open for 5% of the time, Pallas kernels for 19%

profile of v6, /device:TPU:50, one launch (start us, length us, event | category | flops | bytes accessed | tf_op | source)
XLA Modules:
  0.0 348.6 jit_solution(2516758294757658503)
XLA Ops:
  7.2 1.6 slice_reduce_fusion.1
  10.1 0.7 pad_maximum_fusion.3
  10.8 3.8 %collective-permute-start.8 = (s32[128]{0:T(128)}, s32[128]{0:T(128)S(1)}, u32[]{:S(2)}, u32[]{:S(2)}) collective-permute-start(s32[128]{0:T(128)} %param.7), channel_id=1, source_target_pairs={{0,2},{1,3},{2,4},{3,5},{4,6},{5,7},{6,8},{7,9},{8,10},{9,11},{10,... | collective-permute-start | bytes 1544 | tf_op jit(solution)/shard_map/ppermute | solution.py:608
  14.6 3.0 collective-permute-start.7
  17.6 5.2 %collective-permute-start.6 = (s32[128]{0:T(128)}, s32[128]{0:T(128)S(1)}, u32[]{:S(2)}, u32[]{:S(2)}) collective-permute-start(s32[128]{0:T(128)} %param.7), channel_id=1, source_target_pairs={{0,6},{1,7},{2,8},{3,9},{4,10},{5,11},{6,12},{7,13},{8,14},{9,15},... | collective-permute-start | bytes 1544 | tf_op jit(solution)/shard_map/ppermute | solution.py:608
  22.8 3.1 collective-permute-start.5
  25.9 1.1 copy.33.x_in
  27.0 1.9 collective-permute-start.3
  28.9 0.7 broadcast_add_fusion.1
  30.4 6.0 %collective-permute-start.2 = (bf16[128,576]{1,0:T(8,128)(2,1)S(1)}, bf16[128,576]{1,0:T(8,128)(2,1)S(1)}, u32[]{:S(2)}, u32[]{:S(2)}) collective-permute-start(bf16[128,576]{1,0:T(8,128)(2,1)S(1)} %copy.33.x_in), channel_id=1, source_target_pairs={{0,4},{1,5},{2,6},{3,7},{4,8},{5,9},{6,10},{7,11},{8,12},{9,13},{1... | collective-permute-start | bytes 442376 | tf_op jit(solution)/shard_map/ppermute | solution.py:608
  36.4 1.9 collective-permute-start.1
  38.4 3.5 collective-permute-start
  41.9 0.7 constant_dynamic-update-slice_fusion.18
  43.3 1.4 copy.34.segment
  44.7 0.8 collective-permute-done
  46.1 1.1 copy-done.7
  47.7 2.1 multiply_sine_fusion
  49.8 1.0 pad_maximum_fusion
  50.8 0.7 slice.72.cosine
  52.4 0.9 constant_dynamic-update-slice_fusion.5.window
  53.3 40.5 %all-gather.2.cloned.1.call-done = bf16[7864320]{0:T(1024)(128)(2,1)} async-done(((bf16[61440]{0:T(1024)(128)(2,1)}), bf16[7864320]{0:T(1024)(128)(2,1)}) %all-gather.2.cloned.1.call-update) | async-done | bytes 15728656 | tf_op jit(solution)/shard_map/all_gather | solution.py:693
  93.9 8.6 %shard_map.86 = (bf16[576,576]{1,0:T(8,128)(2,1)}, bf16[576,3072]{1,0:T(8,128)(2,1)}, bf16[1536,576]{1,0:T(8,128)(2,1)}, f32[1,640]{1,0:T(1,128)}) custom-call(bf16[128,2,240,128]{3,2,1,0:T(8,128)(2,1)} %bitcast.20), custom_call_target="tpu_custom_call" | custom-call | flops 2000000000 | bytes 30000000 | tf_op jit(solution)/shard_map/pallas_call | solution.py:231
  102.5 7.3 %shard_map.85 = (bf16[576,960]{1,0:T(8,128)(2,1)}, f32[1,640]{1,0:T(1,128)}, bf16[128,576]{1,0:T(8,128)(2,1)}, bf16[640,384]{1,0:T(8,128)(2,1)}, bf16[512,384]{1,0:T(8,128)(2,1)}, /*index=5*/bf16[128,576]{1,0:T(8,128)(2,1)}) custom-call(bf16[1152,576]{1,0:T(8,128)(2,1)} %constant_dynamic-update-slice_fusion.5.window, f32[1152,128]{1,0:T(8,128)} %copy-done.4, ...), custom_call_target="tpu_custom_call" | custom-call | flops 800000000 | bytes 6000000 | tf_op jit(solution)/shard_map/pallas_call | solution.py:70
  109.8 7.7 %shard_map.87 = (f32[128,576]{1,0:T(8,128)}, bf16[128,576]{1,0:T(8,128)(2,1)}, f32[384,3]{1,0:T(8,128)}, f32[128,576]{1,0:T(8,128)}, bf16[128,576]{1,0:T(8,128)(...) custom-call(s32[1]{0:T(128)} %bitcast.first, bf16[128,576]{1,0:T(8,128)(2,1)} %copy-done.6, ...), custom_call_target="tpu_custom_call" | custom-call | flops 2000000000 | bytes 12000000 | tf_op jit(solution)/shard_map/pallas_call | solution.py:70
  117.5 4.2 %shard_map.88 = (bf16[576,960]{1,0:T(8,128)(2,1)}, f32[1,640]{1,0:T(1,128)}, bf16[128,576]{1,0:T(8,128)(2,1)}, bf16[128,384]{1,0:T(8,128)(2,1)}, bf16[128,576]{1,0:T(8,128)(2,1)}) custom-call(f32[128,576]{1,0:T(8,128)} %get-tuple-element.83.x_in, f32[128,128]{1,0:T(8,128)} %slice.72.cosine, f32[128,128]{1,0:T(8,128)} %slice.73.sine, ...), custom_call_target="tpu_custom_call" | custom-call | flops 150000000 | bytes 3000000 | tf_op jit(solution)/shard_map/pallas_call | solution.py:70
  121.8 3.3 collective-permute-start.13
  125.1 5.3 %collective-permute-start.12 = (bf16[128,384]{1,0:T(8,128)(2,1)}, bf16[128,384]{1,0:T(8,128)(2,1)S(1)}, u32[]{:S(2)}, u32[]{:S(2)}) collective-permute-start(bf16[128,384]{1,0:T(8,128)(2,1)} %get-tuple-element.85), channel_id=1, source_target_pairs={{0,4},{1,5},{2,6},{3,7},{4,8},{5,9},{6,10},{7,11},{8,12},{9,13},{1... | collective-permute-start | bytes 294920 | tf_op jit(solution)/shard_map/ppermute | solution.py:608
  130.4 2.4 collective-permute-start.11
  132.9 4.5 %collective-permute-start.10 = (bf16[128,384]{1,0:T(8,128)(2,1)}, bf16[128,384]{1,0:T(8,128)(2,1)S(1)}, u32[]{:S(2)}, u32[]{:S(2)}) collective-permute-start(bf16[128,384]{1,0:T(8,128)(2,1)} %get-tuple-element.85), channel_id=1, source_target_pairs={{0,8},{1,9},{2,10},{3,11},{4,12},{5,13},{6,14},{7,15},{8,16},{9,17... | collective-permute-start | bytes 294920 | tf_op jit(solution)/shard_map/ppermute | solution.py:608
  137.3 8.6 %shard_map.89 = (bf16[576,576]{1,0:T(8,128)(2,1)}, bf16[576,3072]{1,0:T(8,128)(2,1)}, bf16[1536,576]{1,0:T(8,128)(2,1)}, f32[1,640]{1,0:T(1,128)}) custom-call(bf16[128,2,240,128]{3,2,1,0:T(8,128)(2,1)} %bitcast.23), custom_call_target="tpu_custom_call" | custom-call | flops 2000000000 | bytes 30000000 | tf_op jit(solution)/shard_map/pallas_call | solution.py:231
  146.9 0.8 copy.35.g_in
  148.2 0.8 copy-done.23
  149.0 13.7 %shard_map.90 = (bf16[128,576]{1,0:T(8,128)(2,1)}, bf16[128,576]{1,0:T(8,128)(2,1)}, bf16[128,576]{1,0:T(8,128)(2,1)}, bf16[128,1536]{1,0:T(8,128)(2,1)}, bf16[1...) custom-call(s32[1]{0:T(128)} %bitcast.first, ...), custom_call_target="tpu_custom_call" | custom-call | flops 5000000000 | bytes 20000000 | tf_op jit(solution)/shard_map/pallas_call | solution.py:70
  162.9 1.8 collective-permute-done.15
  165.0 3.3 collective-permute-start.19
  168.3 3.2 collective-permute-start.18
  171.5 2.0 collective-permute-start.17
  173.5 4.8 %collective-permute-start.16 = (bf16[128,384]{1,0:T(8,128)(2,1)S(1)}, bf16[128,384]{1,0:T(8,128)(2,1)S(1)}, u32[]{:S(2)}, u32[]{:S(2)}) collective-permute-start(bf16[128,384]{1,0:T(8,128)(2,1)S(1)} %get-tuple-element.168), channel_id=1, source_target_pairs={{8,0},{9,1},{10,2},{11,3},{12,4},{13,5},{14,6},{15,7},{16,8},{17,9... | collective-permute-start | bytes 294920 | tf_op jit(solution)/shard_map/ppermute | solution.py:608
  178.4 12.2 %shard_map.91 = (bf16[10752,128]{1,0:T(8,128)(2,1)}, bf16[10752,128]{1,0:T(8,128)(2,1)}, f32[2616,128]{1,0:T(8,128)}) custom-call(s32[1]{0:T(128)} %bitcast.4.core, bf16[128,576]{1,0:T(8,128)(2,1)} %get-tuple-element.95.mixed, bf16[128,576]{1,0:T(8,128)(2,1)} %get-tuple-element.96.attn, bf16[128,576]{1,0:T(8,128)(2,1)} %get-tuple-element.97.normed_two, ...), custom_call_target="tpu_custom_call" | custom-call | flops 1000000000 | bytes 25000000 | tf_op jit(solution)/shard_map/pallas_call | solution.py:70
  191.1 0.7 slice.74.own
  191.8 5.7 %shard_map.92 = (f32[128,576]{1,0:T(8,128)}, bf16[3584,128]{1,0:T(8,128)(2,1)}, bf16[3584,128]{1,0:T(8,128)(2,1)}) custom-call(s32[1]{0:T(128)} %bitcast.4.core, f32[128,576]{1,0:T(8,128)} %get-tuple-element.83.x_in, bf16[128,576]{1,0:T(8,128)(2,1)} %get-tuple-element.92.dq, f32[128,384]{1,0:T(8,128)} %slice.74.own, bf16[128,384]{1,0:T(8,128)(2,1)} %copy-done.22, ...), custom_call_target="tpu_custom_call" | custom-call | flops 350000000 | bytes 10000000 | tf_op jit(solution)/shard_map/pallas_call | solution.py:70
  198.0 5.4 %shard_map.93.refs_0_ = bf16[14336,128]{1,0:T(8,128)(2,1)} custom-call(bf16[10752,128]{1,0:T(8,128)(2,1)S(1)} %copy-done.1, bf16[10752,128]{1,0:T(8,128)(2,1)} %collective-permute-done.21.got), custom_call_target="tpu_custom_call" | custom-call | bytes 8257536 | tf_op jit(solution)/shard_map/pallas_call | solution.py:646
  203.5 1.1 shard_map.94
  204.6 9.4 %all-to-all-start = ((bf16[64,224,128]{2,1,0:T(8,128)(2,1)}), bf16[64,224,128]{2,1,0:T(8,128)(2,1)}, u32[]{:S(2)}, u32[]{:S(2)}) async-start(bf16[64,224,128]{2,1,0:T(8,128)(2,1)} %bitcast.24), calls=%async_computation | async-start | bytes 7340032 | tf_op jit(solution)/shard_map/all_to_all | solution.py:662
  214.0 12.0 %shard_map.95 = (bf16[128,576]{1,0:T(8,128)(2,1)}, bf16[128,3072]{1,0:T(8,128)(2,1)}, bf16[128,576]{1,0:T(8,128)(2,1)}, f32[128,576]{1,0:T(8,128)}, bf16[128,576...) custom-call(s32[1]{0:T(128)} %bitcast.first, ...), custom_call_target="tpu_custom_call" | custom-call | flops 3000000000 | bytes 15000000 | tf_op jit(solution)/shard_map/pallas_call | solution.py:70
  226.1 1.9 collective-permute-done.22
  228.2 2.5 collective-permute-start.26
  230.7 4.3 %collective-permute-start.25 = (bf16[128,384]{1,0:T(8,128)(2,1)S(1)}, bf16[128,384]{1,0:T(8,128)(2,1)S(1)}, u32[]{:S(2)}, u32[]{:S(2)}) collective-permute-start(bf16[128,384]{1,0:T(8,128)(2,1)S(1)} %get-tuple-element.162), channel_id=1, source_target_pairs={{4,0},{5,1},{6,2},{7,3},{8,4},{9,5},{10,6},{11,7},{12,8},{13,9},{1... | collective-permute-start | bytes 294920 | tf_op jit(solution)/shard_map/ppermute | solution.py:608
  235.0 3.7 %collective-permute-start.24 = (bf16[128,384]{1,0:T(8,128)(2,1)S(1)}, bf16[128,384]{1,0:T(8,128)(2,1)S(1)}, u32[]{:S(2)}, u32[]{:S(2)}) collective-permute-start(bf16[128,384]{1,0:T(8,128)(2,1)S(1)} %get-tuple-element.163), channel_id=1, source_target_pairs={{6,0},{7,1},{8,2},{9,3},{10,4},{11,5},{12,6},{13,7},{14,8},{15,9},... | collective-permute-start | bytes 294920 | tf_op jit(solution)/shard_map/ppermute | solution.py:608
  238.6 4.6 %collective-permute-start.23 = (bf16[128,384]{1,0:T(8,128)(2,1)S(1)}, bf16[128,384]{1,0:T(8,128)(2,1)S(1)}, u32[]{:S(2)}, u32[]{:S(2)}) collective-permute-start(bf16[128,384]{1,0:T(8,128)(2,1)S(1)} %get-tuple-element.164), channel_id=1, source_target_pairs={{8,0},{9,1},{10,2},{11,3},{12,4},{13,5},{14,6},{15,7},{16,8},{17,9... | collective-permute-start | bytes 294920 | tf_op jit(solution)/shard_map/ppermute | solution.py:608
  243.2 12.4 %shard_map.96 = (bf16[10752,128]{1,0:T(8,128)(2,1)}, bf16[10752,128]{1,0:T(8,128)(2,1)}, f32[2616,128]{1,0:T(8,128)}) custom-call(s32[1]{0:T(128)} %bitcast.4.core, bf16[128,576]{1,0:T(8,128)(2,1)} %get-tuple-element.126.mixed, bf16[128,576]{1,0:T(8,128)(2,1)} %get-tuple-element.127.attn, bf16[128,576]{1,0:T(8,128)(2,1)} %get-tuple-element.128.normed_two, ...), custom_call_target="tpu_custom_call" | custom-call | flops 1000000000 | bytes 25000000 | tf_op jit(solution)/shard_map/pallas_call | solution.py:70
  255.7 4.9 %collective-permute-done.26.r2 = bf16[128,384]{1,0:T(8,128)(2,1)S(1)} collective-permute-done((bf16[128,384]{1,0:T(8,128)(2,1)S(1)}, bf16[128,384]{1,0:T(8,128)(2,1)S(1)}, u32[]{:S(2)}, u32[]{:S(2)}) %collective-permute-start.26) | collective-permute-done | bytes 98336 | tf_op jit(solution)/shard_map/ppermute | solution.py:608
  260.7 3.7 %collective-permute-done.24.r6 = bf16[128,384]{1,0:T(8,128)(2,1)S(1)} collective-permute-done((bf16[128,384]{1,0:T(8,128)(2,1)S(1)}, bf16[128,384]{1,0:T(8,128)(2,1)S(1)}, u32[]{:S(2)}, u32[]{:S(2)}) %collective-permute-start.24) | collective-permute-done | bytes 98336 | tf_op jit(solution)/shard_map/ppermute | solution.py:608
  264.7 0.7 slice.79.own
  265.4 5.6 %shard_map.97 = (f32[128,576]{1,0:T(8,128)}, bf16[3584,128]{1,0:T(8,128)(2,1)}, bf16[3584,128]{1,0:T(8,128)(2,1)}) custom-call(s32[1]{0:T(128)} %bitcast.4.core, bf16[128,576]{1,0:T(8,128)(2,1)} %copy-done.6, bf16[128,576]{1,0:T(8,128)(2,1)} %get-tuple-element.121.dq, f32[128,384]{1,0:T(8,128)} %slice.79.own, bf16[128,384]{1,0:T(8,128)(2,1)} %copy-done.19, ...), custom_call_target="tpu_custom_call" | custom-call | flops 350000000 | bytes 10000000 | tf_op jit(solution)/shard_map/pallas_call | solution.py:70
  271.5 5.4 %shard_map.98.refs_0_ = bf16[14336,128]{1,0:T(8,128)(2,1)} custom-call(bf16[10752,128]{1,0:T(8,128)(2,1)S(1)} %copy-done, bf16[10752,128]{1,0:T(8,128)(2,1)} %collective-permute-done.28.got), custom_call_target="tpu_custom_call" | custom-call | bytes 8257536 | tf_op jit(solution)/shard_map/pallas_call | solution.py:646
  276.9 1.1 shard_map.99
  278.1 11.0 %all-to-all-start.1 = ((bf16[64,224,128]{2,1,0:T(8,128)(2,1)}), bf16[64,224,128]{2,1,0:T(8,128)(2,1)}, u32[]{:S(2)}, u32[]{:S(2)}) async-start(bf16[64,224,128]{2,1,0:T(8,128)(2,1)} %bitcast.25), calls=%async_computation.1 | async-start | bytes 7340032 | tf_op jit(solution)/shard_map/all_to_all | solution.py:662
  289.1 0.8 copy.39
  289.9 2.6 convert_reduce_fusion
  292.8 0.9 copy.40
  293.6 44.3 %all-to-all-done.1 = bf16[64,224,128]{2,1,0:T(8,128)(2,1)} async-done(((bf16[64,224,128]{2,1,0:T(8,128)(2,1)}), bf16[64,224,128]{2,1,0:T(8,128)(2,1)}, u32[]{:S(2)}, u32[]{:S(2)}) %all-to-all-start.1) | async-done | bytes 3670048 | tf_op jit(solution)/shard_map/all_to_all | solution.py:662
  337.9 2.6 convert_reduce_fusion.1
  340.7 0.9 pad_maximum_fusion.2
  (129 shorter events, 9.3 us)
Async XLA Ops:
  7.2 86.7 %all-gather.2.cloned.1.call-start = ((), (), s32[]{:S(2)}) async-start(), calls=%async_computation.2 | async-start | bytes 15851520 | tf_op jit(solution)/shard_map/all_gather | solution.py:693
  10.8 31.1 %collective-permute-start.8 = (s32[128]{0:T(128)}, s32[128]{0:T(128)S(1)}, u32[]{:S(2)}, u32[]{:S(2)}) collective-permute-start(s32[128]{0:T(128)} %param.7), channel_id=1, source_target_pairs={{0,2},{1,3},{2,4},{3,5},{4,6},{5,7},{6,8},{7,9},{8,10},{9,11},{10,... | collective-permute-start | bytes 1544 | tf_op jit(solution)/shard_map/ppermute | solution.py:608
  14.6 23.8 %collective-permute-start.7 = (s32[128]{0:T(128)}, s32[128]{0:T(128)S(1)}, u32[]{:S(2)}, u32[]{:S(2)}) collective-permute-start(s32[128]{0:T(128)} %param.7), channel_id=1, source_target_pairs={{0,4},{1,5},{2,6},{3,7},{4,8},{5,9},{6,10},{7,11},{8,12},{9,13},{1... | collective-permute-start | bytes 1544 | tf_op jit(solution)/shard_map/ppermute | solution.py:608
  17.6 18.8 %collective-permute-start.6 = (s32[128]{0:T(128)}, s32[128]{0:T(128)S(1)}, u32[]{:S(2)}, u32[]{:S(2)}) collective-permute-start(s32[128]{0:T(128)} %param.7), channel_id=1, source_target_pairs={{0,6},{1,7},{2,8},{3,9},{4,10},{5,11},{6,12},{7,13},{8,14},{9,15},... | collective-permute-start | bytes 1544 | tf_op jit(solution)/shard_map/ppermute | solution.py:608
  22.8 7.6 %collective-permute-start.5 = (s32[128]{0:T(128)}, s32[128]{0:T(128)S(1)}, u32[]{:S(2)}, u32[]{:S(2)}) collective-permute-start(s32[128]{0:T(128)} %param.7), channel_id=1, source_target_pairs={{0,8},{1,9},{2,10},{3,11},{4,12},{5,13},{6,14},{7,15},{8,16},{9,17... | collective-permute-start | bytes 1544 | tf_op jit(solution)/shard_map/ppermute | solution.py:608
  27.0 20.4 %copy-start.6 = (bf16[128,576]{1,0:T(8,128)(2,1)}, bf16[128,576]{1,0:T(8,128)(2,1)S(1)}, u32[]{:S(2)}) copy-start(bf16[128,576]{1,0:T(8,128)(2,1)S(1)} %copy.33.x_in) | copy-start | bytes 442372
  27.0 19.1 %collective-permute-start.3 = (bf16[128,576]{1,0:T(8,128)(2,1)S(1)}, bf16[128,576]{1,0:T(8,128)(2,1)S(1)}, u32[]{:S(2)}, u32[]{:S(2)}) collective-permute-start(bf16[128,576]{1,0:T(8,128)(2,1)S(1)} %copy.33.x_in), channel_id=1, source_target_pairs={{0,2},{1,3},{2,4},{3,5},{4,6},{5,7},{6,8},{7,9},{8,10},{9,11},{10,... | collective-permute-start | bytes 442376 | tf_op jit(solution)/shard_map/ppermute | solution.py:608
  30.4 15.6 %collective-permute-start.2 = (bf16[128,576]{1,0:T(8,128)(2,1)S(1)}, bf16[128,576]{1,0:T(8,128)(2,1)S(1)}, u32[]{:S(2)}, u32[]{:S(2)}) collective-permute-start(bf16[128,576]{1,0:T(8,128)(2,1)S(1)} %copy.33.x_in), channel_id=1, source_target_pairs={{0,4},{1,5},{2,6},{3,7},{4,8},{5,9},{6,10},{7,11},{8,12},{9,13},{1... | collective-permute-start | bytes 442376 | tf_op jit(solution)/shard_map/ppermute | solution.py:608
  36.4 9.5 %collective-permute-start.1 = (bf16[128,576]{1,0:T(8,128)(2,1)S(1)}, bf16[128,576]{1,0:T(8,128)(2,1)S(1)}, u32[]{:S(2)}, u32[]{:S(2)}) collective-permute-start(bf16[128,576]{1,0:T(8,128)(2,1)S(1)} %copy.33.x_in), channel_id=1, source_target_pairs={{0,6},{1,7},{2,8},{3,9},{4,10},{5,11},{6,12},{7,13},{8,14},{9,15},... | collective-permute-start | bytes 442376 | tf_op jit(solution)/shard_map/ppermute | solution.py:608
  38.4 7.2 %collective-permute-start = (bf16[128,576]{1,0:T(8,128)(2,1)S(1)}, bf16[128,576]{1,0:T(8,128)(2,1)S(1)}, u32[]{:S(2)}, u32[]{:S(2)}) collective-permute-start(bf16[128,576]{1,0:T(8,128)(2,1)S(1)} %copy.33.x_in), channel_id=1, source_target_pairs={{0,8},{1,9},{2,10},{3,11},{4,12},{5,13},{6,14},{7,15},{8,16},{9,17... | collective-permute-start | bytes 442376 | tf_op jit(solution)/shard_map/ppermute | solution.py:608
  42.6 2.0 collective-permute-start.9
  46.1 1.1 copy-start.7
  47.6 4.5 %collective-permute-start.4 = (bf16[512,576]{0,1:T(8,128)(2,1)S(1)}, bf16[512,576]{0,1:T(8,128)(2,1)S(1)}, u32[]{:S(2)}, u32[]{:S(2)}) collective-permute-start(bf16[512,576]{0,1:T(8,128)(2,1)S(1)} %copy.30), channel_id=1, source_target_pairs={{0,1},{1,0},{2,3},{3,2},{4,5},{5,4},{6,7},{7,6},{8,9},{9,8},{10,11... | collective-permute-start | bytes 1769480 | tf_op jit(solution)/shard_map/ppermute | solution.py:612
  50.8 51.7 %copy-start.4 = (f32[1152,128]{1,0:T(8,128)}, f32[1152,128]{1,0:T(8,128)S(1)}, u32[]{:S(2)}) copy-start(f32[1152,128]{1,0:T(8,128)S(1)} %get-tuple-element.191.cosine) | copy-start | bytes 1769476
  50.8 51.7 %copy-start.5 = (f32[1152,128]{1,0:T(8,128)}, f32[1152,128]{1,0:T(8,128)S(1)}, u32[]{:S(2)}) copy-start(f32[1152,128]{1,0:T(8,128)S(1)} %get-tuple-element.192.sine) | copy-start | bytes 1769476
  121.8 24.4 %copy-start.14 = (bf16[128,384]{1,0:T(8,128)(2,1)S(1)}, bf16[128,384]{1,0:T(8,128)(2,1)}, u32[]{:S(2)}) copy-start(bf16[128,384]{1,0:T(8,128)(2,1)} %get-tuple-element.85) | copy-start | bytes 294916
  121.8 24.3 %collective-permute-start.13 = (bf16[128,384]{1,0:T(8,128)(2,1)}, bf16[128,384]{1,0:T(8,128)(2,1)S(1)}, u32[]{:S(2)}, u32[]{:S(2)}) collective-permute-start(bf16[128,384]{1,0:T(8,128)(2,1)} %get-tuple-element.85), channel_id=1, source_target_pairs={{0,2},{1,3},{2,4},{3,5},{4,6},{5,7},{6,8},{7,9},{8,10},{9,11},{10,... | collective-permute-start | bytes 294920 | tf_op jit(solution)/shard_map/ppermute | solution.py:608
  125.1 21.0 %collective-permute-start.12 = (bf16[128,384]{1,0:T(8,128)(2,1)}, bf16[128,384]{1,0:T(8,128)(2,1)S(1)}, u32[]{:S(2)}, u32[]{:S(2)}) collective-permute-start(bf16[128,384]{1,0:T(8,128)(2,1)} %get-tuple-element.85), channel_id=1, source_target_pairs={{0,4},{1,5},{2,6},{3,7},{4,8},{5,9},{6,10},{7,11},{8,12},{9,13},{1... | collective-permute-start | bytes 294920 | tf_op jit(solution)/shard_map/ppermute | solution.py:608
  130.4 15.6 %collective-permute-start.11 = (bf16[128,384]{1,0:T(8,128)(2,1)}, bf16[128,384]{1,0:T(8,128)(2,1)S(1)}, u32[]{:S(2)}, u32[]{:S(2)}) collective-permute-start(bf16[128,384]{1,0:T(8,128)(2,1)} %get-tuple-element.85), channel_id=1, source_target_pairs={{0,6},{1,7},{2,8},{3,9},{4,10},{5,11},{6,12},{7,13},{8,14},{9,15},... | collective-permute-start | bytes 294920 | tf_op jit(solution)/shard_map/ppermute | solution.py:608
  132.9 13.1 %collective-permute-start.10 = (bf16[128,384]{1,0:T(8,128)(2,1)}, bf16[128,384]{1,0:T(8,128)(2,1)S(1)}, u32[]{:S(2)}, u32[]{:S(2)}) collective-permute-start(bf16[128,384]{1,0:T(8,128)(2,1)} %get-tuple-element.85), channel_id=1, source_target_pairs={{0,8},{1,9},{2,10},{3,11},{4,12},{5,13},{6,14},{7,15},{8,16},{9,17... | collective-permute-start | bytes 294920 | tf_op jit(solution)/shard_map/ppermute | solution.py:608
  146.0 0.9 copy-start.13
  146.1 2.1 copy-start.10
  146.2 2.0 collective-permute-start.14
  148.2 0.8 copy-start.23
  162.7 2.1 copy-start.9
  162.7 2.0 collective-permute-start.15
  165.0 25.6 %collective-permute-start.19 = (bf16[128,384]{1,0:T(8,128)(2,1)S(1)}, bf16[128,384]{1,0:T(8,128)(2,1)S(1)}, u32[]{:S(2)}, u32[]{:S(2)}) collective-permute-start(bf16[128,384]{1,0:T(8,128)(2,1)S(1)} %get-tuple-element.165), channel_id=1, source_target_pairs={{2,0},{3,1},{4,2},{5,3},{6,4},{7,5},{8,6},{9,7},{10,8},{11,9},{12,... | collective-permute-start | bytes 294920 | tf_op jit(solution)/shard_map/ppermute | solution.py:608
  168.3 22.3 %collective-permute-start.18 = (bf16[128,384]{1,0:T(8,128)(2,1)S(1)}, bf16[128,384]{1,0:T(8,128)(2,1)S(1)}, u32[]{:S(2)}, u32[]{:S(2)}) collective-permute-start(bf16[128,384]{1,0:T(8,128)(2,1)S(1)} %get-tuple-element.166), channel_id=1, source_target_pairs={{4,0},{5,1},{6,2},{7,3},{8,4},{9,5},{10,6},{11,7},{12,8},{13,9},{1... | collective-permute-start | bytes 294920 | tf_op jit(solution)/shard_map/ppermute | solution.py:608
  171.5 19.1 %collective-permute-start.17 = (bf16[128,384]{1,0:T(8,128)(2,1)S(1)}, bf16[128,384]{1,0:T(8,128)(2,1)S(1)}, u32[]{:S(2)}, u32[]{:S(2)}) collective-permute-start(bf16[128,384]{1,0:T(8,128)(2,1)S(1)} %get-tuple-element.167), channel_id=1, source_target_pairs={{6,0},{7,1},{8,2},{9,3},{10,4},{11,5},{12,6},{13,7},{14,8},{15,9},... | collective-permute-start | bytes 294920 | tf_op jit(solution)/shard_map/ppermute | solution.py:608
  173.5 17.1 %collective-permute-start.16 = (bf16[128,384]{1,0:T(8,128)(2,1)S(1)}, bf16[128,384]{1,0:T(8,128)(2,1)S(1)}, u32[]{:S(2)}, u32[]{:S(2)}) collective-permute-start(bf16[128,384]{1,0:T(8,128)(2,1)S(1)} %get-tuple-element.168), channel_id=1, source_target_pairs={{8,0},{9,1},{10,2},{11,3},{12,4},{13,5},{14,6},{15,7},{16,8},{17,9... | collective-permute-start | bytes 294920 | tf_op jit(solution)/shard_map/ppermute | solution.py:608
  190.6 1.3 copy-start.18
  190.6 1.2 copy-start.20
  190.6 1.2 copy-start.21
  190.6 1.2 copy-start.22
  190.6 7.4 %collective-permute-start.21 = (bf16[10752,128]{1,0:T(8,128)(2,1)}, bf16[10752,128]{1,0:T(8,128)(2,1)}, u32[]{:S(2)}, u32[]{:S(2)}) collective-permute-start(bf16[10752,128]{1,0:T(8,128)(2,1)} %get-tuple-element.116), channel_id=1, source_target_pairs={{0,1},{1,0},{2,3},{3,2},{4,5},{5,4},{6,7},{7,6},{8,9},{9,8},{10,11... | collective-permute-start | bytes 8257544 | tf_op jit(solution)/shard_map/ppermute | solution.py:612
  191.8 6.2 %copy-start.1 = (bf16[10752,128]{1,0:T(8,128)(2,1)S(1)}, bf16[10752,128]{1,0:T(8,128)(2,1)}, u32[]{:S(2)}) copy-start(bf16[10752,128]{1,0:T(8,128)(2,1)} %get-tuple-element.115.keep) | copy-start | bytes 8257540
  197.5 5.9 %collective-permute-start.20 = (bf16[3584,128]{1,0:T(8,128)(2,1)}, bf16[3584,128]{1,0:T(8,128)(2,1)S(1)}, u32[]{:S(2)}, u32[]{:S(2)}) collective-permute-start(bf16[3584,128]{1,0:T(8,128)(2,1)} %get-tuple-element.114), channel_id=1, source_target_pairs={{0,1},{1,0},{2,3},{3,2},{4,5},{5,4},{6,7},{7,6},{8,9},{9,8},{10,11... | collective-permute-start | bytes 2752520 | tf_op jit(solution)/shard_map/ppermute | solution.py:612
  198.0 5.4 %copy-start.3 = (bf16[3584,128]{1,0:T(8,128)(2,1)S(1)}, bf16[3584,128]{1,0:T(8,128)(2,1)}, u32[]{:S(2)}) copy-start(bf16[3584,128]{1,0:T(8,128)(2,1)} %get-tuple-element.113.keep) | copy-start | bytes 2752516
  204.6 60.8 %all-to-all-start = ((bf16[64,224,128]{2,1,0:T(8,128)(2,1)}), bf16[64,224,128]{2,1,0:T(8,128)(2,1)}, u32[]{:S(2)}, u32[]{:S(2)}) async-start(bf16[64,224,128]{2,1,0:T(8,128)(2,1)} %bitcast.24), calls=%async_computation | async-start | bytes 7340032 | tf_op jit(solution)/shard_map/all_to_all | solution.py:662
  226.0 2.1 copy-start.8
  226.0 2.0 collective-permute-start.22
  228.2 32.3 %collective-permute-start.26 = (bf16[128,384]{1,0:T(8,128)(2,1)S(1)}, bf16[128,384]{1,0:T(8,128)(2,1)S(1)}, u32[]{:S(2)}, u32[]{:S(2)}) collective-permute-start(bf16[128,384]{1,0:T(8,128)(2,1)S(1)} %get-tuple-element.161), channel_id=1, source_target_pairs={{2,0},{3,1},{4,2},{5,3},{6,4},{7,5},{8,6},{9,7},{10,8},{11,9},{12,... | collective-permute-start | bytes 294920 | tf_op jit(solution)/shard_map/ppermute | solution.py:608
  230.7 30.0 %collective-permute-start.25 = (bf16[128,384]{1,0:T(8,128)(2,1)S(1)}, bf16[128,384]{1,0:T(8,128)(2,1)S(1)}, u32[]{:S(2)}, u32[]{:S(2)}) collective-permute-start(bf16[128,384]{1,0:T(8,128)(2,1)S(1)} %get-tuple-element.162), channel_id=1, source_target_pairs={{4,0},{5,1},{6,2},{7,3},{8,4},{9,5},{10,6},{11,7},{12,8},{13,9},{1... | collective-permute-start | bytes 294920 | tf_op jit(solution)/shard_map/ppermute | solution.py:608
  235.0 29.4 %collective-permute-start.24 = (bf16[128,384]{1,0:T(8,128)(2,1)S(1)}, bf16[128,384]{1,0:T(8,128)(2,1)S(1)}, u32[]{:S(2)}, u32[]{:S(2)}) collective-permute-start(bf16[128,384]{1,0:T(8,128)(2,1)S(1)} %get-tuple-element.163), channel_id=1, source_target_pairs={{6,0},{7,1},{8,2},{9,3},{10,4},{11,5},{12,6},{13,7},{14,8},{15,9},... | collective-permute-start | bytes 294920 | tf_op jit(solution)/shard_map/ppermute | solution.py:608
  238.6 25.8 %collective-permute-start.23 = (bf16[128,384]{1,0:T(8,128)(2,1)S(1)}, bf16[128,384]{1,0:T(8,128)(2,1)S(1)}, u32[]{:S(2)}, u32[]{:S(2)}) collective-permute-start(bf16[128,384]{1,0:T(8,128)(2,1)S(1)} %get-tuple-element.164), channel_id=1, source_target_pairs={{8,0},{9,1},{10,2},{11,3},{12,4},{13,5},{14,6},{15,7},{16,8},{17,9... | collective-permute-start | bytes 294920 | tf_op jit(solution)/shard_map/ppermute | solution.py:608
  260.6 4.8 %copy-start.15 = (bf16[128,384]{1,0:T(8,128)(2,1)}, bf16[128,384]{1,0:T(8,128)(2,1)S(1)}, u32[]{:S(2)}) copy-start(bf16[128,384]{1,0:T(8,128)(2,1)S(1)} %collective-permute-done.26.r2) | copy-start | bytes 294916
  260.7 4.6 %copy-start.16 = (bf16[128,384]{1,0:T(8,128)(2,1)}, bf16[128,384]{1,0:T(8,128)(2,1)S(1)}, u32[]{:S(2)}) copy-start(bf16[128,384]{1,0:T(8,128)(2,1)S(1)} %collective-permute-done.25.r4) | copy-start | bytes 294916
  264.4 1.0 copy-start.17
  264.4 1.0 copy-start.19
  264.4 7.1 %collective-permute-start.28 = (bf16[10752,128]{1,0:T(8,128)(2,1)}, bf16[10752,128]{1,0:T(8,128)(2,1)}, u32[]{:S(2)}, u32[]{:S(2)}) collective-permute-start(bf16[10752,128]{1,0:T(8,128)(2,1)} %get-tuple-element.147), channel_id=1, source_target_pairs={{0,1},{1,0},{2,3},{3,2},{4,5},{5,4},{6,7},{7,6},{8,9},{9,8},{10,11... | collective-permute-start | bytes 8257544 | tf_op jit(solution)/shard_map/ppermute | solution.py:612
  265.4 6.1 %copy-start = (bf16[10752,128]{1,0:T(8,128)(2,1)S(1)}, bf16[10752,128]{1,0:T(8,128)(2,1)}, u32[]{:S(2)}) copy-start(bf16[10752,128]{1,0:T(8,128)(2,1)} %get-tuple-element.146.keep) | copy-start | bytes 8257540
  271.0 5.9 %collective-permute-start.27 = (bf16[3584,128]{1,0:T(8,128)(2,1)}, bf16[3584,128]{1,0:T(8,128)(2,1)S(1)}, u32[]{:S(2)}, u32[]{:S(2)}) collective-permute-start(bf16[3584,128]{1,0:T(8,128)(2,1)} %get-tuple-element.145), channel_id=1, source_target_pairs={{0,1},{1,0},{2,3},{3,2},{4,5},{5,4},{6,7},{7,6},{8,9},{9,8},{10,11... | collective-permute-start | bytes 2752520 | tf_op jit(solution)/shard_map/ppermute | solution.py:612
  271.5 5.4 %copy-start.2 = (bf16[3584,128]{1,0:T(8,128)(2,1)S(1)}, bf16[3584,128]{1,0:T(8,128)(2,1)}, u32[]{:S(2)}) copy-start(bf16[3584,128]{1,0:T(8,128)(2,1)} %get-tuple-element.144.keep) | copy-start | bytes 2752516
  278.1 11.0 %copy-start.12 = (bf16[128,576]{1,0:T(8,128)(2,1)S(1)}, bf16[128,576]{1,0:T(8,128)(2,1)}, u32[]{:S(2)}) copy-start(bf16[128,576]{1,0:T(8,128)(2,1)} %get-tuple-element.152) | copy-start | bytes 442372
  278.1 59.8 %all-to-all-start.1 = ((bf16[64,224,128]{2,1,0:T(8,128)(2,1)}), bf16[64,224,128]{2,1,0:T(8,128)(2,1)}, u32[]{:S(2)}, u32[]{:S(2)}) async-start(bf16[64,224,128]{2,1,0:T(8,128)(2,1)} %bitcast.25), calls=%async_computation.1 | async-start | bytes 7340032 | tf_op jit(solution)/shard_map/all_to_all | solution.py:662
  289.9 2.8 copy-start.11
Sparse Core Ops, SparseCore 0:
  11.6 82.2 all-gather.1

commit v7 on v6

--- a/solution.py
+++ b/solution.py
@@ -433,7 +433,9 @@
     return mm_t(attn, w_out[...]).astype(bf16)
 
 
-def attend_back(q, kv_s, kv_t, held, grad_mixed, cosine, sine, dq_out, dkv_s, dkv_t):
+def attend_back(
+    q, kv_s, kv_t, held, grad_mixed, cosine, sine, dq_out, dkv_s, dkv_t, factor=1.0
+):
     dq, dk, dv = [], [], []
     for group in range(KVH):
         keys = window_rows(kv_s, kv_t, group * HD)
@@ -447,7 +449,7 @@
         part = mm(grad_scores, keys) * FACTOR
         for n in range(GROUP):
             dq.append(part[n * ROWS : (n + 1) * ROWS, :])
-        dk.append(mm(query.T, grad_scores))
+        dk.append(mm(query.T, grad_scores) * factor)
         dv.append(mm(grad.T, probs.astype(bf16)))
     dkv = jnp.concatenate(dk + dv, axis=0).T
     dkv_s[...] = dkv[0:WIN_S, :]
@@ -469,18 +471,18 @@
     copies[1].start()
     copies[0].start()
     bias = bias_of(first, segment, key_row)
-    q = q_in[...] * FACTOR
+    q = q_in[...]
     held = []
     for group in range(KVH):
         keys = window_rows(kv_s, kv_t, group * HD)
-        scores = mm_t(group_rows(q, group), keys) + bias
+        scores = mm_t(group_rows(q, group), keys) * FACTOR + bias
         held.append(jnp.exp(scores - lse[:, group : group + 1]))
     grad_mixed = feed_back(
         g_in[...].astype(f32), middle_in, gate_up, gain_row, w_out, w_in, w_down,
         ((copies[2], gate_copy), (copies[1],), (copies[0],)),
         branch_out, grad_gu_out, attn_out, middle_grad_out, gain_out,
     )
-    attend_back(q, kv_s, kv_t, held, grad_mixed, cosine, sine, dq_out, dkv_s, dkv_t)
+    attend_back(q, kv_s, kv_t, held, grad_mixed, cosine, sine, dq_out, dkv_s, dkv_t, FACTOR)
 
 
 def last_kernel(
@@ -686,11 +688,10 @@
     core = lax.rem(device, 2)
     first_row = device * ROWS
     layers = weights_flat.shape[0]
-    sections = []
-    for layer in range(layers):
-        blank = jnp.zeros((SECTION * 128,), bf16)
-        sections.append(lax.dynamic_update_slice(blank, weights_flat[layer], (9 * device,)))
-    gathered = lax.all_gather(jnp.concatenate(sections), "fsdp", axis=0, tiled=True)
+    room = SECTION * 128 - SHARD
+    padded = jnp.pad(weights_flat, ((0, 0), (9 * DEVICES, room)))
+    sections = lax.dynamic_slice(padded, (0, 9 * (DEVICES - device)), (layers, SECTION * 128))
+    gathered = lax.all_gather(sections.reshape(-1), "fsdp", axis=0, tiled=True)
     gathered = gathered.reshape(DEVICES, layers, SECTION, 128)
 
     x_same, x_sibling = window_of(hidden_in, core)

time: 355 us -> 360 us (1.014)
  waiting for transfers between devices: 99.1 us -> 106 us
    all_gather x1, waiting for transfers between devices: 40.5 us -> 47.8 us  [body(): gathered = lax.all_gather(sections.reshape(-1), 'fsdp', axis=0, tiled=True)]
    unnamed x65 -> x67, local copies, waits for them, and re-layouts: 6.71 us -> 8.61 us
where the time goes in v7:
time: 360 us; the launch traced here: 354 us
  Pallas kernels  111 us (31%)
  waiting for transfers between devices  106 us (29%)
  starting transfers between devices  95.2 us (26%)
  local copies, waits for them, and re-layouts  15.5 us (4%)
  between operations  15 us (4%)
  other arithmetic  11.1 us (3%)
    pallas_call x9, Pallas kernels, call(): pl.pallas_call(kernel, out_shape=[jax.ShapeDtypeStruct(s, d) for s, d in...  80.9 us
    ppermute x20, starting transfers between devices, hop(): return lax.ppermute(value, 'fsdp', pairs)  72.3 us
    all_gather x1, waiting for transfers between devices, body(): gathered = lax.all_gather(sections.reshape(-1), 'fsdp', axis=0, tiled=True)  47.8 us
    all_to_all x2, waiting for transfers between devices, to_owners(): lax.all_to_all(total.reshape(DEVICES // 2, CHUNK, 128), 'fsdp', split_axi...  44.3 us
    all_to_all x2, starting transfers between devices, to_owners(): lax.all_to_all(total.reshape(DEVICES // 2, CHUNK, 128), 'fsdp', split_axi...  20.4 us
    pallas_call x2, Pallas kernels, unpack_call(): pl.pallas_call(functools.partial(kernel, layer), out_shape=[jax.ShapeDtyp...  17.1 us
    pallas_call x4, Pallas kernels, join(): pl.pallas_call(add_kernel, grid=(keep.shape[0] // block[0],), out_shape=p...  13 us
    ppermute x20, waiting for transfers between devices, hop(): return lax.ppermute(value, 'fsdp', pairs)  9.9 us
  transfers between devices with their start and end apart: 32, of which 10 were waited for; matrix products, arithmetic and copies ran while one was open for 5% of the time, Pallas kernels for 19%

profile of v7, /device:TPU:50, one launch (start us, length us, event | category | flops | bytes accessed | tf_op | source)
XLA Modules:
  0.0 354.2 jit_solution(3191948740337841530)
XLA Ops:
  7.2 1.2 fusion
  8.5 0.7 copy.41
  9.1 3.8 %collective-permute-start.8 = (s32[128]{0:T(128)}, s32[128]{0:T(128)S(1)}, u32[]{:S(2)}, u32[]{:S(2)}) collective-permute-start(s32[128]{0:T(128)} %param.7), channel_id=1, source_target_pairs={{0,2},{1,3},{2,4},{3,5},{4,6},{5,7},{6,8},{7,9},{8,10},{9,11},{10,... | collective-permute-start | bytes 1544 | tf_op jit(solution)/shard_map/ppermute | solution.py:610
  13.0 3.0 collective-permute-start.7
  16.0 5.2 %collective-permute-start.6 = (s32[128]{0:T(128)}, s32[128]{0:T(128)S(1)}, u32[]{:S(2)}, u32[]{:S(2)}) collective-permute-start(s32[128]{0:T(128)} %param.7), channel_id=1, source_target_pairs={{0,6},{1,7},{2,8},{3,9},{4,10},{5,11},{6,12},{7,13},{8,14},{9,15},... | collective-permute-start | bytes 1544 | tf_op jit(solution)/shard_map/ppermute | solution.py:610
  21.2 3.1 collective-permute-start.5
  24.3 1.1 copy.33.x_in
  25.4 1.9 collective-permute-start.3
  27.3 0.7 broadcast_add_fusion.1
  28.8 6.0 %collective-permute-start.2 = (bf16[128,576]{1,0:T(8,128)(2,1)S(1)}, bf16[128,576]{1,0:T(8,128)(2,1)S(1)}, u32[]{:S(2)}, u32[]{:S(2)}) collective-permute-start(bf16[128,576]{1,0:T(8,128)(2,1)S(1)} %copy.33.x_in), channel_id=1, source_target_pairs={{0,4},{1,5},{2,6},{3,7},{4,8},{5,9},{6,10},{7,11},{8,12},{9,13},{1... | collective-permute-start | bytes 442376 | tf_op jit(solution)/shard_map/ppermute | solution.py:610
  34.8 1.9 collective-permute-start.1
  36.8 3.5 collective-permute-start
  40.3 0.7 constant_dynamic-update-slice_fusion.18
  41.7 1.4 copy.34.segment
  43.1 0.8 collective-permute-done
  44.5 1.1 copy-done.7
  46.0 2.1 multiply_sine_fusion
  48.2 1.0 pad_maximum_fusion
  49.2 0.7 slice.64.cosine
  50.8 0.9 constant_dynamic-update-slice_fusion.5.window
  51.7 47.8 %all-gather.2.cloned.1.call-done = bf16[7864320]{0:T(1024)(128)(2,1)} async-done(((bf16[61440]{0:T(1024)(128)(2,1)}), bf16[7864320]{0:T(1024)(128)(2,1)}) %all-gather.2.cloned.1.call-update) | async-done | bytes 15728656 | tf_op jit(solution)/shard_map/all_gather | solution.py:694
  99.5 8.6 %shard_map.86 = (bf16[576,576]{1,0:T(8,128)(2,1)}, bf16[576,3072]{1,0:T(8,128)(2,1)}, bf16[1536,576]{1,0:T(8,128)(2,1)}, f32[1,640]{1,0:T(1,128)}) custom-call(bf16[128,2,240,128]{3,2,1,0:T(8,128)(2,1)} %bitcast.23), custom_call_target="tpu_custom_call" | custom-call | flops 2000000000 | bytes 30000000 | tf_op jit(solution)/shard_map/pallas_call | solution.py:231
  108.1 7.3 %shard_map.85 = (bf16[576,960]{1,0:T(8,128)(2,1)}, f32[1,640]{1,0:T(1,128)}, bf16[128,576]{1,0:T(8,128)(2,1)}, bf16[640,384]{1,0:T(8,128)(2,1)}, bf16[512,384]{1,0:T(8,128)(2,1)}, /*index=5*/bf16[128,576]{1,0:T(8,128)(2,1)}) custom-call(bf16[1152,576]{1,0:T(8,128)(2,1)} %constant_dynamic-update-slice_fusion.5.window, f32[1152,128]{1,0:T(8,128)} %copy-done.4, ...), custom_call_target="tpu_custom_call" | custom-call | flops 800000000 | bytes 6000000 | tf_op jit(solution)/shard_map/pallas_call | solution.py:70
  115.4 7.7 %shard_map.87 = (f32[128,576]{1,0:T(8,128)}, bf16[128,576]{1,0:T(8,128)(2,1)}, f32[384,3]{1,0:T(8,128)}, f32[128,576]{1,0:T(8,128)}, bf16[128,576]{1,0:T(8,128)(...) custom-call(s32[1]{0:T(128)} %bitcast.first, bf16[128,576]{1,0:T(8,128)(2,1)} %copy-done.6, ...), custom_call_target="tpu_custom_call" | custom-call | flops 2000000000 | bytes 12000000 | tf_op jit(solution)/shard_map/pallas_call | solution.py:70
  123.1 4.2 %shard_map.88 = (bf16[576,960]{1,0:T(8,128)(2,1)}, f32[1,640]{1,0:T(1,128)}, bf16[128,576]{1,0:T(8,128)(2,1)}, bf16[128,384]{1,0:T(8,128)(2,1)}, bf16[128,576]{1,0:T(8,128)(2,1)}) custom-call(f32[128,576]{1,0:T(8,128)} %get-tuple-element.83.x_in, f32[128,128]{1,0:T(8,128)} %slice.64.cosine, f32[128,128]{1,0:T(8,128)} %slice.65.sine, ...), custom_call_target="tpu_custom_call" | custom-call | flops 150000000 | bytes 3000000 | tf_op jit(solution)/shard_map/pallas_call | solution.py:70
  127.3 3.3 collective-permute-start.13
  130.6 5.3 %collective-permute-start.12 = (bf16[128,384]{1,0:T(8,128)(2,1)}, bf16[128,384]{1,0:T(8,128)(2,1)S(1)}, u32[]{:S(2)}, u32[]{:S(2)}) collective-permute-start(bf16[128,384]{1,0:T(8,128)(2,1)} %get-tuple-element.85), channel_id=1, source_target_pairs={{0,4},{1,5},{2,6},{3,7},{4,8},{5,9},{6,10},{7,11},{8,12},{9,13},{1... | collective-permute-start | bytes 294920 | tf_op jit(solution)/shard_map/ppermute | solution.py:610
  135.9 2.4 collective-permute-start.11
  138.4 4.5 %collective-permute-start.10 = (bf16[128,384]{1,0:T(8,128)(2,1)}, bf16[128,384]{1,0:T(8,128)(2,1)S(1)}, u32[]{:S(2)}, u32[]{:S(2)}) collective-permute-start(bf16[128,384]{1,0:T(8,128)(2,1)} %get-tuple-element.85), channel_id=1, source_target_pairs={{0,8},{1,9},{2,10},{3,11},{4,12},{5,13},{6,14},{7,15},{8,16},{9,17... | collective-permute-start | bytes 294920 | tf_op jit(solution)/shard_map/ppermute | solution.py:610
  142.9 8.6 %shard_map.89 = (bf16[576,576]{1,0:T(8,128)(2,1)}, bf16[576,3072]{1,0:T(8,128)(2,1)}, bf16[1536,576]{1,0:T(8,128)(2,1)}, f32[1,640]{1,0:T(1,128)}) custom-call(bf16[128,2,240,128]{3,2,1,0:T(8,128)(2,1)} %bitcast.26), custom_call_target="tpu_custom_call" | custom-call | flops 2000000000 | bytes 30000000 | tf_op jit(solution)/shard_map/pallas_call | solution.py:231
  152.4 0.8 copy.35.g_in
  153.7 0.8 copy-done.23
  154.5 13.7 %shard_map.90 = (bf16[128,576]{1,0:T(8,128)(2,1)}, bf16[128,576]{1,0:T(8,128)(2,1)}, bf16[128,576]{1,0:T(8,128)(2,1)}, bf16[128,1536]{1,0:T(8,128)(2,1)}, bf16[1...) custom-call(s32[1]{0:T(128)} %bitcast.first, ...), custom_call_target="tpu_custom_call" | custom-call | flops 5000000000 | bytes 20000000 | tf_op jit(solution)/shard_map/pallas_call | solution.py:70
  168.4 1.8 collective-permute-done.15
  170.5 3.3 collective-permute-start.19
  173.8 3.2 collective-permute-start.18
  177.0 2.0 collective-permute-start.17
  179.0 4.8 %collective-permute-start.16 = (bf16[128,384]{1,0:T(8,128)(2,1)S(1)}, bf16[128,384]{1,0:T(8,128)(2,1)S(1)}, u32[]{:S(2)}, u32[]{:S(2)}) collective-permute-start(bf16[128,384]{1,0:T(8,128)(2,1)S(1)} %get-tuple-element.166), channel_id=1, source_target_pairs={{8,0},{9,1},{10,2},{11,3},{12,4},{13,5},{14,6},{15,7},{16,8},{17,9... | collective-permute-start | bytes 294920 | tf_op jit(solution)/shard_map/ppermute | solution.py:610
  183.9 12.2 %shard_map.91 = (bf16[10752,128]{1,0:T(8,128)(2,1)}, bf16[10752,128]{1,0:T(8,128)(2,1)}, f32[2616,128]{1,0:T(8,128)}) custom-call(s32[1]{0:T(128)} %bitcast.4.core, bf16[128,576]{1,0:T(8,128)(2,1)} %get-tuple-element.95.mixed, bf16[128,576]{1,0:T(8,128)(2,1)} %get-tuple-element.96.attn, bf16[128,576]{1,0:T(8,128)(2,1)} %get-tuple-element.97.normed_two, ...), custom_call_target="tpu_custom_call" | custom-call | flops 1000000000 | bytes 25000000 | tf_op jit(solution)/shard_map/pallas_call | solution.py:70
  196.6 0.7 slice.66.own
  197.4 5.7 %shard_map.92 = (f32[128,576]{1,0:T(8,128)}, bf16[3584,128]{1,0:T(8,128)(2,1)}, bf16[3584,128]{1,0:T(8,128)(2,1)}) custom-call(s32[1]{0:T(128)} %bitcast.4.core, f32[128,576]{1,0:T(8,128)} %get-tuple-element.83.x_in, bf16[128,576]{1,0:T(8,128)(2,1)} %get-tuple-element.92.dq, f32[128,384]{1,0:T(8,128)} %slice.66.own, bf16[128,384]{1,0:T(8,128)(2,1)} %copy-done.22, ...), custom_call_target="tpu_custom_call" | custom-call | flops 350000000 | bytes 10000000 | tf_op jit(solution)/shard_map/pallas_call | solution.py:70
  203.5 5.4 %shard_map.93.refs_0_ = bf16[14336,128]{1,0:T(8,128)(2,1)} custom-call(bf16[10752,128]{1,0:T(8,128)(2,1)S(1)} %copy-done.1, bf16[10752,128]{1,0:T(8,128)(2,1)} %collective-permute-done.21.got), custom_call_target="tpu_custom_call" | custom-call | bytes 8257536 | tf_op jit(solution)/shard_map/pallas_call | solution.py:648
  209.0 1.1 shard_map.94
  210.1 9.4 %all-to-all-start = ((bf16[64,224,128]{2,1,0:T(8,128)(2,1)}), bf16[64,224,128]{2,1,0:T(8,128)(2,1)}, u32[]{:S(2)}, u32[]{:S(2)}) async-start(bf16[64,224,128]{2,1,0:T(8,128)(2,1)} %bitcast.27), calls=%async_computation | async-start | bytes 7340032 | tf_op jit(solution)/shard_map/all_to_all | solution.py:664
  219.5 12.0 %shard_map.95 = (bf16[128,576]{1,0:T(8,128)(2,1)}, bf16[128,3072]{1,0:T(8,128)(2,1)}, bf16[128,576]{1,0:T(8,128)(2,1)}, f32[128,576]{1,0:T(8,128)}, bf16[128,576...) custom-call(s32[1]{0:T(128)} %bitcast.first, ...), custom_call_target="tpu_custom_call" | custom-call | flops 3000000000 | bytes 15000000 | tf_op jit(solution)/shard_map/pallas_call | solution.py:70
  231.6 1.9 collective-permute-done.22
  233.7 2.5 collective-permute-start.26
  236.2 4.3 %collective-permute-start.25 = (bf16[128,384]{1,0:T(8,128)(2,1)S(1)}, bf16[128,384]{1,0:T(8,128)(2,1)S(1)}, u32[]{:S(2)}, u32[]{:S(2)}) collective-permute-start(bf16[128,384]{1,0:T(8,128)(2,1)S(1)} %get-tuple-element.160), channel_id=1, source_target_pairs={{4,0},{5,1},{6,2},{7,3},{8,4},{9,5},{10,6},{11,7},{12,8},{13,9},{1... | collective-permute-start | bytes 294920 | tf_op jit(solution)/shard_map/ppermute | solution.py:610
  240.5 3.7 %collective-permute-start.24 = (bf16[128,384]{1,0:T(8,128)(2,1)S(1)}, bf16[128,384]{1,0:T(8,128)(2,1)S(1)}, u32[]{:S(2)}, u32[]{:S(2)}) collective-permute-start(bf16[128,384]{1,0:T(8,128)(2,1)S(1)} %get-tuple-element.161), channel_id=1, source_target_pairs={{6,0},{7,1},{8,2},{9,3},{10,4},{11,5},{12,6},{13,7},{14,8},{15,9},... | collective-permute-start | bytes 294920 | tf_op jit(solution)/shard_map/ppermute | solution.py:610
  244.1 4.6 %collective-permute-start.23 = (bf16[128,384]{1,0:T(8,128)(2,1)S(1)}, bf16[128,384]{1,0:T(8,128)(2,1)S(1)}, u32[]{:S(2)}, u32[]{:S(2)}) collective-permute-start(bf16[128,384]{1,0:T(8,128)(2,1)S(1)} %get-tuple-element.162), channel_id=1, source_target_pairs={{8,0},{9,1},{10,2},{11,3},{12,4},{13,5},{14,6},{15,7},{16,8},{17,9... | collective-permute-start | bytes 294920 | tf_op jit(solution)/shard_map/ppermute | solution.py:610
  248.7 12.4 %shard_map.96 = (bf16[10752,128]{1,0:T(8,128)(2,1)}, bf16[10752,128]{1,0:T(8,128)(2,1)}, f32[2616,128]{1,0:T(8,128)}) custom-call(s32[1]{0:T(128)} %bitcast.4.core, bf16[128,576]{1,0:T(8,128)(2,1)} %get-tuple-element.126.mixed, bf16[128,576]{1,0:T(8,128)(2,1)} %get-tuple-element.127.attn, bf16[128,576]{1,0:T(8,128)(2,1)} %get-tuple-element.128.normed_two, ...), custom_call_target="tpu_custom_call" | custom-call | flops 1000000000 | bytes 25000000 | tf_op jit(solution)/shard_map/pallas_call | solution.py:70
  261.2 4.9 %collective-permute-done.26.r2 = bf16[128,384]{1,0:T(8,128)(2,1)S(1)} collective-permute-done((bf16[128,384]{1,0:T(8,128)(2,1)S(1)}, bf16[128,384]{1,0:T(8,128)(2,1)S(1)}, u32[]{:S(2)}, u32[]{:S(2)}) %collective-permute-start.26) | collective-permute-done | bytes 98336 | tf_op jit(solution)/shard_map/ppermute | solution.py:610
  266.2 3.6 %collective-permute-done.24.r6 = bf16[128,384]{1,0:T(8,128)(2,1)S(1)} collective-permute-done((bf16[128,384]{1,0:T(8,128)(2,1)S(1)}, bf16[128,384]{1,0:T(8,128)(2,1)S(1)}, u32[]{:S(2)}, u32[]{:S(2)}) %collective-permute-start.24) | collective-permute-done | bytes 98336 | tf_op jit(solution)/shard_map/ppermute | solution.py:610
  270.1 0.7 slice.71.own
  270.9 5.7 %shard_map.97 = (f32[128,576]{1,0:T(8,128)}, bf16[3584,128]{1,0:T(8,128)(2,1)}, bf16[3584,128]{1,0:T(8,128)(2,1)}) custom-call(s32[1]{0:T(128)} %bitcast.4.core, bf16[128,576]{1,0:T(8,128)(2,1)} %copy-done.6, bf16[128,576]{1,0:T(8,128)(2,1)} %get-tuple-element.121.dq, f32[128,384]{1,0:T(8,128)} %slice.71.own, bf16[128,384]{1,0:T(8,128)(2,1)} %copy-done.19, ...), custom_call_target="tpu_custom_call" | custom-call | flops 350000000 | bytes 10000000 | tf_op jit(solution)/shard_map/pallas_call | solution.py:70
  277.0 5.4 %shard_map.98.refs_0_ = bf16[14336,128]{1,0:T(8,128)(2,1)} custom-call(bf16[10752,128]{1,0:T(8,128)(2,1)S(1)} %copy-done, bf16[10752,128]{1,0:T(8,128)(2,1)} %collective-permute-done.28.got), custom_call_target="tpu_custom_call" | custom-call | bytes 8257536 | tf_op jit(solution)/shard_map/pallas_call | solution.py:648
  282.5 1.1 shard_map.99
  283.6 11.1 %all-to-all-start.1 = ((bf16[64,224,128]{2,1,0:T(8,128)(2,1)}), bf16[64,224,128]{2,1,0:T(8,128)(2,1)}, u32[]{:S(2)}, u32[]{:S(2)}) async-start(bf16[64,224,128]{2,1,0:T(8,128)(2,1)} %bitcast.28), calls=%async_computation.1 | async-start | bytes 7340032 | tf_op jit(solution)/shard_map/all_to_all | solution.py:664
  294.7 0.8 copy.39
  295.5 2.6 convert_reduce_fusion
  298.3 0.9 copy.40
  299.2 44.3 %all-to-all-done.1 = bf16[64,224,128]{2,1,0:T(8,128)(2,1)} async-done(((bf16[64,224,128]{2,1,0:T(8,128)(2,1)}), bf16[64,224,128]{2,1,0:T(8,128)(2,1)}, u32[]{:S(2)}, u32[]{:S(2)}) %all-to-all-start.1) | async-done | bytes 3670048 | tf_op jit(solution)/shard_map/all_to_all | solution.py:664
  343.5 2.6 convert_reduce_fusion.1
  346.3 0.9 pad_maximum_fusion.2
  (125 shorter events, 8.0 us)
Async XLA Ops:
  7.2 92.3 %all-gather.2.cloned.1.call-start = ((), (), s32[]{:S(2)}) async-start(), calls=%async_computation.2 | async-start | bytes 15851520 | tf_op jit(solution)/shard_map/all_gather | solution.py:694
  9.1 31.1 %collective-permute-start.8 = (s32[128]{0:T(128)}, s32[128]{0:T(128)S(1)}, u32[]{:S(2)}, u32[]{:S(2)}) collective-permute-start(s32[128]{0:T(128)} %param.7), channel_id=1, source_target_pairs={{0,2},{1,3},{2,4},{3,5},{4,6},{5,7},{6,8},{7,9},{8,10},{9,11},{10,... | collective-permute-start | bytes 1544 | tf_op jit(solution)/shard_map/ppermute | solution.py:610
  13.0 23.8 %collective-permute-start.7 = (s32[128]{0:T(128)}, s32[128]{0:T(128)S(1)}, u32[]{:S(2)}, u32[]{:S(2)}) collective-permute-start(s32[128]{0:T(128)} %param.7), channel_id=1, source_target_pairs={{0,4},{1,5},{2,6},{3,7},{4,8},{5,9},{6,10},{7,11},{8,12},{9,13},{1... | collective-permute-start | bytes 1544 | tf_op jit(solution)/shard_map/ppermute | solution.py:610
  16.0 18.8 %collective-permute-start.6 = (s32[128]{0:T(128)}, s32[128]{0:T(128)S(1)}, u32[]{:S(2)}, u32[]{:S(2)}) collective-permute-start(s32[128]{0:T(128)} %param.7), channel_id=1, source_target_pairs={{0,6},{1,7},{2,8},{3,9},{4,10},{5,11},{6,12},{7,13},{8,14},{9,15},... | collective-permute-start | bytes 1544 | tf_op jit(solution)/shard_map/ppermute | solution.py:610
  21.2 7.6 %collective-permute-start.5 = (s32[128]{0:T(128)}, s32[128]{0:T(128)S(1)}, u32[]{:S(2)}, u32[]{:S(2)}) collective-permute-start(s32[128]{0:T(128)} %param.7), channel_id=1, source_target_pairs={{0,8},{1,9},{2,10},{3,11},{4,12},{5,13},{6,14},{7,15},{8,16},{9,17... | collective-permute-start | bytes 1544 | tf_op jit(solution)/shard_map/ppermute | solution.py:610
  25.4 20.3 %copy-start.6 = (bf16[128,576]{1,0:T(8,128)(2,1)}, bf16[128,576]{1,0:T(8,128)(2,1)S(1)}, u32[]{:S(2)}) copy-start(bf16[128,576]{1,0:T(8,128)(2,1)S(1)} %copy.33.x_in) | copy-start | bytes 442372
  25.4 19.1 %collective-permute-start.3 = (bf16[128,576]{1,0:T(8,128)(2,1)S(1)}, bf16[128,576]{1,0:T(8,128)(2,1)S(1)}, u32[]{:S(2)}, u32[]{:S(2)}) collective-permute-start(bf16[128,576]{1,0:T(8,128)(2,1)S(1)} %copy.33.x_in), channel_id=1, source_target_pairs={{0,2},{1,3},{2,4},{3,5},{4,6},{5,7},{6,8},{7,9},{8,10},{9,11},{10,... | collective-permute-start | bytes 442376 | tf_op jit(solution)/shard_map/ppermute | solution.py:610
  28.8 15.6 %collective-permute-start.2 = (bf16[128,576]{1,0:T(8,128)(2,1)S(1)}, bf16[128,576]{1,0:T(8,128)(2,1)S(1)}, u32[]{:S(2)}, u32[]{:S(2)}) collective-permute-start(bf16[128,576]{1,0:T(8,128)(2,1)S(1)} %copy.33.x_in), channel_id=1, source_target_pairs={{0,4},{1,5},{2,6},{3,7},{4,8},{5,9},{6,10},{7,11},{8,12},{9,13},{1... | collective-permute-start | bytes 442376 | tf_op jit(solution)/shard_map/ppermute | solution.py:610
  34.8 9.5 %collective-permute-start.1 = (bf16[128,576]{1,0:T(8,128)(2,1)S(1)}, bf16[128,576]{1,0:T(8,128)(2,1)S(1)}, u32[]{:S(2)}, u32[]{:S(2)}) collective-permute-start(bf16[128,576]{1,0:T(8,128)(2,1)S(1)} %copy.33.x_in), channel_id=1, source_target_pairs={{0,6},{1,7},{2,8},{3,9},{4,10},{5,11},{6,12},{7,13},{8,14},{9,15},... | collective-permute-start | bytes 442376 | tf_op jit(solution)/shard_map/ppermute | solution.py:610
  36.8 7.2 %collective-permute-start = (bf16[128,576]{1,0:T(8,128)(2,1)S(1)}, bf16[128,576]{1,0:T(8,128)(2,1)S(1)}, u32[]{:S(2)}, u32[]{:S(2)}) collective-permute-start(bf16[128,576]{1,0:T(8,128)(2,1)S(1)} %copy.33.x_in), channel_id=1, source_target_pairs={{0,8},{1,9},{2,10},{3,11},{4,12},{5,13},{6,14},{7,15},{8,16},{9,17... | collective-permute-start | bytes 442376 | tf_op jit(solution)/shard_map/ppermute | solution.py:610
  41.0 2.0 collective-permute-start.9
  44.5 1.1 copy-start.7
  46.0 4.5 %collective-permute-start.4 = (bf16[512,576]{0,1:T(8,128)(2,1)S(1)}, bf16[512,576]{0,1:T(8,128)(2,1)S(1)}, u32[]{:S(2)}, u32[]{:S(2)}) collective-permute-start(bf16[512,576]{0,1:T(8,128)(2,1)S(1)} %copy.30), channel_id=1, source_target_pairs={{0,1},{1,0},{2,3},{3,2},{4,5},{5,4},{6,7},{7,6},{8,9},{9,8},{10,11... | collective-permute-start | bytes 1769480 | tf_op jit(solution)/shard_map/ppermute | solution.py:614
  49.1 58.9 %copy-start.4 = (f32[1152,128]{1,0:T(8,128)}, f32[1152,128]{1,0:T(8,128)S(1)}, u32[]{:S(2)}) copy-start(f32[1152,128]{1,0:T(8,128)S(1)} %get-tuple-element.189.cosine) | copy-start | bytes 1769476
  49.2 58.9 %copy-start.5 = (f32[1152,128]{1,0:T(8,128)}, f32[1152,128]{1,0:T(8,128)S(1)}, u32[]{:S(2)}) copy-start(f32[1152,128]{1,0:T(8,128)S(1)} %get-tuple-element.190.sine) | copy-start | bytes 1769476
  127.3 24.3 %copy-start.14 = (bf16[128,384]{1,0:T(8,128)(2,1)S(1)}, bf16[128,384]{1,0:T(8,128)(2,1)}, u32[]{:S(2)}) copy-start(bf16[128,384]{1,0:T(8,128)(2,1)} %get-tuple-element.85) | copy-start | bytes 294916
  127.3 24.3 %collective-permute-start.13 = (bf16[128,384]{1,0:T(8,128)(2,1)}, bf16[128,384]{1,0:T(8,128)(2,1)S(1)}, u32[]{:S(2)}, u32[]{:S(2)}) collective-permute-start(bf16[128,384]{1,0:T(8,128)(2,1)} %get-tuple-element.85), channel_id=1, source_target_pairs={{0,2},{1,3},{2,4},{3,5},{4,6},{5,7},{6,8},{7,9},{8,10},{9,11},{10,... | collective-permute-start | bytes 294920 | tf_op jit(solution)/shard_map/ppermute | solution.py:610
  130.6 20.9 %collective-permute-start.12 = (bf16[128,384]{1,0:T(8,128)(2,1)}, bf16[128,384]{1,0:T(8,128)(2,1)S(1)}, u32[]{:S(2)}, u32[]{:S(2)}) collective-permute-start(bf16[128,384]{1,0:T(8,128)(2,1)} %get-tuple-element.85), channel_id=1, source_target_pairs={{0,4},{1,5},{2,6},{3,7},{4,8},{5,9},{6,10},{7,11},{8,12},{9,13},{1... | collective-permute-start | bytes 294920 | tf_op jit(solution)/shard_map/ppermute | solution.py:610
  135.9 15.6 %collective-permute-start.11 = (bf16[128,384]{1,0:T(8,128)(2,1)}, bf16[128,384]{1,0:T(8,128)(2,1)S(1)}, u32[]{:S(2)}, u32[]{:S(2)}) collective-permute-start(bf16[128,384]{1,0:T(8,128)(2,1)} %get-tuple-element.85), channel_id=1, source_target_pairs={{0,6},{1,7},{2,8},{3,9},{4,10},{5,11},{6,12},{7,13},{8,14},{9,15},... | collective-permute-start | bytes 294920 | tf_op jit(solution)/shard_map/ppermute | solution.py:610
  138.4 13.1 %collective-permute-start.10 = (bf16[128,384]{1,0:T(8,128)(2,1)}, bf16[128,384]{1,0:T(8,128)(2,1)S(1)}, u32[]{:S(2)}, u32[]{:S(2)}) collective-permute-start(bf16[128,384]{1,0:T(8,128)(2,1)} %get-tuple-element.85), channel_id=1, source_target_pairs={{0,8},{1,9},{2,10},{3,11},{4,12},{5,13},{6,14},{7,15},{8,16},{9,17... | collective-permute-start | bytes 294920 | tf_op jit(solution)/shard_map/ppermute | solution.py:610
  151.5 0.9 copy-start.13
  151.6 2.1 copy-start.10
  151.7 2.0 collective-permute-start.14
  153.7 0.8 copy-start.23
  168.2 2.1 copy-start.9
  168.2 2.0 collective-permute-start.15
  170.5 25.6 %collective-permute-start.19 = (bf16[128,384]{1,0:T(8,128)(2,1)S(1)}, bf16[128,384]{1,0:T(8,128)(2,1)S(1)}, u32[]{:S(2)}, u32[]{:S(2)}) collective-permute-start(bf16[128,384]{1,0:T(8,128)(2,1)S(1)} %get-tuple-element.163), channel_id=1, source_target_pairs={{2,0},{3,1},{4,2},{5,3},{6,4},{7,5},{8,6},{9,7},{10,8},{11,9},{12,... | collective-permute-start | bytes 294920 | tf_op jit(solution)/shard_map/ppermute | solution.py:610
  173.8 22.3 %collective-permute-start.18 = (bf16[128,384]{1,0:T(8,128)(2,1)S(1)}, bf16[128,384]{1,0:T(8,128)(2,1)S(1)}, u32[]{:S(2)}, u32[]{:S(2)}) collective-permute-start(bf16[128,384]{1,0:T(8,128)(2,1)S(1)} %get-tuple-element.164), channel_id=1, source_target_pairs={{4,0},{5,1},{6,2},{7,3},{8,4},{9,5},{10,6},{11,7},{12,8},{13,9},{1... | collective-permute-start | bytes 294920 | tf_op jit(solution)/shard_map/ppermute | solution.py:610
  177.0 19.1 %collective-permute-start.17 = (bf16[128,384]{1,0:T(8,128)(2,1)S(1)}, bf16[128,384]{1,0:T(8,128)(2,1)S(1)}, u32[]{:S(2)}, u32[]{:S(2)}) collective-permute-start(bf16[128,384]{1,0:T(8,128)(2,1)S(1)} %get-tuple-element.165), channel_id=1, source_target_pairs={{6,0},{7,1},{8,2},{9,3},{10,4},{11,5},{12,6},{13,7},{14,8},{15,9},... | collective-permute-start | bytes 294920 | tf_op jit(solution)/shard_map/ppermute | solution.py:610
  179.0 17.1 %collective-permute-start.16 = (bf16[128,384]{1,0:T(8,128)(2,1)S(1)}, bf16[128,384]{1,0:T(8,128)(2,1)S(1)}, u32[]{:S(2)}, u32[]{:S(2)}) collective-permute-start(bf16[128,384]{1,0:T(8,128)(2,1)S(1)} %get-tuple-element.166), channel_id=1, source_target_pairs={{8,0},{9,1},{10,2},{11,3},{12,4},{13,5},{14,6},{15,7},{16,8},{17,9... | collective-permute-start | bytes 294920 | tf_op jit(solution)/shard_map/ppermute | solution.py:610
  196.1 1.3 copy-start.18
  196.1 1.2 copy-start.20
  196.1 1.2 copy-start.21
  196.1 1.2 copy-start.22
  196.1 7.4 %collective-permute-start.21 = (bf16[10752,128]{1,0:T(8,128)(2,1)}, bf16[10752,128]{1,0:T(8,128)(2,1)}, u32[]{:S(2)}, u32[]{:S(2)}) collective-permute-start(bf16[10752,128]{1,0:T(8,128)(2,1)} %get-tuple-element.116), channel_id=1, source_target_pairs={{0,1},{1,0},{2,3},{3,2},{4,5},{5,4},{6,7},{7,6},{8,9},{9,8},{10,11... | collective-permute-start | bytes 8257544 | tf_op jit(solution)/shard_map/ppermute | solution.py:614
  197.3 6.2 %copy-start.1 = (bf16[10752,128]{1,0:T(8,128)(2,1)S(1)}, bf16[10752,128]{1,0:T(8,128)(2,1)}, u32[]{:S(2)}) copy-start(bf16[10752,128]{1,0:T(8,128)(2,1)} %get-tuple-element.115.keep) | copy-start | bytes 8257540
  203.0 5.9 %collective-permute-start.20 = (bf16[3584,128]{1,0:T(8,128)(2,1)}, bf16[3584,128]{1,0:T(8,128)(2,1)S(1)}, u32[]{:S(2)}, u32[]{:S(2)}) collective-permute-start(bf16[3584,128]{1,0:T(8,128)(2,1)} %get-tuple-element.114), channel_id=1, source_target_pairs={{0,1},{1,0},{2,3},{3,2},{4,5},{5,4},{6,7},{7,6},{8,9},{9,8},{10,11... | collective-permute-start | bytes 2752520 | tf_op jit(solution)/shard_map/ppermute | solution.py:614
  203.5 5.4 %copy-start.3 = (bf16[3584,128]{1,0:T(8,128)(2,1)S(1)}, bf16[3584,128]{1,0:T(8,128)(2,1)}, u32[]{:S(2)}) copy-start(bf16[3584,128]{1,0:T(8,128)(2,1)} %get-tuple-element.113.keep) | copy-start | bytes 2752516
  210.1 60.8 %all-to-all-start = ((bf16[64,224,128]{2,1,0:T(8,128)(2,1)}), bf16[64,224,128]{2,1,0:T(8,128)(2,1)}, u32[]{:S(2)}, u32[]{:S(2)}) async-start(bf16[64,224,128]{2,1,0:T(8,128)(2,1)} %bitcast.27), calls=%async_computation | async-start | bytes 7340032 | tf_op jit(solution)/shard_map/all_to_all | solution.py:664
  231.5 2.1 copy-start.8
  231.5 2.0 collective-permute-start.22
  233.7 32.3 %collective-permute-start.26 = (bf16[128,384]{1,0:T(8,128)(2,1)S(1)}, bf16[128,384]{1,0:T(8,128)(2,1)S(1)}, u32[]{:S(2)}, u32[]{:S(2)}) collective-permute-start(bf16[128,384]{1,0:T(8,128)(2,1)S(1)} %get-tuple-element.159), channel_id=1, source_target_pairs={{2,0},{3,1},{4,2},{5,3},{6,4},{7,5},{8,6},{9,7},{10,8},{11,9},{12,... | collective-permute-start | bytes 294920 | tf_op jit(solution)/shard_map/ppermute | solution.py:610
  236.2 30.0 %collective-permute-start.25 = (bf16[128,384]{1,0:T(8,128)(2,1)S(1)}, bf16[128,384]{1,0:T(8,128)(2,1)S(1)}, u32[]{:S(2)}, u32[]{:S(2)}) collective-permute-start(bf16[128,384]{1,0:T(8,128)(2,1)S(1)} %get-tuple-element.160), channel_id=1, source_target_pairs={{4,0},{5,1},{6,2},{7,3},{8,4},{9,5},{10,6},{11,7},{12,8},{13,9},{1... | collective-permute-start | bytes 294920 | tf_op jit(solution)/shard_map/ppermute | solution.py:610
  240.5 29.4 %collective-permute-start.24 = (bf16[128,384]{1,0:T(8,128)(2,1)S(1)}, bf16[128,384]{1,0:T(8,128)(2,1)S(1)}, u32[]{:S(2)}, u32[]{:S(2)}) collective-permute-start(bf16[128,384]{1,0:T(8,128)(2,1)S(1)} %get-tuple-element.161), channel_id=1, source_target_pairs={{6,0},{7,1},{8,2},{9,3},{10,4},{11,5},{12,6},{13,7},{14,8},{15,9},... | collective-permute-start | bytes 294920 | tf_op jit(solution)/shard_map/ppermute | solution.py:610
  244.1 25.7 %collective-permute-start.23 = (bf16[128,384]{1,0:T(8,128)(2,1)S(1)}, bf16[128,384]{1,0:T(8,128)(2,1)S(1)}, u32[]{:S(2)}, u32[]{:S(2)}) collective-permute-start(bf16[128,384]{1,0:T(8,128)(2,1)S(1)} %get-tuple-element.162), channel_id=1, source_target_pairs={{8,0},{9,1},{10,2},{11,3},{12,4},{13,5},{14,6},{15,7},{16,8},{17,9... | collective-permute-start | bytes 294920 | tf_op jit(solution)/shard_map/ppermute | solution.py:610
  266.1 4.8 %copy-start.15 = (bf16[128,384]{1,0:T(8,128)(2,1)}, bf16[128,384]{1,0:T(8,128)(2,1)S(1)}, u32[]{:S(2)}) copy-start(bf16[128,384]{1,0:T(8,128)(2,1)S(1)} %collective-permute-done.26.r2) | copy-start | bytes 294916
  266.2 4.6 %copy-start.16 = (bf16[128,384]{1,0:T(8,128)(2,1)}, bf16[128,384]{1,0:T(8,128)(2,1)S(1)}, u32[]{:S(2)}) copy-start(bf16[128,384]{1,0:T(8,128)(2,1)S(1)} %collective-permute-done.25.r4) | copy-start | bytes 294916
  269.9 1.0 copy-start.17
  269.9 1.0 copy-start.19
  269.9 7.2 %collective-permute-start.28 = (bf16[10752,128]{1,0:T(8,128)(2,1)}, bf16[10752,128]{1,0:T(8,128)(2,1)}, u32[]{:S(2)}, u32[]{:S(2)}) collective-permute-start(bf16[10752,128]{1,0:T(8,128)(2,1)} %get-tuple-element.147), channel_id=1, source_target_pairs={{0,1},{1,0},{2,3},{3,2},{4,5},{5,4},{6,7},{7,6},{8,9},{9,8},{10,11... | collective-permute-start | bytes 8257544 | tf_op jit(solution)/shard_map/ppermute | solution.py:614
  270.9 6.2 %copy-start = (bf16[10752,128]{1,0:T(8,128)(2,1)S(1)}, bf16[10752,128]{1,0:T(8,128)(2,1)}, u32[]{:S(2)}) copy-start(bf16[10752,128]{1,0:T(8,128)(2,1)} %get-tuple-element.146.keep) | copy-start | bytes 8257540
  276.5 5.9 %collective-permute-start.27 = (bf16[3584,128]{1,0:T(8,128)(2,1)}, bf16[3584,128]{1,0:T(8,128)(2,1)S(1)}, u32[]{:S(2)}, u32[]{:S(2)}) collective-permute-start(bf16[3584,128]{1,0:T(8,128)(2,1)} %get-tuple-element.145), channel_id=1, source_target_pairs={{0,1},{1,0},{2,3},{3,2},{4,5},{5,4},{6,7},{7,6},{8,9},{9,8},{10,11... | collective-permute-start | bytes 2752520 | tf_op jit(solution)/shard_map/ppermute | solution.py:614
  277.0 5.4 %copy-start.2 = (bf16[3584,128]{1,0:T(8,128)(2,1)S(1)}, bf16[3584,128]{1,0:T(8,128)(2,1)}, u32[]{:S(2)}) copy-start(bf16[3584,128]{1,0:T(8,128)(2,1)} %get-tuple-element.144.keep) | copy-start | bytes 2752516
  283.6 11.1 %copy-start.12 = (bf16[128,576]{1,0:T(8,128)(2,1)S(1)}, bf16[128,576]{1,0:T(8,128)(2,1)}, u32[]{:S(2)}) copy-start(bf16[128,576]{1,0:T(8,128)(2,1)} %get-tuple-element.152) | copy-start | bytes 442372
  283.6 59.9 %all-to-all-start.1 = ((bf16[64,224,128]{2,1,0:T(8,128)(2,1)}), bf16[64,224,128]{2,1,0:T(8,128)(2,1)}, u32[]{:S(2)}, u32[]{:S(2)}) async-start(bf16[64,224,128]{2,1,0:T(8,128)(2,1)} %bitcast.28), calls=%async_computation.1 | async-start | bytes 7340032 | tf_op jit(solution)/shard_map/all_to_all | solution.py:664
  295.5 2.8 copy-start.11
Sparse Core Ops, SparseCore 0:
  11.6 87.8 all-gather.1
